TPU v7x, 256 devices: a whole 4x4x8 slice. The times are simulated.
256 devices in a mesh: quad: 16 (over z_lo, x), sx: 4 (over z_hi, core), sy: 4 (over y).
Axes of the slice: x: 4, y: 4, z: 8 (z_hi: 2, z_lo: 4; z = z_hi * 4 + z_lo), core: 2. Of those that a mesh axis runs over, the one named last changes fastest.
Arguments:
- probes: bfloat16 [64, 64, 32, 128], P(None, 'sx', 'sy'), may hold values from -6 to 6
- quad_index: int32 [16], P('quad'), may hold values from 0 to 63
- region_label: int32 [64, 64, 32], replicated, may hold values from 0 to 7
- gain_label: int32 [64, 64, 32], replicated, may hold values from 0 to 7
- region_eps: float32 [8], replicated, may hold values from 1 to 3
- gain_rate: float32 [8], replicated, may hold values from 1 to 8
Outputs:
- moment0: float32 [64, 64, 32, 128], P('quad', 'sx', 'sy')
- moment1: float32 [64, 64, 32, 128], P('quad', 'sx', 'sy')
- projections: float32 [2, 2, 64, 64], replicated
All inputs are finite; a program needn't handle non-finite values.
Results may differ from a plain program's by a relative error of at most 0.0003.
Values may be sent and summed in bfloat16 or wider, within the bound.
No kernel may reach another device: no remote copies, remote signals or barrier semaphores. Data moves between devices by JAX's collectives and lax.ppermute only.
A program may use at most 128 MiB of HBM per device.

v0:
```python
import math

import jax
import jax.numpy as jnp
from jax import lax
from jax.sharding import PartitionSpec as P

QUAD = 16


def with_halo(block, sides, width):
    for axis, dim in sides:
        count = lax.axis_size(axis)
        forward = [(i, i + 1) for i in range(count - 1)]
        backward = [(target, source) for source, target in forward]
        low = lax.ppermute(
            lax.slice_in_dim(block, block.shape[dim] - width, None, axis=dim), axis, forward
        )
        high = lax.ppermute(lax.slice_in_dim(block, 0, width, axis=dim), axis, backward)
        block = jnp.concatenate([low, block, high], axis=dim)
    return block


def multiply_by(coef_real, coef_imag, field):
    half = field.shape[-1] // 2
    field_real = field[..., :half]
    field_imag = field[..., half:]
    return jnp.concatenate(
        [
            coef_real * field_real - coef_imag * field_imag,
            coef_real * field_imag + coef_imag * field_real,
        ],
        axis=-1,
    )


def plane_sum(padded):
    total = padded[:, :, 2:, 1:-1] + padded[:, :, :-2, 1:-1]
    return total + padded[:, :, 1:-1, 2:] + padded[:, :, 1:-1, :-2]


def depth_sum(field):
    padded = jnp.pad(field, ((0, 0), (1, 1), (0, 0), (0, 0), (0, 0)))
    return padded[:, 2:] + padded[:, :-2]


def lookup(table, labels):
    levels = jnp.arange(table.shape[0], dtype=jnp.int32)
    return jnp.sum(jnp.where(labels[..., None] == levels, table, 0.0), axis=-1)[..., None]


def inverse_of(mat_real, mat_imag, node_real, node_imag):
    diag_real = 6.0 + node_real * mat_real - node_imag * mat_imag
    diag_imag = node_real * mat_imag + node_imag * mat_real
    modulus = diag_real * diag_real + diag_imag * diag_imag
    return (diag_real / modulus, -diag_imag / modulus)


def assemble(cross, half):
    blocks = []
    for moment in range(2):
        first_col = 2 * half * moment
        real_cols = cross[:, first_col : first_col + half]
        imag_cols = cross[:, first_col + half : first_col + 2 * half]
        blocks.append(
            jnp.stack([real_cols[:half] + imag_cols[half:], imag_cols[:half] - real_cols[half:]])
        )
    return jnp.stack(blocks)


def local_cross(left, right):
    columns = left.shape[-1]
    return lax.dot_general(
        left.reshape(-1, columns),
        right.reshape(-1, 2 * columns),
        (((0,), (0,)), ((), ())),
        precision=lax.Precision.HIGHEST,
        preferred_element_type=jnp.float32,
    )


def body(probes, quad_index, region_label, gain_label, region_eps, gain_rate):
    depth_cells, cells_x, cells_y, columns = probes.shape
    start_x = lax.axis_index("sx") * cells_x
    start_y = lax.axis_index("sy") * cells_y
    angle_node = 2.0 * math.pi * (quad_index.astype(jnp.float32) + 0.5) / (4 * QUAD)
    angle_node = angle_node[:, None, None, None, None]
    weight_real = jnp.cos(angle_node)
    weight_imag = jnp.sin(angle_node)
    node_real = 2.0 + weight_real
    source = probes.astype(jnp.float32)[None]
    region_block = lax.dynamic_slice(
        region_label, (0, start_x, start_y), (depth_cells, cells_x, cells_y)
    )
    gain_block = lax.dynamic_slice(
        gain_label, (0, start_x, start_y), (depth_cells, cells_x, cells_y)
    )
    inverse_real, inverse_imag = inverse_of(
        lookup(region_eps, region_block), lookup(gain_rate, gain_block), node_real, weight_imag
    )
    iterate = multiply_by(inverse_real, inverse_imag, source)
    for sweep in range(2):
        padded = with_halo(iterate, (("sx", 2), ("sy", 3)), 1)
        iterate = multiply_by(
            inverse_real, inverse_imag, source + plane_sum(padded) + depth_sum(iterate)
        )
    scaled_real = weight_real * node_real - weight_imag * weight_imag
    scaled_imag = weight_real * weight_imag + weight_imag * node_real
    first = jnp.sum(multiply_by(weight_real, weight_imag, iterate), axis=0)
    second = jnp.sum(multiply_by(scaled_real, scaled_imag, iterate), axis=0)
    both = jnp.concatenate([first, second], axis=-1)
    reduced = lax.psum_scatter(both, "quad", scatter_dimension=0, tiled=True)
    slab_rows = reduced.shape[0]
    start_z = lax.axis_index("quad") * slab_rows
    slab_source = lax.dynamic_slice_in_dim(probes, start_z, slab_rows, 0).astype(jnp.float32)
    summed = lax.psum(local_cross(slab_source, reduced), ("quad", "sx", "sy"))
    cells_total = depth_cells * cells_x * cells_y * lax.axis_size("sx") * lax.axis_size("sy")
    projections = assemble(summed, columns // 2) / cells_total
    return (reduced[..., :columns], reduced[..., columns:], projections)


def solution(mesh):
    placed = (P(None, "sx", "sy", None), P("quad"), P(), P(), P(), P())
    return jax.shard_map(
        body,
        mesh=mesh,
        in_specs=placed,
        out_specs=(P("quad", "sx", "sy", None), P("quad", "sx", "sy", None), P()),
        check_vma=False,
    )
```

profile of v0, /device:TPU:1, one launch (start us, length us, event | category | flops | bytes accessed | tf_op | source)
XLA Modules:
  0.0 496.0 jit_solution(4955377792394716702)
XLA Ops:
  8.2 1.2 constant_dynamic-slice_fusion.1
  9.4 0.1 copy.14
  9.5 0.1 copy.13
  9.7 0.9 select_reduce_fusion
  10.6 0.9 select_reduce_fusion.1
  11.6 1.1 copy.15
  12.6 1.0 copy.16
  13.7 0.5 bitcast_convert_fusion
  14.2 0.5 copy-done.3
  14.7 0.2 copy-done.4
  14.9 3.8 multiply_add_fusion.4
  18.7 0.2 fusion.14
  18.9 5.1 %collective-permute-start = (f32[1,64,1,8,128]{4,3,2,1,0:T(8,128)S(1)}, f32[1,64,1,8,128]{4,3,2,1,0:T(8,128)S(1)}, u32[]{:S(2)}, u32[]{:S(2)}) collective-permute-start(f32[1,64,1,8,128]{4,3,2,1,0:T(8,128)S(1)} %get-tuple-element.16), channel_id=1, source_target_pairs={{4,0},{8,4},{12,8},{5,1},{9,5},{13,9},{6,2},{10,6},{14,10},{7,3},{... | collective-permute-start | bytes 786440 | tf_op jit(solution)/shard_map/ppermute | solution.py:19
  24.1 7.0 %collective-permute-start.1 = (f32[1,64,1,8,128]{4,3,2,1,0:T(8,128)S(1)}, f32[1,64,1,8,128]{4,3,2,1,0:T(8,128)S(1)}, u32[]{:S(2)}, u32[]{:S(2)}) collective-permute-start(f32[1,64,1,8,128]{4,3,2,1,0:T(8,128)S(1)} %get-tuple-element.15), channel_id=1, source_target_pairs={{0,4},{4,8},{8,12},{1,5},{5,9},{9,13},{2,6},{6,10},{10,14},{3,7},{... | collective-permute-start | bytes 786440 | tf_op jit(solution)/shard_map/ppermute | solution.py:16
  31.1 2.2 collective-permute-done
  33.3 2.9 collective-permute-done.1
  36.2 2.4 pad_maximum_fusion.34
  38.6 1.3 collective-permute-start.2
  39.9 4.9 collective-permute-start.3
  44.8 3.1 pad_maximum_fusion.25
  47.9 1.4 collective-permute-done.2
  49.3 1.4 collective-permute-done.3
  50.7 13.2 %fusion.7 = f32[1,64,16,8,128]{4,3,2,1,0:T(8,128)} fusion(f32[1,64,18,1,128]{4,3,2,1,0:T(1,128)} %collective-permute-done.3, f32[1,64,1,8,128]{4,3,2,1,0:T(8,128)S(1)} %collective-permute-done, f32[1,64,1,8,128]{4,3,2,1,0:T(8,128)} %copy-done.6, f32[1,64,16,8,64]{4,3,2,1,0:T(8,128)S(1)} %get-tuple-element.19, f32[1,64,16,8,64]{4,3,2,1,0:T(8,128)} %copy-done.1, ...), kind=kLoop, calls=%fused_computation.21 | loop fusion | flops 19922944 | bytes 16384000 | tf_op jit(solution)/shard_map/add | solution.py:105
  63.9 7.1 %multiply_add_fusion.3 = (f32[1,64,16,8,64]{4,3,2,1,0:T(8,128)S(1)}, f32[1,64,16,8,64]{4,3,2,1,0:T(8,128)S(1)}) fusion(f32[1,64,16,8,128]{4,3,2,1,0:T(8,128)} %fusion.7, f32[64,16,8]{2,1,0:T(8,128)} %copy.16, f32[64,16,8]{2,1,0:T(8,128)} %copy.15), kind=kLoop, calls=%fused_computation.43 | loop fusion | flops 3145728 | bytes 8454144 | tf_op jit(solution)/shard_map/add | solution.py:31
  71.0 0.2 fusion.12
  71.2 1.9 collective-permute-start.4
  73.1 9.5 %collective-permute-start.5 = (f32[1,64,1,8,128]{4,3,2,1,0:T(8,128)S(1)}, f32[1,64,1,8,128]{4,3,2,1,0:T(8,128)S(1)}, u32[]{:S(2)}, u32[]{:S(2)}) collective-permute-start(f32[1,64,1,8,128]{4,3,2,1,0:T(8,128)S(1)} %get-tuple-element.13), channel_id=1, source_target_pairs={{0,4},{4,8},{8,12},{1,5},{5,9},{9,13},{2,6},{6,10},{10,14},{3,7},{... | collective-permute-start | bytes 786440 | tf_op jit(solution)/shard_map/ppermute | solution.py:16
  82.7 2.2 collective-permute-done.4
  84.9 2.1 collective-permute-done.5
  87.0 2.4 pad_maximum_fusion.30
  89.4 1.3 collective-permute-start.6
  90.7 5.7 %collective-permute-start.7 = (f32[1,64,18,1,128]{4,3,2,1,0:T(1,128)S(1)}, f32[1,64,18,1,128]{4,3,2,1,0:T(1,128)}, u32[]{:S(2)}, u32[]{:S(2)}) collective-permute-start(f32[1,64,18,1,128]{4,3,2,1,0:T(1,128)S(1)} %get-tuple-element.7), channel_id=1, source_target_pairs={{0,1},{1,2},{2,3},{4,5},{5,6},{6,7},{8,9},{9,10},{10,11},{12,13},{... | collective-permute-start | bytes 1769480 | tf_op jit(solution)/shard_map/ppermute | solution.py:16
  96.4 3.1 pad_maximum_fusion.26
  99.5 1.4 collective-permute-done.6
  101.0 1.4 collective-permute-done.7
  102.4 13.2 %fusion.2 = f32[1,64,16,8,128]{4,3,2,1,0:T(8,128)} fusion(f32[1,64,18,1,128]{4,3,2,1,0:T(1,128)} %collective-permute-done.7, f32[1,64,1,8,128]{4,3,2,1,0:T(8,128)S(1)} %collective-permute-done.4, f32[1,64,1,8,128]{4,3,2,1,0:T(8,128)} %copy-done.5, f32[1,64,16,8,64]{4,3,2,1,0:T(8,128)S(1)} %get-tuple-element.17, f32[1,64,16,8,64]{4,3,2,1,0:T(8,128)} %copy-done, ...), kind=kLoop, calls=%fused_computation.4 | loop fusion | flops 19922944 | bytes 16384000 | tf_op jit(solution)/shard_map/add | solution.py:105
  115.6 6.9 %multiply_subtract_fusion.1 = (f32[1,64,16,8,64]{4,3,2,1,0:T(8,128)S(1)}, f32[1,64,16,8,64]{4,3,2,1,0:T(8,128)S(1)}, f32[1,64,16,8,64]{4,3,2,1,0:T(8,128)S(1)}) fusion(f32[]{:T(128)} %bitcast.3, f32[]{:T(128)} %bitcast, f32[1,64,16,8,128]{4,3,2,1,0:T(8,128)} %fusion.2, f32[64,16,8]{2,1,0:T(8,128)} %copy.16, f32[64,16,8]{2,1,0:T(8,128)} %copy.15), kind=kLoop, calls=%fused_computation.40 | loop fusion | flops 4718592 | bytes 10551304 | tf_op jit(solution)/shard_map/sub | solution.py:30
  122.5 2.4 multiply_add_fusion.1
  124.9 1.1 maximum_bitcast_fusion
  126.1 1.1 maximum_bitcast_fusion.1
  127.2 4.0 pad_maximum_fusion
  131.2 0.0 all-reduce.4.cloned.1.call-start
  131.3 104.4 %reduce-scatter.2.cloned.1.call-done = f32[4,16,8,256]{3,2,1,0:T(8,128)} async-done(((f32[64,16,8,256]{3,2,1,0:T(8,128)}), f32[4,16,8,256]{3,2,1,0:T(8,128)}) %reduce-scatter.2.cloned.1.call-update) | async-done | bytes 524304 | tf_op jit(solution)/shard_map/reduce_scatter | solution.py:112
  235.6 2.2 convolution_bitcast_fusion
  237.8 1.9 fusion.21
  239.7 247.8 %all-reduce.4.cloned.1.call-done = f32[128,256]{1,0:T(8,128)} async-done(((f32[128,256]{1,0:T(8,128)}), f32[128,256]{1,0:T(8,128)}) %all-reduce.4.cloned.1.call-update) | async-done | bytes 131088 | tf_op jit(solution)/shard_map/psum | solution.py:116
  487.5 1.0 fusion.20
  488.5 0.7 maximum_multiply_fusion
  (19 shorter events, 0.2 us)
Async XLA Ops:
  7.2 6.5 %copy-start.2 = (bf16[64,16,8,128]{3,2,1,0:T(8,128)(2,1)S(1)}, bf16[64,16,8,128]{3,2,1,0:T(8,128)(2,1)}, u32[]{:S(2)}) copy-start(bf16[64,16,8,128]{3,2,1,0:T(8,128)(2,1)} %param.6) | copy-start | bytes 6291460
  7.2 228.5 %reduce-scatter.2.cloned.1.call-start = ((), (), s32[]{:S(2)}) async-start(), calls=%async_computation.1 | async-start | bytes 8912896 | tf_op jit(solution)/shard_map/reduce_scatter | solution.py:112
  13.7 1.0 copy-start.3
  13.7 1.2 copy-start.4
  18.7 26.1 %copy-start.1 = (f32[1,64,16,8,64]{4,3,2,1,0:T(8,128)}, f32[1,64,16,8,64]{4,3,2,1,0:T(8,128)S(1)}, u32[]{:S(2)}) copy-start(f32[1,64,16,8,64]{4,3,2,1,0:T(8,128)S(1)} %get-tuple-element.20) | copy-start | bytes 6291460
  18.9 14.4 %collective-permute-start = (f32[1,64,1,8,128]{4,3,2,1,0:T(8,128)S(1)}, f32[1,64,1,8,128]{4,3,2,1,0:T(8,128)S(1)}, u32[]{:S(2)}, u32[]{:S(2)}) collective-permute-start(f32[1,64,1,8,128]{4,3,2,1,0:T(8,128)S(1)} %get-tuple-element.16), channel_id=1, source_target_pairs={{4,0},{8,4},{12,8},{5,1},{9,5},{13,9},{6,2},{10,6},{14,10},{7,3},{... | collective-permute-start | bytes 786440 | tf_op jit(solution)/shard_map/ppermute | solution.py:19
  24.1 12.1 %collective-permute-start.1 = (f32[1,64,1,8,128]{4,3,2,1,0:T(8,128)S(1)}, f32[1,64,1,8,128]{4,3,2,1,0:T(8,128)S(1)}, u32[]{:S(2)}, u32[]{:S(2)}) collective-permute-start(f32[1,64,1,8,128]{4,3,2,1,0:T(8,128)S(1)} %get-tuple-element.15), channel_id=1, source_target_pairs={{0,4},{4,8},{8,12},{1,5},{5,9},{9,13},{2,6},{6,10},{10,14},{3,7},{... | collective-permute-start | bytes 786440 | tf_op jit(solution)/shard_map/ppermute | solution.py:16
  36.2 2.4 copy-start.6
  38.6 10.7 %collective-permute-start.2 = (f32[1,64,18,1,128]{4,3,2,1,0:T(1,128)S(1)}, f32[1,64,18,1,128]{4,3,2,1,0:T(1,128)}, u32[]{:S(2)}, u32[]{:S(2)}) collective-permute-start(f32[1,64,18,1,128]{4,3,2,1,0:T(1,128)S(1)} %get-tuple-element.8), channel_id=1, source_target_pairs={{1,0},{2,1},{3,2},{5,4},{6,5},{7,6},{9,8},{10,9},{11,10},{13,12},{... | collective-permute-start | bytes 1769480 | tf_op jit(solution)/shard_map/ppermute | solution.py:19
  39.9 10.8 %collective-permute-start.3 = (f32[1,64,18,1,128]{4,3,2,1,0:T(1,128)S(1)}, f32[1,64,18,1,128]{4,3,2,1,0:T(1,128)}, u32[]{:S(2)}, u32[]{:S(2)}) collective-permute-start(f32[1,64,18,1,128]{4,3,2,1,0:T(1,128)S(1)} %get-tuple-element.9), channel_id=1, source_target_pairs={{0,1},{1,2},{2,3},{4,5},{5,6},{6,7},{8,9},{9,10},{10,11},{12,13},{... | collective-permute-start | bytes 1769480 | tf_op jit(solution)/shard_map/ppermute | solution.py:16
  71.0 25.4 %copy-start = (f32[1,64,16,8,64]{4,3,2,1,0:T(8,128)}, f32[1,64,16,8,64]{4,3,2,1,0:T(8,128)S(1)}, u32[]{:S(2)}) copy-start(f32[1,64,16,8,64]{4,3,2,1,0:T(8,128)S(1)} %get-tuple-element.18) | copy-start | bytes 6291460
  71.2 13.7 %collective-permute-start.4 = (f32[1,64,1,8,128]{4,3,2,1,0:T(8,128)S(1)}, f32[1,64,1,8,128]{4,3,2,1,0:T(8,128)S(1)}, u32[]{:S(2)}, u32[]{:S(2)}) collective-permute-start(f32[1,64,1,8,128]{4,3,2,1,0:T(8,128)S(1)} %get-tuple-element.14), channel_id=1, source_target_pairs={{4,0},{8,4},{12,8},{5,1},{9,5},{13,9},{6,2},{10,6},{14,10},{7,3},{... | collective-permute-start | bytes 786440 | tf_op jit(solution)/shard_map/ppermute | solution.py:19
  73.1 13.8 %collective-permute-start.5 = (f32[1,64,1,8,128]{4,3,2,1,0:T(8,128)S(1)}, f32[1,64,1,8,128]{4,3,2,1,0:T(8,128)S(1)}, u32[]{:S(2)}, u32[]{:S(2)}) collective-permute-start(f32[1,64,1,8,128]{4,3,2,1,0:T(8,128)S(1)} %get-tuple-element.13), channel_id=1, source_target_pairs={{0,4},{4,8},{8,12},{1,5},{5,9},{9,13},{2,6},{6,10},{10,14},{3,7},{... | collective-permute-start | bytes 786440 | tf_op jit(solution)/shard_map/ppermute | solution.py:16
  87.0 2.4 copy-start.5
  89.4 11.6 %collective-permute-start.6 = (f32[1,64,18,1,128]{4,3,2,1,0:T(1,128)S(1)}, f32[1,64,18,1,128]{4,3,2,1,0:T(1,128)}, u32[]{:S(2)}, u32[]{:S(2)}) collective-permute-start(f32[1,64,18,1,128]{4,3,2,1,0:T(1,128)S(1)} %get-tuple-element.6), channel_id=1, source_target_pairs={{1,0},{2,1},{3,2},{5,4},{6,5},{7,6},{9,8},{10,9},{11,10},{13,12},{... | collective-permute-start | bytes 1769480 | tf_op jit(solution)/shard_map/ppermute | solution.py:19
  90.7 11.7 %collective-permute-start.7 = (f32[1,64,18,1,128]{4,3,2,1,0:T(1,128)S(1)}, f32[1,64,18,1,128]{4,3,2,1,0:T(1,128)}, u32[]{:S(2)}, u32[]{:S(2)}) collective-permute-start(f32[1,64,18,1,128]{4,3,2,1,0:T(1,128)S(1)} %get-tuple-element.7), channel_id=1, source_target_pairs={{0,1},{1,2},{2,3},{4,5},{5,6},{6,7},{8,9},{9,10},{10,11},{12,13},{... | collective-permute-start | bytes 1769480 | tf_op jit(solution)/shard_map/ppermute | solution.py:16
  131.2 356.3 %all-reduce.4.cloned.1.call-start = ((), (), s32[]{:S(2)}) async-start(), calls=%async_computation.2 | async-start | bytes 262144 | tf_op jit(solution)/shard_map/psum | solution.py:116
Sparse Core Ops, SparseCore 0:
  131.3 104.2 reduce-scatter.1
  241.7 245.7 all-reduce.3
where the time goes:
time: 497 us; the launch traced here: 496 us
  waiting for transfers between devices  367 us (74%)
  other arithmetic  68.4 us (14%)
  starting transfers between devices  36.9 us (7%)
  between operations  15.2 us (3%)
  local copies, waits for them, and re-layouts  6.18 us (1%)
    psum x1, waiting for transfers between devices, body(): summed = lax.psum(local_cross(slab_source, reduced), ('quad', 'sx', 'sy'))  248 us
    reduce_scatter x1, waiting for transfers between devices, body(): reduced = lax.psum_scatter(both, 'quad', scatter_dimension=0, tiled=True)  104 us
    ppermute x4, starting transfers between devices, with_halo(): lax.ppermute(lax.slice_in_dim(block, block.shape[dim] - width, None, axis...  27.1 us
    add x2, other arithmetic, body(): source + plane_sum(padded) + depth_sum(iterate)  26.4 us
    add x3, other arithmetic, multiply_by(): coef_real * field_imag + coef_imag * field_real  13.3 us
  transfers between devices with their start and end apart: 10, of which 10 were waited for; matrix products, arithmetic and copies ran while one was open for 2% of the time, Pallas kernels for 0%

commit v1 on v0

v1 whole, which is shorter than its diff:
```python
import functools
import math

import jax
import jax.numpy as jnp
import numpy as np
from jax import lax
from jax.experimental import pallas as pl
from jax.experimental.pallas import tpu as pltpu
from jax.sharding import PartitionSpec as P

QUAD = 16
SLAB = 4
CX = 16
CY = 8
LANES = CX * CY
OUTSIDE = 64

OFFSETS = sorted(
    [(dx, dy) for dx in range(-2, 3) for dy in range(-2, 3) if abs(dx) + abs(dy) <= 2],
    key=lambda o: (abs(o[0]) + abs(o[1]), o),
)
REACH = {0: 13, 1: 5, 2: 1}
TAPS = [(dz, off) for dz in range(-2, 3) for off in range(REACH[abs(dz)])]
TAP_AT = {(dz,) + OFFSETS[off]: i for i, (dz, off) in enumerate(TAPS)}
UNITS = [(1, 0, 0), (-1, 0, 0), (0, 1, 0), (0, -1, 0), (0, 0, 1), (0, 0, -1)]
WIDE = len(OFFSETS) * LANES


def selector(cells):
    row_of = {cell: row for row, cell in enumerate(cells) if cell is not None}
    pick = np.zeros((256, WIDE), np.float32)
    for o, (dx, dy) in enumerate(OFFSETS):
        for x in range(CX):
            for y in range(CY):
                row = row_of.get((x + dx, y + dy))
                if row is not None:
                    pick[row, o * LANES + x * CY + y] = 1.0
    return pick.astype(jnp.bfloat16)


def source_cells():
    cells = [(x, y) for x in range(CX) for y in range(CY)]
    cells += [(x, y) for x in range(CX) for y in (-2, -1)]
    cells += [(x, y) for x in range(CX) for y in (CY, CY + 1)]
    for xs in ((-2, -1), (CX, CX + 1)):
        cells += [(x, y) for x in xs for y in range(CY)]
        cells += [(x, y) for x in xs for y in (-2, -1)]
        cells += [(x, y) for x in xs for y in (CY, CY + 1)]
        cells += [None] * 8
    return cells


def window_cells():
    return [(x, y) for x in range(-2, CX + 2) for y in range(-2, CY + 2)]


def material_kernel(eps_ref, gain_ref, code_ref, pick_ref, real_ref, imag_ref, inside_ref):
    codes = jnp.dot(code_ref[...], pick_ref[...], preferred_element_type=jnp.float32)
    for t, (dz, off) in enumerate(TAPS):
        row = (dz + 2) * 8
        code = codes[row : row + 8, off * LANES : (off + 1) * LANES].astype(jnp.int32)
        region = lax.shift_right_logical(code, 3)
        level = code & 7
        real = jnp.zeros((8, LANES), jnp.float32)
        imag = jnp.zeros((8, LANES), jnp.float32)
        for value in range(8):
            real = jnp.where(region == value, eps_ref[value], real)
            imag = jnp.where(level == value, gain_ref[value], imag)
        real_ref[t] = real
        imag_ref[t] = imag
        inside_ref[t] = jnp.where(code < OUTSIDE, 1.0, 0.0)


def cmul(a, b):
    return (a[0] * b[0] - a[1] * b[1], a[0] * b[1] + a[1] * b[0])


def cadd(a, b):
    return (a[0] + b[0], a[1] + b[1])


def moment_kernel(
    weight_ref,
    real_ref,
    imag_ref,
    inside_ref,
    own_ref,
    ylo_ref,
    yhi_ref,
    xlo_ref,
    xhi_ref,
    pick_ref,
    moments_ref,
    cross_ref,
    shifted,
    coef,
):
    for plane in range(SLAB + 4):
        reach = 13 if 2 <= plane < SLAB + 2 else (5 if plane in (1, SLAB + 2) else 1)
        rows = jnp.concatenate(
            [own_ref[plane], ylo_ref[plane], yhi_ref[plane], xlo_ref[plane], xhi_ref[plane]], axis=0
        )
        picked = lax.dot_general(
            rows,
            pick_ref[:, : reach * LANES],
            (((0,), (0,)), ((), ())),
            preferred_element_type=jnp.float32,
        )
        for off in range(reach):
            shifted[plane, off] = picked[:, off * LANES : (off + 1) * LANES]

    coef[...] = jnp.zeros(coef.shape, jnp.float32)
    first_half = lax.broadcasted_iota(jnp.int32, (8, LANES), 0) < SLAB

    def one_pair(pair, carry):
        weight = (
            jnp.where(first_half, weight_ref[0, 2 * pair], weight_ref[0, 2 * pair + 1]),
            jnp.where(
                first_half, weight_ref[0, QUAD + 2 * pair], weight_ref[0, QUAD + 2 * pair + 1]
            ),
        )
        node = (2.0 + weight[0], weight[1])
        inv = []
        for t in range(len(TAPS)):
            diag_real = 6.0 + node[0] * real_ref[t] - node[1] * imag_ref[t]
            diag_imag = node[0] * imag_ref[t] + node[1] * real_ref[t]
            scale = inside_ref[t] / (diag_real * diag_real + diag_imag * diag_imag)
            inv.append((diag_real * scale, -(diag_imag * scale)))
        centre = inv[TAP_AT[(0, 0, 0)]]
        lead0 = cmul(weight, centre)
        lead1 = cmul(node, lead0)
        for t, (dz, off) in enumerate(TAPS):
            step = (dz,) + OFFSETS[off]
            size = sum(abs(d) for d in step)
            if size == 0:
                near = functools.reduce(cadd, [inv[TAP_AT[u]] for u in UNITS])
                term = cmul(centre, near)
                term = (1.0 + term[0], term[1])
            elif size == 1:
                term = inv[t]
            else:
                mids = [
                    inv[TAP_AT[u]]
                    for u in UNITS
                    if sum(abs(s - d) for s, d in zip(step, u)) == 1
                ]
                term = cmul(inv[t], functools.reduce(cadd, mids))
            for k, lead in enumerate((lead0, lead1)):
                real, imag = cmul(lead, term)
                coef[4 * t + 2 * k] += real
                coef[4 * t + 2 * k + 1] += imag
        return carry

    lax.fori_loop(0, QUAD // 2, one_pair, 0)
    for i in range(4 * len(TAPS)):
        both = coef[i]
        coef[i] = both + pltpu.roll(both, SLAB, axis=0)

    half = 64
    part = 32

    def one_chunk(step, carry):
        z = step // 2
        col = pl.multiple_of((step % 2) * part, part)
        sums = [jnp.zeros((part, LANES), jnp.float32) for _ in range(4)]
        for t, (dz, off) in enumerate(TAPS):
            real = shifted[z + 2 + dz, off, pl.ds(col, part), :]
            imag = shifted[z + 2 + dz, off, pl.ds(half + col, part), :]
            for k in range(2):
                coef_real = coef[4 * t + 2 * k, pl.ds(z, 1), :]
                coef_imag = coef[4 * t + 2 * k + 1, pl.ds(z, 1), :]
                sums[2 * k] += coef_real * real - coef_imag * imag
                sums[2 * k + 1] += coef_real * imag + coef_imag * real
        for k in range(2):
            moments_ref[k, z, pl.ds(col, part), :] = sums[2 * k]
            moments_ref[k, z, pl.ds(half + col, part), :] = sums[2 * k + 1]
        return carry

    lax.fori_loop(0, 2 * SLAB, one_chunk, 0)

    cross = jnp.zeros((half, 4 * half), jnp.float32)
    for z in range(SLAB):
        left = jnp.concatenate([shifted[z + 2, 0, :half], shifted[z + 2, 0, half:]], axis=1)
        left = left.astype(jnp.bfloat16)
        rows = []
        for k in range(2):
            real = moments_ref[k, z, :half]
            imag = moments_ref[k, z, half:]
            rows.append(jnp.concatenate([real, imag], axis=1))
            rows.append(jnp.concatenate([imag, -real], axis=1))
        right = jnp.concatenate(rows, axis=0)
        high = right.astype(jnp.bfloat16)
        low = (right - high.astype(jnp.float32)).astype(jnp.bfloat16)
        for piece in (high, low):
            cross += lax.dot_general(
                left, piece, (((1,), (1,)), ((), ())), preferred_element_type=jnp.float32
            )
    cross_ref[...] = cross * (1.0 / 131072)


def turn_kernel(moments_ref, first_ref, second_ref):
    for k, out_ref in enumerate((first_ref, second_ref)):
        for z in range(SLAB):
            out_ref[z] = moments_ref[k, z].T


def swap(block, axis, bit):
    count = lax.axis_size(axis)
    return lax.ppermute(block, axis, [(i, i ^ bit) for i in range(count)])


def sum_of_four(block, axis, bits):
    first, second, third = (swap(block, axis, bit) for bit in bits)
    return (block + first) + (second + third)


def reduce_cross(cross):
    width = cross.shape[1] // 2
    core = lax.axis_index("sx") & 1
    low, high = cross[:, :width], cross[:, width:]
    mine = jnp.where(core == 0, low, high)
    block = mine + swap(jnp.where(core == 0, high, low), "sx", 1)
    block = sum_of_four(block, "sy", (1, 2, 3))
    block = sum_of_four(block, "quad", (1, 2, 3))
    block = sum_of_four(block, "quad", (4, 8, 12))
    block = block + swap(block, "sx", 2)
    other = swap(block, "sx", 1)
    return jnp.where(core == 0, block, other), jnp.where(core == 0, other, block)


def beside(block, axis, forward):
    count = lax.axis_size(axis)
    pairs = [(i, i + 1) for i in range(count - 1)]
    return lax.ppermute(block, axis, pairs if forward else [(b, a) for a, b in pairs])


def body(probes, quad_index, region_label, gain_label, region_eps, gain_rate):
    depth, cells_x, cells_y, columns = probes.shape
    me = lax.axis_index("quad")
    start_z = me * SLAB
    start_x = lax.axis_index("sx") * cells_x
    start_y = lax.axis_index("sy") * cells_y

    angle = 2.0 * math.pi * (quad_index.astype(jnp.float32) + 0.5) / (4 * QUAD)
    lane = lax.broadcasted_iota(jnp.int32, (1, 128), 1)
    weight = jnp.where(lane == me, jnp.cos(angle), 0.0)
    weight = jnp.where(lane == me + QUAD, jnp.sin(angle), weight)

    flat = probes.reshape(depth, cells_x * cells_y, columns)
    own = jnp.concatenate(
        [
            lax.dynamic_slice_in_dim(flat, jnp.maximum(start_z - 2, 0), 2, 0),
            lax.dynamic_slice_in_dim(flat, start_z, SLAB, 0),
            lax.dynamic_slice_in_dim(flat, jnp.minimum(start_z + SLAB, depth - 2), 2, 0),
        ],
        axis=0,
    )
    planes = SLAB + 4
    cube = own.reshape(planes, cells_x, cells_y, columns)
    ylo = beside(cube[:, :, -2:, :].reshape(planes, -1, columns), "sy", True)
    yhi = beside(cube[:, :, :2, :].reshape(planes, -1, columns), "sy", False)
    weight = sum_of_four(weight, "quad", (1, 2, 3))

    def edge(first):
        at = 0 if first else (cells_x - 2)
        pieces = [
            own[:, at * cells_y : (at + 2) * cells_y],
            ylo[:, at * 2 : (at + 2) * 2],
            yhi[:, at * 2 : (at + 2) * 2],
        ]
        return jnp.pad(jnp.concatenate(pieces, axis=1), ((0, 0), (0, 8), (0, 0)))

    xlo = beside(edge(False), "sx", True)
    xhi = beside(edge(True), "sx", False)
    weight = sum_of_four(weight, "quad", (4, 8, 12))

    code = jnp.pad(region_label * 8 + gain_label, 2, constant_values=OUTSIDE)
    code = lax.dynamic_slice(
        code, (start_z, start_x, start_y), (planes, cells_x + 4, cells_y + 4)
    ).astype(jnp.bfloat16)
    code = jnp.pad(code.reshape(planes, -1), ((0, 0), (0, 16)))
    code = jnp.concatenate([code[d : d + SLAB] for d in range(5) for _ in range(2)], axis=0)
    code = jnp.pad(code, ((0, 8), (0, 0)))

    smem = pl.BlockSpec(memory_space=pltpu.SMEM)
    vmem = pl.BlockSpec(memory_space=pltpu.VMEM)
    taps = len(TAPS)
    per_tap = jax.ShapeDtypeStruct((taps, 8, LANES), jnp.float32)
    real, imag, inside = pl.pallas_call(
        material_kernel,
        out_shape=[per_tap] * 3,
        in_specs=[smem, smem, vmem, vmem],
        out_specs=[vmem] * 3,
        cost_estimate=pl.CostEstimate(flops=40000000, bytes_accessed=1200000, transcendentals=0),
        name="material",
    )(region_eps, gain_rate, code, jnp.asarray(selector(window_cells())))

    moments, cross = pl.pallas_call(
        moment_kernel,
        out_shape=[
            jax.ShapeDtypeStruct((2, SLAB, columns, LANES), jnp.float32),
            jax.ShapeDtypeStruct((64, 256), jnp.float32),
        ],
        in_specs=[smem] + [vmem] * 9,
        out_specs=[vmem] * 2,
        scratch_shapes=[
            pltpu.VMEM((planes, len(OFFSETS), columns, LANES), jnp.float32),
            pltpu.VMEM((4 * taps, 8, LANES), jnp.float32),
        ],
        compiler_params=pltpu.CompilerParams(vmem_limit_bytes=32 * 1024 * 1024),
        cost_estimate=pl.CostEstimate(flops=600000000, bytes_accessed=3000000, transcendentals=0),
        name="moments",
    )(weight, real, imag, inside, own, ylo, yhi, xlo, xhi, jnp.asarray(selector(source_cells())))

    out = jax.ShapeDtypeStruct((SLAB, LANES, columns), jnp.float32)
    first, second = pl.pallas_call(
        turn_kernel,
        out_shape=[out] * 2,
        in_specs=[vmem],
        out_specs=[vmem] * 2,
        cost_estimate=pl.CostEstimate(flops=1000000, bytes_accessed=1000000, transcendentals=0),
        name="turn",
    )(moments)
    shape = (SLAB, cells_x, cells_y, columns)

    halves = reduce_cross(cross)
    projections = jnp.stack(
        [jnp.stack([half[:, :64], half[:, 64:]], axis=0) for half in halves], axis=0
    )
    return (first.reshape(shape), second.reshape(shape), projections)


def solution(mesh):
    placed = (P(None, "sx", "sy", None), P("quad"), P(), P(), P(), P())
    return jax.shard_map(
        body,
        mesh=mesh,
        in_specs=placed,
        out_specs=(P("quad", "sx", "sy", None), P("quad", "sx", "sy", None), P()),
        check_vma=False,
    )
```

time: 497 us -> 90.8 us (0.18)
  waiting for transfers between devices: 367 us -> 25.2 us
  other arithmetic: 68.4 us -> 3.41 us
  between operations: 15.2 us -> 1.81 us
  Pallas kernels: 0 us -> 9.54 us
  starting transfers between devices: 36.9 us -> 43.9 us
    psum x1 -> x0, waiting for transfers between devices: 248 us -> none  [body(): summed = lax.psum(local_cross(slab_source, reduced), ('quad', 'sx', 'sy'))]
    reduce_scatter x1 -> x0, waiting for transfers between devices: 104 us -> none  [body(): reduced = lax.psum_scatter(both, 'quad', scatter_dimension=0, tiled=True)]
    add x5 -> x8, other arithmetic: 39.8 us -> 2.51 us  [the longest x1 2.45 us: body(): code = jnp.pad(region_label * 8 + gain_label, 2, constant_values=OUTSIDE)]
    concatenate x5 -> x2, other arithmetic: 10.6 us -> 0.04 us  [edge(): return jnp.pad(jnp.concatenate(pieces, axis=1), ((0, 0), (0, 8), (0, 0)))]
    ppermute x8 -> x22, waiting for transfers between devices: 15 us -> 25.2 us  [the longest x18 17.7 us: swap(): return lax.ppermute(block, axis, [(i, i ^ bit) for i in range(count)])]
    pallas_call x0 -> x3, Pallas kernels: none -> 9.54 us  [the longest x1 5.36 us: body(): pl.pallas_call(moment_kernel, out_shape=[jax.ShapeDtypeStruct((2, SLAB, c...]
    ppermute x8 -> x22, starting transfers between devices: 36.8 us -> 43.9 us  [the longest x18 28.4 us: swap(): return lax.ppermute(block, axis, [(i, i ^ bit) for i in range(count)])]
    sub x1 -> x0, other arithmetic: 6.93 us -> none  [multiply_by(): coef_real * field_real - coef_imag * field_imag]
  transfers between devices with their start and end apart: 10 -> 22, of which waited for: 10 -> 9; matrix products, arithmetic and copies ran while one was open for 2% -> 6% of each run, Pallas kernels for 0% -> 5%
where the time goes in v1:
time: 90.8 us; the launch traced here: 90.4 us
  starting transfers between devices  43.9 us (48%)
  waiting for transfers between devices  25.2 us (28%)
  Pallas kernels  9.54 us (11%)
  local copies, waits for them, and re-layouts  6.47 us (7%)
  other arithmetic  3.41 us (4%)
  between operations  1.81 us (2%)
    ppermute x18, starting transfers between devices, swap(): return lax.ppermute(block, axis, [(i, i ^ bit) for i in range(count)])  28.4 us
    ppermute x18, waiting for transfers between devices, swap(): return lax.ppermute(block, axis, [(i, i ^ bit) for i in range(count)])  17.7 us
    ppermute x4, starting transfers between devices, beside(): lax.ppermute(block, axis, pairs if forward else [(b, a) for a, b in pairs])  15.5 us
    ppermute x4, waiting for transfers between devices, beside(): lax.ppermute(block, axis, pairs if forward else [(b, a) for a, b in pairs])  7.59 us
    pallas_call x1, Pallas kernels, body(): pl.pallas_call(moment_kernel, out_shape=[jax.ShapeDtypeStruct((2, SLAB, c...  5.36 us
    unnamed x12, local copies, waits for them, and re-layouts  3.48 us
    add x1, other arithmetic, body(): code = jnp.pad(region_label * 8 + gain_label, 2, constant_values=OUTSIDE)  2.45 us
    pallas_call x1, Pallas kernels, body(): pl.pallas_call(material_kernel, out_shape=[per_tap] * 3, in_specs=[smem,...  2.21 us
  transfers between devices with their start and end apart: 22, of which 9 were waited for; matrix products, arithmetic and copies ran while one was open for 6% of the time, Pallas kernels for 5%

profile of v1, /device:TPU:1, one launch (start us, length us, event | category | flops | bytes accessed | tf_op | source)
XLA Modules:
  0.0 90.4 jit_solution(13385483609569034347)
XLA Ops:
  1.5 3.7 %collective-permute-start.1 = (f32[1,128]{1,0:T(1,128)S(1)}, f32[1,128]{1,0:T(1,128)S(1)}, u32[]{:S(2)}, u32[]{:S(2)}) collective-permute-start(f32[1,128]{1,0:T(1,128)S(1)} %compare_select_fusion.1), channel_id=1, source_target_pairs={{0,32},{16,48},{32,0},{48,16},{64,96},{80,112},{96,64},{112,80},{1... | collective-permute-start | bytes 1544 | tf_op jit(solution)/shard_map/ppermute | solution.py:210
  5.2 0.9 collective-permute-start.2
  6.1 0.0 collective-permute-start
  6.1 0.9 %constant_dynamic-slice_fusion.1 = bf16[4,128,128]{2,1,0:T(8,128)(2,1)S(1)} fusion(bf16[64,128,128]{2,1,0:T(8,128)(2,1)} %bitcast.23, s32[]{:T(128)S(6)} %select_n.65), kind=kLoop, calls=%fused_computation.38 | loop fusion | bytes 262148 | tf_op jit(solution)/shard_map/dynamic_slice | solution.py:254
  7.0 0.9 constant_dynamic-slice_fusion.2
  7.9 0.1 fusion.13
  8.0 3.2 %collective-permute-start.6 = (bf16[8,32,128]{2,1,0:T(8,128)(2,1)S(1)}, bf16[8,32,128]{2,1,0:T(8,128)(2,1)S(1)}, u32[]{:S(2)}, u32[]{:S(2)}) collective-permute-start(bf16[8,32,128]{2,1,0:T(8,128)(2,1)S(1)} %bitcast.21), channel_id=1, source_target_pairs={{0,1},{1,2},{2,3},{4,5},{5,6},{6,7},{8,9},{9,10},{10,11},{12,13},{... | collective-permute-start | bytes 196616 | tf_op jit(solution)/shard_map/ppermute | solution.py:235
  11.2 1.3 %collective-permute-start.7 = (bf16[8,32,128]{2,1,0:T(8,128)(2,1)S(1)}, bf16[8,32,128]{2,1,0:T(8,128)(2,1)S(1)}, u32[]{:S(2)}, u32[]{:S(2)}) collective-permute-start(bf16[8,32,128]{2,1,0:T(8,128)(2,1)S(1)} %bitcast.22), channel_id=1, source_target_pairs={{1,0},{2,1},{3,2},{5,4},{6,5},{7,6},{9,8},{10,9},{11,10},{13,12},{... | collective-permute-start | bytes 196616 | tf_op jit(solution)/shard_map/ppermute | solution.py:235
  12.6 2.4 %copy_add_fusion = s32[64,64,32]{1,0,2:T(8,128)S(1)} fusion(s32[64,64,32]{1,2,0:T(8,128)S(1)} %copy-done.5, s32[64,64,32]{1,2,0:T(8,128)} %param.10), kind=kLoop, calls=%fused_computation.1 | loop fusion | flops 262144 | bytes 1572864 | tf_op jit(solution)/shard_map/add | solution.py:278
  15.0 0.0 copy-start.4
  15.0 0.1 fusion.10
  15.1 0.2 copy.15
  15.3 0.1 reshape.57
  15.4 0.1 concatenate.12
  15.6 0.6 pad.21.code_ref
  16.2 2.2 %material.1 = (f32[25,8,128]{2,1,0:T(8,128)}, f32[25,8,128]{2,1,0:T(8,128)}, f32[25,8,128]{2,1,0:T(8,128)}) custom-call(f32[8]{0:T(128)} %eps_ref.1, f32[8]{0:T(128)} %gain_ref.1, bf16[48,256]{1,0:T(8,128)(2,1)} %pad.21.code_ref, bf16[256,1664]{1,0:T(8,128)(2,1)} %constant.50.clone.pick_ref), custom_call_target="tpu_custom_call" | custom-call | flops 40000000 | bytes 1200000 | tf_op jit(solution)/shard_map/material/pallas_call | solution.py:290
  18.4 0.0 collective-permute-done
  18.4 3.1 %collective-permute-start.4 = (f32[1,128]{1,0:T(1,128)S(1)}, f32[1,128]{1,0:T(1,128)S(1)}, u32[]{:S(2)}, u32[]{:S(2)}) collective-permute-start(f32[1,128]{1,0:T(1,128)S(1)} %add_add_fusion.4), channel_id=1, source_target_pairs={{0,128},{16,144},{32,160},{48,176},{64,192},{80,208},{96,224},{112... | collective-permute-start | bytes 1544 | tf_op jit(solution)/shard_map/ppermute | solution.py:210
  21.5 1.5 %collective-permute-start.5 = (f32[1,128]{1,0:T(1,128)S(1)}, f32[1,128]{1,0:T(1,128)S(1)}, u32[]{:S(2)}, u32[]{:S(2)}) collective-permute-start(f32[1,128]{1,0:T(1,128)S(1)} %add_add_fusion.4), channel_id=1, source_target_pairs={{0,192},{16,208},{32,224},{48,240},{64,128},{80,144},{96,160},{112... | collective-permute-start | bytes 1544 | tf_op jit(solution)/shard_map/ppermute | solution.py:210
  22.9 0.2 collective-permute-start.3
  23.1 0.0 collective-permute-done.7.yhi_ref
  23.2 9.1 %collective-permute-start.8 = (bf16[8,32,128]{2,1,0:T(8,128)(2,1)S(1)}, bf16[8,32,128]{2,1,0:T(8,128)(2,1)S(1)}, u32[]{:S(2)}, u32[]{:S(2)}) collective-permute-start(bf16[8,32,128]{2,1,0:T(8,128)(2,1)S(1)} %fusion.7), channel_id=1, source_target_pairs={{0,4},{4,8},{8,12},{1,5},{5,9},{9,13},{2,6},{6,10},{10,14},{3,7},{... | collective-permute-start | bytes 196616 | tf_op jit(solution)/shard_map/ppermute | solution.py:235
  32.3 1.9 %collective-permute-start.9 = (bf16[8,32,128]{2,1,0:T(8,128)(2,1)S(1)}, bf16[8,32,128]{2,1,0:T(8,128)(2,1)S(1)}, u32[]{:S(2)}, u32[]{:S(2)}) collective-permute-start(bf16[8,32,128]{2,1,0:T(8,128)(2,1)S(1)} %fusion.9), channel_id=1, source_target_pairs={{4,0},{8,4},{12,8},{5,1},{9,5},{13,9},{6,2},{10,6},{14,10},{7,3},{... | collective-permute-start | bytes 196616 | tf_op jit(solution)/shard_map/ppermute | solution.py:235
  34.3 7.6 %collective-permute-done.9.xhi_ref = bf16[8,32,128]{2,1,0:T(8,128)(2,1)S(1)} collective-permute-done((bf16[8,32,128]{2,1,0:T(8,128)(2,1)S(1)}, bf16[8,32,128]{2,1,0:T(8,128)(2,1)S(1)}, u32[]{:S(2)}, u32[]{:S(2)}) %collective-permute-start.9) | collective-permute-done | bytes 65568 | tf_op jit(solution)/shard_map/ppermute | solution.py:235
  41.9 0.9 copy-done.1
  42.8 0.9 copy-done.2
  43.7 0.9 copy-done.3
  44.6 5.4 %moments.1 = (f32[2,4,128,128]{3,2,1,0:T(8,128)S(1)}, f32[64,256]{1,0:T(8,128)S(1)}) custom-call(f32[1,128]{1,0:T(1,128)S(1)} %add_add_fusion.3.weight_ref, f32[25,8,128]{2,1,0:T(8,128)S(1)} %copy-done.1, f32[25,8,128]{2,1,0:T(8,128)S(1)} %copy-done.2, f32[25,8,128]{2,1,0:T(8,128)S(1)} %copy-done.3, bf16[8,128,128]{2,1,0:T(8,128)(2,1)S(1)} %get-tuple-element.24.own_ref, ...), custom_call_target="tpu_custom_call" | custom-call | flops 600000000 | bytes 3000000 | tf_op jit(solution)/shard_map/moments/pallas_call | solution.py:299
  49.9 0.8 copy-done
  50.7 1.2 %collective-permute-done.10 = f32[64,128]{1,0:T(8,128)S(1)} collective-permute-done((f32[64,128]{1,0:T(8,128)S(1)}, f32[64,128]{1,0:T(8,128)S(1)}, u32[]{:S(2)}, u32[]{:S(2)}) %collective-permute-start.10) | collective-permute-done | bytes 32800 | tf_op jit(solution)/shard_map/ppermute | solution.py:210
  51.9 4.1 %collective-permute-start.12 = (f32[64,128]{1,0:T(8,128)S(1)}, f32[64,128]{1,0:T(8,128)S(1)}, u32[]{:S(2)}, u32[]{:S(2)}) collective-permute-start(f32[64,128]{1,0:T(8,128)S(1)} %select_add_fusion), channel_id=1, source_target_pairs={{0,2},{1,3},{2,0},{3,1},{4,6},{5,7},{6,4},{7,5},{8,10},{9,11},{10,... | collective-permute-start | bytes 98312 | tf_op jit(solution)/shard_map/ppermute | solution.py:210
  56.0 0.8 collective-permute-start.13
  56.8 0.9 collective-permute-done.12
  57.7 2.3 %collective-permute-done.13 = f32[64,128]{1,0:T(8,128)S(1)} collective-permute-done((f32[64,128]{1,0:T(8,128)S(1)}, f32[64,128]{1,0:T(8,128)S(1)}, u32[]{:S(2)}, u32[]{:S(2)}) %collective-permute-start.13) | collective-permute-done | bytes 32800 | tf_op jit(solution)/shard_map/ppermute | solution.py:210
  60.0 3.4 %collective-permute-start.15 = (f32[64,128]{1,0:T(8,128)S(1)}, f32[64,128]{1,0:T(8,128)S(1)}, u32[]{:S(2)}, u32[]{:S(2)}) collective-permute-start(f32[64,128]{1,0:T(8,128)S(1)} %add_add_fusion.2), channel_id=1, source_target_pairs={{0,32},{16,48},{32,0},{48,16},{64,96},{80,112},{96,64},{112,80},{1... | collective-permute-start | bytes 98312 | tf_op jit(solution)/shard_map/ppermute | solution.py:210
  63.4 0.9 collective-permute-start.16
  64.2 0.4 collective-permute-done.15
  64.7 2.7 %collective-permute-done.16 = f32[64,128]{1,0:T(8,128)S(1)} collective-permute-done((f32[64,128]{1,0:T(8,128)S(1)}, f32[64,128]{1,0:T(8,128)S(1)}, u32[]{:S(2)}, u32[]{:S(2)}) %collective-permute-start.16) | collective-permute-done | bytes 32800 | tf_op jit(solution)/shard_map/ppermute | solution.py:210
  67.4 2.8 %collective-permute-start.18 = (f32[64,128]{1,0:T(8,128)S(1)}, f32[64,128]{1,0:T(8,128)S(1)}, u32[]{:S(2)}, u32[]{:S(2)}) collective-permute-start(f32[64,128]{1,0:T(8,128)S(1)} %add_add_fusion.1), channel_id=1, source_target_pairs={{0,128},{16,144},{32,160},{48,176},{64,192},{80,208},{96,224},{112... | collective-permute-start | bytes 98312 | tf_op jit(solution)/shard_map/ppermute | solution.py:210
  70.2 1.6 %collective-permute-start.19 = (f32[64,128]{1,0:T(8,128)S(1)}, f32[64,128]{1,0:T(8,128)S(1)}, u32[]{:S(2)}, u32[]{:S(2)}) collective-permute-start(f32[64,128]{1,0:T(8,128)S(1)} %add_add_fusion.1), channel_id=1, source_target_pairs={{0,192},{16,208},{32,224},{48,240},{64,128},{80,144},{96,160},{112... | collective-permute-start | bytes 98312 | tf_op jit(solution)/shard_map/ppermute | solution.py:210
  71.8 3.1 %collective-permute-done.19 = f32[64,128]{1,0:T(8,128)S(1)} collective-permute-done((f32[64,128]{1,0:T(8,128)S(1)}, f32[64,128]{1,0:T(8,128)S(1)}, u32[]{:S(2)}, u32[]{:S(2)}) %collective-permute-start.19) | collective-permute-done | bytes 32800 | tf_op jit(solution)/shard_map/ppermute | solution.py:210
  74.9 0.3 collective-permute-done.17
  75.3 0.1 collective-permute-start.20
  75.4 6.7 %collective-permute-done.20 = f32[64,128]{1,0:T(8,128)S(1)} collective-permute-done((f32[64,128]{1,0:T(8,128)S(1)}, f32[64,128]{1,0:T(8,128)S(1)}, u32[]{:S(2)}, u32[]{:S(2)}) %collective-permute-start.20) | collective-permute-done | bytes 32800 | tf_op jit(solution)/shard_map/ppermute | solution.py:210
  82.1 5.6 %collective-permute-start.21 = (f32[64,128]{1,0:T(8,128)S(1)}, f32[64,128]{1,0:T(8,128)S(1)}, u32[]{:S(2)}, u32[]{:S(2)}) collective-permute-start(f32[64,128]{1,0:T(8,128)S(1)} %add.115), channel_id=1, source_target_pairs={{0,4},{4,0},{8,12},{12,8},{1,5},{5,1},{9,13},{13,9},{2,6},{6,2},{1... | collective-permute-start | bytes 98312 | tf_op jit(solution)/shard_map/ppermute | solution.py:210
  87.6 2.0 %turn.1 = (f32[4,128,128]{2,1,0:T(8,128)}, f32[4,128,128]{2,1,0:T(8,128)}) custom-call(f32[2,4,128,128]{3,2,1,0:T(8,128)} %copy-done), custom_call_target="tpu_custom_call" | custom-call | flops 1000000 | bytes 1000000 | tf_op jit(solution)/shard_map/turn/pallas_call | solution.py:317
  89.6 0.1 slice_bitcast_fusion.1
  89.7 0.7 pad_maximum_fusion.1
  (41 shorter events, 0.3 us)
Async XLA Ops:
  0.6 11.9 %copy-start.5 = (s32[64,64,32]{1,2,0:T(8,128)S(1)}, s32[64,64,32]{1,2,0:T(8,128)}, u32[]{:S(2)}) copy-start(s32[64,64,32]{1,2,0:T(8,128)} %param.11) | copy-start | bytes 1572868
  1.5 16.8 %collective-permute-start.1 = (f32[1,128]{1,0:T(1,128)S(1)}, f32[1,128]{1,0:T(1,128)S(1)}, u32[]{:S(2)}, u32[]{:S(2)}) collective-permute-start(f32[1,128]{1,0:T(1,128)S(1)} %compare_select_fusion.1), channel_id=1, source_target_pairs={{0,32},{16,48},{32,0},{48,16},{64,96},{80,112},{96,64},{112,80},{1... | collective-permute-start | bytes 1544 | tf_op jit(solution)/shard_map/ppermute | solution.py:210
  5.2 13.2 %collective-permute-start.2 = (f32[1,128]{1,0:T(1,128)S(1)}, f32[1,128]{1,0:T(1,128)S(1)}, u32[]{:S(2)}, u32[]{:S(2)}) collective-permute-start(f32[1,128]{1,0:T(1,128)S(1)} %compare_select_fusion.1), channel_id=1, source_target_pairs={{0,48},{16,32},{32,16},{48,0},{64,112},{80,96},{96,80},{112,64},{1... | collective-permute-start | bytes 1544 | tf_op jit(solution)/shard_map/ppermute | solution.py:210
  6.1 12.3 %collective-permute-start = (f32[1,128]{1,0:T(1,128)S(1)}, f32[1,128]{1,0:T(1,128)S(1)}, u32[]{:S(2)}, u32[]{:S(2)}) collective-permute-start(f32[1,128]{1,0:T(1,128)S(1)} %compare_select_fusion.1), channel_id=1, source_target_pairs={{0,16},{16,0},{32,48},{48,32},{64,80},{80,64},{96,112},{112,96},{1... | collective-permute-start | bytes 1544 | tf_op jit(solution)/shard_map/ppermute | solution.py:210
  8.0 15.1 %collective-permute-start.6 = (bf16[8,32,128]{2,1,0:T(8,128)(2,1)S(1)}, bf16[8,32,128]{2,1,0:T(8,128)(2,1)S(1)}, u32[]{:S(2)}, u32[]{:S(2)}) collective-permute-start(bf16[8,32,128]{2,1,0:T(8,128)(2,1)S(1)} %bitcast.21), channel_id=1, source_target_pairs={{0,1},{1,2},{2,3},{4,5},{5,6},{6,7},{8,9},{9,10},{10,11},{12,13},{... | collective-permute-start | bytes 196616 | tf_op jit(solution)/shard_map/ppermute | solution.py:235
  11.2 11.9 %collective-permute-start.7 = (bf16[8,32,128]{2,1,0:T(8,128)(2,1)S(1)}, bf16[8,32,128]{2,1,0:T(8,128)(2,1)S(1)}, u32[]{:S(2)}, u32[]{:S(2)}) collective-permute-start(bf16[8,32,128]{2,1,0:T(8,128)(2,1)S(1)} %bitcast.22), channel_id=1, source_target_pairs={{1,0},{2,1},{3,2},{5,4},{6,5},{7,6},{9,8},{10,9},{11,10},{13,12},{... | collective-permute-start | bytes 196616 | tf_op jit(solution)/shard_map/ppermute | solution.py:235
  15.0 26.9 %copy-start.4 = (bf16[256,1664]{1,0:T(8,128)(2,1)S(1)}, bf16[256,1664]{1,0:T(8,128)(2,1)}, u32[]{:S(2)}) copy-start(bf16[256,1664]{1,0:T(8,128)(2,1)} %constant.51.clone.pick_ref) | copy-start | bytes 2555908
  18.4 15.8 %collective-permute-start.4 = (f32[1,128]{1,0:T(1,128)S(1)}, f32[1,128]{1,0:T(1,128)S(1)}, u32[]{:S(2)}, u32[]{:S(2)}) collective-permute-start(f32[1,128]{1,0:T(1,128)S(1)} %add_add_fusion.4), channel_id=1, source_target_pairs={{0,128},{16,144},{32,160},{48,176},{64,192},{80,208},{96,224},{112... | collective-permute-start | bytes 1544 | tf_op jit(solution)/shard_map/ppermute | solution.py:210
  21.5 12.8 %collective-permute-start.5 = (f32[1,128]{1,0:T(1,128)S(1)}, f32[1,128]{1,0:T(1,128)S(1)}, u32[]{:S(2)}, u32[]{:S(2)}) collective-permute-start(f32[1,128]{1,0:T(1,128)S(1)} %add_add_fusion.4), channel_id=1, source_target_pairs={{0,192},{16,208},{32,224},{48,240},{64,128},{80,144},{96,160},{112... | collective-permute-start | bytes 1544 | tf_op jit(solution)/shard_map/ppermute | solution.py:210
  22.9 11.3 %collective-permute-start.3 = (f32[1,128]{1,0:T(1,128)S(1)}, f32[1,128]{1,0:T(1,128)S(1)}, u32[]{:S(2)}, u32[]{:S(2)}) collective-permute-start(f32[1,128]{1,0:T(1,128)S(1)} %add_add_fusion.4), channel_id=1, source_target_pairs={{0,64},{16,80},{32,96},{48,112},{64,0},{80,16},{96,32},{112,48},{1... | collective-permute-start | bytes 1544 | tf_op jit(solution)/shard_map/ppermute | solution.py:210
  23.2 11.1 %collective-permute-start.8 = (bf16[8,32,128]{2,1,0:T(8,128)(2,1)S(1)}, bf16[8,32,128]{2,1,0:T(8,128)(2,1)S(1)}, u32[]{:S(2)}, u32[]{:S(2)}) collective-permute-start(bf16[8,32,128]{2,1,0:T(8,128)(2,1)S(1)} %fusion.7), channel_id=1, source_target_pairs={{0,4},{4,8},{8,12},{1,5},{5,9},{9,13},{2,6},{6,10},{10,14},{3,7},{... | collective-permute-start | bytes 196616 | tf_op jit(solution)/shard_map/ppermute | solution.py:235
  32.3 9.6 %collective-permute-start.9 = (bf16[8,32,128]{2,1,0:T(8,128)(2,1)S(1)}, bf16[8,32,128]{2,1,0:T(8,128)(2,1)S(1)}, u32[]{:S(2)}, u32[]{:S(2)}) collective-permute-start(bf16[8,32,128]{2,1,0:T(8,128)(2,1)S(1)} %fusion.9), channel_id=1, source_target_pairs={{4,0},{8,4},{12,8},{5,1},{9,5},{13,9},{6,2},{10,6},{14,10},{7,3},{... | collective-permute-start | bytes 196616 | tf_op jit(solution)/shard_map/ppermute | solution.py:235
  41.9 0.9 copy-start.1
  42.8 0.9 copy-start.2
  43.7 0.9 copy-start.3
  49.9 0.8 copy-start
  50.7 1.2 %collective-permute-start.10 = (f32[64,128]{1,0:T(8,128)S(1)}, f32[64,128]{1,0:T(8,128)S(1)}, u32[]{:S(2)}, u32[]{:S(2)}) collective-permute-start(f32[64,128]{1,0:T(8,128)S(1)} %slice_select_fusion), channel_id=1, source_target_pairs={{0,4},{4,0},{8,12},{12,8},{1,5},{5,1},{9,13},{13,9},{2,6},{6,2},{1... | collective-permute-start | bytes 98312 | tf_op jit(solution)/shard_map/ppermute | solution.py:210
  51.9 5.7 %collective-permute-start.12 = (f32[64,128]{1,0:T(8,128)S(1)}, f32[64,128]{1,0:T(8,128)S(1)}, u32[]{:S(2)}, u32[]{:S(2)}) collective-permute-start(f32[64,128]{1,0:T(8,128)S(1)} %select_add_fusion), channel_id=1, source_target_pairs={{0,2},{1,3},{2,0},{3,1},{4,6},{5,7},{6,4},{7,5},{8,10},{9,11},{10,... | collective-permute-start | bytes 98312 | tf_op jit(solution)/shard_map/ppermute | solution.py:210
  56.0 4.0 %collective-permute-start.13 = (f32[64,128]{1,0:T(8,128)S(1)}, f32[64,128]{1,0:T(8,128)S(1)}, u32[]{:S(2)}, u32[]{:S(2)}) collective-permute-start(f32[64,128]{1,0:T(8,128)S(1)} %select_add_fusion), channel_id=1, source_target_pairs={{0,3},{1,2},{2,1},{3,0},{4,7},{5,6},{6,5},{7,4},{8,11},{9,10},{10,... | collective-permute-start | bytes 98312 | tf_op jit(solution)/shard_map/ppermute | solution.py:210
  56.8 3.2 %collective-permute-start.11 = (f32[64,128]{1,0:T(8,128)S(1)}, f32[64,128]{1,0:T(8,128)S(1)}, u32[]{:S(2)}, u32[]{:S(2)}) collective-permute-start(f32[64,128]{1,0:T(8,128)S(1)} %select_add_fusion), channel_id=1, source_target_pairs={{0,1},{1,0},{2,3},{3,2},{4,5},{5,4},{6,7},{7,6},{8,9},{9,8},{10,11... | collective-permute-start | bytes 98312 | tf_op jit(solution)/shard_map/ppermute | solution.py:210
  60.0 4.7 %collective-permute-start.15 = (f32[64,128]{1,0:T(8,128)S(1)}, f32[64,128]{1,0:T(8,128)S(1)}, u32[]{:S(2)}, u32[]{:S(2)}) collective-permute-start(f32[64,128]{1,0:T(8,128)S(1)} %add_add_fusion.2), channel_id=1, source_target_pairs={{0,32},{16,48},{32,0},{48,16},{64,96},{80,112},{96,64},{112,80},{1... | collective-permute-start | bytes 98312 | tf_op jit(solution)/shard_map/ppermute | solution.py:210
  63.4 4.0 %collective-permute-start.16 = (f32[64,128]{1,0:T(8,128)S(1)}, f32[64,128]{1,0:T(8,128)S(1)}, u32[]{:S(2)}, u32[]{:S(2)}) collective-permute-start(f32[64,128]{1,0:T(8,128)S(1)} %add_add_fusion.2), channel_id=1, source_target_pairs={{0,48},{16,32},{32,16},{48,0},{64,112},{80,96},{96,80},{112,64},{1... | collective-permute-start | bytes 98312 | tf_op jit(solution)/shard_map/ppermute | solution.py:210
  64.2 3.1 %collective-permute-start.14 = (f32[64,128]{1,0:T(8,128)S(1)}, f32[64,128]{1,0:T(8,128)S(1)}, u32[]{:S(2)}, u32[]{:S(2)}) collective-permute-start(f32[64,128]{1,0:T(8,128)S(1)} %add_add_fusion.2), channel_id=1, source_target_pairs={{0,16},{16,0},{32,48},{48,32},{64,80},{80,64},{96,112},{112,96},{1... | collective-permute-start | bytes 98312 | tf_op jit(solution)/shard_map/ppermute | solution.py:210
  67.4 4.4 %collective-permute-start.18 = (f32[64,128]{1,0:T(8,128)S(1)}, f32[64,128]{1,0:T(8,128)S(1)}, u32[]{:S(2)}, u32[]{:S(2)}) collective-permute-start(f32[64,128]{1,0:T(8,128)S(1)} %add_add_fusion.1), channel_id=1, source_target_pairs={{0,128},{16,144},{32,160},{48,176},{64,192},{80,208},{96,224},{112... | collective-permute-start | bytes 98312 | tf_op jit(solution)/shard_map/ppermute | solution.py:210
  70.2 4.8 %collective-permute-start.19 = (f32[64,128]{1,0:T(8,128)S(1)}, f32[64,128]{1,0:T(8,128)S(1)}, u32[]{:S(2)}, u32[]{:S(2)}) collective-permute-start(f32[64,128]{1,0:T(8,128)S(1)} %add_add_fusion.1), channel_id=1, source_target_pairs={{0,192},{16,208},{32,224},{48,240},{64,128},{80,144},{96,160},{112... | collective-permute-start | bytes 98312 | tf_op jit(solution)/shard_map/ppermute | solution.py:210
  71.8 3.5 %collective-permute-start.17 = (f32[64,128]{1,0:T(8,128)S(1)}, f32[64,128]{1,0:T(8,128)S(1)}, u32[]{:S(2)}, u32[]{:S(2)}) collective-permute-start(f32[64,128]{1,0:T(8,128)S(1)} %add_add_fusion.1), channel_id=1, source_target_pairs={{0,64},{16,80},{32,96},{48,112},{64,0},{80,16},{96,32},{112,48},{1... | collective-permute-start | bytes 98312 | tf_op jit(solution)/shard_map/ppermute | solution.py:210
  75.3 6.8 %collective-permute-start.20 = (f32[64,128]{1,0:T(8,128)S(1)}, f32[64,128]{1,0:T(8,128)S(1)}, u32[]{:S(2)}, u32[]{:S(2)}) collective-permute-start(f32[64,128]{1,0:T(8,128)S(1)} %add_add_fusion), channel_id=1, source_target_pairs={{0,8},{4,12},{8,0},{12,4},{1,9},{5,13},{9,1},{13,5},{2,10},{6,14},... | collective-permute-start | bytes 98312 | tf_op jit(solution)/shard_map/ppermute | solution.py:210
  82.1 7.5 %collective-permute-start.21 = (f32[64,128]{1,0:T(8,128)S(1)}, f32[64,128]{1,0:T(8,128)S(1)}, u32[]{:S(2)}, u32[]{:S(2)}) collective-permute-start(f32[64,128]{1,0:T(8,128)S(1)} %add.115), channel_id=1, source_target_pairs={{0,4},{4,0},{8,12},{12,8},{1,5},{5,1},{9,13},{13,9},{2,6},{6,2},{1... | collective-permute-start | bytes 98312 | tf_op jit(solution)/shard_map/ppermute | solution.py:210

commit v2 on v1

--- a/solution.py
+++ b/solution.py
@@ -14,7 +14,6 @@
 CX = 16
 CY = 8
 LANES = CX * CY
-OUTSIDE = 64
 
 OFFSETS = sorted(
     [(dx, dy) for dx in range(-2, 3) for dy in range(-2, 3) if abs(dx) + abs(dy) <= 2],
@@ -27,39 +26,60 @@
 WIDE = len(OFFSETS) * LANES
 
 
-def selector(cells):
-    row_of = {cell: row for row, cell in enumerate(cells) if cell is not None}
+def source_cells():
+    cells = [(x, y) for x in range(CX) for y in range(CY)]
+    for y in (-1, -2, CY, CY + 1):
+        cells += [(x, y) for x in range(CX)]
+    for xs, near in (((-2, -1), -1), ((CX, CX + 1), CX)):
+        cells += [(x, y) for x in xs for y in range(CY)]
+        cells += [(near, -1), (near, CY)] + [None] * 14
+    return cells
+
+
+def selector():
+    row_of = {cell: row for row, cell in enumerate(source_cells()) if cell is not None}
     pick = np.zeros((256, WIDE), np.float32)
     for o, (dx, dy) in enumerate(OFFSETS):
         for x in range(CX):
             for y in range(CY):
-                row = row_of.get((x + dx, y + dy))
-                if row is not None:
-                    pick[row, o * LANES + x * CY + y] = 1.0
+                pick[row_of[(x + dx, y + dy)], o * LANES + x * CY + y] = 1.0
     return pick.astype(jnp.bfloat16)
 
 
-def source_cells():
-    cells = [(x, y) for x in range(CX) for y in range(CY)]
-    cells += [(x, y) for x in range(CX) for y in (-2, -1)]
-    cells += [(x, y) for x in range(CX) for y in (CY, CY + 1)]
-    for xs in ((-2, -1), (CX, CX + 1)):
-        cells += [(x, y) for x in xs for y in range(CY)]
-        cells += [(x, y) for x in xs for y in (-2, -1)]
-        cells += [(x, y) for x in xs for y in (CY, CY + 1)]
-        cells += [None] * 8
-    return cells
-
-
-def window_cells():
-    return [(x, y) for x in range(-2, CX + 2) for y in range(-2, CY + 2)]
-
-
-def material_kernel(eps_ref, gain_ref, code_ref, pick_ref, real_ref, imag_ref, inside_ref):
-    codes = jnp.dot(code_ref[...], pick_ref[...], preferred_element_type=jnp.float32)
+def material_kernel(place_ref, eps_ref, gain_ref, region_ref, level_ref, out_ref, labels, codes, sems):
+    planes = SLAB + 4
+    first, ahead = place_ref[0], place_ref[1]
+    copies = [
+        pltpu.make_async_copy(ref.at[pl.ds(first, planes)], labels.at[i], sems.at[i])
+        for i, ref in enumerate((region_ref, level_ref))
+    ]
+    for copy in copies:
+        copy.start()
+    depth_y, depth_x = labels.shape[2:]
+    lane = lax.broadcasted_iota(jnp.int32, (depth_x, LANES), 1)
+    x_row = lax.broadcasted_iota(jnp.int32, (depth_x, LANES), 0) - place_ref[2]
+    picks = [
+        jnp.where(x_row == lax.shift_right_logical(lane, 3) + dx, 1.0, 0.0) for dx in range(-2, 3)
+    ]
+    pick = jnp.concatenate(picks, axis=1).astype(jnp.bfloat16)
+    y_lane = lax.broadcasted_iota(jnp.int32, (depth_y, LANES), 1) & 7
+    y_row = lax.broadcasted_iota(jnp.int32, (depth_y, LANES), 0) - place_ref[3]
+    for copy in copies:
+        copy.wait()
+    code = labels[0] * 8 + labels[1] + 1
+    code = code.astype(jnp.float32).astype(jnp.bfloat16).reshape(planes * depth_y, depth_x)
+    spread = jnp.dot(code, pick, preferred_element_type=jnp.float32)
+    codes[...] = jnp.zeros(codes.shape, jnp.float32)
+    for off, (dx, dy) in enumerate(OFFSETS):
+        block = spread[:, (dx + 2) * LANES : (dx + 3) * LANES].reshape(planes, depth_y, LANES)
+        picked = jnp.sum(jnp.where((y_row == y_lane + dy)[None], block, 0.0), axis=1)
+        codes[off, pl.ds(ahead, planes), :] = picked
     for t, (dz, off) in enumerate(TAPS):
-        row = (dz + 2) * 8
-        code = codes[row : row + 8, off * LANES : (off + 1) * LANES].astype(jnp.int32)
+        row = dz + 4
+        code = codes[off, row : row + SLAB, :]
+        code = jnp.concatenate([code, code], axis=0).astype(jnp.int32)
+        inside = code > 0
+        code = code - 1
         region = lax.shift_right_logical(code, 3)
         level = code & 7
         real = jnp.zeros((8, LANES), jnp.float32)
@@ -67,9 +87,9 @@
         for value in range(8):
             real = jnp.where(region == value, eps_ref[value], real)
             imag = jnp.where(level == value, gain_ref[value], imag)
-        real_ref[t] = real
-        imag_ref[t] = imag
-        inside_ref[t] = jnp.where(code < OUTSIDE, 1.0, 0.0)
+        out_ref[t] = real
+        out_ref[len(TAPS) + t] = imag
+        out_ref[2 * len(TAPS) + t] = jnp.where(inside, 1.0, 0.0)
 
 
 def cmul(a, b):
@@ -82,9 +102,7 @@
 
 def moment_kernel(
     weight_ref,
-    real_ref,
-    imag_ref,
-    inside_ref,
+    material_ref,
     own_ref,
     ylo_ref,
     yhi_ref,
@@ -97,13 +115,19 @@
     coef,
 ):
     for plane in range(SLAB + 4):
-        reach = 13 if 2 <= plane < SLAB + 2 else (5 if plane in (1, SLAB + 2) else 1)
-        rows = jnp.concatenate(
-            [own_ref[plane], ylo_ref[plane], yhi_ref[plane], xlo_ref[plane], xhi_ref[plane]], axis=0
-        )
+        near, far = (plane - 1) * 16, 96 + (plane - 2) * 16
+        sides = (ylo_ref, yhi_ref, xlo_ref, xhi_ref)
+        if 2 <= plane < SLAB + 2:
+            reach, starts = 13, (near, far)
+        elif plane in (1, SLAB + 2):
+            reach, starts = 5, (near, near)
+        else:
+            reach, starts = 1, ()
+        rows = [own_ref[plane]] + [ref[i : i + 16] for ref in sides for i in starts]
+        rows = jnp.concatenate(rows, axis=0) if starts else rows[0]
         picked = lax.dot_general(
             rows,
-            pick_ref[:, : reach * LANES],
+            pick_ref[: rows.shape[0], : reach * LANES],
             (((0,), (0,)), ((), ())),
             preferred_element_type=jnp.float32,
         )
@@ -123,9 +147,10 @@
         node = (2.0 + weight[0], weight[1])
         inv = []
         for t in range(len(TAPS)):
-            diag_real = 6.0 + node[0] * real_ref[t] - node[1] * imag_ref[t]
-            diag_imag = node[0] * imag_ref[t] + node[1] * real_ref[t]
-            scale = inside_ref[t] / (diag_real * diag_real + diag_imag * diag_imag)
+            real, imag = material_ref[t], material_ref[len(TAPS) + t]
+            diag_real = 6.0 + node[0] * real - node[1] * imag
+            diag_imag = node[0] * imag + node[1] * real
+            scale = material_ref[2 * len(TAPS) + t] / (diag_real * diag_real + diag_imag * diag_imag)
             inv.append((diag_real * scale, -(diag_imag * scale)))
         centre = inv[TAP_AT[(0, 0, 0)]]
         lead0 = cmul(weight, centre)
@@ -205,28 +230,14 @@
             out_ref[z] = moments_ref[k, z].T
 
 
-def swap(block, axis, bit):
-    count = lax.axis_size(axis)
-    return lax.ppermute(block, axis, [(i, i ^ bit) for i in range(count)])
-
-
-def sum_of_four(block, axis, bits):
-    first, second, third = (swap(block, axis, bit) for bit in bits)
-    return (block + first) + (second + third)
-
-
-def reduce_cross(cross):
-    width = cross.shape[1] // 2
-    core = lax.axis_index("sx") & 1
-    low, high = cross[:, :width], cross[:, width:]
-    mine = jnp.where(core == 0, low, high)
-    block = mine + swap(jnp.where(core == 0, high, low), "sx", 1)
-    block = sum_of_four(block, "sy", (1, 2, 3))
-    block = sum_of_four(block, "quad", (1, 2, 3))
-    block = sum_of_four(block, "quad", (4, 8, 12))
-    block = block + swap(block, "sx", 2)
-    other = swap(block, "sx", 1)
-    return jnp.where(core == 0, block, other), jnp.where(core == 0, other, block)
+def swap(block, **bits):
+    axes = tuple(bits)
+    sizes = [lax.axis_size(axis) for axis in axes]
+    pairs = []
+    for place in np.ndindex(*sizes):
+        other = tuple(i ^ bit for i, bit in zip(place, bits.values()))
+        pairs.append((int(np.ravel_multi_index(place, sizes)), int(np.ravel_multi_index(other, sizes))))
+    return lax.ppermute(block, axes, pairs)
 
 
 def beside(block, axis, forward):
@@ -237,15 +248,18 @@
 
 def body(probes, quad_index, region_label, gain_label, region_eps, gain_rate):
     depth, cells_x, cells_y, columns = probes.shape
+    planes = SLAB + 4
     me = lax.axis_index("quad")
     start_z = me * SLAB
     start_x = lax.axis_index("sx") * cells_x
     start_y = lax.axis_index("sy") * cells_y
+    core = lax.axis_index("sx") & 1
 
     angle = 2.0 * math.pi * (quad_index.astype(jnp.float32) + 0.5) / (4 * QUAD)
     lane = lax.broadcasted_iota(jnp.int32, (1, 128), 1)
     weight = jnp.where(lane == me, jnp.cos(angle), 0.0)
     weight = jnp.where(lane == me + QUAD, jnp.sin(angle), weight)
+    weight = weight + swap(weight, quad=1)
 
     flat = probes.reshape(depth, cells_x * cells_y, columns)
     own = jnp.concatenate(
@@ -256,62 +270,86 @@
         ],
         axis=0,
     )
-    planes = SLAB + 4
     cube = own.reshape(planes, cells_x, cells_y, columns)
-    ylo = beside(cube[:, :, -2:, :].reshape(planes, -1, columns), "sy", True)
-    yhi = beside(cube[:, :, :2, :].reshape(planes, -1, columns), "sy", False)
-    weight = sum_of_four(weight, "quad", (1, 2, 3))
-
-    def edge(first):
-        at = 0 if first else (cells_x - 2)
-        pieces = [
-            own[:, at * cells_y : (at + 2) * cells_y],
-            ylo[:, at * 2 : (at + 2) * 2],
-            yhi[:, at * 2 : (at + 2) * 2],
+
+    def layers(near, far):
+        pieces = [cube[1 : planes - 1, :, near], cube[2 : planes - 2, :, far]]
+        return jnp.concatenate(pieces, axis=0).reshape(-1, columns)
+
+    ylo = beside(layers(cells_y - 1, cells_y - 2), "sy", True)
+    yhi = beside(layers(0, 1), "sy", False)
+    weight = weight + swap(weight, quad=3)
+
+    def edge(at, x):
+        rows = own[1 : planes - 1, at * cells_y : (at + 2) * cells_y].reshape(-1, columns)
+        corners = [
+            side[16 : 16 + SLAB * 16].reshape(SLAB, 16, columns)[:, x : x + 1] for side in (ylo, yhi)
         ]
-        return jnp.pad(jnp.concatenate(pieces, axis=1), ((0, 0), (0, 8), (0, 0)))
-
-    xlo = beside(edge(False), "sx", True)
-    xhi = beside(edge(True), "sx", False)
-    weight = sum_of_four(weight, "quad", (4, 8, 12))
-
-    code = jnp.pad(region_label * 8 + gain_label, 2, constant_values=OUTSIDE)
-    code = lax.dynamic_slice(
-        code, (start_z, start_x, start_y), (planes, cells_x + 4, cells_y + 4)
-    ).astype(jnp.bfloat16)
-    code = jnp.pad(code.reshape(planes, -1), ((0, 0), (0, 16)))
-    code = jnp.concatenate([code[d : d + SLAB] for d in range(5) for _ in range(2)], axis=0)
-    code = jnp.pad(code, ((0, 8), (0, 0)))
-
+        corners = jnp.pad(jnp.concatenate(corners, axis=1), ((0, 0), (0, 14), (0, 0)))
+        return jnp.concatenate([rows, corners.reshape(-1, columns)], axis=0)
+
+    low, high = edge(0, 0), edge(cells_x - 2, cells_x - 1)
+    inner = jnp.where(core == 0, high, low)
+    outer = jnp.where(core == 0, low, high)
+    weight, inner, outer = lax.optimization_barrier((weight, inner, outer))
+    outer = lax.ppermute(outer, "sx", [(1, 2), (2, 1)])
+    inner = swap(inner, sx=1)
+    weight = weight + swap(weight, quad=4)
+    weight, region_label, gain_label = lax.optimization_barrier((weight, region_label, gain_label))
+    weight = weight + swap(weight, quad=8)
+
+    first_plane = jnp.clip(start_z - 2, 0, depth - planes)
+    place = jnp.stack([first_plane, first_plane - start_z + 4, start_x, start_y]).astype(jnp.int32)
     smem = pl.BlockSpec(memory_space=pltpu.SMEM)
     vmem = pl.BlockSpec(memory_space=pltpu.VMEM)
+    anywhere = pl.BlockSpec(memory_space=pl.ANY)
     taps = len(TAPS)
-    per_tap = jax.ShapeDtypeStruct((taps, 8, LANES), jnp.float32)
-    real, imag, inside = pl.pallas_call(
+    mib = 1024 * 1024
+    material = pl.pallas_call(
         material_kernel,
-        out_shape=[per_tap] * 3,
-        in_specs=[smem, smem, vmem, vmem],
-        out_specs=[vmem] * 3,
+        out_shape=jax.ShapeDtypeStruct((3 * taps, 8, LANES), jnp.float32),
+        in_specs=[smem, smem, smem, anywhere, anywhere],
+        out_specs=vmem,
+        scratch_shapes=[
+            pltpu.VMEM((2, planes) + region_label.shape[:0:-1], jnp.int32),
+            pltpu.VMEM((len(OFFSETS), 16, LANES), jnp.float32),
+            pltpu.SemaphoreType.DMA((2,)),
+        ],
+        compiler_params=pltpu.CompilerParams(vmem_limit_bytes=8 * mib),
         cost_estimate=pl.CostEstimate(flops=40000000, bytes_accessed=1200000, transcendentals=0),
         name="material",
-    )(region_eps, gain_rate, code, jnp.asarray(selector(window_cells())))
-
+    )(place, region_eps, gain_rate, region_label.swapaxes(1, 2), gain_label.swapaxes(1, 2))
+
+    xlo = jnp.where(core == 0, outer, inner)
+    xhi = jnp.where(core == 0, inner, outer)
     moments, cross = pl.pallas_call(
         moment_kernel,
         out_shape=[
             jax.ShapeDtypeStruct((2, SLAB, columns, LANES), jnp.float32),
             jax.ShapeDtypeStruct((64, 256), jnp.float32),
         ],
-        in_specs=[smem] + [vmem] * 9,
+        in_specs=[smem] + [vmem] * 7,
         out_specs=[vmem] * 2,
         scratch_shapes=[
             pltpu.VMEM((planes, len(OFFSETS), columns, LANES), jnp.float32),
             pltpu.VMEM((4 * taps, 8, LANES), jnp.float32),
         ],
-        compiler_params=pltpu.CompilerParams(vmem_limit_bytes=32 * 1024 * 1024),
+        compiler_params=pltpu.CompilerParams(vmem_limit_bytes=24 * mib),
         cost_estimate=pl.CostEstimate(flops=600000000, bytes_accessed=3000000, transcendentals=0),
         name="moments",
-    )(weight, real, imag, inside, own, ylo, yhi, xlo, xhi, jnp.asarray(selector(source_cells())))
+    )(weight, material, own, ylo, yhi, xlo, xhi, jnp.asarray(selector()))
+
+    width = cross.shape[1] // 2
+    block = jnp.where(core == 0, cross[:, :width], cross[:, width:])
+    block = block + swap(jnp.where(core == 0, cross[:, width:], cross[:, :width]), sx=1)
+    block = block + swap(block, sy=1)
+    block = block + swap(block, sy=3)
+    block = block + swap(block, quad=1)
+    block = block + swap(block, quad=3)
+    block = block + swap(block, quad=4)
+    block = block + swap(block, quad=8)
+    block, moments = lax.optimization_barrier((block, moments))
+    block = block + swap(block, quad=8, sx=2)
 
     out = jax.ShapeDtypeStruct((SLAB, LANES, columns), jnp.float32)
     first, second = pl.pallas_call(
@@ -319,15 +357,17 @@
         out_shape=[out] * 2,
         in_specs=[vmem],
         out_specs=[vmem] * 2,
+        compiler_params=pltpu.CompilerParams(vmem_limit_bytes=8 * mib),
         cost_estimate=pl.CostEstimate(flops=1000000, bytes_accessed=1000000, transcendentals=0),
         name="turn",
     )(moments)
-    shape = (SLAB, cells_x, cells_y, columns)
-
-    halves = reduce_cross(cross)
+    block, first, second = lax.optimization_barrier((block, first, second))
+    other = swap(block, sx=1)
+    halves = (jnp.where(core == 0, block, other), jnp.where(core == 0, other, block))
     projections = jnp.stack(
         [jnp.stack([half[:, :64], half[:, 64:]], axis=0) for half in halves], axis=0
     )
+    shape = (SLAB, cells_x, cells_y, columns)
     return (first.reshape(shape), second.reshape(shape), projections)
 
 

time: 90.8 us -> 74.3 us (0.82)
  waiting for transfers between devices: 25.2 us -> 18.8 us
  local copies, waits for them, and re-layouts: 6.47 us -> 2.15 us
  other arithmetic: 3.41 us -> 0.97 us
  Pallas kernels: 9.54 us -> 7.93 us
  starting transfers between devices: 43.9 us -> 42.3 us
    ppermute x4 -> x2, starting transfers between devices: 15.5 us -> 4.49 us  [beside(): lax.ppermute(block, axis, pairs if forward else [(b, a) for a, b in pairs])]
    ppermute x18 -> x15, starting transfers between devices: 28.4 us -> 37.8 us  [the longest x14 27.4 us: swap(): return lax.ppermute(block, axes, pairs)]
    ppermute x4 -> x2, waiting for transfers between devices: 7.59 us -> 0.01 us  [beside(): lax.ppermute(block, axis, pairs if forward else [(b, a) for a, b in pairs])]
    unnamed x12 -> x10, local copies, waits for them, and re-layouts: 3.48 us -> 0.02 us
    add x8 -> x12, other arithmetic: 2.51 us -> 0.06 us  [the longest x1 0.01 us: body(): weight = weight + swap(weight, quad=1)]
    ppermute x18 -> x15, waiting for transfers between devices: 17.7 us -> 18.8 us  [the longest x14 18.8 us: swap(): return lax.ppermute(block, axes, pairs)]
    pallas_call x1, Pallas kernels: 1.96 us -> 0.92 us  [body(): pl.pallas_call(turn_kernel, out_shape=[out] * 2, in_specs=[vmem], out_spe...]
  transfers between devices with their start and end apart: 22 -> 17, of which waited for: 9 -> 11; matrix products, arithmetic and copies ran while one was open for 6% -> 3% of each run, Pallas kernels for 5% -> 3%
where the time goes in v2:
time: 74.3 us; the launch traced here: 74.1 us
  starting transfers between devices  42.3 us (57%)
  waiting for transfers between devices  18.8 us (25%)
  Pallas kernels  7.93 us (11%)
  local copies, waits for them, and re-layouts  2.15 us (3%)
  between operations  1.91 us (3%)
  other arithmetic  0.97 us (1%)
    ppermute x14, starting transfers between devices, swap(): return lax.ppermute(block, axes, pairs)  27.4 us
    ppermute x14, waiting for transfers between devices, swap(): return lax.ppermute(block, axes, pairs)  18.8 us
    ppermute x1, starting transfers between devices, body(): outer = lax.ppermute(outer, 'sx', [(1, 2), (2, 1)])  10.5 us
    pallas_call x1, Pallas kernels, body(): pl.pallas_call(moment_kernel, out_shape=[jax.ShapeDtypeStruct((2, SLAB, c...  5.58 us
    ppermute x2, starting transfers between devices, beside(): lax.ppermute(block, axis, pairs if forward else [(b, a) for a, b in pairs])  4.49 us
  transfers between devices with their start and end apart: 17, of which 11 were waited for; matrix products, arithmetic and copies ran while one was open for 3% of the time, Pallas kernels for 3%

profile of v2, /device:TPU:1, one launch (start us, length us, event | category | flops | bytes accessed | tf_op | source)
XLA Modules:
  0.0 74.1 jit_solution(1187613078069495663)
XLA Ops:
  0.6 0.0 copy-start.1
  1.6 2.1 %collective-permute-start = (f32[1,128]{1,0:T(1,128)S(1)}, f32[1,128]{1,0:T(1,128)S(1)}, u32[]{:S(2)}, u32[]{:S(2)}) collective-permute-start(f32[1,128]{1,0:T(1,128)S(1)} %compare_select_fusion.1), channel_id=1, source_target_pairs={{0,16},{16,0},{32,48},{48,32},{64,80},{80,64},{96,112},{112,96},{1... | collective-permute-start | bytes 1544 | tf_op jit(solution)/shard_map/ppermute | solution.py:240
  3.8 0.9 %constant_dynamic-slice_fusion.1 = bf16[4,128,128]{2,1,0:T(8,128)(2,1)S(1)} fusion(bf16[64,128,128]{2,1,0:T(8,128)(2,1)} %bitcast.49, s32[]{:T(128)S(6)} %select_n.75), kind=kLoop, calls=%fused_computation.34 | loop fusion | bytes 262148 | tf_op jit(solution)/shard_map/dynamic_slice | solution.py:268
  4.7 0.9 %constant_dynamic-slice_fusion.2 = (bf16[2,128,128]{2,1,0:T(8,128)(2,1)S(1)}, bf16[2,128,128]{2,1,0:T(8,128)(2,1)S(1)}) fusion(bf16[64,128,128]{2,1,0:T(8,128)(2,1)} %bitcast.50, s32[]{:T(128)S(6)} %max.5, s32[]{:T(128)S(6)} %select_n.76), kind=kLoop, calls=%fused_computation.35 | loop fusion | bytes 262152 | tf_op jit(solution)/shard_map/dynamic_slice | solution.py:267
  5.6 0.0 copy-start.4
  5.6 0.1 fusion.9
  5.7 0.1 fusion.8
  5.8 3.2 %collective-permute-start.2 = (bf16[160,128]{1,0:T(8,128)(2,1)S(1)}, bf16[160,128]{1,0:T(8,128)(2,1)S(1)}, u32[]{:S(2)}, u32[]{:S(2)}) collective-permute-start(bf16[160,128]{1,0:T(8,128)(2,1)S(1)} %bitcast.47), channel_id=1, source_target_pairs={{0,1},{1,2},{2,3},{4,5},{5,6},{6,7},{8,9},{9,10},{10,11},{12,13},{... | collective-permute-start | bytes 122888 | tf_op jit(solution)/shard_map/ppermute | solution.py:246
  9.1 1.3 %collective-permute-start.3 = (bf16[160,128]{1,0:T(8,128)(2,1)S(1)}, bf16[160,128]{1,0:T(8,128)(2,1)S(1)}, u32[]{:S(2)}, u32[]{:S(2)}) collective-permute-start(bf16[160,128]{1,0:T(8,128)(2,1)S(1)} %bitcast.48), channel_id=1, source_target_pairs={{1,0},{2,1},{3,2},{5,4},{6,5},{7,6},{9,8},{10,9},{11,10},{13,12},{... | collective-permute-start | bytes 122888 | tf_op jit(solution)/shard_map/ppermute | solution.py:246
  10.4 0.0 collective-permute-done
  10.4 1.9 %collective-permute-start.1 = (f32[1,128]{1,0:T(1,128)S(1)}, f32[1,128]{1,0:T(1,128)S(1)}, u32[]{:S(2)}, u32[]{:S(2)}) collective-permute-start(f32[1,128]{1,0:T(1,128)S(1)} %fusion.12), channel_id=1, source_target_pairs={{0,48},{16,32},{32,16},{48,0},{64,112},{80,96},{96,80},{112,64},{1... | collective-permute-start | bytes 1544 | tf_op jit(solution)/shard_map/ppermute | solution.py:240
  12.3 1.8 %collective-permute-done.1 = f32[1,128]{1,0:T(1,128)S(1)} collective-permute-done((f32[1,128]{1,0:T(1,128)S(1)}, f32[1,128]{1,0:T(1,128)S(1)}, u32[]{:S(2)}, u32[]{:S(2)}) %collective-permute-start.1) | collective-permute-done | bytes 544 | tf_op jit(solution)/shard_map/ppermute | solution.py:240
  14.1 0.0 collective-permute-done.2.ylo_ref
  14.1 0.0 collective-permute-done.3.yhi_ref
  14.2 1.7 %collective-permute-start.4 = (f32[1,128]{1,0:T(1,128)S(1)}, f32[1,128]{1,0:T(1,128)S(1)}, u32[]{:S(2)}, u32[]{:S(2)}) collective-permute-start(f32[1,128]{1,0:T(1,128)S(1)} %fusion.13), channel_id=1, source_target_pairs={{0,64},{16,80},{32,96},{48,112},{64,0},{80,16},{96,32},{112,48},{1... | collective-permute-start | bytes 1544 | tf_op jit(solution)/shard_map/ppermute | solution.py:240
  16.0 10.5 %collective-permute-start.6 = (bf16[160,128]{1,0:T(8,128)(2,1)S(1)}, bf16[160,128]{1,0:T(8,128)(2,1)S(1)}, u32[]{:S(2)}, u32[]{:S(2)}) collective-permute-start(bf16[160,128]{1,0:T(8,128)(2,1)S(1)} %get-tuple-element.22), channel_id=1, source_target_pairs={{4,8},{8,4},{5,9},{9,5},{6,10},{10,6},{7,11},{11,7},{20,24},{24,20... | collective-permute-start | bytes 122888 | tf_op jit(solution)/shard_map/ppermute | solution.py:295
  26.4 0.1 collective-permute-start.7
  26.5 0.1 pad_add_fusion.place_ref
  26.6 0.0 collective-permute-done.4
  26.6 1.3 %collective-permute-start.5 = (f32[1,128]{1,0:T(1,128)S(1)}, f32[1,128]{1,0:T(1,128)S(1)}, u32[]{:S(2)}, u32[]{:S(2)}) collective-permute-start(f32[1,128]{1,0:T(1,128)S(1)} %add.67), channel_id=1, source_target_pairs={{0,128},{16,144},{32,160},{48,176},{64,192},{80,208},{96,224},{112... | collective-permute-start | bytes 1544 | tf_op jit(solution)/shard_map/ppermute | solution.py:240
  27.9 0.0 copy-done.1
  27.9 1.4 %material.1.material_ref = f32[75,8,128]{2,1,0:T(8,128)S(1)} custom-call(s32[4]{0:T(128)S(1)} %pad_add_fusion.place_ref, f32[8]{0:T(128)S(1)} %copy-done.2, f32[8]{0:T(128)S(1)} %copy-done.3, s32[64,32,64]{2,1,0:T(8,128)S(1)} %bitcast.41, s32[64,32,64]{2,1,0:T(8,128)S(1)} %bitcast.42), custom_call_target="tpu_custom_call" | custom-call | flops 40000000 | bytes 1200000 | tf_op jit(solution)/shard_map/material/pallas_call | solution.py:308
  29.3 0.7 collective-permute-done.5
  30.0 0.0 collective-permute-done.6
  30.0 0.0 collective-permute-done.7
  30.0 5.6 %moments.1 = (f32[2,4,128,128]{3,2,1,0:T(8,128)S(1)}, f32[64,256]{1,0:T(8,128)S(1)}) custom-call(f32[1,128]{1,0:T(1,128)S(1)} %add.68.weight_ref, f32[75,8,128]{2,1,0:T(8,128)S(1)} %material.1.material_ref, bf16[8,128,128]{2,1,0:T(8,128)(2,1)S(1)} %get-tuple-element.37.own_ref, bf16[160,128]{1,0:T(8,128)(2,1)S(1)} %collective-permute-done.2.ylo_ref, ...), custom_call_target="tpu_custom_call" | custom-call | flops 600000000 | bytes 3000000 | tf_op jit(solution)/shard_map/moments/pallas_call | solution.py:325
  35.6 1.7 %collective-permute-start.8 = (f32[64,128]{1,0:T(8,128)S(1)}, f32[64,128]{1,0:T(8,128)S(1)}, u32[]{:S(2)}, u32[]{:S(2)}) collective-permute-start(f32[64,128]{1,0:T(8,128)S(1)} %slice_select_fusion), channel_id=1, source_target_pairs={{0,4},{4,0},{8,12},{12,8},{1,5},{5,1},{9,13},{13,9},{2,6},{6,2},{1... | collective-permute-start | bytes 98312 | tf_op jit(solution)/shard_map/ppermute | solution.py:240
  37.4 0.9 %collective-permute-done.8 = f32[64,128]{1,0:T(8,128)S(1)} collective-permute-done((f32[64,128]{1,0:T(8,128)S(1)}, f32[64,128]{1,0:T(8,128)S(1)}, u32[]{:S(2)}, u32[]{:S(2)}) %collective-permute-start.8) | collective-permute-done | bytes 32800 | tf_op jit(solution)/shard_map/ppermute | solution.py:240
  38.2 2.4 %collective-permute-start.9 = (f32[64,128]{1,0:T(8,128)S(1)}, f32[64,128]{1,0:T(8,128)S(1)}, u32[]{:S(2)}, u32[]{:S(2)}) collective-permute-start(f32[64,128]{1,0:T(8,128)S(1)} %select_add_fusion), channel_id=1, source_target_pairs={{0,1},{1,0},{2,3},{3,2},{4,5},{5,4},{6,7},{7,6},{8,9},{9,8},{10,11... | collective-permute-start | bytes 98312 | tf_op jit(solution)/shard_map/ppermute | solution.py:240
  40.6 1.3 %collective-permute-done.9 = f32[64,128]{1,0:T(8,128)S(1)} collective-permute-done((f32[64,128]{1,0:T(8,128)S(1)}, f32[64,128]{1,0:T(8,128)S(1)}, u32[]{:S(2)}, u32[]{:S(2)}) %collective-permute-start.9) | collective-permute-done | bytes 32800 | tf_op jit(solution)/shard_map/ppermute | solution.py:240
  41.9 2.9 %collective-permute-start.10 = (f32[64,128]{1,0:T(8,128)S(1)}, f32[64,128]{1,0:T(8,128)S(1)}, u32[]{:S(2)}, u32[]{:S(2)}) collective-permute-start(f32[64,128]{1,0:T(8,128)S(1)} %add.71), channel_id=1, source_target_pairs={{0,3},{1,2},{2,1},{3,0},{4,7},{5,6},{6,5},{7,4},{8,11},{9,10},{10,... | collective-permute-start | bytes 98312 | tf_op jit(solution)/shard_map/ppermute | solution.py:240
  44.8 1.3 %collective-permute-done.10 = f32[64,128]{1,0:T(8,128)S(1)} collective-permute-done((f32[64,128]{1,0:T(8,128)S(1)}, f32[64,128]{1,0:T(8,128)S(1)}, u32[]{:S(2)}, u32[]{:S(2)}) %collective-permute-start.10) | collective-permute-done | bytes 32800 | tf_op jit(solution)/shard_map/ppermute | solution.py:240
  46.1 0.0 collective-permute-start.11
  46.1 2.8 %collective-permute-done.11 = f32[64,128]{1,0:T(8,128)S(1)} collective-permute-done((f32[64,128]{1,0:T(8,128)S(1)}, f32[64,128]{1,0:T(8,128)S(1)}, u32[]{:S(2)}, u32[]{:S(2)}) %collective-permute-start.11) | collective-permute-done | bytes 32800 | tf_op jit(solution)/shard_map/ppermute | solution.py:240
  48.9 1.8 %collective-permute-start.12 = (f32[64,128]{1,0:T(8,128)S(1)}, f32[64,128]{1,0:T(8,128)S(1)}, u32[]{:S(2)}, u32[]{:S(2)}) collective-permute-start(f32[64,128]{1,0:T(8,128)S(1)} %add.73), channel_id=1, source_target_pairs={{0,48},{16,32},{32,16},{48,0},{64,112},{80,96},{96,80},{112,64},{1... | collective-permute-start | bytes 98312 | tf_op jit(solution)/shard_map/ppermute | solution.py:240
  50.7 2.2 %collective-permute-done.12 = f32[64,128]{1,0:T(8,128)S(1)} collective-permute-done((f32[64,128]{1,0:T(8,128)S(1)}, f32[64,128]{1,0:T(8,128)S(1)}, u32[]{:S(2)}, u32[]{:S(2)}) %collective-permute-start.12) | collective-permute-done | bytes 32800 | tf_op jit(solution)/shard_map/ppermute | solution.py:240
  52.9 0.7 collective-permute-start.13
  53.6 2.0 %collective-permute-done.13 = f32[64,128]{1,0:T(8,128)S(1)} collective-permute-done((f32[64,128]{1,0:T(8,128)S(1)}, f32[64,128]{1,0:T(8,128)S(1)}, u32[]{:S(2)}, u32[]{:S(2)}) %collective-permute-start.13) | collective-permute-done | bytes 32800 | tf_op jit(solution)/shard_map/ppermute | solution.py:240
  55.6 1.2 %collective-permute-start.14 = (f32[64,128]{1,0:T(8,128)S(1)}, f32[64,128]{1,0:T(8,128)S(1)}, u32[]{:S(2)}, u32[]{:S(2)}) collective-permute-start(f32[64,128]{1,0:T(8,128)S(1)} %add.75), channel_id=1, source_target_pairs={{0,128},{16,144},{32,160},{48,176},{64,192},{80,208},{96,224},{112... | collective-permute-start | bytes 98312 | tf_op jit(solution)/shard_map/ppermute | solution.py:240
  56.8 2.5 %collective-permute-done.14 = f32[64,128]{1,0:T(8,128)S(1)} collective-permute-done((f32[64,128]{1,0:T(8,128)S(1)}, f32[64,128]{1,0:T(8,128)S(1)}, u32[]{:S(2)}, u32[]{:S(2)}) %collective-permute-start.14) | collective-permute-done | bytes 32800 | tf_op jit(solution)/shard_map/ppermute | solution.py:240
  59.3 1.3 %collective-permute-start.15 = (f32[64,128]{1,0:T(8,128)S(1)}, f32[64,128]{1,0:T(8,128)S(1)}, u32[]{:S(2)}, u32[]{:S(2)}) collective-permute-start(f32[64,128]{1,0:T(8,128)S(1)} %add.76), channel_id=1, source_target_pairs={{0,136},{4,140},{8,128},{12,132},{16,152},{20,156},{24,144},{28,14... | collective-permute-start | bytes 98312 | tf_op jit(solution)/shard_map/ppermute | solution.py:240
  60.6 0.9 %turn.1 = (f32[4,128,128]{2,1,0:T(8,128)}, f32[4,128,128]{2,1,0:T(8,128)}) custom-call(f32[2,4,128,128]{3,2,1,0:T(8,128)S(1)} %get-tuple-element.27.moments_ref), custom_call_target="tpu_custom_call" | custom-call | flops 1000000 | bytes 1000000 | tf_op jit(solution)/shard_map/turn/pallas_call | solution.py:355
  61.6 2.6 %collective-permute-done.15 = f32[64,128]{1,0:T(8,128)S(1)} collective-permute-done((f32[64,128]{1,0:T(8,128)S(1)}, f32[64,128]{1,0:T(8,128)S(1)}, u32[]{:S(2)}, u32[]{:S(2)}) %collective-permute-start.15) | collective-permute-done | bytes 32800 | tf_op jit(solution)/shard_map/ppermute | solution.py:240
  64.2 8.2 %collective-permute-start.16 = (f32[64,128]{1,0:T(8,128)S(1)}, f32[64,128]{1,0:T(8,128)S(1)}, u32[]{:S(2)}, u32[]{:S(2)}) collective-permute-start(f32[64,128]{1,0:T(8,128)S(1)} %add.77), channel_id=1, source_target_pairs={{0,4},{4,0},{8,12},{12,8},{1,5},{5,1},{9,13},{13,9},{2,6},{6,2},{1... | collective-permute-start | bytes 98312 | tf_op jit(solution)/shard_map/ppermute | solution.py:240
  72.4 0.9 %collective-permute-done.16 = f32[64,128]{1,0:T(8,128)S(1)} collective-permute-done((f32[64,128]{1,0:T(8,128)S(1)}, f32[64,128]{1,0:T(8,128)S(1)}, u32[]{:S(2)}, u32[]{:S(2)}) %collective-permute-start.16) | collective-permute-done | bytes 32800 | tf_op jit(solution)/shard_map/ppermute | solution.py:240
  73.3 0.1 slice_bitcast_fusion.3
  73.3 0.1 slice_bitcast_fusion.1
  73.4 0.7 pad_maximum_fusion.1
  (38 shorter events, 0.3 us)
Async XLA Ops:
  0.6 27.3 %copy-start.1 = (s32[64,64,32]{1,2,0:T(8,128)S(1)}, s32[64,64,32]{1,2,0:T(8,128)}, u32[]{:S(2)}) copy-start(s32[64,64,32]{1,2,0:T(8,128)} %param.10) | copy-start | bytes 1572868
  0.6 27.3 %copy-start = (s32[64,64,32]{1,2,0:T(8,128)S(1)}, s32[64,64,32]{1,2,0:T(8,128)}, u32[]{:S(2)}) copy-start(s32[64,64,32]{1,2,0:T(8,128)} %param.9) | copy-start | bytes 1572868
  0.7 27.2 %copy-start.3 = (f32[8]{0:T(128)S(1)}, f32[8]{0:T(128)}, u32[]{:S(2)}) copy-start(f32[8]{0:T(128)} %gain_ref.1) | copy-start | bytes 100
  0.7 27.2 %copy-start.2 = (f32[8]{0:T(128)S(1)}, f32[8]{0:T(128)}, u32[]{:S(2)}) copy-start(f32[8]{0:T(128)} %eps_ref.1) | copy-start | bytes 100
  1.6 8.7 %collective-permute-start = (f32[1,128]{1,0:T(1,128)S(1)}, f32[1,128]{1,0:T(1,128)S(1)}, u32[]{:S(2)}, u32[]{:S(2)}) collective-permute-start(f32[1,128]{1,0:T(1,128)S(1)} %compare_select_fusion.1), channel_id=1, source_target_pairs={{0,16},{16,0},{32,48},{48,32},{64,80},{80,64},{96,112},{112,96},{1... | collective-permute-start | bytes 1544 | tf_op jit(solution)/shard_map/ppermute | solution.py:240
  5.6 24.5 %copy-start.4 = (bf16[256,1664]{1,0:T(8,128)(2,1)S(1)}, bf16[256,1664]{1,0:T(8,128)(2,1)}, u32[]{:S(2)}) copy-start(bf16[256,1664]{1,0:T(8,128)(2,1)} %constant.45.clone.pick_ref) | copy-start | bytes 2555908
  5.8 8.3 %collective-permute-start.2 = (bf16[160,128]{1,0:T(8,128)(2,1)S(1)}, bf16[160,128]{1,0:T(8,128)(2,1)S(1)}, u32[]{:S(2)}, u32[]{:S(2)}) collective-permute-start(bf16[160,128]{1,0:T(8,128)(2,1)S(1)} %bitcast.47), channel_id=1, source_target_pairs={{0,1},{1,2},{2,3},{4,5},{5,6},{6,7},{8,9},{9,10},{10,11},{12,13},{... | collective-permute-start | bytes 122888 | tf_op jit(solution)/shard_map/ppermute | solution.py:246
  9.1 5.1 %collective-permute-start.3 = (bf16[160,128]{1,0:T(8,128)(2,1)S(1)}, bf16[160,128]{1,0:T(8,128)(2,1)S(1)}, u32[]{:S(2)}, u32[]{:S(2)}) collective-permute-start(bf16[160,128]{1,0:T(8,128)(2,1)S(1)} %bitcast.48), channel_id=1, source_target_pairs={{1,0},{2,1},{3,2},{5,4},{6,5},{7,6},{9,8},{10,9},{11,10},{13,12},{... | collective-permute-start | bytes 122888 | tf_op jit(solution)/shard_map/ppermute | solution.py:246
  10.4 3.7 %collective-permute-start.1 = (f32[1,128]{1,0:T(1,128)S(1)}, f32[1,128]{1,0:T(1,128)S(1)}, u32[]{:S(2)}, u32[]{:S(2)}) collective-permute-start(f32[1,128]{1,0:T(1,128)S(1)} %fusion.12), channel_id=1, source_target_pairs={{0,48},{16,32},{32,16},{48,0},{64,112},{80,96},{96,80},{112,64},{1... | collective-permute-start | bytes 1544 | tf_op jit(solution)/shard_map/ppermute | solution.py:240
  14.2 12.4 %collective-permute-start.4 = (f32[1,128]{1,0:T(1,128)S(1)}, f32[1,128]{1,0:T(1,128)S(1)}, u32[]{:S(2)}, u32[]{:S(2)}) collective-permute-start(f32[1,128]{1,0:T(1,128)S(1)} %fusion.13), channel_id=1, source_target_pairs={{0,64},{16,80},{32,96},{48,112},{64,0},{80,16},{96,32},{112,48},{1... | collective-permute-start | bytes 1544 | tf_op jit(solution)/shard_map/ppermute | solution.py:240
  16.0 14.0 %collective-permute-start.6 = (bf16[160,128]{1,0:T(8,128)(2,1)S(1)}, bf16[160,128]{1,0:T(8,128)(2,1)S(1)}, u32[]{:S(2)}, u32[]{:S(2)}) collective-permute-start(bf16[160,128]{1,0:T(8,128)(2,1)S(1)} %get-tuple-element.22), channel_id=1, source_target_pairs={{4,8},{8,4},{5,9},{9,5},{6,10},{10,6},{7,11},{11,7},{20,24},{24,20... | collective-permute-start | bytes 122888 | tf_op jit(solution)/shard_map/ppermute | solution.py:295
  26.4 3.6 %collective-permute-start.7 = (bf16[160,128]{1,0:T(8,128)(2,1)S(1)}, bf16[160,128]{1,0:T(8,128)(2,1)S(1)}, u32[]{:S(2)}, u32[]{:S(2)}) collective-permute-start(bf16[160,128]{1,0:T(8,128)(2,1)S(1)} %get-tuple-element.23), channel_id=1, source_target_pairs={{0,4},{4,0},{8,12},{12,8},{1,5},{5,1},{9,13},{13,9},{2,6},{6,2},{1... | collective-permute-start | bytes 122888 | tf_op jit(solution)/shard_map/ppermute | solution.py:240
  26.6 3.4 %collective-permute-start.5 = (f32[1,128]{1,0:T(1,128)S(1)}, f32[1,128]{1,0:T(1,128)S(1)}, u32[]{:S(2)}, u32[]{:S(2)}) collective-permute-start(f32[1,128]{1,0:T(1,128)S(1)} %add.67), channel_id=1, source_target_pairs={{0,128},{16,144},{32,160},{48,176},{64,192},{80,208},{96,224},{112... | collective-permute-start | bytes 1544 | tf_op jit(solution)/shard_map/ppermute | solution.py:240
  35.6 2.6 %collective-permute-start.8 = (f32[64,128]{1,0:T(8,128)S(1)}, f32[64,128]{1,0:T(8,128)S(1)}, u32[]{:S(2)}, u32[]{:S(2)}) collective-permute-start(f32[64,128]{1,0:T(8,128)S(1)} %slice_select_fusion), channel_id=1, source_target_pairs={{0,4},{4,0},{8,12},{12,8},{1,5},{5,1},{9,13},{13,9},{2,6},{6,2},{1... | collective-permute-start | bytes 98312 | tf_op jit(solution)/shard_map/ppermute | solution.py:240
  38.2 3.7 %collective-permute-start.9 = (f32[64,128]{1,0:T(8,128)S(1)}, f32[64,128]{1,0:T(8,128)S(1)}, u32[]{:S(2)}, u32[]{:S(2)}) collective-permute-start(f32[64,128]{1,0:T(8,128)S(1)} %select_add_fusion), channel_id=1, source_target_pairs={{0,1},{1,0},{2,3},{3,2},{4,5},{5,4},{6,7},{7,6},{8,9},{9,8},{10,11... | collective-permute-start | bytes 98312 | tf_op jit(solution)/shard_map/ppermute | solution.py:240
  41.9 4.2 %collective-permute-start.10 = (f32[64,128]{1,0:T(8,128)S(1)}, f32[64,128]{1,0:T(8,128)S(1)}, u32[]{:S(2)}, u32[]{:S(2)}) collective-permute-start(f32[64,128]{1,0:T(8,128)S(1)} %add.71), channel_id=1, source_target_pairs={{0,3},{1,2},{2,1},{3,0},{4,7},{5,6},{6,5},{7,4},{8,11},{9,10},{10,... | collective-permute-start | bytes 98312 | tf_op jit(solution)/shard_map/ppermute | solution.py:240
  46.1 2.8 %collective-permute-start.11 = (f32[64,128]{1,0:T(8,128)S(1)}, f32[64,128]{1,0:T(8,128)S(1)}, u32[]{:S(2)}, u32[]{:S(2)}) collective-permute-start(f32[64,128]{1,0:T(8,128)S(1)} %add.72), channel_id=1, source_target_pairs={{0,16},{16,0},{32,48},{48,32},{64,80},{80,64},{96,112},{112,96},{1... | collective-permute-start | bytes 98312 | tf_op jit(solution)/shard_map/ppermute | solution.py:240
  48.9 4.0 %collective-permute-start.12 = (f32[64,128]{1,0:T(8,128)S(1)}, f32[64,128]{1,0:T(8,128)S(1)}, u32[]{:S(2)}, u32[]{:S(2)}) collective-permute-start(f32[64,128]{1,0:T(8,128)S(1)} %add.73), channel_id=1, source_target_pairs={{0,48},{16,32},{32,16},{48,0},{64,112},{80,96},{96,80},{112,64},{1... | collective-permute-start | bytes 98312 | tf_op jit(solution)/shard_map/ppermute | solution.py:240
  52.9 2.8 %collective-permute-start.13 = (f32[64,128]{1,0:T(8,128)S(1)}, f32[64,128]{1,0:T(8,128)S(1)}, u32[]{:S(2)}, u32[]{:S(2)}) collective-permute-start(f32[64,128]{1,0:T(8,128)S(1)} %add.74), channel_id=1, source_target_pairs={{0,64},{16,80},{32,96},{48,112},{64,0},{80,16},{96,32},{112,48},{1... | collective-permute-start | bytes 98312 | tf_op jit(solution)/shard_map/ppermute | solution.py:240
  55.6 3.7 %collective-permute-start.14 = (f32[64,128]{1,0:T(8,128)S(1)}, f32[64,128]{1,0:T(8,128)S(1)}, u32[]{:S(2)}, u32[]{:S(2)}) collective-permute-start(f32[64,128]{1,0:T(8,128)S(1)} %add.75), channel_id=1, source_target_pairs={{0,128},{16,144},{32,160},{48,176},{64,192},{80,208},{96,224},{112... | collective-permute-start | bytes 98312 | tf_op jit(solution)/shard_map/ppermute | solution.py:240
  59.3 4.9 %collective-permute-start.15 = (f32[64,128]{1,0:T(8,128)S(1)}, f32[64,128]{1,0:T(8,128)S(1)}, u32[]{:S(2)}, u32[]{:S(2)}) collective-permute-start(f32[64,128]{1,0:T(8,128)S(1)} %add.76), channel_id=1, source_target_pairs={{0,136},{4,140},{8,128},{12,132},{16,152},{20,156},{24,144},{28,14... | collective-permute-start | bytes 98312 | tf_op jit(solution)/shard_map/ppermute | solution.py:240
  64.2 9.1 %collective-permute-start.16 = (f32[64,128]{1,0:T(8,128)S(1)}, f32[64,128]{1,0:T(8,128)S(1)}, u32[]{:S(2)}, u32[]{:S(2)}) collective-permute-start(f32[64,128]{1,0:T(8,128)S(1)} %add.77), channel_id=1, source_target_pairs={{0,4},{4,0},{8,12},{12,8},{1,5},{5,1},{9,13},{13,9},{2,6},{6,2},{1... | collective-permute-start | bytes 98312 | tf_op jit(solution)/shard_map/ppermute | solution.py:240

commit v3 on v2

--- a/solution.py
+++ b/solution.py
@@ -46,9 +46,51 @@
     return pick.astype(jnp.bfloat16)
 
 
-def material_kernel(place_ref, eps_ref, gain_ref, region_ref, level_ref, out_ref, labels, codes, sems):
+def slab_kernel(quad_ref, probes_ref, weight_ref, own_ref, inner_ref, outer_ref, sems):
+    depth = probes_ref.shape[0]
+    start = lax.axis_index("quad") * SLAB
+    spans = (
+        (jnp.maximum(start - 2, 0), 0, 2),
+        (start, 2, SLAB),
+        (jnp.minimum(start + SLAB, depth - 2), SLAB + 2, 2),
+    )
+    copies = [
+        pltpu.make_async_copy(probes_ref.at[pl.ds(a, n)], own_ref.at[b : b + n], sems.at[i])
+        for i, (a, b, n) in enumerate(spans)
+    ]
+    for copy in copies:
+        copy.start()
+    me = lax.axis_index("quad")
+    index = jnp.full((1, LANES), quad_ref[0], jnp.int32).astype(jnp.float32)
+    angle = 2.0 * math.pi * (index + 0.5) / (4 * QUAD)
+    lane = lax.broadcasted_iota(jnp.int32, (1, LANES), 1)
+    weight = jnp.where(lane == me, jnp.cos(angle), 0.0)
+    weight_ref[...] = jnp.where(lane == me + QUAD, jnp.sin(angle), weight)
+    row = lax.broadcasted_iota(jnp.int32, (32, LANES), 0)
+    cell = lax.broadcasted_iota(jnp.int32, (32, LANES), 1)
+    even = (lax.axis_index("sy") & 1) == 0
+    deep = jnp.where(row < CX, 0, 1)
+    picks = []
+    for high in (even, jnp.logical_not(even)):
+        y = jnp.where(high, CY - 1 - deep, deep)
+        picks.append(jnp.where(cell == (row & (CX - 1)) * CY + y, 1.0, 0.0).astype(jnp.bfloat16))
+    for copy in copies:
+        copy.wait()
+    for pick, out_ref in zip(picks, (inner_ref, outer_ref)):
+        for plane in range(1, SLAB + 3):
+            layers = jnp.dot(pick, own_ref[plane], preferred_element_type=jnp.float32)
+            layers = layers.astype(jnp.bfloat16)
+            out_ref[(plane - 1) * CX : plane * CX] = layers[:CX]
+            if 2 <= plane < SLAB + 2:
+                at = (SLAB + 2 + plane - 2) * CX
+                out_ref[at : at + CX] = layers[CX:]
+
+
+def material_kernel(eps_ref, gain_ref, region_ref, level_ref, out_ref, labels, codes, sems):
     planes = SLAB + 4
-    first, ahead = place_ref[0], place_ref[1]
+    start = lax.axis_index("quad") * SLAB
+    first = jnp.clip(start - 2, 0, region_ref.shape[0] - planes)
+    ahead = first - start + 4
     copies = [
         pltpu.make_async_copy(ref.at[pl.ds(first, planes)], labels.at[i], sems.at[i])
         for i, ref in enumerate((region_ref, level_ref))
@@ -57,13 +99,13 @@
         copy.start()
     depth_y, depth_x = labels.shape[2:]
     lane = lax.broadcasted_iota(jnp.int32, (depth_x, LANES), 1)
-    x_row = lax.broadcasted_iota(jnp.int32, (depth_x, LANES), 0) - place_ref[2]
+    x_row = lax.broadcasted_iota(jnp.int32, (depth_x, LANES), 0) - lax.axis_index("sx") * CX
     picks = [
         jnp.where(x_row == lax.shift_right_logical(lane, 3) + dx, 1.0, 0.0) for dx in range(-2, 3)
     ]
     pick = jnp.concatenate(picks, axis=1).astype(jnp.bfloat16)
     y_lane = lax.broadcasted_iota(jnp.int32, (depth_y, LANES), 1) & 7
-    y_row = lax.broadcasted_iota(jnp.int32, (depth_y, LANES), 0) - place_ref[3]
+    y_row = lax.broadcasted_iota(jnp.int32, (depth_y, LANES), 0) - lax.axis_index("sy") * CY
     for copy in copies:
         copy.wait()
     code = labels[0] * 8 + labels[1] + 1
@@ -113,6 +155,7 @@
     cross_ref,
     shifted,
     coef,
+    folded,
 ):
     for plane in range(SLAB + 4):
         near, far = (plane - 1) * 16, 96 + (plane - 2) * 16
@@ -178,9 +221,13 @@
         return carry
 
     lax.fori_loop(0, QUAD // 2, one_pair, 0)
-    for i in range(4 * len(TAPS)):
-        both = coef[i]
-        coef[i] = both + pltpu.roll(both, SLAB, axis=0)
+    for i in range(2 * len(TAPS)):
+        real, imag = coef[2 * i], coef[2 * i + 1]
+        real = real + pltpu.roll(real, SLAB, axis=0)
+        imag = imag + pltpu.roll(imag, SLAB, axis=0)
+        folded[3 * i] = real
+        folded[3 * i + 1] = imag - real
+        folded[3 * i + 2] = real + imag
 
     half = 64
     part = 32
@@ -188,18 +235,17 @@
     def one_chunk(step, carry):
         z = step // 2
         col = pl.multiple_of((step % 2) * part, part)
-        sums = [jnp.zeros((part, LANES), jnp.float32) for _ in range(4)]
+        sums = [jnp.zeros((part, LANES), jnp.float32) for _ in range(6)]
         for t, (dz, off) in enumerate(TAPS):
             real = shifted[z + 2 + dz, off, pl.ds(col, part), :]
             imag = shifted[z + 2 + dz, off, pl.ds(half + col, part), :]
-            for k in range(2):
-                coef_real = coef[4 * t + 2 * k, pl.ds(z, 1), :]
-                coef_imag = coef[4 * t + 2 * k + 1, pl.ds(z, 1), :]
-                sums[2 * k] += coef_real * real - coef_imag * imag
-                sums[2 * k + 1] += coef_real * imag + coef_imag * real
+            factors = (real + imag, real, imag)
+            for i in range(6):
+                sums[i] += folded[6 * t + i, pl.ds(z, 1), :] * factors[i % 3]
         for k in range(2):
-            moments_ref[k, z, pl.ds(col, part), :] = sums[2 * k]
-            moments_ref[k, z, pl.ds(half + col, part), :] = sums[2 * k + 1]
+            both, minus, plus = sums[3 * k : 3 * k + 3]
+            moments_ref[k, z, pl.ds(col, part), :] = both - plus
+            moments_ref[k, z, pl.ds(half + col, part), :] = both + minus
         return carry
 
     lax.fori_loop(0, 2 * SLAB, one_chunk, 0)
@@ -230,6 +276,20 @@
             out_ref[z] = moments_ref[k, z].T
 
 
+def turn(moments, columns):
+    out = jax.ShapeDtypeStruct((SLAB, LANES, columns), jnp.float32)
+    vmem = pl.BlockSpec(memory_space=pltpu.VMEM)
+    return pl.pallas_call(
+        turn_kernel,
+        out_shape=[out] * 2,
+        in_specs=[vmem],
+        out_specs=[vmem] * 2,
+        compiler_params=pltpu.CompilerParams(vmem_limit_bytes=8 * 1024 * 1024),
+        cost_estimate=pl.CostEstimate(flops=1000000, bytes_accessed=1000000, transcendentals=0),
+        name="turn",
+    )(moments)
+
+
 def swap(block, **bits):
     axes = tuple(bits)
     sizes = [lax.axis_size(axis) for axis in axes]
@@ -240,45 +300,40 @@
     return lax.ppermute(block, axes, pairs)
 
 
-def beside(block, axis, forward):
-    count = lax.axis_size(axis)
-    pairs = [(i, i + 1) for i in range(count - 1)]
-    return lax.ppermute(block, axis, pairs if forward else [(b, a) for a, b in pairs])
-
-
 def body(probes, quad_index, region_label, gain_label, region_eps, gain_rate):
     depth, cells_x, cells_y, columns = probes.shape
     planes = SLAB + 4
-    me = lax.axis_index("quad")
-    start_z = me * SLAB
-    start_x = lax.axis_index("sx") * cells_x
-    start_y = lax.axis_index("sy") * cells_y
     core = lax.axis_index("sx") & 1
 
-    angle = 2.0 * math.pi * (quad_index.astype(jnp.float32) + 0.5) / (4 * QUAD)
-    lane = lax.broadcasted_iota(jnp.int32, (1, 128), 1)
-    weight = jnp.where(lane == me, jnp.cos(angle), 0.0)
-    weight = jnp.where(lane == me + QUAD, jnp.sin(angle), weight)
+    smem = pl.BlockSpec(memory_space=pltpu.SMEM)
+    vmem = pl.BlockSpec(memory_space=pltpu.VMEM)
+    hbm = pl.BlockSpec(memory_space=pltpu.HBM)
+    mib = 1024 * 1024
+    layers = jax.ShapeDtypeStruct(((2 * SLAB + 2) * CX, columns), probes.dtype)
+    weight, own, inner, outer = pl.pallas_call(
+        slab_kernel,
+        out_shape=[
+            jax.ShapeDtypeStruct((1, LANES), jnp.float32),
+            jax.ShapeDtypeStruct((planes, cells_x * cells_y, columns), probes.dtype),
+            layers,
+            layers,
+        ],
+        in_specs=[smem, hbm],
+        out_specs=[vmem] * 4,
+        scratch_shapes=[pltpu.SemaphoreType.DMA((3,))],
+        compiler_params=pltpu.CompilerParams(vmem_limit_bytes=4 * mib),
+        cost_estimate=pl.CostEstimate(flops=10000000, bytes_accessed=600000, transcendentals=0),
+        name="slab",
+    )(quad_index, probes.reshape(depth, cells_x * cells_y, columns))
+
+    def sides(axis, inner, outer):
+        even = (lax.axis_index(axis) & 1) == 0
+        return jnp.where(even, outer, inner), jnp.where(even, inner, outer)
+
+    middle = [(1, 2), (2, 1)]
+    ylo, yhi = sides("sy", swap(inner, sy=1), lax.ppermute(outer, "sy", middle))
+
     weight = weight + swap(weight, quad=1)
-
-    flat = probes.reshape(depth, cells_x * cells_y, columns)
-    own = jnp.concatenate(
-        [
-            lax.dynamic_slice_in_dim(flat, jnp.maximum(start_z - 2, 0), 2, 0),
-            lax.dynamic_slice_in_dim(flat, start_z, SLAB, 0),
-            lax.dynamic_slice_in_dim(flat, jnp.minimum(start_z + SLAB, depth - 2), 2, 0),
-        ],
-        axis=0,
-    )
-    cube = own.reshape(planes, cells_x, cells_y, columns)
-
-    def layers(near, far):
-        pieces = [cube[1 : planes - 1, :, near], cube[2 : planes - 2, :, far]]
-        return jnp.concatenate(pieces, axis=0).reshape(-1, columns)
-
-    ylo = beside(layers(cells_y - 1, cells_y - 2), "sy", True)
-    yhi = beside(layers(0, 1), "sy", False)
-    weight = weight + swap(weight, quad=3)
 
     def edge(at, x):
         rows = own[1 : planes - 1, at * cells_y : (at + 2) * cells_y].reshape(-1, columns)
@@ -291,24 +346,21 @@
     low, high = edge(0, 0), edge(cells_x - 2, cells_x - 1)
     inner = jnp.where(core == 0, high, low)
     outer = jnp.where(core == 0, low, high)
-    weight, inner, outer = lax.optimization_barrier((weight, inner, outer))
-    outer = lax.ppermute(outer, "sx", [(1, 2), (2, 1)])
+    weight, inner, outer, region_label, gain_label = lax.optimization_barrier(
+        (weight, inner, outer, region_label, gain_label)
+    )
+    outer = lax.ppermute(outer, "sx", middle)
     inner = swap(inner, sx=1)
+    xlo, xhi = sides("sx", inner, outer)
+    weight = weight + swap(weight, quad=3)
     weight = weight + swap(weight, quad=4)
-    weight, region_label, gain_label = lax.optimization_barrier((weight, region_label, gain_label))
     weight = weight + swap(weight, quad=8)
 
-    first_plane = jnp.clip(start_z - 2, 0, depth - planes)
-    place = jnp.stack([first_plane, first_plane - start_z + 4, start_x, start_y]).astype(jnp.int32)
-    smem = pl.BlockSpec(memory_space=pltpu.SMEM)
-    vmem = pl.BlockSpec(memory_space=pltpu.VMEM)
-    anywhere = pl.BlockSpec(memory_space=pl.ANY)
     taps = len(TAPS)
-    mib = 1024 * 1024
     material = pl.pallas_call(
         material_kernel,
         out_shape=jax.ShapeDtypeStruct((3 * taps, 8, LANES), jnp.float32),
-        in_specs=[smem, smem, smem, anywhere, anywhere],
+        in_specs=[smem, smem, hbm, hbm],
         out_specs=vmem,
         scratch_shapes=[
             pltpu.VMEM((2, planes) + region_label.shape[:0:-1], jnp.int32),
@@ -318,10 +370,8 @@
         compiler_params=pltpu.CompilerParams(vmem_limit_bytes=8 * mib),
         cost_estimate=pl.CostEstimate(flops=40000000, bytes_accessed=1200000, transcendentals=0),
         name="material",
-    )(place, region_eps, gain_rate, region_label.swapaxes(1, 2), gain_label.swapaxes(1, 2))
-
-    xlo = jnp.where(core == 0, outer, inner)
-    xhi = jnp.where(core == 0, inner, outer)
+    )(region_eps, gain_rate, region_label.swapaxes(1, 2), gain_label.swapaxes(1, 2))
+
     moments, cross = pl.pallas_call(
         moment_kernel,
         out_shape=[
@@ -333,6 +383,7 @@
         scratch_shapes=[
             pltpu.VMEM((planes, len(OFFSETS), columns, LANES), jnp.float32),
             pltpu.VMEM((4 * taps, 8, LANES), jnp.float32),
+            pltpu.VMEM((6 * taps, 8, LANES), jnp.float32),
         ],
         compiler_params=pltpu.CompilerParams(vmem_limit_bytes=24 * mib),
         cost_estimate=pl.CostEstimate(flops=600000000, bytes_accessed=3000000, transcendentals=0),
@@ -342,26 +393,21 @@
     width = cross.shape[1] // 2
     block = jnp.where(core == 0, cross[:, :width], cross[:, width:])
     block = block + swap(jnp.where(core == 0, cross[:, width:], cross[:, :width]), sx=1)
-    block = block + swap(block, sy=1)
-    block = block + swap(block, sy=3)
-    block = block + swap(block, quad=1)
-    block = block + swap(block, quad=3)
-    block = block + swap(block, quad=4)
-    block = block + swap(block, quad=8)
-    block, moments = lax.optimization_barrier((block, moments))
-    block = block + swap(block, quad=8, sx=2)
-
-    out = jax.ShapeDtypeStruct((SLAB, LANES, columns), jnp.float32)
-    first, second = pl.pallas_call(
-        turn_kernel,
-        out_shape=[out] * 2,
-        in_specs=[vmem],
-        out_specs=[vmem] * 2,
-        compiler_params=pltpu.CompilerParams(vmem_limit_bytes=8 * mib),
-        cost_estimate=pl.CostEstimate(flops=1000000, bytes_accessed=1000000, transcendentals=0),
-        name="turn",
-    )(moments)
-    block, first, second = lax.optimization_barrier((block, first, second))
+    along_y = [dict(sy=1), dict(sy=3)]
+    along_x = [dict(quad=1), dict(quad=3)]
+    along_z = [dict(quad=4), dict(quad=8), dict(quad=8, sx=2)]
+    rows = block.shape[0] // 2
+    upper, lower = block[:rows], block[rows:]
+    orders = zip(along_y + along_x + along_z, along_z + along_y + along_x)
+    for i, (upper_step, lower_step) in enumerate(orders):
+        if i == 3:
+            upper, moments = lax.optimization_barrier((upper, moments))
+        if i == 6:
+            first, second = turn(moments, columns)
+            upper, first, second = lax.optimization_barrier((upper, first, second))
+        upper_in, lower_in = swap(upper, **upper_step), swap(lower, **lower_step)
+        upper, lower = upper + upper_in, lower + lower_in
+    block = jnp.concatenate([upper, lower], axis=0)
     other = swap(block, sx=1)
     halves = (jnp.where(core == 0, block, other), jnp.where(core == 0, other, block))
     projections = jnp.stack(

time: 74.3 us -> 80.9 us (1.089)
  starting transfers between devices: 42.3 us -> 46.4 us
  waiting for transfers between devices: 18.8 us -> 22.3 us
    ppermute x14 -> x22, starting transfers between devices: 27.4 us -> 34.9 us  [swap(): return lax.ppermute(block, axes, pairs)]
    ppermute x14 -> x22, waiting for transfers between devices: 18.8 us -> 22.3 us  [swap(): return lax.ppermute(block, axes, pairs)]
    ppermute x3 -> x2, starting transfers between devices: 15 us -> 11.5 us  [the longest x1 10.8 us: body(): outer = lax.ppermute(outer, 'sx', middle)]
    dynamic_slice x2 -> x0, local copies, waits for them, and re-layouts: 1.8 us -> none  [the longest x1 0.91 us: body(): lax.dynamic_slice_in_dim(flat, start_z, SLAB, 0)]
    unnamed x10 -> x12, local copies, waits for them, and re-layouts: 0.02 us -> 1.61 us
  transfers between devices with their start and end apart: 17 -> 24, of which waited for: 11 -> 17; matrix products, arithmetic and copies ran while one was open for 3% -> 0% of each run, Pallas kernels for 3% -> 3%
where the time goes in v3:
time: 80.9 us; the launch traced here: 80.7 us
  starting transfers between devices  46.4 us (57%)
  waiting for transfers between devices  22.3 us (28%)
  Pallas kernels  7.84 us (10%)
  local copies, waits for them, and re-layouts  1.79 us (2%)
  between operations  1.52 us (2%)
  other arithmetic  0.85 us (1%)
    ppermute x22, starting transfers between devices, swap(): return lax.ppermute(block, axes, pairs)  34.9 us
    ppermute x22, waiting for transfers between devices, swap(): return lax.ppermute(block, axes, pairs)  22.3 us
    ppermute x1, starting transfers between devices, body(): outer = lax.ppermute(outer, 'sx', middle)  10.8 us
    pallas_call x1, Pallas kernels, body(): pl.pallas_call(moment_kernel, out_shape=[jax.ShapeDtypeStruct((2, SLAB, c...  4.87 us
  transfers between devices with their start and end apart: 24, of which 17 were waited for; matrix products, arithmetic and copies ran while one was open for 0% of the time, Pallas kernels for 3%

profile of v3, /device:TPU:1, one launch (start us, length us, event | category | flops | bytes accessed | tf_op | source)
XLA Modules:
  0.0 80.7 jit_solution(9660567187718776316)
XLA Ops:
  1.3 1.6 %copy-done = bf16[64,16,8,128]{3,2,1,0:T(8,128)(2,1)S(1)} copy-done((bf16[64,16,8,128]{3,2,1,0:T(8,128)(2,1)S(1)}, bf16[64,16,8,128]{3,2,1,0:T(8,128)(2,1)}, u32[]{:S(2)}) %copy-start) | copy-done | bytes 2097176
  2.9 0.6 slab.1
  3.5 0.0 copy-start.5
  3.6 2.1 %collective-permute-start = (f32[1,128]{1,0:T(1,128)S(1)}, f32[1,128]{1,0:T(1,128)S(1)}, u32[]{:S(2)}, u32[]{:S(2)}) collective-permute-start(f32[1,128]{1,0:T(1,128)S(1)} %get-tuple-element.21), channel_id=1, source_target_pairs={{0,16},{16,0},{32,48},{48,32},{64,80},{80,64},{96,112},{112,96},{1... | collective-permute-start | bytes 1544 | tf_op jit(solution)/shard_map/ppermute | solution.py:300
  5.7 0.7 collective-permute-start.1
  6.3 3.9 %collective-permute-start.2 = (bf16[160,128]{1,0:T(8,128)(2,1)S(1)}, bf16[160,128]{1,0:T(8,128)(2,1)S(1)}, u32[]{:S(2)}, u32[]{:S(2)}) collective-permute-start(bf16[160,128]{1,0:T(8,128)(2,1)S(1)} %get-tuple-element.24), channel_id=1, source_target_pairs={{0,1},{1,0},{2,3},{3,2},{4,5},{5,4},{6,7},{7,6},{8,9},{9,8},{10,11... | collective-permute-start | bytes 122888 | tf_op jit(solution)/shard_map/ppermute | solution.py:300
  10.3 1.4 %collective-permute-done.2 = bf16[160,128]{1,0:T(8,128)(2,1)S(1)} collective-permute-done((bf16[160,128]{1,0:T(8,128)(2,1)S(1)}, bf16[160,128]{1,0:T(8,128)(2,1)S(1)}, u32[]{:S(2)}, u32[]{:S(2)}) %collective-permute-start.2) | collective-permute-done | bytes 40992 | tf_op jit(solution)/shard_map/ppermute | solution.py:300
  11.8 10.8 %collective-permute-start.6 = (bf16[160,128]{1,0:T(8,128)(2,1)S(1)}, bf16[160,128]{1,0:T(8,128)(2,1)S(1)}, u32[]{:S(2)}, u32[]{:S(2)}) collective-permute-start(bf16[160,128]{1,0:T(8,128)(2,1)S(1)} %get-tuple-element.28), channel_id=1, source_target_pairs={{4,8},{8,4},{5,9},{9,5},{6,10},{10,6},{7,11},{11,7},{20,24},{24,20... | collective-permute-start | bytes 122888 | tf_op jit(solution)/shard_map/ppermute | solution.py:352
  22.6 0.1 collective-permute-start.7
  22.7 1.9 %collective-permute-start.3 = (f32[1,128]{1,0:T(1,128)S(1)}, f32[1,128]{1,0:T(1,128)S(1)}, u32[]{:S(2)}, u32[]{:S(2)}) collective-permute-start(f32[1,128]{1,0:T(1,128)S(1)} %add.61), channel_id=1, source_target_pairs={{0,48},{16,32},{32,16},{48,0},{64,112},{80,96},{96,80},{112,64},{1... | collective-permute-start | bytes 1544 | tf_op jit(solution)/shard_map/ppermute | solution.py:300
  24.6 1.8 %collective-permute-done.3 = f32[1,128]{1,0:T(1,128)S(1)} collective-permute-done((f32[1,128]{1,0:T(1,128)S(1)}, f32[1,128]{1,0:T(1,128)S(1)}, u32[]{:S(2)}, u32[]{:S(2)}) %collective-permute-start.3) | collective-permute-done | bytes 544 | tf_op jit(solution)/shard_map/ppermute | solution.py:300
  26.4 0.7 collective-permute-start.4
  27.1 1.7 %collective-permute-done.4 = f32[1,128]{1,0:T(1,128)S(1)} collective-permute-done((f32[1,128]{1,0:T(1,128)S(1)}, f32[1,128]{1,0:T(1,128)S(1)}, u32[]{:S(2)}, u32[]{:S(2)}) %collective-permute-start.4) | collective-permute-done | bytes 544 | tf_op jit(solution)/shard_map/ppermute | solution.py:300
  28.8 1.2 %collective-permute-start.5 = (f32[1,128]{1,0:T(1,128)S(1)}, f32[1,128]{1,0:T(1,128)S(1)}, u32[]{:S(2)}, u32[]{:S(2)}) collective-permute-start(f32[1,128]{1,0:T(1,128)S(1)} %add.63), channel_id=1, source_target_pairs={{0,128},{16,144},{32,160},{48,176},{64,192},{80,208},{96,224},{112... | collective-permute-start | bytes 1544 | tf_op jit(solution)/shard_map/ppermute | solution.py:300
  30.0 1.4 %material.1.material_ref = f32[75,8,128]{2,1,0:T(8,128)S(1)} custom-call(f32[8]{0:T(128)S(1)} %copy-done.3, f32[8]{0:T(128)S(1)} %copy-done.4, s32[64,32,64]{2,1,0:T(8,128)S(1)} %bitcast.24, s32[64,32,64]{2,1,0:T(8,128)S(1)} %bitcast.25), custom_call_target="tpu_custom_call" | custom-call | flops 40000000 | bytes 1200000 | tf_op jit(solution)/shard_map/material/pallas_call | solution.py:360
  31.4 0.7 collective-permute-done.5
  32.1 4.9 %moments.1 = (f32[2,4,128,128]{3,2,1,0:T(8,128)S(1)}, f32[64,256]{1,0:T(8,128)S(1)}) custom-call(f32[1,128]{1,0:T(1,128)S(1)} %add.64.weight_ref, f32[75,8,128]{2,1,0:T(8,128)S(1)} %material.1.material_ref, bf16[8,128,128]{2,1,0:T(8,128)(2,1)S(1)} %get-tuple-element.22.own_ref, bf16[160,128]{1,0:T(8,128)(2,1)S(1)} %get-tuple-element.45.ylo_ref, ...), custom_call_target="tpu_custom_call" | custom-call | flops 600000000 | bytes 3000000 | tf_op jit(solution)/shard_map/moments/pallas_call | solution.py:375
  37.0 3.9 %collective-permute-start.8 = (f32[64,128]{1,0:T(8,128)S(1)}, f32[64,128]{1,0:T(8,128)S(1)}, u32[]{:S(2)}, u32[]{:S(2)}) collective-permute-start(f32[64,128]{1,0:T(8,128)S(1)} %slice_select_fusion), channel_id=1, source_target_pairs={{0,4},{4,0},{8,12},{12,8},{1,5},{5,1},{9,13},{13,9},{2,6},{6,2},{1... | collective-permute-start | bytes 98312 | tf_op jit(solution)/shard_map/ppermute | solution.py:300
  41.0 0.9 %collective-permute-done.8 = f32[64,128]{1,0:T(8,128)S(1)} collective-permute-done((f32[64,128]{1,0:T(8,128)S(1)}, f32[64,128]{1,0:T(8,128)S(1)}, u32[]{:S(2)}, u32[]{:S(2)}) %collective-permute-start.8) | collective-permute-done | bytes 32800 | tf_op jit(solution)/shard_map/ppermute | solution.py:300
  41.8 0.8 %collective-permute-start.16 = (f32[32,128]{1,0:T(8,128)S(1)}, f32[32,128]{1,0:T(8,128)S(1)}, u32[]{:S(2)}, u32[]{:S(2)}) collective-permute-start(f32[32,128]{1,0:T(8,128)S(1)} %get-tuple-element.55), channel_id=1, source_target_pairs={{0,64},{16,80},{32,96},{48,112},{64,0},{80,16},{96,32},{112,48},{1... | collective-permute-start | bytes 49160 | tf_op jit(solution)/shard_map/ppermute | solution.py:300
  42.7 1.7 %collective-permute-start.9 = (f32[32,128]{1,0:T(8,128)S(1)}, f32[32,128]{1,0:T(8,128)S(1)}, u32[]{:S(2)}, u32[]{:S(2)}) collective-permute-start(f32[32,128]{1,0:T(8,128)S(1)} %get-tuple-element.56), channel_id=1, source_target_pairs={{0,1},{1,0},{2,3},{3,2},{4,5},{5,4},{6,7},{7,6},{8,9},{9,8},{10,11... | collective-permute-start | bytes 49160 | tf_op jit(solution)/shard_map/ppermute | solution.py:300
  44.4 0.1 collective-permute-done.16
  44.5 1.1 %collective-permute-done.9 = f32[32,128]{1,0:T(8,128)S(1)} collective-permute-done((f32[32,128]{1,0:T(8,128)S(1)}, f32[32,128]{1,0:T(8,128)S(1)}, u32[]{:S(2)}, u32[]{:S(2)}) %collective-permute-start.9) | collective-permute-done | bytes 16416 | tf_op jit(solution)/shard_map/ppermute | solution.py:300
  45.6 1.2 %collective-permute-start.17 = (f32[32,128]{1,0:T(8,128)S(1)}, f32[32,128]{1,0:T(8,128)S(1)}, u32[]{:S(2)}, u32[]{:S(2)}) collective-permute-start(f32[32,128]{1,0:T(8,128)S(1)} %get-tuple-element.53), channel_id=1, source_target_pairs={{0,128},{16,144},{32,160},{48,176},{64,192},{80,208},{96,224},{112... | collective-permute-start | bytes 49160 | tf_op jit(solution)/shard_map/ppermute | solution.py:300
  46.8 0.8 collective-permute-start.10
  47.6 1.5 %collective-permute-done.17 = f32[32,128]{1,0:T(8,128)S(1)} collective-permute-done((f32[32,128]{1,0:T(8,128)S(1)}, f32[32,128]{1,0:T(8,128)S(1)}, u32[]{:S(2)}, u32[]{:S(2)}) %collective-permute-start.17) | collective-permute-done | bytes 16416 | tf_op jit(solution)/shard_map/ppermute | solution.py:300
  49.1 1.5 %collective-permute-done.10 = f32[32,128]{1,0:T(8,128)S(1)} collective-permute-done((f32[32,128]{1,0:T(8,128)S(1)}, f32[32,128]{1,0:T(8,128)S(1)}, u32[]{:S(2)}, u32[]{:S(2)}) %collective-permute-start.10) | collective-permute-done | bytes 16416 | tf_op jit(solution)/shard_map/ppermute | solution.py:300
  50.6 3.2 %collective-permute-done.18 = f32[32,128]{1,0:T(8,128)S(1)} collective-permute-done((f32[32,128]{1,0:T(8,128)S(1)}, f32[32,128]{1,0:T(8,128)S(1)}, u32[]{:S(2)}, u32[]{:S(2)}) %collective-permute-start.18) | collective-permute-done | bytes 16416 | tf_op jit(solution)/shard_map/ppermute | solution.py:300
  53.8 1.7 %collective-permute-start.19 = (f32[32,128]{1,0:T(8,128)S(1)}, f32[32,128]{1,0:T(8,128)S(1)}, u32[]{:S(2)}, u32[]{:S(2)}) collective-permute-start(f32[32,128]{1,0:T(8,128)S(1)} %add.75), channel_id=1, source_target_pairs={{0,1},{1,0},{2,3},{3,2},{4,5},{5,4},{6,7},{7,6},{8,9},{9,8},{10,11... | collective-permute-start | bytes 49160 | tf_op jit(solution)/shard_map/ppermute | solution.py:300
  55.5 1.9 %collective-permute-start.12 = (f32[32,128]{1,0:T(8,128)S(1)}, f32[32,128]{1,0:T(8,128)S(1)}, u32[]{:S(2)}, u32[]{:S(2)}) collective-permute-start(f32[32,128]{1,0:T(8,128)S(1)} %add.68), channel_id=1, source_target_pairs={{0,48},{16,32},{32,16},{48,0},{64,112},{80,96},{96,80},{112,64},{1... | collective-permute-start | bytes 49160 | tf_op jit(solution)/shard_map/ppermute | solution.py:300
  57.4 0.9 %collective-permute-start.20 = (f32[32,128]{1,0:T(8,128)S(1)}, f32[32,128]{1,0:T(8,128)S(1)}, u32[]{:S(2)}, u32[]{:S(2)}) collective-permute-start(f32[32,128]{1,0:T(8,128)S(1)} %add.76), channel_id=1, source_target_pairs={{0,3},{1,2},{2,1},{3,0},{4,7},{5,6},{6,5},{7,4},{8,11},{9,10},{10,... | collective-permute-start | bytes 49160 | tf_op jit(solution)/shard_map/ppermute | solution.py:300
  58.3 1.1 %collective-permute-done.12 = f32[32,128]{1,0:T(8,128)S(1)} collective-permute-done((f32[32,128]{1,0:T(8,128)S(1)}, f32[32,128]{1,0:T(8,128)S(1)}, u32[]{:S(2)}, u32[]{:S(2)}) %collective-permute-start.12) | collective-permute-done | bytes 16416 | tf_op jit(solution)/shard_map/ppermute | solution.py:300
  59.4 0.7 collective-permute-start.13
  60.1 1.2 %collective-permute-done.20 = f32[32,128]{1,0:T(8,128)S(1)} collective-permute-done((f32[32,128]{1,0:T(8,128)S(1)}, f32[32,128]{1,0:T(8,128)S(1)}, u32[]{:S(2)}, u32[]{:S(2)}) %collective-permute-start.20) | collective-permute-done | bytes 16416 | tf_op jit(solution)/shard_map/ppermute | solution.py:300
  61.3 0.0 collective-permute-start.21
  61.3 0.7 collective-permute-done.13
  62.0 1.2 %collective-permute-start.14 = (f32[32,128]{1,0:T(8,128)S(1)}, f32[32,128]{1,0:T(8,128)S(1)}, u32[]{:S(2)}, u32[]{:S(2)}) collective-permute-start(f32[32,128]{1,0:T(8,128)S(1)} %add.70), channel_id=1, source_target_pairs={{0,128},{16,144},{32,160},{48,176},{64,192},{80,208},{96,224},{112... | collective-permute-start | bytes 49160 | tf_op jit(solution)/shard_map/ppermute | solution.py:300
  63.2 0.9 %turn.1 = (f32[4,128,128]{2,1,0:T(8,128)}, f32[4,128,128]{2,1,0:T(8,128)}) custom-call(f32[2,4,128,128]{3,2,1,0:T(8,128)S(1)} %get-tuple-element.33.moments_ref), custom_call_target="tpu_custom_call" | custom-call | flops 1000000 | bytes 1000000 | tf_op jit(solution)/shard_map/turn/pallas_call | solution.py:282
  64.1 0.1 collective-permute-done.21
  64.2 1.8 %collective-permute-start.22 = (f32[32,128]{1,0:T(8,128)S(1)}, f32[32,128]{1,0:T(8,128)S(1)}, u32[]{:S(2)}, u32[]{:S(2)}) collective-permute-start(f32[32,128]{1,0:T(8,128)S(1)} %add.78), channel_id=1, source_target_pairs={{0,48},{16,32},{32,16},{48,0},{64,112},{80,96},{96,80},{112,64},{1... | collective-permute-start | bytes 49160 | tf_op jit(solution)/shard_map/ppermute | solution.py:300
  66.0 0.1 collective-permute-start.15
  66.1 1.9 %collective-permute-done.22 = f32[32,128]{1,0:T(8,128)S(1)} collective-permute-done((f32[32,128]{1,0:T(8,128)S(1)}, f32[32,128]{1,0:T(8,128)S(1)}, u32[]{:S(2)}, u32[]{:S(2)}) %collective-permute-start.22) | collective-permute-done | bytes 16416 | tf_op jit(solution)/shard_map/ppermute | solution.py:300
  68.0 2.8 %collective-permute-done.15 = f32[32,128]{1,0:T(8,128)S(1)} collective-permute-done((f32[32,128]{1,0:T(8,128)S(1)}, f32[32,128]{1,0:T(8,128)S(1)}, u32[]{:S(2)}, u32[]{:S(2)}) %collective-permute-start.15) | collective-permute-done | bytes 16416 | tf_op jit(solution)/shard_map/ppermute | solution.py:300
  70.8 8.2 %collective-permute-start.23 = (f32[64,128]{1,0:T(8,128)S(1)}, f32[64,128]{1,0:T(8,128)S(1)}, u32[]{:S(2)}, u32[]{:S(2)}) collective-permute-start(f32[64,128]{1,0:T(8,128)S(1)} %pad_maximum_fusion.3), channel_id=1, source_target_pairs={{0,4},{4,0},{8,12},{12,8},{1,5},{5,1},{9,13},{13,9},{2,6},{6,2},{1... | collective-permute-start | bytes 98312 | tf_op jit(solution)/shard_map/ppermute | solution.py:300
  79.0 0.9 %collective-permute-done.23 = f32[64,128]{1,0:T(8,128)S(1)} collective-permute-done((f32[64,128]{1,0:T(8,128)S(1)}, f32[64,128]{1,0:T(8,128)S(1)}, u32[]{:S(2)}, u32[]{:S(2)}) %collective-permute-start.23) | collective-permute-done | bytes 32800 | tf_op jit(solution)/shard_map/ppermute | solution.py:300
  79.9 0.1 slice_bitcast_fusion.3
  80.0 0.1 slice_bitcast_fusion.1
  80.1 0.7 pad_maximum_fusion
  (52 shorter events, 0.3 us)
Async XLA Ops:
  0.6 29.4 %copy-start.4 = (f32[8]{0:T(128)S(1)}, f32[8]{0:T(128)}, u32[]{:S(2)}) copy-start(f32[8]{0:T(128)} %gain_ref.1) | copy-start | bytes 100
  0.6 29.3 %copy-start.3 = (f32[8]{0:T(128)S(1)}, f32[8]{0:T(128)}, u32[]{:S(2)}) copy-start(f32[8]{0:T(128)} %eps_ref.1) | copy-start | bytes 100
  1.3 1.6 %copy-start = (bf16[64,16,8,128]{3,2,1,0:T(8,128)(2,1)S(1)}, bf16[64,16,8,128]{3,2,1,0:T(8,128)(2,1)}, u32[]{:S(2)}) copy-start(bf16[64,16,8,128]{3,2,1,0:T(8,128)(2,1)} %param.7) | copy-start | bytes 6291460
  2.9 27.1 %copy-start.1 = (s32[64,64,32]{1,2,0:T(8,128)S(1)}, s32[64,64,32]{1,2,0:T(8,128)}, u32[]{:S(2)}) copy-start(s32[64,64,32]{1,2,0:T(8,128)} %param.9) | copy-start | bytes 1572868
  2.9 27.1 %copy-start.2 = (s32[64,64,32]{1,2,0:T(8,128)S(1)}, s32[64,64,32]{1,2,0:T(8,128)}, u32[]{:S(2)}) copy-start(s32[64,64,32]{1,2,0:T(8,128)} %param.10) | copy-start | bytes 1572868
  3.5 28.6 %copy-start.5 = (bf16[256,1664]{1,0:T(8,128)(2,1)S(1)}, bf16[256,1664]{1,0:T(8,128)(2,1)}, u32[]{:S(2)}) copy-start(bf16[256,1664]{1,0:T(8,128)(2,1)} %constant.15.clone.pick_ref) | copy-start | bytes 2555908
  3.6 6.7 %collective-permute-start = (f32[1,128]{1,0:T(1,128)S(1)}, f32[1,128]{1,0:T(1,128)S(1)}, u32[]{:S(2)}, u32[]{:S(2)}) collective-permute-start(f32[1,128]{1,0:T(1,128)S(1)} %get-tuple-element.21), channel_id=1, source_target_pairs={{0,16},{16,0},{32,48},{48,32},{64,80},{80,64},{96,112},{112,96},{1... | collective-permute-start | bytes 1544 | tf_op jit(solution)/shard_map/ppermute | solution.py:300
  5.7 4.6 %collective-permute-start.1 = (bf16[160,128]{1,0:T(8,128)(2,1)S(1)}, bf16[160,128]{1,0:T(8,128)(2,1)S(1)}, u32[]{:S(2)}, u32[]{:S(2)}) collective-permute-start(bf16[160,128]{1,0:T(8,128)(2,1)S(1)} %get-tuple-element.23), channel_id=1, source_target_pairs={{1,2},{2,1},{5,6},{6,5},{9,10},{10,9},{13,14},{14,13},{17,18},{18,... | collective-permute-start | bytes 122888 | tf_op jit(solution)/shard_map/ppermute | solution.py:334
  6.3 5.3 %collective-permute-start.2 = (bf16[160,128]{1,0:T(8,128)(2,1)S(1)}, bf16[160,128]{1,0:T(8,128)(2,1)S(1)}, u32[]{:S(2)}, u32[]{:S(2)}) collective-permute-start(bf16[160,128]{1,0:T(8,128)(2,1)S(1)} %get-tuple-element.24), channel_id=1, source_target_pairs={{0,1},{1,0},{2,3},{3,2},{4,5},{5,4},{6,7},{7,6},{8,9},{9,8},{10,11... | collective-permute-start | bytes 122888 | tf_op jit(solution)/shard_map/ppermute | solution.py:300
  11.8 20.3 %collective-permute-start.6 = (bf16[160,128]{1,0:T(8,128)(2,1)S(1)}, bf16[160,128]{1,0:T(8,128)(2,1)S(1)}, u32[]{:S(2)}, u32[]{:S(2)}) collective-permute-start(bf16[160,128]{1,0:T(8,128)(2,1)S(1)} %get-tuple-element.28), channel_id=1, source_target_pairs={{4,8},{8,4},{5,9},{9,5},{6,10},{10,6},{7,11},{11,7},{20,24},{24,20... | collective-permute-start | bytes 122888 | tf_op jit(solution)/shard_map/ppermute | solution.py:352
  22.6 9.5 %collective-permute-start.7 = (bf16[160,128]{1,0:T(8,128)(2,1)S(1)}, bf16[160,128]{1,0:T(8,128)(2,1)S(1)}, u32[]{:S(2)}, u32[]{:S(2)}) collective-permute-start(bf16[160,128]{1,0:T(8,128)(2,1)S(1)} %get-tuple-element.29), channel_id=1, source_target_pairs={{0,4},{4,0},{8,12},{12,8},{1,5},{5,1},{9,13},{13,9},{2,6},{6,2},{1... | collective-permute-start | bytes 122888 | tf_op jit(solution)/shard_map/ppermute | solution.py:300
  22.7 3.7 %collective-permute-start.3 = (f32[1,128]{1,0:T(1,128)S(1)}, f32[1,128]{1,0:T(1,128)S(1)}, u32[]{:S(2)}, u32[]{:S(2)}) collective-permute-start(f32[1,128]{1,0:T(1,128)S(1)} %add.61), channel_id=1, source_target_pairs={{0,48},{16,32},{32,16},{48,0},{64,112},{80,96},{96,80},{112,64},{1... | collective-permute-start | bytes 1544 | tf_op jit(solution)/shard_map/ppermute | solution.py:300
  26.4 2.4 %collective-permute-start.4 = (f32[1,128]{1,0:T(1,128)S(1)}, f32[1,128]{1,0:T(1,128)S(1)}, u32[]{:S(2)}, u32[]{:S(2)}) collective-permute-start(f32[1,128]{1,0:T(1,128)S(1)} %add.62), channel_id=1, source_target_pairs={{0,64},{16,80},{32,96},{48,112},{64,0},{80,16},{96,32},{112,48},{1... | collective-permute-start | bytes 1544 | tf_op jit(solution)/shard_map/ppermute | solution.py:300
  28.8 3.3 %collective-permute-start.5 = (f32[1,128]{1,0:T(1,128)S(1)}, f32[1,128]{1,0:T(1,128)S(1)}, u32[]{:S(2)}, u32[]{:S(2)}) collective-permute-start(f32[1,128]{1,0:T(1,128)S(1)} %add.63), channel_id=1, source_target_pairs={{0,128},{16,144},{32,160},{48,176},{64,192},{80,208},{96,224},{112... | collective-permute-start | bytes 1544 | tf_op jit(solution)/shard_map/ppermute | solution.py:300
  37.0 4.8 %collective-permute-start.8 = (f32[64,128]{1,0:T(8,128)S(1)}, f32[64,128]{1,0:T(8,128)S(1)}, u32[]{:S(2)}, u32[]{:S(2)}) collective-permute-start(f32[64,128]{1,0:T(8,128)S(1)} %slice_select_fusion), channel_id=1, source_target_pairs={{0,4},{4,0},{8,12},{12,8},{1,5},{5,1},{9,13},{13,9},{2,6},{6,2},{1... | collective-permute-start | bytes 98312 | tf_op jit(solution)/shard_map/ppermute | solution.py:300
  41.8 2.7 %collective-permute-start.16 = (f32[32,128]{1,0:T(8,128)S(1)}, f32[32,128]{1,0:T(8,128)S(1)}, u32[]{:S(2)}, u32[]{:S(2)}) collective-permute-start(f32[32,128]{1,0:T(8,128)S(1)} %get-tuple-element.55), channel_id=1, source_target_pairs={{0,64},{16,80},{32,96},{48,112},{64,0},{80,16},{96,32},{112,48},{1... | collective-permute-start | bytes 49160 | tf_op jit(solution)/shard_map/ppermute | solution.py:300
  42.7 3.0 %collective-permute-start.9 = (f32[32,128]{1,0:T(8,128)S(1)}, f32[32,128]{1,0:T(8,128)S(1)}, u32[]{:S(2)}, u32[]{:S(2)}) collective-permute-start(f32[32,128]{1,0:T(8,128)S(1)} %get-tuple-element.56), channel_id=1, source_target_pairs={{0,1},{1,0},{2,3},{3,2},{4,5},{5,4},{6,7},{7,6},{8,9},{9,8},{10,11... | collective-permute-start | bytes 49160 | tf_op jit(solution)/shard_map/ppermute | solution.py:300
  45.6 3.5 %collective-permute-start.17 = (f32[32,128]{1,0:T(8,128)S(1)}, f32[32,128]{1,0:T(8,128)S(1)}, u32[]{:S(2)}, u32[]{:S(2)}) collective-permute-start(f32[32,128]{1,0:T(8,128)S(1)} %get-tuple-element.53), channel_id=1, source_target_pairs={{0,128},{16,144},{32,160},{48,176},{64,192},{80,208},{96,224},{112... | collective-permute-start | bytes 49160 | tf_op jit(solution)/shard_map/ppermute | solution.py:300
  46.8 3.8 %collective-permute-start.10 = (f32[32,128]{1,0:T(8,128)S(1)}, f32[32,128]{1,0:T(8,128)S(1)}, u32[]{:S(2)}, u32[]{:S(2)}) collective-permute-start(f32[32,128]{1,0:T(8,128)S(1)} %get-tuple-element.54), channel_id=1, source_target_pairs={{0,3},{1,2},{2,1},{3,0},{4,7},{5,6},{6,5},{7,4},{8,11},{9,10},{10,... | collective-permute-start | bytes 49160 | tf_op jit(solution)/shard_map/ppermute | solution.py:300
  49.1 4.7 %collective-permute-start.18 = (f32[32,128]{1,0:T(8,128)S(1)}, f32[32,128]{1,0:T(8,128)S(1)}, u32[]{:S(2)}, u32[]{:S(2)}) collective-permute-start(f32[32,128]{1,0:T(8,128)S(1)} %add.74), channel_id=1, source_target_pairs={{0,136},{4,140},{8,128},{12,132},{16,152},{20,156},{24,144},{28,14... | collective-permute-start | bytes 49160 | tf_op jit(solution)/shard_map/ppermute | solution.py:300
  50.6 4.9 %collective-permute-start.11 = (f32[32,128]{1,0:T(8,128)S(1)}, f32[32,128]{1,0:T(8,128)S(1)}, u32[]{:S(2)}, u32[]{:S(2)}) collective-permute-start(f32[32,128]{1,0:T(8,128)S(1)} %add.67), channel_id=1, source_target_pairs={{0,16},{16,0},{32,48},{48,32},{64,80},{80,64},{96,112},{112,96},{1... | collective-permute-start | bytes 49160 | tf_op jit(solution)/shard_map/ppermute | solution.py:300
  53.8 3.6 %collective-permute-start.19 = (f32[32,128]{1,0:T(8,128)S(1)}, f32[32,128]{1,0:T(8,128)S(1)}, u32[]{:S(2)}, u32[]{:S(2)}) collective-permute-start(f32[32,128]{1,0:T(8,128)S(1)} %add.75), channel_id=1, source_target_pairs={{0,1},{1,0},{2,3},{3,2},{4,5},{5,4},{6,7},{7,6},{8,9},{9,8},{10,11... | collective-permute-start | bytes 49160 | tf_op jit(solution)/shard_map/ppermute | solution.py:300
  55.5 3.9 %collective-permute-start.12 = (f32[32,128]{1,0:T(8,128)S(1)}, f32[32,128]{1,0:T(8,128)S(1)}, u32[]{:S(2)}, u32[]{:S(2)}) collective-permute-start(f32[32,128]{1,0:T(8,128)S(1)} %add.68), channel_id=1, source_target_pairs={{0,48},{16,32},{32,16},{48,0},{64,112},{80,96},{96,80},{112,64},{1... | collective-permute-start | bytes 49160 | tf_op jit(solution)/shard_map/ppermute | solution.py:300
  57.4 3.9 %collective-permute-start.20 = (f32[32,128]{1,0:T(8,128)S(1)}, f32[32,128]{1,0:T(8,128)S(1)}, u32[]{:S(2)}, u32[]{:S(2)}) collective-permute-start(f32[32,128]{1,0:T(8,128)S(1)} %add.76), channel_id=1, source_target_pairs={{0,3},{1,2},{2,1},{3,0},{4,7},{5,6},{6,5},{7,4},{8,11},{9,10},{10,... | collective-permute-start | bytes 49160 | tf_op jit(solution)/shard_map/ppermute | solution.py:300
  59.4 2.6 %collective-permute-start.13 = (f32[32,128]{1,0:T(8,128)S(1)}, f32[32,128]{1,0:T(8,128)S(1)}, u32[]{:S(2)}, u32[]{:S(2)}) collective-permute-start(f32[32,128]{1,0:T(8,128)S(1)} %add.69), channel_id=1, source_target_pairs={{0,64},{16,80},{32,96},{48,112},{64,0},{80,16},{96,32},{112,48},{1... | collective-permute-start | bytes 49160 | tf_op jit(solution)/shard_map/ppermute | solution.py:300
  61.3 2.9 %collective-permute-start.21 = (f32[32,128]{1,0:T(8,128)S(1)}, f32[32,128]{1,0:T(8,128)S(1)}, u32[]{:S(2)}, u32[]{:S(2)}) collective-permute-start(f32[32,128]{1,0:T(8,128)S(1)} %add.77), channel_id=1, source_target_pairs={{0,16},{16,0},{32,48},{48,32},{64,80},{80,64},{96,112},{112,96},{1... | collective-permute-start | bytes 49160 | tf_op jit(solution)/shard_map/ppermute | solution.py:300
  62.0 4.0 %collective-permute-start.14 = (f32[32,128]{1,0:T(8,128)S(1)}, f32[32,128]{1,0:T(8,128)S(1)}, u32[]{:S(2)}, u32[]{:S(2)}) collective-permute-start(f32[32,128]{1,0:T(8,128)S(1)} %add.70), channel_id=1, source_target_pairs={{0,128},{16,144},{32,160},{48,176},{64,192},{80,208},{96,224},{112... | collective-permute-start | bytes 49160 | tf_op jit(solution)/shard_map/ppermute | solution.py:300
  64.2 3.8 %collective-permute-start.22 = (f32[32,128]{1,0:T(8,128)S(1)}, f32[32,128]{1,0:T(8,128)S(1)}, u32[]{:S(2)}, u32[]{:S(2)}) collective-permute-start(f32[32,128]{1,0:T(8,128)S(1)} %add.78), channel_id=1, source_target_pairs={{0,48},{16,32},{32,16},{48,0},{64,112},{80,96},{96,80},{112,64},{1... | collective-permute-start | bytes 49160 | tf_op jit(solution)/shard_map/ppermute | solution.py:300
  66.0 4.8 %collective-permute-start.15 = (f32[32,128]{1,0:T(8,128)S(1)}, f32[32,128]{1,0:T(8,128)S(1)}, u32[]{:S(2)}, u32[]{:S(2)}) collective-permute-start(f32[32,128]{1,0:T(8,128)S(1)} %add.71), channel_id=1, source_target_pairs={{0,136},{4,140},{8,128},{12,132},{16,152},{20,156},{24,144},{28,14... | collective-permute-start | bytes 49160 | tf_op jit(solution)/shard_map/ppermute | solution.py:300
  70.8 9.1 %collective-permute-start.23 = (f32[64,128]{1,0:T(8,128)S(1)}, f32[64,128]{1,0:T(8,128)S(1)}, u32[]{:S(2)}, u32[]{:S(2)}) collective-permute-start(f32[64,128]{1,0:T(8,128)S(1)} %pad_maximum_fusion.3), channel_id=1, source_target_pairs={{0,4},{4,0},{8,12},{12,8},{1,5},{5,1},{9,13},{13,9},{2,6},{6,2},{1... | collective-permute-start | bytes 98312 | tf_op jit(solution)/shard_map/ppermute | solution.py:300

commit v4 on v3

--- a/solution.py
+++ b/solution.py
@@ -24,6 +24,9 @@
 TAP_AT = {(dz,) + OFFSETS[off]: i for i, (dz, off) in enumerate(TAPS)}
 UNITS = [(1, 0, 0), (-1, 0, 0), (0, 1, 0), (0, -1, 0), (0, 0, 1), (0, 0, -1)]
 WIDE = len(OFFSETS) * LANES
+FAR = (SLAB + 2) * CX
+CORNERS = FAR + SLAB * CX
+PARTS = CORNERS + 16
 
 
 def source_cells():
@@ -46,44 +49,57 @@
     return pick.astype(jnp.bfloat16)
 
 
-def slab_kernel(quad_ref, probes_ref, weight_ref, own_ref, inner_ref, outer_ref, sems):
+def slab_kernel(quad_ref, probes_ref, own_ref, first_ref, second_ref, third_ref, fourth_ref, *whole):
     depth = probes_ref.shape[0]
-    start = lax.axis_index("quad") * SLAB
-    spans = (
-        (jnp.maximum(start - 2, 0), 0, 2),
-        (start, 2, SLAB),
-        (jnp.minimum(start + SLAB, depth - 2), SLAB + 2, 2),
-    )
-    copies = [
-        pltpu.make_async_copy(probes_ref.at[pl.ds(a, n)], own_ref.at[b : b + n], sems.at[i])
-        for i, (a, b, n) in enumerate(spans)
-    ]
-    for copy in copies:
-        copy.start()
     me = lax.axis_index("quad")
+    even_x = (lax.axis_index("sx") & 1) == 0
+    even_y = (lax.axis_index("sy") & 1) == 0
+
+    def plane(slab, p):
+        return probes_ref[jnp.clip(slab * SLAB + (p - 2), 0, depth - 1)]
+
+    def x_edge(slab, p, high):
+        block = plane(slab, p)
+        return jnp.where(high, block[LANES - 16 :].astype(jnp.float32), block[:16].astype(jnp.float32))
+
     index = jnp.full((1, LANES), quad_ref[0], jnp.int32).astype(jnp.float32)
     angle = 2.0 * math.pi * (index + 0.5) / (4 * QUAD)
     lane = lax.broadcasted_iota(jnp.int32, (1, LANES), 1)
     weight = jnp.where(lane == me, jnp.cos(angle), 0.0)
-    weight_ref[...] = jnp.where(lane == me + QUAD, jnp.sin(angle), weight)
-    row = lax.broadcasted_iota(jnp.int32, (32, LANES), 0)
-    cell = lax.broadcasted_iota(jnp.int32, (32, LANES), 1)
-    even = (lax.axis_index("sy") & 1) == 0
-    deep = jnp.where(row < CX, 0, 1)
-    picks = []
-    for high in (even, jnp.logical_not(even)):
-        y = jnp.where(high, CY - 1 - deep, deep)
-        picks.append(jnp.where(cell == (row & (CX - 1)) * CY + y, 1.0, 0.0).astype(jnp.bfloat16))
-    for copy in copies:
-        copy.wait()
-    for pick, out_ref in zip(picks, (inner_ref, outer_ref)):
-        for plane in range(1, SLAB + 3):
-            layers = jnp.dot(pick, own_ref[plane], preferred_element_type=jnp.float32)
-            layers = layers.astype(jnp.bfloat16)
-            out_ref[(plane - 1) * CX : plane * CX] = layers[:CX]
-            if 2 <= plane < SLAB + 2:
-                at = (SLAB + 2 + plane - 2) * CX
-                out_ref[at : at + CX] = layers[CX:]
+    weight = jnp.where(lane == me + QUAD, jnp.sin(angle), weight)
+    row = lax.broadcasted_iota(jnp.int32, (16, LANES), 0)
+    parts = jnp.zeros((16, LANES), jnp.float32)
+    for i in range(3):
+        part = weight.astype(jnp.bfloat16).astype(jnp.float32)
+        parts = jnp.where(row == i, part, parts)
+        weight = weight - part
+    first_ref[PARTS : PARTS + 16] = parts.astype(jnp.bfloat16)
+
+    for out_ref, scratch, step, high in (
+        (first_ref, whole[0], 1, even_y),
+        (second_ref, whole[1], 3, jnp.logical_not(even_y)),
+    ):
+        target = me ^ step
+        for p in range(1, SLAB + 3):
+            scratch[(p - 1) * LANES : p * LANES] = plane(target, p).astype(jnp.float32)
+        for at, start, count, deep in ((0, 0, SLAB + 2, 0), (FAR, LANES, SLAB, 1)):
+            low = scratch[pl.ds(start + deep, count * CX, stride=CY), :]
+            top = scratch[pl.ds(start + CY - 1 - deep, count * CX, stride=CY), :]
+            out_ref[at : at + count * CX] = jnp.where(high, top, low).astype(jnp.bfloat16)
+        corners = jnp.zeros((16, LANES), jnp.float32)
+        for i, (bit, edge) in enumerate(((4, even_x), (8, jnp.logical_not(even_x)))):
+            cell = jnp.where(edge, CY, 0) + jnp.where(high, CY - 1, 0)
+            for p in range(SLAB):
+                picked = jnp.where(row == cell, x_edge(target ^ bit, p + 2, edge), 0.0)
+                picked = jnp.sum(picked, axis=0, keepdims=True)
+                corners = jnp.where(row == i * SLAB + p, picked, corners)
+        out_ref[CORNERS : CORNERS + 16] = corners.astype(jnp.bfloat16)
+
+    for out_ref, bit, high in ((third_ref, 4, even_x), (fourth_ref, 8, jnp.logical_not(even_x))):
+        for p in range(1, SLAB + 3):
+            out_ref[(p - 1) * 16 : p * 16] = x_edge(me ^ bit, p, high).astype(jnp.bfloat16)
+    for p in range(SLAB + 4):
+        own_ref[p] = plane(me, p)
 
 
 def material_kernel(eps_ref, gain_ref, region_ref, level_ref, out_ref, labels, codes, sems):
@@ -290,7 +306,7 @@
     )(moments)
 
 
-def swap(block, **bits):
+def swap(block, bits):
     axes = tuple(bits)
     sizes = [lax.axis_size(axis) for axis in axes]
     pairs = []
@@ -304,57 +320,50 @@
     depth, cells_x, cells_y, columns = probes.shape
     planes = SLAB + 4
     core = lax.axis_index("sx") & 1
-
+    even_x = core == 0
+    even_y = (lax.axis_index("sy") & 1) == 0
     smem = pl.BlockSpec(memory_space=pltpu.SMEM)
     vmem = pl.BlockSpec(memory_space=pltpu.VMEM)
     hbm = pl.BlockSpec(memory_space=pltpu.HBM)
     mib = 1024 * 1024
-    layers = jax.ShapeDtypeStruct(((2 * SLAB + 2) * CX, columns), probes.dtype)
-    weight, own, inner, outer = pl.pallas_call(
+    shapes = [
+        (planes, cells_x * cells_y, columns),
+        (PARTS + 16, columns),
+        (PARTS, columns),
+        (FAR, columns),
+        (FAR, columns),
+    ]
+    own, first, second, third, fourth = pl.pallas_call(
         slab_kernel,
-        out_shape=[
-            jax.ShapeDtypeStruct((1, LANES), jnp.float32),
-            jax.ShapeDtypeStruct((planes, cells_x * cells_y, columns), probes.dtype),
-            layers,
-            layers,
-        ],
-        in_specs=[smem, hbm],
-        out_specs=[vmem] * 4,
-        scratch_shapes=[pltpu.SemaphoreType.DMA((3,))],
-        compiler_params=pltpu.CompilerParams(vmem_limit_bytes=4 * mib),
+        out_shape=[jax.ShapeDtypeStruct(shape, probes.dtype) for shape in shapes],
+        in_specs=[smem, vmem],
+        out_specs=[vmem] * 5,
+        scratch_shapes=[pltpu.VMEM(((SLAB + 2) * LANES, columns), jnp.float32)] * 2,
+        compiler_params=pltpu.CompilerParams(vmem_limit_bytes=8 * mib),
         cost_estimate=pl.CostEstimate(flops=10000000, bytes_accessed=600000, transcendentals=0),
         name="slab",
     )(quad_index, probes.reshape(depth, cells_x * cells_y, columns))
 
-    def sides(axis, inner, outer):
-        even = (lax.axis_index(axis) & 1) == 0
-        return jnp.where(even, outer, inner), jnp.where(even, inner, outer)
-
-    middle = [(1, 2), (2, 1)]
-    ylo, yhi = sides("sy", swap(inner, sy=1), lax.ppermute(outer, "sy", middle))
-
-    weight = weight + swap(weight, quad=1)
-
-    def edge(at, x):
-        rows = own[1 : planes - 1, at * cells_y : (at + 2) * cells_y].reshape(-1, columns)
-        corners = [
-            side[16 : 16 + SLAB * 16].reshape(SLAB, 16, columns)[:, x : x + 1] for side in (ylo, yhi)
-        ]
-        corners = jnp.pad(jnp.concatenate(corners, axis=1), ((0, 0), (0, 14), (0, 0)))
-        return jnp.concatenate([rows, corners.reshape(-1, columns)], axis=0)
-
-    low, high = edge(0, 0), edge(cells_x - 2, cells_x - 1)
-    inner = jnp.where(core == 0, high, low)
-    outer = jnp.where(core == 0, low, high)
-    weight, inner, outer, region_label, gain_label = lax.optimization_barrier(
-        (weight, inner, outer, region_label, gain_label)
-    )
-    outer = lax.ppermute(outer, "sx", middle)
-    inner = swap(inner, sx=1)
-    xlo, xhi = sides("sx", inner, outer)
-    weight = weight + swap(weight, quad=3)
-    weight = weight + swap(weight, quad=4)
-    weight = weight + swap(weight, quad=8)
+    def corner_rows(at):
+        cells = [inner[at : at + SLAB], outer[at : at + SLAB]]
+        low, high = jnp.where(even_y, cells[1], cells[0]), jnp.where(even_y, cells[0], cells[1])
+        rows = jnp.pad(jnp.stack([low, high], axis=1), ((0, 0), (0, 14), (0, 0)))
+        return rows.reshape(SLAB * 16, columns)
+
+    inner = swap(first, dict(quad=1, sy=1))
+    parts = first[PARTS:] + inner[PARTS:]
+    outer = swap(jnp.concatenate([second, parts], axis=0), dict(quad=3, sy=3))
+    parts = parts + outer[PARTS:]
+    ylo = jnp.where(even_y, outer, inner)[:CORNERS]
+    yhi = jnp.where(even_y, inner, outer)[:CORNERS]
+    near = swap(jnp.concatenate([third, corner_rows(CORNERS), parts], axis=0), dict(quad=4, sx=1))
+    parts = parts + near[CORNERS:]
+    fourth = jnp.concatenate([fourth, corner_rows(CORNERS + SLAB), parts], axis=0)
+    beyond = swap(fourth, dict(quad=8, sx=3))
+    parts = parts + beyond[CORNERS:]
+    xlo = jnp.where(even_x, beyond, near)[:CORNERS]
+    xhi = jnp.where(even_x, near, beyond)[:CORNERS]
+    weight = jnp.sum(parts[:3].astype(jnp.float32), axis=0, keepdims=True)
 
     taps = len(TAPS)
     material = pl.pallas_call(
@@ -392,23 +401,14 @@
 
     width = cross.shape[1] // 2
     block = jnp.where(core == 0, cross[:, :width], cross[:, width:])
-    block = block + swap(jnp.where(core == 0, cross[:, width:], cross[:, :width]), sx=1)
-    along_y = [dict(sy=1), dict(sy=3)]
-    along_x = [dict(quad=1), dict(quad=3)]
-    along_z = [dict(quad=4), dict(quad=8), dict(quad=8, sx=2)]
-    rows = block.shape[0] // 2
-    upper, lower = block[:rows], block[rows:]
-    orders = zip(along_y + along_x + along_z, along_z + along_y + along_x)
-    for i, (upper_step, lower_step) in enumerate(orders):
-        if i == 3:
-            upper, moments = lax.optimization_barrier((upper, moments))
-        if i == 6:
-            first, second = turn(moments, columns)
-            upper, first, second = lax.optimization_barrier((upper, first, second))
-        upper_in, lower_in = swap(upper, **upper_step), swap(lower, **lower_step)
-        upper, lower = upper + upper_in, lower + lower_in
-    block = jnp.concatenate([upper, lower], axis=0)
-    other = swap(block, sx=1)
+    block = block + swap(jnp.where(core == 0, cross[:, width:], cross[:, :width]), dict(sx=1))
+    for step in (dict(sy=1), dict(sy=3), dict(quad=1), dict(quad=3), dict(quad=4), dict(quad=8)):
+        block = block + swap(block, step)
+    block, moments = lax.optimization_barrier((block, moments))
+    block = block + swap(block, dict(quad=8, sx=2))
+    first, second = turn(moments, columns)
+    block, first, second = lax.optimization_barrier((block, first, second))
+    other = swap(block, dict(sx=1))
     halves = (jnp.where(core == 0, block, other), jnp.where(core == 0, other, block))
     projections = jnp.stack(
         [jnp.stack([half[:, :64], half[:, 64:]], axis=0) for half in halves], axis=0

time: 80.9 us -> 71.1 us (0.88)
  starting transfers between devices: 46.4 us -> 39 us
  waiting for transfers between devices: 22.3 us -> 20.5 us
    ppermute x2 -> x0, starting transfers between devices: 11.5 us -> none  [the longest x1 10.8 us: body(): outer = lax.ppermute(outer, 'sx', middle)]
    ppermute x22 -> x13, starting transfers between devices: 34.9 us -> 39 us  [swap(): return lax.ppermute(block, axes, pairs)]
    ppermute x22 -> x13, waiting for transfers between devices: 22.3 us -> 20.5 us  [swap(): return lax.ppermute(block, axes, pairs)]
  transfers between devices with their start and end apart: 24 -> 13, of which waited for: 17 -> 13; matrix products, arithmetic and copies ran while one was open for 0% -> 0% of each run, Pallas kernels for 3% -> 3%
where the time goes in v4:
time: 71.1 us; the launch traced here: 71 us
  starting transfers between devices  39 us (55%)
  waiting for transfers between devices  20.5 us (29%)
  Pallas kernels  7.38 us (10%)
  local copies, waits for them, and re-layouts  1.78 us (3%)
  between operations  1.46 us (2%)
  other arithmetic  0.83 us (1%)
    ppermute x13, starting transfers between devices, swap(): return lax.ppermute(block, axes, pairs)  39 us
    ppermute x13, waiting for transfers between devices, swap(): return lax.ppermute(block, axes, pairs)  20.5 us
    pallas_call x1, Pallas kernels, body(): pl.pallas_call(moment_kernel, out_shape=[jax.ShapeDtypeStruct((2, SLAB, c...  4.85 us
    unnamed x14, local copies, waits for them, and re-layouts  1.62 us
    pallas_call x1, Pallas kernels, body(): pl.pallas_call(material_kernel, out_shape=jax.ShapeDtypeStruct((3 * taps,...  1.42 us
  transfers between devices with their start and end apart: 13, of which 13 were waited for; matrix products, arithmetic and copies ran while one was open for 0% of the time, Pallas kernels for 3%

profile of v4, /device:TPU:1, one launch (start us, length us, event | category | flops | bytes accessed | tf_op | source)
XLA Modules:
  0.0 71.0 jit_solution(11929830377719234718)
XLA Ops:
  0.6 0.0 copy-start.4
  0.6 0.0 copy-start.3
  1.3 0.0 copy-start
  1.3 1.6 %copy-done = bf16[64,16,8,128]{3,2,1,0:T(8,128)(2,1)S(1)} copy-done((bf16[64,16,8,128]{3,2,1,0:T(8,128)(2,1)S(1)}, bf16[64,16,8,128]{3,2,1,0:T(8,128)(2,1)}, u32[]{:S(2)}) %copy-start) | copy-done | bytes 2097176
  2.9 0.0 copy-start.1
  2.9 0.0 copy-start.2
  2.9 0.2 slab.1
  3.1 0.0 copy-start.5
  3.1 3.1 %collective-permute-start = (bf16[192,128]{1,0:T(8,128)(2,1)S(1)}, bf16[192,128]{1,0:T(8,128)(2,1)S(1)}, u32[]{:S(2)}, u32[]{:S(2)}) collective-permute-start(bf16[192,128]{1,0:T(8,128)(2,1)S(1)} %get-tuple-element.17), channel_id=1, source_target_pairs={{0,17},{1,16},{2,19},{3,18},{16,1},{17,0},{18,3},{19,2},{32,49},{3... | collective-permute-start | bytes 147464 | tf_op jit(solution)/shard_map/ppermute | solution.py:316
  6.2 1.5 %collective-permute-done = bf16[192,128]{1,0:T(8,128)(2,1)S(1)} collective-permute-done((bf16[192,128]{1,0:T(8,128)(2,1)S(1)}, bf16[192,128]{1,0:T(8,128)(2,1)S(1)}, u32[]{:S(2)}, u32[]{:S(2)}) %collective-permute-start) | collective-permute-done | bytes 49184 | tf_op jit(solution)/shard_map/ppermute | solution.py:316
  7.7 5.2 %collective-permute-start.1 = (bf16[192,128]{1,0:T(8,128)(2,1)S(1)}, bf16[192,128]{1,0:T(8,128)(2,1)S(1)}, u32[]{:S(2)}, u32[]{:S(2)}) collective-permute-start(bf16[192,128]{1,0:T(8,128)(2,1)S(1)} %pad_maximum_fusion.1), channel_id=1, source_target_pairs={{0,51},{1,50},{2,49},{3,48},{16,35},{17,34},{18,33},{19,32},{32,19... | collective-permute-start | bytes 147464 | tf_op jit(solution)/shard_map/ppermute | solution.py:316
  12.9 1.5 %collective-permute-done.1 = bf16[192,128]{1,0:T(8,128)(2,1)S(1)} collective-permute-done((bf16[192,128]{1,0:T(8,128)(2,1)S(1)}, bf16[192,128]{1,0:T(8,128)(2,1)S(1)}, u32[]{:S(2)}, u32[]{:S(2)}) %collective-permute-start.1) | collective-permute-done | bytes 49184 | tf_op jit(solution)/shard_map/ppermute | solution.py:316
  14.4 4.4 %collective-permute-start.2 = (bf16[176,128]{1,0:T(8,128)(2,1)S(1)}, bf16[176,128]{1,0:T(8,128)(2,1)S(1)}, u32[]{:S(2)}, u32[]{:S(2)}) collective-permute-start(bf16[176,128]{1,0:T(8,128)(2,1)S(1)} %pad_maximum_fusion.2), channel_id=1, source_target_pairs={{0,68},{4,64},{8,76},{12,72},{16,84},{20,80},{24,92},{28,88},{32,1... | collective-permute-start | bytes 135176 | tf_op jit(solution)/shard_map/ppermute | solution.py:316
  18.9 0.0 copy-done.4
  18.9 0.0 copy-done.3
  18.9 0.0 copy-done.1
  18.9 0.0 copy-done.2
  18.9 1.4 %material.1.material_ref = f32[75,8,128]{2,1,0:T(8,128)S(1)} custom-call(f32[8]{0:T(128)S(1)} %copy-done.3, f32[8]{0:T(128)S(1)} %copy-done.4, s32[64,32,64]{2,1,0:T(8,128)S(1)} %bitcast.29, s32[64,32,64]{2,1,0:T(8,128)S(1)} %bitcast.30), custom_call_target="tpu_custom_call" | custom-call | flops 40000000 | bytes 1200000 | tf_op jit(solution)/shard_map/material/pallas_call | solution.py:369
  20.3 0.3 collective-permute-done.2
  20.6 6.3 %collective-permute-start.3 = (bf16[176,128]{1,0:T(8,128)(2,1)S(1)}, bf16[176,128]{1,0:T(8,128)(2,1)S(1)}, u32[]{:S(2)}, u32[]{:S(2)}) collective-permute-start(bf16[176,128]{1,0:T(8,128)(2,1)S(1)} %pad_maximum_fusion.3), channel_id=1, source_target_pairs={{0,140},{4,136},{8,132},{12,128},{16,156},{20,152},{24,148},{28,14... | collective-permute-start | bytes 135176 | tf_op jit(solution)/shard_map/ppermute | solution.py:316
  26.9 2.4 %collective-permute-done.3 = bf16[176,128]{1,0:T(8,128)(2,1)S(1)} collective-permute-done((bf16[176,128]{1,0:T(8,128)(2,1)S(1)}, bf16[176,128]{1,0:T(8,128)(2,1)S(1)}, u32[]{:S(2)}, u32[]{:S(2)}) %collective-permute-start.3) | collective-permute-done | bytes 45088 | tf_op jit(solution)/shard_map/ppermute | solution.py:316
  29.3 0.0 copy-done.5
  29.3 4.9 %moments.1 = (f32[2,4,128,128]{3,2,1,0:T(8,128)S(1)}, f32[64,256]{1,0:T(8,128)S(1)}) custom-call(f32[1,128]{1,0:T(1,128)S(1)} %bitcast.31, f32[75,8,128]{2,1,0:T(8,128)S(1)} %material.1.material_ref, bf16[8,128,128]{2,1,0:T(8,128)(2,1)S(1)} %get-tuple-element.21.own_ref, bf16[160,128]{1,0:T(8,128)(2,1)S(1)} %get-tuple-element.32.ylo_ref, ...), custom_call_target="tpu_custom_call" | custom-call | flops 600000000 | bytes 3000000 | tf_op jit(solution)/shard_map/moments/pallas_call | solution.py:384
  34.2 0.2 collective-permute-start.4
  34.5 1.0 %collective-permute-done.4 = f32[64,128]{1,0:T(8,128)S(1)} collective-permute-done((f32[64,128]{1,0:T(8,128)S(1)}, f32[64,128]{1,0:T(8,128)S(1)}, u32[]{:S(2)}, u32[]{:S(2)}) %collective-permute-start.4) | collective-permute-done | bytes 32800 | tf_op jit(solution)/shard_map/ppermute | solution.py:316
  35.5 0.2 collective-permute-start.5
  35.7 2.7 %collective-permute-done.5 = f32[64,128]{1,0:T(8,128)S(1)} collective-permute-done((f32[64,128]{1,0:T(8,128)S(1)}, f32[64,128]{1,0:T(8,128)S(1)}, u32[]{:S(2)}, u32[]{:S(2)}) %collective-permute-start.5) | collective-permute-done | bytes 32800 | tf_op jit(solution)/shard_map/ppermute | solution.py:316
  38.4 2.7 %collective-permute-start.6 = (f32[64,128]{1,0:T(8,128)S(1)}, f32[64,128]{1,0:T(8,128)S(1)}, u32[]{:S(2)}, u32[]{:S(2)}) collective-permute-start(f32[64,128]{1,0:T(8,128)S(1)} %add.45), channel_id=1, source_target_pairs={{0,3},{1,2},{2,1},{3,0},{4,7},{5,6},{6,5},{7,4},{8,11},{9,10},{10,... | collective-permute-start | bytes 98312 | tf_op jit(solution)/shard_map/ppermute | solution.py:316
  41.1 1.3 %collective-permute-done.6 = f32[64,128]{1,0:T(8,128)S(1)} collective-permute-done((f32[64,128]{1,0:T(8,128)S(1)}, f32[64,128]{1,0:T(8,128)S(1)}, u32[]{:S(2)}, u32[]{:S(2)}) %collective-permute-start.6) | collective-permute-done | bytes 32800 | tf_op jit(solution)/shard_map/ppermute | solution.py:316
  42.4 0.0 collective-permute-start.7
  42.4 2.8 %collective-permute-done.7 = f32[64,128]{1,0:T(8,128)S(1)} collective-permute-done((f32[64,128]{1,0:T(8,128)S(1)}, f32[64,128]{1,0:T(8,128)S(1)}, u32[]{:S(2)}, u32[]{:S(2)}) %collective-permute-start.7) | collective-permute-done | bytes 32800 | tf_op jit(solution)/shard_map/ppermute | solution.py:316
  45.2 2.5 %collective-permute-start.8 = (f32[64,128]{1,0:T(8,128)S(1)}, f32[64,128]{1,0:T(8,128)S(1)}, u32[]{:S(2)}, u32[]{:S(2)}) collective-permute-start(f32[64,128]{1,0:T(8,128)S(1)} %add.47), channel_id=1, source_target_pairs={{0,48},{16,32},{32,16},{48,0},{64,112},{80,96},{96,80},{112,64},{1... | collective-permute-start | bytes 98312 | tf_op jit(solution)/shard_map/ppermute | solution.py:316
  47.7 1.5 %collective-permute-done.8 = f32[64,128]{1,0:T(8,128)S(1)} collective-permute-done((f32[64,128]{1,0:T(8,128)S(1)}, f32[64,128]{1,0:T(8,128)S(1)}, u32[]{:S(2)}, u32[]{:S(2)}) %collective-permute-start.8) | collective-permute-done | bytes 32800 | tf_op jit(solution)/shard_map/ppermute | solution.py:316
  49.2 0.6 collective-permute-start.9
  49.7 2.2 %collective-permute-done.9 = f32[64,128]{1,0:T(8,128)S(1)} collective-permute-done((f32[64,128]{1,0:T(8,128)S(1)}, f32[64,128]{1,0:T(8,128)S(1)}, u32[]{:S(2)}, u32[]{:S(2)}) %collective-permute-start.9) | collective-permute-done | bytes 32800 | tf_op jit(solution)/shard_map/ppermute | solution.py:316
  51.9 1.5 %collective-permute-start.10 = (f32[64,128]{1,0:T(8,128)S(1)}, f32[64,128]{1,0:T(8,128)S(1)}, u32[]{:S(2)}, u32[]{:S(2)}) collective-permute-start(f32[64,128]{1,0:T(8,128)S(1)} %add.49), channel_id=1, source_target_pairs={{0,128},{16,144},{32,160},{48,176},{64,192},{80,208},{96,224},{112... | collective-permute-start | bytes 98312 | tf_op jit(solution)/shard_map/ppermute | solution.py:316
  53.4 2.2 %collective-permute-done.10 = f32[64,128]{1,0:T(8,128)S(1)} collective-permute-done((f32[64,128]{1,0:T(8,128)S(1)}, f32[64,128]{1,0:T(8,128)S(1)}, u32[]{:S(2)}, u32[]{:S(2)}) %collective-permute-start.10) | collective-permute-done | bytes 32800 | tf_op jit(solution)/shard_map/ppermute | solution.py:316
  55.6 4.3 %collective-permute-start.11 = (f32[64,128]{1,0:T(8,128)S(1)}, f32[64,128]{1,0:T(8,128)S(1)}, u32[]{:S(2)}, u32[]{:S(2)}) collective-permute-start(f32[64,128]{1,0:T(8,128)S(1)} %add.50), channel_id=1, source_target_pairs={{0,136},{4,140},{8,128},{12,132},{16,152},{20,156},{24,144},{28,14... | collective-permute-start | bytes 98312 | tf_op jit(solution)/shard_map/ppermute | solution.py:316
  59.9 0.9 %turn.1 = (f32[4,128,128]{2,1,0:T(8,128)}, f32[4,128,128]{2,1,0:T(8,128)}) custom-call(f32[2,4,128,128]{3,2,1,0:T(8,128)S(1)} %get-tuple-element.25.moments_ref), custom_call_target="tpu_custom_call" | custom-call | flops 1000000 | bytes 1000000 | tf_op jit(solution)/shard_map/turn/pallas_call | solution.py:298
  60.8 0.4 collective-permute-done.11
  61.2 8.1 %collective-permute-start.12 = (f32[64,128]{1,0:T(8,128)S(1)}, f32[64,128]{1,0:T(8,128)S(1)}, u32[]{:S(2)}, u32[]{:S(2)}) collective-permute-start(f32[64,128]{1,0:T(8,128)S(1)} %add.51), channel_id=1, source_target_pairs={{0,4},{4,0},{8,12},{12,8},{1,5},{5,1},{9,13},{13,9},{2,6},{6,2},{1... | collective-permute-start | bytes 98312 | tf_op jit(solution)/shard_map/ppermute | solution.py:316
  69.3 0.9 %collective-permute-done.12 = f32[64,128]{1,0:T(8,128)S(1)} collective-permute-done((f32[64,128]{1,0:T(8,128)S(1)}, f32[64,128]{1,0:T(8,128)S(1)}, u32[]{:S(2)}, u32[]{:S(2)}) %collective-permute-start.12) | collective-permute-done | bytes 32800 | tf_op jit(solution)/shard_map/ppermute | solution.py:316
  70.2 0.1 slice_bitcast_fusion.3
  70.2 0.1 slice_bitcast_fusion.1
  70.4 0.7 pad_maximum_fusion
  (28 shorter events, 0.2 us)
Async XLA Ops:
  0.6 18.2 %copy-start.4 = (f32[8]{0:T(128)S(1)}, f32[8]{0:T(128)}, u32[]{:S(2)}) copy-start(f32[8]{0:T(128)} %gain_ref.1) | copy-start | bytes 100
  0.6 18.2 %copy-start.3 = (f32[8]{0:T(128)S(1)}, f32[8]{0:T(128)}, u32[]{:S(2)}) copy-start(f32[8]{0:T(128)} %eps_ref.1) | copy-start | bytes 100
  1.3 1.6 %copy-start = (bf16[64,16,8,128]{3,2,1,0:T(8,128)(2,1)S(1)}, bf16[64,16,8,128]{3,2,1,0:T(8,128)(2,1)}, u32[]{:S(2)}) copy-start(bf16[64,16,8,128]{3,2,1,0:T(8,128)(2,1)} %param.7) | copy-start | bytes 6291460
  2.9 16.0 %copy-start.1 = (s32[64,64,32]{1,2,0:T(8,128)S(1)}, s32[64,64,32]{1,2,0:T(8,128)}, u32[]{:S(2)}) copy-start(s32[64,64,32]{1,2,0:T(8,128)} %param.9) | copy-start | bytes 1572868
  2.9 16.0 %copy-start.2 = (s32[64,64,32]{1,2,0:T(8,128)S(1)}, s32[64,64,32]{1,2,0:T(8,128)}, u32[]{:S(2)}) copy-start(s32[64,64,32]{1,2,0:T(8,128)} %param.10) | copy-start | bytes 1572868
  3.1 26.2 %copy-start.5 = (bf16[256,1664]{1,0:T(8,128)(2,1)S(1)}, bf16[256,1664]{1,0:T(8,128)(2,1)}, u32[]{:S(2)}) copy-start(bf16[256,1664]{1,0:T(8,128)(2,1)} %constant.17.clone.pick_ref) | copy-start | bytes 2555908
  3.1 4.6 %collective-permute-start = (bf16[192,128]{1,0:T(8,128)(2,1)S(1)}, bf16[192,128]{1,0:T(8,128)(2,1)S(1)}, u32[]{:S(2)}, u32[]{:S(2)}) collective-permute-start(bf16[192,128]{1,0:T(8,128)(2,1)S(1)} %get-tuple-element.17), channel_id=1, source_target_pairs={{0,17},{1,16},{2,19},{3,18},{16,1},{17,0},{18,3},{19,2},{32,49},{3... | collective-permute-start | bytes 147464 | tf_op jit(solution)/shard_map/ppermute | solution.py:316
  7.7 6.6 %collective-permute-start.1 = (bf16[192,128]{1,0:T(8,128)(2,1)S(1)}, bf16[192,128]{1,0:T(8,128)(2,1)S(1)}, u32[]{:S(2)}, u32[]{:S(2)}) collective-permute-start(bf16[192,128]{1,0:T(8,128)(2,1)S(1)} %pad_maximum_fusion.1), channel_id=1, source_target_pairs={{0,51},{1,50},{2,49},{3,48},{16,35},{17,34},{18,33},{19,32},{32,19... | collective-permute-start | bytes 147464 | tf_op jit(solution)/shard_map/ppermute | solution.py:316
  14.4 6.2 %collective-permute-start.2 = (bf16[176,128]{1,0:T(8,128)(2,1)S(1)}, bf16[176,128]{1,0:T(8,128)(2,1)S(1)}, u32[]{:S(2)}, u32[]{:S(2)}) collective-permute-start(bf16[176,128]{1,0:T(8,128)(2,1)S(1)} %pad_maximum_fusion.2), channel_id=1, source_target_pairs={{0,68},{4,64},{8,76},{12,72},{16,84},{20,80},{24,92},{28,88},{32,1... | collective-permute-start | bytes 135176 | tf_op jit(solution)/shard_map/ppermute | solution.py:316
  20.6 8.7 %collective-permute-start.3 = (bf16[176,128]{1,0:T(8,128)(2,1)S(1)}, bf16[176,128]{1,0:T(8,128)(2,1)S(1)}, u32[]{:S(2)}, u32[]{:S(2)}) collective-permute-start(bf16[176,128]{1,0:T(8,128)(2,1)S(1)} %pad_maximum_fusion.3), channel_id=1, source_target_pairs={{0,140},{4,136},{8,132},{12,128},{16,156},{20,152},{24,148},{28,14... | collective-permute-start | bytes 135176 | tf_op jit(solution)/shard_map/ppermute | solution.py:316
  34.2 1.3 %collective-permute-start.4 = (f32[64,128]{1,0:T(8,128)S(1)}, f32[64,128]{1,0:T(8,128)S(1)}, u32[]{:S(2)}, u32[]{:S(2)}) collective-permute-start(f32[64,128]{1,0:T(8,128)S(1)} %slice_select_fusion), channel_id=1, source_target_pairs={{0,4},{4,0},{8,12},{12,8},{1,5},{5,1},{9,13},{13,9},{2,6},{6,2},{1... | collective-permute-start | bytes 98312 | tf_op jit(solution)/shard_map/ppermute | solution.py:316
  35.5 2.8 %collective-permute-start.5 = (f32[64,128]{1,0:T(8,128)S(1)}, f32[64,128]{1,0:T(8,128)S(1)}, u32[]{:S(2)}, u32[]{:S(2)}) collective-permute-start(f32[64,128]{1,0:T(8,128)S(1)} %select_add_fusion), channel_id=1, source_target_pairs={{0,1},{1,0},{2,3},{3,2},{4,5},{5,4},{6,7},{7,6},{8,9},{9,8},{10,11... | collective-permute-start | bytes 98312 | tf_op jit(solution)/shard_map/ppermute | solution.py:316
  38.4 4.0 %collective-permute-start.6 = (f32[64,128]{1,0:T(8,128)S(1)}, f32[64,128]{1,0:T(8,128)S(1)}, u32[]{:S(2)}, u32[]{:S(2)}) collective-permute-start(f32[64,128]{1,0:T(8,128)S(1)} %add.45), channel_id=1, source_target_pairs={{0,3},{1,2},{2,1},{3,0},{4,7},{5,6},{6,5},{7,4},{8,11},{9,10},{10,... | collective-permute-start | bytes 98312 | tf_op jit(solution)/shard_map/ppermute | solution.py:316
  42.4 2.8 %collective-permute-start.7 = (f32[64,128]{1,0:T(8,128)S(1)}, f32[64,128]{1,0:T(8,128)S(1)}, u32[]{:S(2)}, u32[]{:S(2)}) collective-permute-start(f32[64,128]{1,0:T(8,128)S(1)} %add.46), channel_id=1, source_target_pairs={{0,16},{16,0},{32,48},{48,32},{64,80},{80,64},{96,112},{112,96},{1... | collective-permute-start | bytes 98312 | tf_op jit(solution)/shard_map/ppermute | solution.py:316
  45.2 4.0 %collective-permute-start.8 = (f32[64,128]{1,0:T(8,128)S(1)}, f32[64,128]{1,0:T(8,128)S(1)}, u32[]{:S(2)}, u32[]{:S(2)}) collective-permute-start(f32[64,128]{1,0:T(8,128)S(1)} %add.47), channel_id=1, source_target_pairs={{0,48},{16,32},{32,16},{48,0},{64,112},{80,96},{96,80},{112,64},{1... | collective-permute-start | bytes 98312 | tf_op jit(solution)/shard_map/ppermute | solution.py:316
  49.2 2.8 %collective-permute-start.9 = (f32[64,128]{1,0:T(8,128)S(1)}, f32[64,128]{1,0:T(8,128)S(1)}, u32[]{:S(2)}, u32[]{:S(2)}) collective-permute-start(f32[64,128]{1,0:T(8,128)S(1)} %add.48), channel_id=1, source_target_pairs={{0,64},{16,80},{32,96},{48,112},{64,0},{80,16},{96,32},{112,48},{1... | collective-permute-start | bytes 98312 | tf_op jit(solution)/shard_map/ppermute | solution.py:316
  51.9 3.7 %collective-permute-start.10 = (f32[64,128]{1,0:T(8,128)S(1)}, f32[64,128]{1,0:T(8,128)S(1)}, u32[]{:S(2)}, u32[]{:S(2)}) collective-permute-start(f32[64,128]{1,0:T(8,128)S(1)} %add.49), channel_id=1, source_target_pairs={{0,128},{16,144},{32,160},{48,176},{64,192},{80,208},{96,224},{112... | collective-permute-start | bytes 98312 | tf_op jit(solution)/shard_map/ppermute | solution.py:316
  55.6 5.6 %collective-permute-start.11 = (f32[64,128]{1,0:T(8,128)S(1)}, f32[64,128]{1,0:T(8,128)S(1)}, u32[]{:S(2)}, u32[]{:S(2)}) collective-permute-start(f32[64,128]{1,0:T(8,128)S(1)} %add.50), channel_id=1, source_target_pairs={{0,136},{4,140},{8,128},{12,132},{16,152},{20,156},{24,144},{28,14... | collective-permute-start | bytes 98312 | tf_op jit(solution)/shard_map/ppermute | solution.py:316
  61.2 9.0 %collective-permute-start.12 = (f32[64,128]{1,0:T(8,128)S(1)}, f32[64,128]{1,0:T(8,128)S(1)}, u32[]{:S(2)}, u32[]{:S(2)}) collective-permute-start(f32[64,128]{1,0:T(8,128)S(1)} %add.51), channel_id=1, source_target_pairs={{0,4},{4,0},{8,12},{12,8},{1,5},{5,1},{9,13},{13,9},{2,6},{6,2},{1... | collective-permute-start | bytes 98312 | tf_op jit(solution)/shard_map/ppermute | solution.py:316

commit v5 on v4

--- a/solution.py
+++ b/solution.py
@@ -74,6 +74,7 @@
         parts = jnp.where(row == i, part, parts)
         weight = weight - part
     first_ref[PARTS : PARTS + 16] = parts.astype(jnp.bfloat16)
+    second_ref[PARTS : PARTS + 16] = parts.astype(jnp.bfloat16)
 
     for out_ref, scratch, step, high in (
         (first_ref, whole[0], 1, even_y),
@@ -316,6 +317,11 @@
     return lax.ppermute(block, axes, pairs)
 
 
+def sum_of_four(block, *steps):
+    first, second, third = (swap(block, step) for step in steps)
+    return (block + first) + (second + third)
+
+
 def body(probes, quad_index, region_label, gain_label, region_eps, gain_rate):
     depth, cells_x, cells_y, columns = probes.shape
     planes = SLAB + 4
@@ -329,7 +335,7 @@
     shapes = [
         (planes, cells_x * cells_y, columns),
         (PARTS + 16, columns),
-        (PARTS, columns),
+        (PARTS + 16, columns),
         (FAR, columns),
         (FAR, columns),
     ]
@@ -350,17 +356,19 @@
         rows = jnp.pad(jnp.stack([low, high], axis=1), ((0, 0), (0, 14), (0, 0)))
         return rows.reshape(SLAB * 16, columns)
 
+    parts = first[PARTS:]
     inner = swap(first, dict(quad=1, sy=1))
-    parts = first[PARTS:] + inner[PARTS:]
-    outer = swap(jnp.concatenate([second, parts], axis=0), dict(quad=3, sy=3))
-    parts = parts + outer[PARTS:]
+    outer = swap(second, dict(quad=3, sy=3))
+    last = swap(parts, dict(quad=2))
+    parts = (parts + inner[PARTS:]) + (outer[PARTS:] + last)
     ylo = jnp.where(even_y, outer, inner)[:CORNERS]
     yhi = jnp.where(even_y, inner, outer)[:CORNERS]
-    near = swap(jnp.concatenate([third, corner_rows(CORNERS), parts], axis=0), dict(quad=4, sx=1))
-    parts = parts + near[CORNERS:]
+    third = jnp.concatenate([third, corner_rows(CORNERS), parts], axis=0)
     fourth = jnp.concatenate([fourth, corner_rows(CORNERS + SLAB), parts], axis=0)
+    near = swap(third, dict(quad=4, sx=1))
     beyond = swap(fourth, dict(quad=8, sx=3))
-    parts = parts + beyond[CORNERS:]
+    last = swap(parts, dict(quad=12))
+    parts = (parts + near[CORNERS:]) + (beyond[CORNERS:] + last)
     xlo = jnp.where(even_x, beyond, near)[:CORNERS]
     xhi = jnp.where(even_x, near, beyond)[:CORNERS]
     weight = jnp.sum(parts[:3].astype(jnp.float32), axis=0, keepdims=True)
@@ -402,7 +410,9 @@
     width = cross.shape[1] // 2
     block = jnp.where(core == 0, cross[:, :width], cross[:, width:])
     block = block + swap(jnp.where(core == 0, cross[:, width:], cross[:, :width]), dict(sx=1))
-    for step in (dict(sy=1), dict(sy=3), dict(quad=1), dict(quad=3), dict(quad=4), dict(quad=8)):
+    block = sum_of_four(block, dict(sy=1), dict(sy=3), dict(sy=2))
+    block = sum_of_four(block, dict(quad=1), dict(quad=3), dict(quad=2))
+    for step in (dict(quad=4), dict(quad=8)):
         block = block + swap(block, step)
     block, moments = lax.optimization_barrier((block, moments))
     block = block + swap(block, dict(quad=8, sx=2))

time: 71.1 us -> 66.6 us (0.937)
  waiting for transfers between devices: 20.5 us -> 17.7 us
  starting transfers between devices: 39 us -> 37.3 us
    ppermute x13 -> x17, waiting for transfers between devices: 20.5 us -> 17.7 us  [swap(): return lax.ppermute(block, axes, pairs)]
    ppermute x13 -> x17, starting transfers between devices: 39 us -> 37.3 us  [swap(): return lax.ppermute(block, axes, pairs)]
  transfers between devices with their start and end apart: 13 -> 17, of which waited for: 13 -> 14; matrix products, arithmetic and copies ran while one was open for 0% -> 0% of each run, Pallas kernels for 3% -> 4%
where the time goes in v5:
time: 66.6 us; the launch traced here: 66.4 us
  starting transfers between devices  37.3 us (56%)
  waiting for transfers between devices  17.7 us (27%)
  Pallas kernels  7.39 us (11%)
  local copies, waits for them, and re-layouts  1.78 us (3%)
  between operations  1.47 us (2%)
  other arithmetic  0.82 us (1%)
    ppermute x17, starting transfers between devices, swap(): return lax.ppermute(block, axes, pairs)  37.3 us
    ppermute x17, waiting for transfers between devices, swap(): return lax.ppermute(block, axes, pairs)  17.7 us
    pallas_call x1, Pallas kernels, body(): pl.pallas_call(moment_kernel, out_shape=[jax.ShapeDtypeStruct((2, SLAB, c...  4.86 us
    unnamed x14, local copies, waits for them, and re-layouts  1.61 us
    pallas_call x1, Pallas kernels, body(): pl.pallas_call(material_kernel, out_shape=jax.ShapeDtypeStruct((3 * taps,...  1.43 us
  transfers between devices with their start and end apart: 17, of which 14 were waited for; matrix products, arithmetic and copies ran while one was open for 0% of the time, Pallas kernels for 4%

profile of v5, /device:TPU:1, one launch (start us, length us, event | category | flops | bytes accessed | tf_op | source)
XLA Modules:
  0.0 66.4 jit_solution(12929301999957067292)
XLA Ops:
  0.6 0.0 copy-start.4
  0.6 0.0 copy-start.3
  1.3 0.0 copy-start
  1.3 1.6 %copy-done = bf16[64,16,8,128]{3,2,1,0:T(8,128)(2,1)S(1)} copy-done((bf16[64,16,8,128]{3,2,1,0:T(8,128)(2,1)S(1)}, bf16[64,16,8,128]{3,2,1,0:T(8,128)(2,1)}, u32[]{:S(2)}) %copy-start) | copy-done | bytes 2097176
  2.9 0.2 slab.1
  3.1 5.8 %collective-permute-start.1 = (bf16[192,128]{1,0:T(8,128)(2,1)S(1)}, bf16[192,128]{1,0:T(8,128)(2,1)S(1)}, u32[]{:S(2)}, u32[]{:S(2)}) collective-permute-start(bf16[192,128]{1,0:T(8,128)(2,1)S(1)} %get-tuple-element.18), channel_id=1, source_target_pairs={{0,51},{1,50},{2,49},{3,48},{16,35},{17,34},{18,33},{19,32},{32,19... | collective-permute-start | bytes 147464 | tf_op jit(solution)/shard_map/ppermute | solution.py:317
  8.9 0.0 collective-permute-start
  8.9 1.0 %collective-permute-start.2 = (bf16[16,128]{1,0:T(8,128)(2,1)S(1)}, bf16[16,128]{1,0:T(8,128)(2,1)S(1)}, u32[]{:S(2)}, u32[]{:S(2)}) collective-permute-start(bf16[16,128]{1,0:T(8,128)(2,1)S(1)} %slice.62), channel_id=1, source_target_pairs={{0,32},{16,48},{32,0},{48,16},{64,96},{80,112},{96,64},{112,80},{1... | collective-permute-start | bytes 12296 | tf_op jit(solution)/shard_map/ppermute | solution.py:317
  9.9 0.0 copy-done.4
  9.9 0.0 copy-done.3
  9.9 0.0 copy-done.2
  9.9 1.4 %material.1.material_ref = f32[75,8,128]{2,1,0:T(8,128)S(1)} custom-call(f32[8]{0:T(128)S(1)} %copy-done.3, f32[8]{0:T(128)S(1)} %copy-done.4, s32[64,32,64]{2,1,0:T(8,128)S(1)} %bitcast.29, s32[64,32,64]{2,1,0:T(8,128)S(1)} %bitcast.30), custom_call_target="tpu_custom_call" | custom-call | flops 40000000 | bytes 1200000 | tf_op jit(solution)/shard_map/material/pallas_call | solution.py:377
  11.3 0.0 collective-permute-done.1
  11.4 1.7 %collective-permute-done = bf16[192,128]{1,0:T(8,128)(2,1)S(1)} collective-permute-done((bf16[192,128]{1,0:T(8,128)(2,1)S(1)}, bf16[192,128]{1,0:T(8,128)(2,1)S(1)}, u32[]{:S(2)}, u32[]{:S(2)}) %collective-permute-start) | collective-permute-done | bytes 49184 | tf_op jit(solution)/shard_map/ppermute | solution.py:317
  13.1 0.1 collective-permute-done.2
  13.2 4.1 %collective-permute-start.5 = (bf16[16,128]{1,0:T(8,128)(2,1)S(1)}, bf16[16,128]{1,0:T(8,128)(2,1)S(1)}, u32[]{:S(2)}, u32[]{:S(2)}) collective-permute-start(bf16[16,128]{1,0:T(8,128)(2,1)S(1)} %fusion), channel_id=1, source_target_pairs={{0,192},{16,208},{32,224},{48,240},{64,128},{80,144},{96,160},{112... | collective-permute-start | bytes 12296 | tf_op jit(solution)/shard_map/ppermute | solution.py:317
  17.3 1.3 %collective-permute-start.3 = (bf16[176,128]{1,0:T(8,128)(2,1)S(1)}, bf16[176,128]{1,0:T(8,128)(2,1)S(1)}, u32[]{:S(2)}, u32[]{:S(2)}) collective-permute-start(bf16[176,128]{1,0:T(8,128)(2,1)S(1)} %get-tuple-element.45), channel_id=1, source_target_pairs={{0,68},{4,64},{8,76},{12,72},{16,84},{20,80},{24,92},{28,88},{32,1... | collective-permute-start | bytes 135176 | tf_op jit(solution)/shard_map/ppermute | solution.py:317
  18.6 3.6 %collective-permute-start.4 = (bf16[176,128]{1,0:T(8,128)(2,1)S(1)}, bf16[176,128]{1,0:T(8,128)(2,1)S(1)}, u32[]{:S(2)}, u32[]{:S(2)}) collective-permute-start(bf16[176,128]{1,0:T(8,128)(2,1)S(1)} %get-tuple-element.46), channel_id=1, source_target_pairs={{0,140},{4,136},{8,132},{12,128},{16,156},{20,152},{24,148},{28,14... | collective-permute-start | bytes 135176 | tf_op jit(solution)/shard_map/ppermute | solution.py:317
  22.2 0.0 collective-permute-done.3
  22.2 2.1 %collective-permute-done.4 = bf16[176,128]{1,0:T(8,128)(2,1)S(1)} collective-permute-done((bf16[176,128]{1,0:T(8,128)(2,1)S(1)}, bf16[176,128]{1,0:T(8,128)(2,1)S(1)}, u32[]{:S(2)}, u32[]{:S(2)}) %collective-permute-start.4) | collective-permute-done | bytes 45088 | tf_op jit(solution)/shard_map/ppermute | solution.py:317
  24.3 0.0 collective-permute-done.5
  24.4 4.9 %moments.1 = (f32[2,4,128,128]{3,2,1,0:T(8,128)S(1)}, f32[64,256]{1,0:T(8,128)S(1)}) custom-call(f32[1,128]{1,0:T(1,128)S(1)} %bitcast.31, f32[75,8,128]{2,1,0:T(8,128)S(1)} %material.1.material_ref, bf16[8,128,128]{2,1,0:T(8,128)(2,1)S(1)} %get-tuple-element.21.own_ref, bf16[160,128]{1,0:T(8,128)(2,1)S(1)} %get-tuple-element.32.ylo_ref, ...), custom_call_target="tpu_custom_call" | custom-call | flops 600000000 | bytes 3000000 | tf_op jit(solution)/shard_map/moments/pallas_call | solution.py:392
  29.2 2.2 %collective-permute-start.6 = (f32[64,128]{1,0:T(8,128)S(1)}, f32[64,128]{1,0:T(8,128)S(1)}, u32[]{:S(2)}, u32[]{:S(2)}) collective-permute-start(f32[64,128]{1,0:T(8,128)S(1)} %slice_select_fusion), channel_id=1, source_target_pairs={{0,4},{4,0},{8,12},{12,8},{1,5},{5,1},{9,13},{13,9},{2,6},{6,2},{1... | collective-permute-start | bytes 98312 | tf_op jit(solution)/shard_map/ppermute | solution.py:317
  31.5 0.9 %collective-permute-done.6 = f32[64,128]{1,0:T(8,128)S(1)} collective-permute-done((f32[64,128]{1,0:T(8,128)S(1)}, f32[64,128]{1,0:T(8,128)S(1)}, u32[]{:S(2)}, u32[]{:S(2)}) %collective-permute-start.6) | collective-permute-done | bytes 32800 | tf_op jit(solution)/shard_map/ppermute | solution.py:317
  32.4 1.0 %collective-permute-start.9 = (f32[64,128]{1,0:T(8,128)S(1)}, f32[64,128]{1,0:T(8,128)S(1)}, u32[]{:S(2)}, u32[]{:S(2)}) collective-permute-start(f32[64,128]{1,0:T(8,128)S(1)} %select_add_fusion), channel_id=1, source_target_pairs={{0,2},{1,3},{2,0},{3,1},{4,6},{5,7},{6,4},{7,5},{8,10},{9,11},{10,... | collective-permute-start | bytes 98312 | tf_op jit(solution)/shard_map/ppermute | solution.py:317
  33.4 2.7 %collective-permute-start.8 = (f32[64,128]{1,0:T(8,128)S(1)}, f32[64,128]{1,0:T(8,128)S(1)}, u32[]{:S(2)}, u32[]{:S(2)}) collective-permute-start(f32[64,128]{1,0:T(8,128)S(1)} %select_add_fusion), channel_id=1, source_target_pairs={{0,3},{1,2},{2,1},{3,0},{4,7},{5,6},{6,5},{7,4},{8,11},{9,10},{10,... | collective-permute-start | bytes 98312 | tf_op jit(solution)/shard_map/ppermute | solution.py:317
  36.1 0.0 collective-permute-start.7
  36.1 0.5 collective-permute-done.9
  36.6 1.2 %collective-permute-done.8 = f32[64,128]{1,0:T(8,128)S(1)} collective-permute-done((f32[64,128]{1,0:T(8,128)S(1)}, f32[64,128]{1,0:T(8,128)S(1)}, u32[]{:S(2)}, u32[]{:S(2)}) %collective-permute-start.8) | collective-permute-done | bytes 32800 | tf_op jit(solution)/shard_map/ppermute | solution.py:317
  37.8 1.1 %collective-permute-done.7 = f32[64,128]{1,0:T(8,128)S(1)} collective-permute-done((f32[64,128]{1,0:T(8,128)S(1)}, f32[64,128]{1,0:T(8,128)S(1)}, u32[]{:S(2)}, u32[]{:S(2)}) %collective-permute-start.7) | collective-permute-done | bytes 32800 | tf_op jit(solution)/shard_map/ppermute | solution.py:317
  38.9 1.5 %collective-permute-start.12 = (f32[64,128]{1,0:T(8,128)S(1)}, f32[64,128]{1,0:T(8,128)S(1)}, u32[]{:S(2)}, u32[]{:S(2)}) collective-permute-start(f32[64,128]{1,0:T(8,128)S(1)} %add_add_fusion.1), channel_id=1, source_target_pairs={{0,32},{16,48},{32,0},{48,16},{64,96},{80,112},{96,64},{112,80},{1... | collective-permute-start | bytes 98312 | tf_op jit(solution)/shard_map/ppermute | solution.py:317
  40.4 2.5 %collective-permute-start.11 = (f32[64,128]{1,0:T(8,128)S(1)}, f32[64,128]{1,0:T(8,128)S(1)}, u32[]{:S(2)}, u32[]{:S(2)}) collective-permute-start(f32[64,128]{1,0:T(8,128)S(1)} %add_add_fusion.1), channel_id=1, source_target_pairs={{0,48},{16,32},{32,16},{48,0},{64,112},{80,96},{96,80},{112,64},{1... | collective-permute-start | bytes 98312 | tf_op jit(solution)/shard_map/ppermute | solution.py:317
  42.9 0.0 collective-permute-start.10
  42.9 0.4 collective-permute-done.12
  43.3 1.1 %collective-permute-done.11 = f32[64,128]{1,0:T(8,128)S(1)} collective-permute-done((f32[64,128]{1,0:T(8,128)S(1)}, f32[64,128]{1,0:T(8,128)S(1)}, u32[]{:S(2)}, u32[]{:S(2)}) %collective-permute-start.11) | collective-permute-done | bytes 32800 | tf_op jit(solution)/shard_map/ppermute | solution.py:317
  44.4 1.6 %collective-permute-done.10 = f32[64,128]{1,0:T(8,128)S(1)} collective-permute-done((f32[64,128]{1,0:T(8,128)S(1)}, f32[64,128]{1,0:T(8,128)S(1)}, u32[]{:S(2)}, u32[]{:S(2)}) %collective-permute-start.10) | collective-permute-done | bytes 32800 | tf_op jit(solution)/shard_map/ppermute | solution.py:317
  46.0 1.3 %collective-permute-start.13 = (f32[64,128]{1,0:T(8,128)S(1)}, f32[64,128]{1,0:T(8,128)S(1)}, u32[]{:S(2)}, u32[]{:S(2)}) collective-permute-start(f32[64,128]{1,0:T(8,128)S(1)} %add_add_fusion), channel_id=1, source_target_pairs={{0,64},{16,80},{32,96},{48,112},{64,0},{80,16},{96,32},{112,48},{1... | collective-permute-start | bytes 98312 | tf_op jit(solution)/shard_map/ppermute | solution.py:317
  47.3 1.9 %collective-permute-done.13 = f32[64,128]{1,0:T(8,128)S(1)} collective-permute-done((f32[64,128]{1,0:T(8,128)S(1)}, f32[64,128]{1,0:T(8,128)S(1)}, u32[]{:S(2)}, u32[]{:S(2)}) %collective-permute-start.13) | collective-permute-done | bytes 32800 | tf_op jit(solution)/shard_map/ppermute | solution.py:317
  49.1 0.1 collective-permute-start.14
  49.3 3.6 %collective-permute-done.14 = f32[64,128]{1,0:T(8,128)S(1)} collective-permute-done((f32[64,128]{1,0:T(8,128)S(1)}, f32[64,128]{1,0:T(8,128)S(1)}, u32[]{:S(2)}, u32[]{:S(2)}) %collective-permute-start.14) | collective-permute-done | bytes 32800 | tf_op jit(solution)/shard_map/ppermute | solution.py:317
  52.8 3.2 %collective-permute-start.15 = (f32[64,128]{1,0:T(8,128)S(1)}, f32[64,128]{1,0:T(8,128)S(1)}, u32[]{:S(2)}, u32[]{:S(2)}) collective-permute-start(f32[64,128]{1,0:T(8,128)S(1)} %add.66), channel_id=1, source_target_pairs={{0,136},{4,140},{8,128},{12,132},{16,152},{20,156},{24,144},{28,14... | collective-permute-start | bytes 98312 | tf_op jit(solution)/shard_map/ppermute | solution.py:317
  56.0 0.9 %turn.1 = (f32[4,128,128]{2,1,0:T(8,128)}, f32[4,128,128]{2,1,0:T(8,128)}) custom-call(f32[2,4,128,128]{3,2,1,0:T(8,128)S(1)} %get-tuple-element.25.moments_ref), custom_call_target="tpu_custom_call" | custom-call | flops 1000000 | bytes 1000000 | tf_op jit(solution)/shard_map/turn/pallas_call | solution.py:299
  56.9 0.8 %collective-permute-done.15 = f32[64,128]{1,0:T(8,128)S(1)} collective-permute-done((f32[64,128]{1,0:T(8,128)S(1)}, f32[64,128]{1,0:T(8,128)S(1)}, u32[]{:S(2)}, u32[]{:S(2)}) %collective-permute-start.15) | collective-permute-done | bytes 32800 | tf_op jit(solution)/shard_map/ppermute | solution.py:317
  57.8 7.0 %collective-permute-start.16 = (f32[64,128]{1,0:T(8,128)S(1)}, f32[64,128]{1,0:T(8,128)S(1)}, u32[]{:S(2)}, u32[]{:S(2)}) collective-permute-start(f32[64,128]{1,0:T(8,128)S(1)} %add.67), channel_id=1, source_target_pairs={{0,4},{4,0},{8,12},{12,8},{1,5},{5,1},{9,13},{13,9},{2,6},{6,2},{1... | collective-permute-start | bytes 98312 | tf_op jit(solution)/shard_map/ppermute | solution.py:317
  64.7 0.9 %collective-permute-done.16 = f32[64,128]{1,0:T(8,128)S(1)} collective-permute-done((f32[64,128]{1,0:T(8,128)S(1)}, f32[64,128]{1,0:T(8,128)S(1)}, u32[]{:S(2)}, u32[]{:S(2)}) %collective-permute-start.16) | collective-permute-done | bytes 32800 | tf_op jit(solution)/shard_map/ppermute | solution.py:317
  65.6 0.1 slice_bitcast_fusion.3
  65.7 0.1 slice_bitcast_fusion.1
  65.8 0.7 %pad_maximum_fusion = f32[2,2,64,64]{3,2,1,0:T(8,128)} fusion(f32[1,2,64,64]{3,2,1,0:T(8,128)S(1)} %maximum_bitcast_fusion.1, f32[1,2,64,64]{3,2,1,0:T(8,128)S(1)} %maximum_bitcast_fusion), kind=kLoop, calls=%fused_computation | loop fusion | flops 16384 | bytes 131072 | tf_op jit(solution)/shard_map/stack | solution.py:423
  (29 shorter events, 0.2 us)
Async XLA Ops:
  0.6 9.3 %copy-start.4 = (f32[8]{0:T(128)S(1)}, f32[8]{0:T(128)}, u32[]{:S(2)}) copy-start(f32[8]{0:T(128)} %gain_ref.1) | copy-start | bytes 100
  0.6 9.3 %copy-start.3 = (f32[8]{0:T(128)S(1)}, f32[8]{0:T(128)}, u32[]{:S(2)}) copy-start(f32[8]{0:T(128)} %eps_ref.1) | copy-start | bytes 100
  1.3 1.6 %copy-start = (bf16[64,16,8,128]{3,2,1,0:T(8,128)(2,1)S(1)}, bf16[64,16,8,128]{3,2,1,0:T(8,128)(2,1)}, u32[]{:S(2)}) copy-start(bf16[64,16,8,128]{3,2,1,0:T(8,128)(2,1)} %param.7) | copy-start | bytes 6291460
  2.9 7.0 %copy-start.1 = (s32[64,64,32]{1,2,0:T(8,128)S(1)}, s32[64,64,32]{1,2,0:T(8,128)}, u32[]{:S(2)}) copy-start(s32[64,64,32]{1,2,0:T(8,128)} %param.9) | copy-start | bytes 1572868
  2.9 7.0 %copy-start.2 = (s32[64,64,32]{1,2,0:T(8,128)S(1)}, s32[64,64,32]{1,2,0:T(8,128)}, u32[]{:S(2)}) copy-start(s32[64,64,32]{1,2,0:T(8,128)} %param.10) | copy-start | bytes 1572868
  2.9 21.4 %copy-start.5 = (bf16[256,1664]{1,0:T(8,128)(2,1)S(1)}, bf16[256,1664]{1,0:T(8,128)(2,1)}, u32[]{:S(2)}) copy-start(bf16[256,1664]{1,0:T(8,128)(2,1)} %constant.17.clone.pick_ref) | copy-start | bytes 2555908
  3.1 8.3 %collective-permute-start.1 = (bf16[192,128]{1,0:T(8,128)(2,1)S(1)}, bf16[192,128]{1,0:T(8,128)(2,1)S(1)}, u32[]{:S(2)}, u32[]{:S(2)}) collective-permute-start(bf16[192,128]{1,0:T(8,128)(2,1)S(1)} %get-tuple-element.18), channel_id=1, source_target_pairs={{0,51},{1,50},{2,49},{3,48},{16,35},{17,34},{18,33},{19,32},{32,19... | collective-permute-start | bytes 147464 | tf_op jit(solution)/shard_map/ppermute | solution.py:317
  8.9 4.1 %collective-permute-start = (bf16[192,128]{1,0:T(8,128)(2,1)S(1)}, bf16[192,128]{1,0:T(8,128)(2,1)S(1)}, u32[]{:S(2)}, u32[]{:S(2)}) collective-permute-start(bf16[192,128]{1,0:T(8,128)(2,1)S(1)} %get-tuple-element.17), channel_id=1, source_target_pairs={{0,17},{1,16},{2,19},{3,18},{16,1},{17,0},{18,3},{19,2},{32,49},{3... | collective-permute-start | bytes 147464 | tf_op jit(solution)/shard_map/ppermute | solution.py:317
  8.9 4.3 %collective-permute-start.2 = (bf16[16,128]{1,0:T(8,128)(2,1)S(1)}, bf16[16,128]{1,0:T(8,128)(2,1)S(1)}, u32[]{:S(2)}, u32[]{:S(2)}) collective-permute-start(bf16[16,128]{1,0:T(8,128)(2,1)S(1)} %slice.62), channel_id=1, source_target_pairs={{0,32},{16,48},{32,0},{48,16},{64,96},{80,112},{96,64},{112,80},{1... | collective-permute-start | bytes 12296 | tf_op jit(solution)/shard_map/ppermute | solution.py:317
  13.2 11.1 %collective-permute-start.5 = (bf16[16,128]{1,0:T(8,128)(2,1)S(1)}, bf16[16,128]{1,0:T(8,128)(2,1)S(1)}, u32[]{:S(2)}, u32[]{:S(2)}) collective-permute-start(bf16[16,128]{1,0:T(8,128)(2,1)S(1)} %fusion), channel_id=1, source_target_pairs={{0,192},{16,208},{32,224},{48,240},{64,128},{80,144},{96,160},{112... | collective-permute-start | bytes 12296 | tf_op jit(solution)/shard_map/ppermute | solution.py:317
  17.3 4.9 %collective-permute-start.3 = (bf16[176,128]{1,0:T(8,128)(2,1)S(1)}, bf16[176,128]{1,0:T(8,128)(2,1)S(1)}, u32[]{:S(2)}, u32[]{:S(2)}) collective-permute-start(bf16[176,128]{1,0:T(8,128)(2,1)S(1)} %get-tuple-element.45), channel_id=1, source_target_pairs={{0,68},{4,64},{8,76},{12,72},{16,84},{20,80},{24,92},{28,88},{32,1... | collective-permute-start | bytes 135176 | tf_op jit(solution)/shard_map/ppermute | solution.py:317
  18.6 5.7 %collective-permute-start.4 = (bf16[176,128]{1,0:T(8,128)(2,1)S(1)}, bf16[176,128]{1,0:T(8,128)(2,1)S(1)}, u32[]{:S(2)}, u32[]{:S(2)}) collective-permute-start(bf16[176,128]{1,0:T(8,128)(2,1)S(1)} %get-tuple-element.46), channel_id=1, source_target_pairs={{0,140},{4,136},{8,132},{12,128},{16,156},{20,152},{24,148},{28,14... | collective-permute-start | bytes 135176 | tf_op jit(solution)/shard_map/ppermute | solution.py:317
  29.2 3.1 %collective-permute-start.6 = (f32[64,128]{1,0:T(8,128)S(1)}, f32[64,128]{1,0:T(8,128)S(1)}, u32[]{:S(2)}, u32[]{:S(2)}) collective-permute-start(f32[64,128]{1,0:T(8,128)S(1)} %slice_select_fusion), channel_id=1, source_target_pairs={{0,4},{4,0},{8,12},{12,8},{1,5},{5,1},{9,13},{13,9},{2,6},{6,2},{1... | collective-permute-start | bytes 98312 | tf_op jit(solution)/shard_map/ppermute | solution.py:317
  32.4 4.3 %collective-permute-start.9 = (f32[64,128]{1,0:T(8,128)S(1)}, f32[64,128]{1,0:T(8,128)S(1)}, u32[]{:S(2)}, u32[]{:S(2)}) collective-permute-start(f32[64,128]{1,0:T(8,128)S(1)} %select_add_fusion), channel_id=1, source_target_pairs={{0,2},{1,3},{2,0},{3,1},{4,6},{5,7},{6,4},{7,5},{8,10},{9,11},{10,... | collective-permute-start | bytes 98312 | tf_op jit(solution)/shard_map/ppermute | solution.py:317
  33.4 4.4 %collective-permute-start.8 = (f32[64,128]{1,0:T(8,128)S(1)}, f32[64,128]{1,0:T(8,128)S(1)}, u32[]{:S(2)}, u32[]{:S(2)}) collective-permute-start(f32[64,128]{1,0:T(8,128)S(1)} %select_add_fusion), channel_id=1, source_target_pairs={{0,3},{1,2},{2,1},{3,0},{4,7},{5,6},{6,5},{7,4},{8,11},{9,10},{10,... | collective-permute-start | bytes 98312 | tf_op jit(solution)/shard_map/ppermute | solution.py:317
  36.1 2.8 %collective-permute-start.7 = (f32[64,128]{1,0:T(8,128)S(1)}, f32[64,128]{1,0:T(8,128)S(1)}, u32[]{:S(2)}, u32[]{:S(2)}) collective-permute-start(f32[64,128]{1,0:T(8,128)S(1)} %select_add_fusion), channel_id=1, source_target_pairs={{0,1},{1,0},{2,3},{3,2},{4,5},{5,4},{6,7},{7,6},{8,9},{9,8},{10,11... | collective-permute-start | bytes 98312 | tf_op jit(solution)/shard_map/ppermute | solution.py:317
  38.9 4.4 %collective-permute-start.12 = (f32[64,128]{1,0:T(8,128)S(1)}, f32[64,128]{1,0:T(8,128)S(1)}, u32[]{:S(2)}, u32[]{:S(2)}) collective-permute-start(f32[64,128]{1,0:T(8,128)S(1)} %add_add_fusion.1), channel_id=1, source_target_pairs={{0,32},{16,48},{32,0},{48,16},{64,96},{80,112},{96,64},{112,80},{1... | collective-permute-start | bytes 98312 | tf_op jit(solution)/shard_map/ppermute | solution.py:317
  40.4 4.0 %collective-permute-start.11 = (f32[64,128]{1,0:T(8,128)S(1)}, f32[64,128]{1,0:T(8,128)S(1)}, u32[]{:S(2)}, u32[]{:S(2)}) collective-permute-start(f32[64,128]{1,0:T(8,128)S(1)} %add_add_fusion.1), channel_id=1, source_target_pairs={{0,48},{16,32},{32,16},{48,0},{64,112},{80,96},{96,80},{112,64},{1... | collective-permute-start | bytes 98312 | tf_op jit(solution)/shard_map/ppermute | solution.py:317
  42.9 3.1 %collective-permute-start.10 = (f32[64,128]{1,0:T(8,128)S(1)}, f32[64,128]{1,0:T(8,128)S(1)}, u32[]{:S(2)}, u32[]{:S(2)}) collective-permute-start(f32[64,128]{1,0:T(8,128)S(1)} %add_add_fusion.1), channel_id=1, source_target_pairs={{0,16},{16,0},{32,48},{48,32},{64,80},{80,64},{96,112},{112,96},{1... | collective-permute-start | bytes 98312 | tf_op jit(solution)/shard_map/ppermute | solution.py:317
  46.0 3.1 %collective-permute-start.13 = (f32[64,128]{1,0:T(8,128)S(1)}, f32[64,128]{1,0:T(8,128)S(1)}, u32[]{:S(2)}, u32[]{:S(2)}) collective-permute-start(f32[64,128]{1,0:T(8,128)S(1)} %add_add_fusion), channel_id=1, source_target_pairs={{0,64},{16,80},{32,96},{48,112},{64,0},{80,16},{96,32},{112,48},{1... | collective-permute-start | bytes 98312 | tf_op jit(solution)/shard_map/ppermute | solution.py:317
  49.1 3.7 %collective-permute-start.14 = (f32[64,128]{1,0:T(8,128)S(1)}, f32[64,128]{1,0:T(8,128)S(1)}, u32[]{:S(2)}, u32[]{:S(2)}) collective-permute-start(f32[64,128]{1,0:T(8,128)S(1)} %add.65), channel_id=1, source_target_pairs={{0,128},{16,144},{32,160},{48,176},{64,192},{80,208},{96,224},{112... | collective-permute-start | bytes 98312 | tf_op jit(solution)/shard_map/ppermute | solution.py:317
  52.8 4.9 %collective-permute-start.15 = (f32[64,128]{1,0:T(8,128)S(1)}, f32[64,128]{1,0:T(8,128)S(1)}, u32[]{:S(2)}, u32[]{:S(2)}) collective-permute-start(f32[64,128]{1,0:T(8,128)S(1)} %add.66), channel_id=1, source_target_pairs={{0,136},{4,140},{8,128},{12,132},{16,152},{20,156},{24,144},{28,14... | collective-permute-start | bytes 98312 | tf_op jit(solution)/shard_map/ppermute | solution.py:317
  57.8 7.8 %collective-permute-start.16 = (f32[64,128]{1,0:T(8,128)S(1)}, f32[64,128]{1,0:T(8,128)S(1)}, u32[]{:S(2)}, u32[]{:S(2)}) collective-permute-start(f32[64,128]{1,0:T(8,128)S(1)} %add.67), channel_id=1, source_target_pairs={{0,4},{4,0},{8,12},{12,8},{1,5},{5,1},{9,13},{13,9},{2,6},{6,2},{1... | collective-permute-start | bytes 98312 | tf_op jit(solution)/shard_map/ppermute | solution.py:317

commit v6 on v5

--- a/solution.py
+++ b/solution.py
@@ -49,18 +49,40 @@
     return pick.astype(jnp.bfloat16)
 
 
-def slab_kernel(quad_ref, probes_ref, own_ref, first_ref, second_ref, third_ref, fourth_ref, *whole):
+def slab_kernel(
+    quad_ref, probes_ref, own_ref, first_ref, second_ref, third_ref, fourth_ref, block, side, rim, sems, *whole
+):
     depth = probes_ref.shape[0]
     me = lax.axis_index("quad")
     even_x = (lax.axis_index("sx") & 1) == 0
     even_y = (lax.axis_index("sy") & 1) == 0
 
-    def plane(slab, p):
-        return probes_ref[jnp.clip(slab * SLAB + (p - 2), 0, depth - 1)]
-
-    def x_edge(slab, p, high):
-        block = plane(slab, p)
-        return jnp.where(high, block[LANES - 16 :].astype(jnp.float32), block[:16].astype(jnp.float32))
+    group = 4 * SLAB + 4
+    bases = [jnp.clip((me & ~3) * SLAB - 2, 0, depth - group)]
+    bases += [jnp.clip((me ^ bit) * SLAB - 2, 0, depth - SLAB - 4) for bit in (4, 8)]
+    held = (block, side.at[0], side.at[1])
+    copies = [
+        pltpu.make_async_copy(probes_ref.at[pl.ds(base, to.shape[0])], to, sems.at[i])
+        for i, (base, to) in enumerate(zip(bases, held))
+    ]
+    edges = ((4, even_x), (8, jnp.logical_not(even_x)))
+    for i, step in enumerate((1, 3)):
+        for j, (bit, high) in enumerate(edges):
+            at = pl.multiple_of(jnp.where(high, LANES - 16, 0), 16)
+            start = ((me ^ step) ^ bit) * SLAB
+            edge = probes_ref.at[pl.ds(start, SLAB), pl.ds(at, 16)]
+            copies.append(pltpu.make_async_copy(edge, rim.at[2 * i + j], sems.at[len(copies)]))
+    for copy in copies:
+        copy.start()
+
+    def plane(slab, p, bit=0):
+        z = jnp.clip(slab * SLAB + (p - 2), 0, depth - 1)
+        at = {0: 0, 4: 1, 8: 2}[bit]
+        return held[at][z - bases[at]]
+
+    def x_edge(values, high):
+        low, top = values[:16].astype(jnp.float32), values[LANES - 16 :].astype(jnp.float32)
+        return jnp.where(high, top, low)
 
     index = jnp.full((1, LANES), quad_ref[0], jnp.int32).astype(jnp.float32)
     angle = 2.0 * math.pi * (index + 0.5) / (4 * QUAD)
@@ -76,10 +98,10 @@
     first_ref[PARTS : PARTS + 16] = parts.astype(jnp.bfloat16)
     second_ref[PARTS : PARTS + 16] = parts.astype(jnp.bfloat16)
 
-    for out_ref, scratch, step, high in (
-        (first_ref, whole[0], 1, even_y),
-        (second_ref, whole[1], 3, jnp.logical_not(even_y)),
-    ):
+    for copy in copies:
+        copy.wait()
+    sends = ((first_ref, whole[0], 1, even_y), (second_ref, whole[1], 3, jnp.logical_not(even_y)))
+    for send, (out_ref, scratch, step, high) in enumerate(sends):
         target = me ^ step
         for p in range(1, SLAB + 3):
             scratch[(p - 1) * LANES : p * LANES] = plane(target, p).astype(jnp.float32)
@@ -88,17 +110,17 @@
             top = scratch[pl.ds(start + CY - 1 - deep, count * CX, stride=CY), :]
             out_ref[at : at + count * CX] = jnp.where(high, top, low).astype(jnp.bfloat16)
         corners = jnp.zeros((16, LANES), jnp.float32)
-        for i, (bit, edge) in enumerate(((4, even_x), (8, jnp.logical_not(even_x)))):
+        for i, (bit, edge) in enumerate(edges):
             cell = jnp.where(edge, CY, 0) + jnp.where(high, CY - 1, 0)
             for p in range(SLAB):
-                picked = jnp.where(row == cell, x_edge(target ^ bit, p + 2, edge), 0.0)
+                picked = jnp.where(row == cell, rim[2 * send + i, p].astype(jnp.float32), 0.0)
                 picked = jnp.sum(picked, axis=0, keepdims=True)
                 corners = jnp.where(row == i * SLAB + p, picked, corners)
         out_ref[CORNERS : CORNERS + 16] = corners.astype(jnp.bfloat16)
 
-    for out_ref, bit, high in ((third_ref, 4, even_x), (fourth_ref, 8, jnp.logical_not(even_x))):
+    for out_ref, (bit, high) in zip((third_ref, fourth_ref), edges):
         for p in range(1, SLAB + 3):
-            out_ref[(p - 1) * 16 : p * 16] = x_edge(me ^ bit, p, high).astype(jnp.bfloat16)
+            out_ref[(p - 1) * 16 : p * 16] = x_edge(plane(me ^ bit, p, bit), high).astype(jnp.bfloat16)
     for p in range(SLAB + 4):
         own_ref[p] = plane(me, p)
 
@@ -342,10 +364,16 @@
     own, first, second, third, fourth = pl.pallas_call(
         slab_kernel,
         out_shape=[jax.ShapeDtypeStruct(shape, probes.dtype) for shape in shapes],
-        in_specs=[smem, vmem],
+        in_specs=[smem, hbm],
         out_specs=[vmem] * 5,
-        scratch_shapes=[pltpu.VMEM(((SLAB + 2) * LANES, columns), jnp.float32)] * 2,
-        compiler_params=pltpu.CompilerParams(vmem_limit_bytes=8 * mib),
+        scratch_shapes=[
+            pltpu.VMEM((4 * SLAB + 4, cells_x * cells_y, columns), probes.dtype),
+            pltpu.VMEM((2, planes, cells_x * cells_y, columns), probes.dtype),
+            pltpu.VMEM((4, SLAB, 16, columns), probes.dtype),
+            pltpu.SemaphoreType.DMA((7,)),
+        ]
+        + [pltpu.VMEM(((SLAB + 2) * LANES, columns), jnp.float32)] * 2,
+        compiler_params=pltpu.CompilerParams(vmem_limit_bytes=52 * mib),
         cost_estimate=pl.CostEstimate(flops=10000000, bytes_accessed=600000, transcendentals=0),
         name="slab",
     )(quad_index, probes.reshape(depth, cells_x * cells_y, columns))

time: 66.6 us -> 66.8 us (level)
  local copies, waits for them, and re-layouts: 1.78 us -> 0.2 us
  Pallas kernels: 7.39 us -> 8.74 us
    unnamed x14 -> x12, local copies, waits for them, and re-layouts: 1.61 us -> 0.03 us
    pallas_call x1, Pallas kernels: 0.18 us -> 1.53 us  [body(): pl.pallas_call(slab_kernel, out_shape=[jax.ShapeDtypeStruct(shape, probes...]
where the time goes in v6:
time: 66.8 us; the launch traced here: 66.7 us
  starting transfers between devices  37.6 us (56%)
  waiting for transfers between devices  17.7 us (26%)
  Pallas kernels  8.74 us (13%)
  between operations  1.61 us (2%)
  other arithmetic  0.82 us (1%)
    ppermute x17, starting transfers between devices, swap(): return lax.ppermute(block, axes, pairs)  37.6 us
    ppermute x17, waiting for transfers between devices, swap(): return lax.ppermute(block, axes, pairs)  17.7 us
    pallas_call x1, Pallas kernels, body(): pl.pallas_call(moment_kernel, out_shape=[jax.ShapeDtypeStruct((2, SLAB, c...  4.86 us
    pallas_call x1, Pallas kernels, body(): pl.pallas_call(slab_kernel, out_shape=[jax.ShapeDtypeStruct(shape, probes...  1.53 us
    pallas_call x1, Pallas kernels, body(): pl.pallas_call(material_kernel, out_shape=jax.ShapeDtypeStruct((3 * taps,...  1.43 us
  transfers between devices with their start and end apart: 17, of which 14 were waited for; matrix products, arithmetic and copies ran while one was open for 0% of the time, Pallas kernels for 4%

profile of v6, /device:TPU:1, one launch (start us, length us, event | category | flops | bytes accessed | tf_op | source)
XLA Modules:
  0.0 66.7 jit_solution(3244447272655706136)
XLA Ops:
  0.6 0.0 copy-start.3
  0.6 0.0 copy-start.2
  0.7 0.0 copy-start.1
  0.7 0.0 copy-start
  1.5 0.0 copy-start.4
  1.5 1.5 %slab.1 = (bf16[8,128,128]{2,1,0:T(8,128)(2,1)S(1)}, bf16[192,128]{1,0:T(8,128)(2,1)S(1)}, bf16[192,128]{1,0:T(8,128)(2,1)S(1)}, bf16[96,128]{1,0:T(8,128)(2,1)S(1)}, bf16[96,128]{1,0:T(8,128)(2,1)S(1)}) custom-call(s32[1]{0:T(128)S(6)} %copy.14.quad_ref, bf16[64,128,128]{2,1,0:T(8,128)(2,1)} %bitcast.31), custom_call_target="tpu_custom_call" | custom-call | flops 10000000 | bytes 600000 | tf_op jit(solution)/shard_map/slab/pallas_call | solution.py:364
  3.0 5.8 %collective-permute-start.1 = (bf16[192,128]{1,0:T(8,128)(2,1)S(1)}, bf16[192,128]{1,0:T(8,128)(2,1)S(1)}, u32[]{:S(2)}, u32[]{:S(2)}) collective-permute-start(bf16[192,128]{1,0:T(8,128)(2,1)S(1)} %get-tuple-element.18), channel_id=1, source_target_pairs={{0,51},{1,50},{2,49},{3,48},{16,35},{17,34},{18,33},{19,32},{32,19... | collective-permute-start | bytes 147464 | tf_op jit(solution)/shard_map/ppermute | solution.py:339
  8.9 0.0 collective-permute-start
  8.9 1.0 %collective-permute-start.2 = (bf16[16,128]{1,0:T(8,128)(2,1)S(1)}, bf16[16,128]{1,0:T(8,128)(2,1)S(1)}, u32[]{:S(2)}, u32[]{:S(2)}) collective-permute-start(bf16[16,128]{1,0:T(8,128)(2,1)S(1)} %slice.62), channel_id=1, source_target_pairs={{0,32},{16,48},{32,0},{48,16},{64,96},{80,112},{96,64},{112,80},{1... | collective-permute-start | bytes 12296 | tf_op jit(solution)/shard_map/ppermute | solution.py:339
  9.8 0.0 copy-done.3
  9.8 0.0 copy-done.2
  9.8 1.4 %material.1.material_ref = f32[75,8,128]{2,1,0:T(8,128)S(1)} custom-call(f32[8]{0:T(128)S(1)} %copy-done.2, f32[8]{0:T(128)S(1)} %copy-done.3, s32[64,32,64]{2,1,0:T(8,128)S(1)} %bitcast.28, s32[64,32,64]{2,1,0:T(8,128)S(1)} %bitcast.29), custom_call_target="tpu_custom_call" | custom-call | flops 40000000 | bytes 1200000 | tf_op jit(solution)/shard_map/material/pallas_call | solution.py:405
  11.3 0.0 collective-permute-done.1
  11.3 1.7 %collective-permute-done = bf16[192,128]{1,0:T(8,128)(2,1)S(1)} collective-permute-done((bf16[192,128]{1,0:T(8,128)(2,1)S(1)}, bf16[192,128]{1,0:T(8,128)(2,1)S(1)}, u32[]{:S(2)}, u32[]{:S(2)}) %collective-permute-start) | collective-permute-done | bytes 49184 | tf_op jit(solution)/shard_map/ppermute | solution.py:339
  13.0 0.1 collective-permute-done.2
  13.1 4.1 %collective-permute-start.5 = (bf16[16,128]{1,0:T(8,128)(2,1)S(1)}, bf16[16,128]{1,0:T(8,128)(2,1)S(1)}, u32[]{:S(2)}, u32[]{:S(2)}) collective-permute-start(bf16[16,128]{1,0:T(8,128)(2,1)S(1)} %fusion), channel_id=1, source_target_pairs={{0,192},{16,208},{32,224},{48,240},{64,128},{80,144},{96,160},{112... | collective-permute-start | bytes 12296 | tf_op jit(solution)/shard_map/ppermute | solution.py:339
  17.2 1.3 %collective-permute-start.3 = (bf16[176,128]{1,0:T(8,128)(2,1)S(1)}, bf16[176,128]{1,0:T(8,128)(2,1)S(1)}, u32[]{:S(2)}, u32[]{:S(2)}) collective-permute-start(bf16[176,128]{1,0:T(8,128)(2,1)S(1)} %get-tuple-element.45), channel_id=1, source_target_pairs={{0,68},{4,64},{8,76},{12,72},{16,84},{20,80},{24,92},{28,88},{32,1... | collective-permute-start | bytes 135176 | tf_op jit(solution)/shard_map/ppermute | solution.py:339
  18.5 3.6 %collective-permute-start.4 = (bf16[176,128]{1,0:T(8,128)(2,1)S(1)}, bf16[176,128]{1,0:T(8,128)(2,1)S(1)}, u32[]{:S(2)}, u32[]{:S(2)}) collective-permute-start(bf16[176,128]{1,0:T(8,128)(2,1)S(1)} %get-tuple-element.46), channel_id=1, source_target_pairs={{0,140},{4,136},{8,132},{12,128},{16,156},{20,152},{24,148},{28,14... | collective-permute-start | bytes 135176 | tf_op jit(solution)/shard_map/ppermute | solution.py:339
  22.1 0.0 collective-permute-done.3
  22.1 2.1 %collective-permute-done.4 = bf16[176,128]{1,0:T(8,128)(2,1)S(1)} collective-permute-done((bf16[176,128]{1,0:T(8,128)(2,1)S(1)}, bf16[176,128]{1,0:T(8,128)(2,1)S(1)}, u32[]{:S(2)}, u32[]{:S(2)}) %collective-permute-start.4) | collective-permute-done | bytes 45088 | tf_op jit(solution)/shard_map/ppermute | solution.py:339
  24.2 0.0 collective-permute-done.5
  24.3 4.9 %moments.1 = (f32[2,4,128,128]{3,2,1,0:T(8,128)S(1)}, f32[64,256]{1,0:T(8,128)S(1)}) custom-call(f32[1,128]{1,0:T(1,128)S(1)} %bitcast.30, f32[75,8,128]{2,1,0:T(8,128)S(1)} %material.1.material_ref, bf16[8,128,128]{2,1,0:T(8,128)(2,1)S(1)} %get-tuple-element.21.own_ref, bf16[160,128]{1,0:T(8,128)(2,1)S(1)} %get-tuple-element.32.ylo_ref, ...), custom_call_target="tpu_custom_call" | custom-call | flops 600000000 | bytes 3000000 | tf_op jit(solution)/shard_map/moments/pallas_call | solution.py:420
  29.2 2.2 %collective-permute-start.6 = (f32[64,128]{1,0:T(8,128)S(1)}, f32[64,128]{1,0:T(8,128)S(1)}, u32[]{:S(2)}, u32[]{:S(2)}) collective-permute-start(f32[64,128]{1,0:T(8,128)S(1)} %slice_select_fusion), channel_id=1, source_target_pairs={{0,4},{4,0},{8,12},{12,8},{1,5},{5,1},{9,13},{13,9},{2,6},{6,2},{1... | collective-permute-start | bytes 98312 | tf_op jit(solution)/shard_map/ppermute | solution.py:339
  31.4 0.9 %collective-permute-done.6 = f32[64,128]{1,0:T(8,128)S(1)} collective-permute-done((f32[64,128]{1,0:T(8,128)S(1)}, f32[64,128]{1,0:T(8,128)S(1)}, u32[]{:S(2)}, u32[]{:S(2)}) %collective-permute-start.6) | collective-permute-done | bytes 32800 | tf_op jit(solution)/shard_map/ppermute | solution.py:339
  32.3 1.0 %collective-permute-start.9 = (f32[64,128]{1,0:T(8,128)S(1)}, f32[64,128]{1,0:T(8,128)S(1)}, u32[]{:S(2)}, u32[]{:S(2)}) collective-permute-start(f32[64,128]{1,0:T(8,128)S(1)} %select_add_fusion), channel_id=1, source_target_pairs={{0,2},{1,3},{2,0},{3,1},{4,6},{5,7},{6,4},{7,5},{8,10},{9,11},{10,... | collective-permute-start | bytes 98312 | tf_op jit(solution)/shard_map/ppermute | solution.py:339
  33.3 2.7 %collective-permute-start.8 = (f32[64,128]{1,0:T(8,128)S(1)}, f32[64,128]{1,0:T(8,128)S(1)}, u32[]{:S(2)}, u32[]{:S(2)}) collective-permute-start(f32[64,128]{1,0:T(8,128)S(1)} %select_add_fusion), channel_id=1, source_target_pairs={{0,3},{1,2},{2,1},{3,0},{4,7},{5,6},{6,5},{7,4},{8,11},{9,10},{10,... | collective-permute-start | bytes 98312 | tf_op jit(solution)/shard_map/ppermute | solution.py:339
  36.1 0.0 collective-permute-start.7
  36.1 0.5 collective-permute-done.9
  36.5 1.2 %collective-permute-done.8 = f32[64,128]{1,0:T(8,128)S(1)} collective-permute-done((f32[64,128]{1,0:T(8,128)S(1)}, f32[64,128]{1,0:T(8,128)S(1)}, u32[]{:S(2)}, u32[]{:S(2)}) %collective-permute-start.8) | collective-permute-done | bytes 32800 | tf_op jit(solution)/shard_map/ppermute | solution.py:339
  37.7 1.1 %collective-permute-done.7 = f32[64,128]{1,0:T(8,128)S(1)} collective-permute-done((f32[64,128]{1,0:T(8,128)S(1)}, f32[64,128]{1,0:T(8,128)S(1)}, u32[]{:S(2)}, u32[]{:S(2)}) %collective-permute-start.7) | collective-permute-done | bytes 32800 | tf_op jit(solution)/shard_map/ppermute | solution.py:339
  38.8 1.5 %collective-permute-start.12 = (f32[64,128]{1,0:T(8,128)S(1)}, f32[64,128]{1,0:T(8,128)S(1)}, u32[]{:S(2)}, u32[]{:S(2)}) collective-permute-start(f32[64,128]{1,0:T(8,128)S(1)} %add_add_fusion.1), channel_id=1, source_target_pairs={{0,32},{16,48},{32,0},{48,16},{64,96},{80,112},{96,64},{112,80},{1... | collective-permute-start | bytes 98312 | tf_op jit(solution)/shard_map/ppermute | solution.py:339
  40.4 2.5 %collective-permute-start.11 = (f32[64,128]{1,0:T(8,128)S(1)}, f32[64,128]{1,0:T(8,128)S(1)}, u32[]{:S(2)}, u32[]{:S(2)}) collective-permute-start(f32[64,128]{1,0:T(8,128)S(1)} %add_add_fusion.1), channel_id=1, source_target_pairs={{0,48},{16,32},{32,16},{48,0},{64,112},{80,96},{96,80},{112,64},{1... | collective-permute-start | bytes 98312 | tf_op jit(solution)/shard_map/ppermute | solution.py:339
  42.8 0.0 collective-permute-start.10
  42.8 0.3 collective-permute-done.12
  43.2 1.1 %collective-permute-done.11 = f32[64,128]{1,0:T(8,128)S(1)} collective-permute-done((f32[64,128]{1,0:T(8,128)S(1)}, f32[64,128]{1,0:T(8,128)S(1)}, u32[]{:S(2)}, u32[]{:S(2)}) %collective-permute-start.11) | collective-permute-done | bytes 32800 | tf_op jit(solution)/shard_map/ppermute | solution.py:339
  44.3 1.6 %collective-permute-done.10 = f32[64,128]{1,0:T(8,128)S(1)} collective-permute-done((f32[64,128]{1,0:T(8,128)S(1)}, f32[64,128]{1,0:T(8,128)S(1)}, u32[]{:S(2)}, u32[]{:S(2)}) %collective-permute-start.10) | collective-permute-done | bytes 32800 | tf_op jit(solution)/shard_map/ppermute | solution.py:339
  45.9 1.3 %collective-permute-start.13 = (f32[64,128]{1,0:T(8,128)S(1)}, f32[64,128]{1,0:T(8,128)S(1)}, u32[]{:S(2)}, u32[]{:S(2)}) collective-permute-start(f32[64,128]{1,0:T(8,128)S(1)} %add_add_fusion), channel_id=1, source_target_pairs={{0,64},{16,80},{32,96},{48,112},{64,0},{80,16},{96,32},{112,48},{1... | collective-permute-start | bytes 98312 | tf_op jit(solution)/shard_map/ppermute | solution.py:339
  47.2 1.9 %collective-permute-done.13 = f32[64,128]{1,0:T(8,128)S(1)} collective-permute-done((f32[64,128]{1,0:T(8,128)S(1)}, f32[64,128]{1,0:T(8,128)S(1)}, u32[]{:S(2)}, u32[]{:S(2)}) %collective-permute-start.13) | collective-permute-done | bytes 32800 | tf_op jit(solution)/shard_map/ppermute | solution.py:339
  49.1 0.1 collective-permute-start.14
  49.2 3.6 %collective-permute-done.14 = f32[64,128]{1,0:T(8,128)S(1)} collective-permute-done((f32[64,128]{1,0:T(8,128)S(1)}, f32[64,128]{1,0:T(8,128)S(1)}, u32[]{:S(2)}, u32[]{:S(2)}) %collective-permute-start.14) | collective-permute-done | bytes 32800 | tf_op jit(solution)/shard_map/ppermute | solution.py:339
  52.8 3.2 %collective-permute-start.15 = (f32[64,128]{1,0:T(8,128)S(1)}, f32[64,128]{1,0:T(8,128)S(1)}, u32[]{:S(2)}, u32[]{:S(2)}) collective-permute-start(f32[64,128]{1,0:T(8,128)S(1)} %add.66), channel_id=1, source_target_pairs={{0,136},{4,140},{8,128},{12,132},{16,152},{20,156},{24,144},{28,14... | collective-permute-start | bytes 98312 | tf_op jit(solution)/shard_map/ppermute | solution.py:339
  55.9 0.9 %turn.1 = (f32[4,128,128]{2,1,0:T(8,128)}, f32[4,128,128]{2,1,0:T(8,128)}) custom-call(f32[2,4,128,128]{3,2,1,0:T(8,128)S(1)} %get-tuple-element.25.moments_ref), custom_call_target="tpu_custom_call" | custom-call | flops 1000000 | bytes 1000000 | tf_op jit(solution)/shard_map/turn/pallas_call | solution.py:321
  56.8 0.8 %collective-permute-done.15 = f32[64,128]{1,0:T(8,128)S(1)} collective-permute-done((f32[64,128]{1,0:T(8,128)S(1)}, f32[64,128]{1,0:T(8,128)S(1)}, u32[]{:S(2)}, u32[]{:S(2)}) %collective-permute-start.15) | collective-permute-done | bytes 32800 | tf_op jit(solution)/shard_map/ppermute | solution.py:339
  57.7 7.3 %collective-permute-start.16 = (f32[64,128]{1,0:T(8,128)S(1)}, f32[64,128]{1,0:T(8,128)S(1)}, u32[]{:S(2)}, u32[]{:S(2)}) collective-permute-start(f32[64,128]{1,0:T(8,128)S(1)} %add.67), channel_id=1, source_target_pairs={{0,4},{4,0},{8,12},{12,8},{1,5},{5,1},{9,13},{13,9},{2,6},{6,2},{1... | collective-permute-start | bytes 98312 | tf_op jit(solution)/shard_map/ppermute | solution.py:339
  65.0 0.9 %collective-permute-done.16 = f32[64,128]{1,0:T(8,128)S(1)} collective-permute-done((f32[64,128]{1,0:T(8,128)S(1)}, f32[64,128]{1,0:T(8,128)S(1)}, u32[]{:S(2)}, u32[]{:S(2)}) %collective-permute-start.16) | collective-permute-done | bytes 32800 | tf_op jit(solution)/shard_map/ppermute | solution.py:339
  65.8 0.1 slice_bitcast_fusion.3
  65.9 0.1 slice_bitcast_fusion.1
  66.0 0.7 %pad_maximum_fusion = f32[2,2,64,64]{3,2,1,0:T(8,128)} fusion(f32[1,2,64,64]{3,2,1,0:T(8,128)S(1)} %maximum_bitcast_fusion.1, f32[1,2,64,64]{3,2,1,0:T(8,128)S(1)} %maximum_bitcast_fusion), kind=kLoop, calls=%fused_computation | loop fusion | flops 16384 | bytes 131072 | tf_op jit(solution)/shard_map/stack | solution.py:451
  (27 shorter events, 0.2 us)
Async XLA Ops:
  0.6 9.2 %copy-start.3 = (f32[8]{0:T(128)S(1)}, f32[8]{0:T(128)}, u32[]{:S(2)}) copy-start(f32[8]{0:T(128)} %gain_ref.1) | copy-start | bytes 100
  0.6 9.2 %copy-start.2 = (f32[8]{0:T(128)S(1)}, f32[8]{0:T(128)}, u32[]{:S(2)}) copy-start(f32[8]{0:T(128)} %eps_ref.1) | copy-start | bytes 100
  0.7 9.2 %copy-start.1 = (s32[64,64,32]{1,2,0:T(8,128)S(1)}, s32[64,64,32]{1,2,0:T(8,128)}, u32[]{:S(2)}) copy-start(s32[64,64,32]{1,2,0:T(8,128)} %param.10) | copy-start | bytes 1572868
  0.7 9.2 %copy-start = (s32[64,64,32]{1,2,0:T(8,128)S(1)}, s32[64,64,32]{1,2,0:T(8,128)}, u32[]{:S(2)}) copy-start(s32[64,64,32]{1,2,0:T(8,128)} %param.9) | copy-start | bytes 1572868
  1.5 22.8 %copy-start.4 = (bf16[256,1664]{1,0:T(8,128)(2,1)S(1)}, bf16[256,1664]{1,0:T(8,128)(2,1)}, u32[]{:S(2)}) copy-start(bf16[256,1664]{1,0:T(8,128)(2,1)} %constant.17.clone.pick_ref) | copy-start | bytes 2555908
  3.0 8.3 %collective-permute-start.1 = (bf16[192,128]{1,0:T(8,128)(2,1)S(1)}, bf16[192,128]{1,0:T(8,128)(2,1)S(1)}, u32[]{:S(2)}, u32[]{:S(2)}) collective-permute-start(bf16[192,128]{1,0:T(8,128)(2,1)S(1)} %get-tuple-element.18), channel_id=1, source_target_pairs={{0,51},{1,50},{2,49},{3,48},{16,35},{17,34},{18,33},{19,32},{32,19... | collective-permute-start | bytes 147464 | tf_op jit(solution)/shard_map/ppermute | solution.py:339
  8.9 4.1 %collective-permute-start = (bf16[192,128]{1,0:T(8,128)(2,1)S(1)}, bf16[192,128]{1,0:T(8,128)(2,1)S(1)}, u32[]{:S(2)}, u32[]{:S(2)}) collective-permute-start(bf16[192,128]{1,0:T(8,128)(2,1)S(1)} %get-tuple-element.17), channel_id=1, source_target_pairs={{0,17},{1,16},{2,19},{3,18},{16,1},{17,0},{18,3},{19,2},{32,49},{3... | collective-permute-start | bytes 147464 | tf_op jit(solution)/shard_map/ppermute | solution.py:339
  8.9 4.3 %collective-permute-start.2 = (bf16[16,128]{1,0:T(8,128)(2,1)S(1)}, bf16[16,128]{1,0:T(8,128)(2,1)S(1)}, u32[]{:S(2)}, u32[]{:S(2)}) collective-permute-start(bf16[16,128]{1,0:T(8,128)(2,1)S(1)} %slice.62), channel_id=1, source_target_pairs={{0,32},{16,48},{32,0},{48,16},{64,96},{80,112},{96,64},{112,80},{1... | collective-permute-start | bytes 12296 | tf_op jit(solution)/shard_map/ppermute | solution.py:339
  13.1 11.1 %collective-permute-start.5 = (bf16[16,128]{1,0:T(8,128)(2,1)S(1)}, bf16[16,128]{1,0:T(8,128)(2,1)S(1)}, u32[]{:S(2)}, u32[]{:S(2)}) collective-permute-start(bf16[16,128]{1,0:T(8,128)(2,1)S(1)} %fusion), channel_id=1, source_target_pairs={{0,192},{16,208},{32,224},{48,240},{64,128},{80,144},{96,160},{112... | collective-permute-start | bytes 12296 | tf_op jit(solution)/shard_map/ppermute | solution.py:339
  17.2 4.9 %collective-permute-start.3 = (bf16[176,128]{1,0:T(8,128)(2,1)S(1)}, bf16[176,128]{1,0:T(8,128)(2,1)S(1)}, u32[]{:S(2)}, u32[]{:S(2)}) collective-permute-start(bf16[176,128]{1,0:T(8,128)(2,1)S(1)} %get-tuple-element.45), channel_id=1, source_target_pairs={{0,68},{4,64},{8,76},{12,72},{16,84},{20,80},{24,92},{28,88},{32,1... | collective-permute-start | bytes 135176 | tf_op jit(solution)/shard_map/ppermute | solution.py:339
  18.5 5.7 %collective-permute-start.4 = (bf16[176,128]{1,0:T(8,128)(2,1)S(1)}, bf16[176,128]{1,0:T(8,128)(2,1)S(1)}, u32[]{:S(2)}, u32[]{:S(2)}) collective-permute-start(bf16[176,128]{1,0:T(8,128)(2,1)S(1)} %get-tuple-element.46), channel_id=1, source_target_pairs={{0,140},{4,136},{8,132},{12,128},{16,156},{20,152},{24,148},{28,14... | collective-permute-start | bytes 135176 | tf_op jit(solution)/shard_map/ppermute | solution.py:339
  29.2 3.1 %collective-permute-start.6 = (f32[64,128]{1,0:T(8,128)S(1)}, f32[64,128]{1,0:T(8,128)S(1)}, u32[]{:S(2)}, u32[]{:S(2)}) collective-permute-start(f32[64,128]{1,0:T(8,128)S(1)} %slice_select_fusion), channel_id=1, source_target_pairs={{0,4},{4,0},{8,12},{12,8},{1,5},{5,1},{9,13},{13,9},{2,6},{6,2},{1... | collective-permute-start | bytes 98312 | tf_op jit(solution)/shard_map/ppermute | solution.py:339
  32.3 4.3 %collective-permute-start.9 = (f32[64,128]{1,0:T(8,128)S(1)}, f32[64,128]{1,0:T(8,128)S(1)}, u32[]{:S(2)}, u32[]{:S(2)}) collective-permute-start(f32[64,128]{1,0:T(8,128)S(1)} %select_add_fusion), channel_id=1, source_target_pairs={{0,2},{1,3},{2,0},{3,1},{4,6},{5,7},{6,4},{7,5},{8,10},{9,11},{10,... | collective-permute-start | bytes 98312 | tf_op jit(solution)/shard_map/ppermute | solution.py:339
  33.3 4.4 %collective-permute-start.8 = (f32[64,128]{1,0:T(8,128)S(1)}, f32[64,128]{1,0:T(8,128)S(1)}, u32[]{:S(2)}, u32[]{:S(2)}) collective-permute-start(f32[64,128]{1,0:T(8,128)S(1)} %select_add_fusion), channel_id=1, source_target_pairs={{0,3},{1,2},{2,1},{3,0},{4,7},{5,6},{6,5},{7,4},{8,11},{9,10},{10,... | collective-permute-start | bytes 98312 | tf_op jit(solution)/shard_map/ppermute | solution.py:339
  36.1 2.8 %collective-permute-start.7 = (f32[64,128]{1,0:T(8,128)S(1)}, f32[64,128]{1,0:T(8,128)S(1)}, u32[]{:S(2)}, u32[]{:S(2)}) collective-permute-start(f32[64,128]{1,0:T(8,128)S(1)} %select_add_fusion), channel_id=1, source_target_pairs={{0,1},{1,0},{2,3},{3,2},{4,5},{5,4},{6,7},{7,6},{8,9},{9,8},{10,11... | collective-permute-start | bytes 98312 | tf_op jit(solution)/shard_map/ppermute | solution.py:339
  38.8 4.4 %collective-permute-start.12 = (f32[64,128]{1,0:T(8,128)S(1)}, f32[64,128]{1,0:T(8,128)S(1)}, u32[]{:S(2)}, u32[]{:S(2)}) collective-permute-start(f32[64,128]{1,0:T(8,128)S(1)} %add_add_fusion.1), channel_id=1, source_target_pairs={{0,32},{16,48},{32,0},{48,16},{64,96},{80,112},{96,64},{112,80},{1... | collective-permute-start | bytes 98312 | tf_op jit(solution)/shard_map/ppermute | solution.py:339
  40.4 4.0 %collective-permute-start.11 = (f32[64,128]{1,0:T(8,128)S(1)}, f32[64,128]{1,0:T(8,128)S(1)}, u32[]{:S(2)}, u32[]{:S(2)}) collective-permute-start(f32[64,128]{1,0:T(8,128)S(1)} %add_add_fusion.1), channel_id=1, source_target_pairs={{0,48},{16,32},{32,16},{48,0},{64,112},{80,96},{96,80},{112,64},{1... | collective-permute-start | bytes 98312 | tf_op jit(solution)/shard_map/ppermute | solution.py:339
  42.8 3.1 %collective-permute-start.10 = (f32[64,128]{1,0:T(8,128)S(1)}, f32[64,128]{1,0:T(8,128)S(1)}, u32[]{:S(2)}, u32[]{:S(2)}) collective-permute-start(f32[64,128]{1,0:T(8,128)S(1)} %add_add_fusion.1), channel_id=1, source_target_pairs={{0,16},{16,0},{32,48},{48,32},{64,80},{80,64},{96,112},{112,96},{1... | collective-permute-start | bytes 98312 | tf_op jit(solution)/shard_map/ppermute | solution.py:339
  45.9 3.1 %collective-permute-start.13 = (f32[64,128]{1,0:T(8,128)S(1)}, f32[64,128]{1,0:T(8,128)S(1)}, u32[]{:S(2)}, u32[]{:S(2)}) collective-permute-start(f32[64,128]{1,0:T(8,128)S(1)} %add_add_fusion), channel_id=1, source_target_pairs={{0,64},{16,80},{32,96},{48,112},{64,0},{80,16},{96,32},{112,48},{1... | collective-permute-start | bytes 98312 | tf_op jit(solution)/shard_map/ppermute | solution.py:339
  49.1 3.7 %collective-permute-start.14 = (f32[64,128]{1,0:T(8,128)S(1)}, f32[64,128]{1,0:T(8,128)S(1)}, u32[]{:S(2)}, u32[]{:S(2)}) collective-permute-start(f32[64,128]{1,0:T(8,128)S(1)} %add.65), channel_id=1, source_target_pairs={{0,128},{16,144},{32,160},{48,176},{64,192},{80,208},{96,224},{112... | collective-permute-start | bytes 98312 | tf_op jit(solution)/shard_map/ppermute | solution.py:339
  52.8 4.9 %collective-permute-start.15 = (f32[64,128]{1,0:T(8,128)S(1)}, f32[64,128]{1,0:T(8,128)S(1)}, u32[]{:S(2)}, u32[]{:S(2)}) collective-permute-start(f32[64,128]{1,0:T(8,128)S(1)} %add.66), channel_id=1, source_target_pairs={{0,136},{4,140},{8,128},{12,132},{16,152},{20,156},{24,144},{28,14... | collective-permute-start | bytes 98312 | tf_op jit(solution)/shard_map/ppermute | solution.py:339
  57.7 8.2 %collective-permute-start.16 = (f32[64,128]{1,0:T(8,128)S(1)}, f32[64,128]{1,0:T(8,128)S(1)}, u32[]{:S(2)}, u32[]{:S(2)}) collective-permute-start(f32[64,128]{1,0:T(8,128)S(1)} %add.67), channel_id=1, source_target_pairs={{0,4},{4,0},{8,12},{12,8},{1,5},{5,1},{9,13},{13,9},{2,6},{6,2},{1... | collective-permute-start | bytes 98312 | tf_op jit(solution)/shard_map/ppermute | solution.py:339

commit v7 on v6

--- a/solution.py
+++ b/solution.py
@@ -29,24 +29,27 @@
 PARTS = CORNERS + 16
 
 
-def source_cells():
-    cells = [(x, y) for x in range(CX) for y in range(CY)]
-    for y in (-1, -2, CY, CY + 1):
-        cells += [(x, y) for x in range(CX)]
-    for xs, near in (((-2, -1), -1), ((CX, CX + 1), CX)):
-        cells += [(x, y) for x in xs for y in range(CY)]
-        cells += [(near, -1), (near, CY)] + [None] * 14
-    return cells
-
-
-def selector():
-    row_of = {cell: row for row, cell in enumerate(source_cells()) if cell is not None}
-    pick = np.zeros((256, WIDE), np.float32)
-    for o, (dx, dy) in enumerate(OFFSETS):
-        for x in range(CX):
-            for y in range(CY):
-                pick[row_of[(x + dx, y + dy)], o * LANES + x * CY + y] = 1.0
-    return pick.astype(jnp.bfloat16)
+def cell_code(x, y):
+    return (x + 2) * 32 + y + 2
+
+
+def write_selector(pick_ref):
+    row = lax.broadcasted_iota(jnp.int32, (16, LANES), 0)
+    lane = lax.broadcasted_iota(jnp.int32, (16, LANES), 1)
+    own = cell_code(lax.shift_right_logical(lane, 3), lane & 7)
+
+    def pair_of_x(x):
+        return cell_code(x + lax.shift_right_logical(row, 3), row & 7)
+
+    tiles = [pair_of_x(2 * i) for i in range(CX // 2)]
+    tiles += [cell_code(row, y) for y in (-1, -2, CY, CY + 1)]
+    for first, near in ((-2, -1), (CX, CX)):
+        corners = jnp.where(row == 1, cell_code(near, CY), -1)
+        tiles += [pair_of_x(first), jnp.where(row == 0, cell_code(near, -1), corners)]
+    for i, tile in enumerate(tiles):
+        for off, (dx, dy) in enumerate(OFFSETS):
+            hit = jnp.where(tile == own + (dx * 32 + dy), 1.0, 0.0).astype(jnp.bfloat16)
+            pick_ref[i * 16 : i * 16 + 16, off * LANES : (off + 1) * LANES] = hit
 
 
 def slab_kernel(
@@ -125,7 +128,7 @@
         own_ref[p] = plane(me, p)
 
 
-def material_kernel(eps_ref, gain_ref, region_ref, level_ref, out_ref, labels, codes, sems):
+def material_kernel(eps_ref, gain_ref, region_ref, level_ref, out_ref, pick_ref, labels, codes, sems):
     planes = SLAB + 4
     start = lax.axis_index("quad") * SLAB
     first = jnp.clip(start - 2, 0, region_ref.shape[0] - planes)
@@ -136,6 +139,7 @@
     ]
     for copy in copies:
         copy.start()
+    write_selector(pick_ref)
     depth_y, depth_x = labels.shape[2:]
     lane = lax.broadcasted_iota(jnp.int32, (depth_x, LANES), 1)
     x_row = lax.broadcasted_iota(jnp.int32, (depth_x, LANES), 0) - lax.axis_index("sx") * CX
@@ -181,6 +185,44 @@
     return (a[0] + b[0], a[1] + b[1])
 
 
+def apply_stencil(moment, folded, shifted, moment_ref, cross_ref):
+    half = 64
+    part = 32
+
+    def one_chunk(step, carry):
+        z = step // 2
+        col = pl.multiple_of((step % 2) * part, part)
+        sums = [jnp.zeros((part, LANES), jnp.float32) for _ in range(3)]
+        for t, (dz, off) in enumerate(TAPS):
+            real = shifted[z + 2 + dz, off, pl.ds(col, part), :]
+            imag = shifted[z + 2 + dz, off, pl.ds(half + col, part), :]
+            factors = (real + imag, real, imag)
+            for i in range(3):
+                sums[i] += folded[6 * t + 3 * moment + i, pl.ds(z, 1), :] * factors[i]
+        both, minus, plus = sums
+        moment_ref[z, pl.ds(col, part), :] = both - plus
+        moment_ref[z, pl.ds(half + col, part), :] = both + minus
+        return carry
+
+    lax.fori_loop(0, 2 * SLAB, one_chunk, 0)
+
+    cross = jnp.zeros((half, 2 * half), jnp.float32)
+    for z in range(SLAB):
+        left = jnp.concatenate([shifted[z + 2, 0, :half], shifted[z + 2, 0, half:]], axis=1)
+        left = left.astype(jnp.bfloat16)
+        real = moment_ref[z, :half]
+        imag = moment_ref[z, half:]
+        rows = [jnp.concatenate([real, imag], axis=1), jnp.concatenate([imag, -real], axis=1)]
+        right = jnp.concatenate(rows, axis=0)
+        high = right.astype(jnp.bfloat16)
+        low = (right - high.astype(jnp.float32)).astype(jnp.bfloat16)
+        for piece in (high, low):
+            cross += lax.dot_general(
+                left, piece, (((1,), (1,)), ((), ())), preferred_element_type=jnp.float32
+            )
+    cross_ref[...] = cross * (1.0 / 131072)
+
+
 def moment_kernel(
     weight_ref,
     material_ref,
@@ -190,11 +232,11 @@
     xlo_ref,
     xhi_ref,
     pick_ref,
-    moments_ref,
+    moment_ref,
     cross_ref,
     shifted,
+    folded,
     coef,
-    folded,
 ):
     for plane in range(SLAB + 4):
         near, far = (plane - 1) * 16, 96 + (plane - 2) * 16
@@ -268,65 +310,33 @@
         folded[3 * i + 1] = imag - real
         folded[3 * i + 2] = real + imag
 
-    half = 64
-    part = 32
-
-    def one_chunk(step, carry):
-        z = step // 2
-        col = pl.multiple_of((step % 2) * part, part)
-        sums = [jnp.zeros((part, LANES), jnp.float32) for _ in range(6)]
-        for t, (dz, off) in enumerate(TAPS):
-            real = shifted[z + 2 + dz, off, pl.ds(col, part), :]
-            imag = shifted[z + 2 + dz, off, pl.ds(half + col, part), :]
-            factors = (real + imag, real, imag)
-            for i in range(6):
-                sums[i] += folded[6 * t + i, pl.ds(z, 1), :] * factors[i % 3]
-        for k in range(2):
-            both, minus, plus = sums[3 * k : 3 * k + 3]
-            moments_ref[k, z, pl.ds(col, part), :] = both - plus
-            moments_ref[k, z, pl.ds(half + col, part), :] = both + minus
-        return carry
-
-    lax.fori_loop(0, 2 * SLAB, one_chunk, 0)
-
-    cross = jnp.zeros((half, 4 * half), jnp.float32)
+    apply_stencil(1 - (lax.axis_index("sx") & 1), folded, shifted, moment_ref, cross_ref)
+
+
+def second_kernel(shifted, folded, moment_ref, cross_ref):
+    apply_stencil(lax.axis_index("sx") & 1, folded, shifted, moment_ref, cross_ref)
+
+
+def turn_kernel(other_ref, mine_ref, first_ref, second_ref):
+    even = (lax.axis_index("sx") & 1) == 0
     for z in range(SLAB):
-        left = jnp.concatenate([shifted[z + 2, 0, :half], shifted[z + 2, 0, half:]], axis=1)
-        left = left.astype(jnp.bfloat16)
-        rows = []
-        for k in range(2):
-            real = moments_ref[k, z, :half]
-            imag = moments_ref[k, z, half:]
-            rows.append(jnp.concatenate([real, imag], axis=1))
-            rows.append(jnp.concatenate([imag, -real], axis=1))
-        right = jnp.concatenate(rows, axis=0)
-        high = right.astype(jnp.bfloat16)
-        low = (right - high.astype(jnp.float32)).astype(jnp.bfloat16)
-        for piece in (high, low):
-            cross += lax.dot_general(
-                left, piece, (((1,), (1,)), ((), ())), preferred_element_type=jnp.float32
-            )
-    cross_ref[...] = cross * (1.0 / 131072)
-
-
-def turn_kernel(moments_ref, first_ref, second_ref):
-    for k, out_ref in enumerate((first_ref, second_ref)):
-        for z in range(SLAB):
-            out_ref[z] = moments_ref[k, z].T
-
-
-def turn(moments, columns):
+        other, mine = other_ref[z].T, mine_ref[z].T
+        first_ref[z] = jnp.where(even, mine, other)
+        second_ref[z] = jnp.where(even, other, mine)
+
+
+def turn(other, mine, columns):
     out = jax.ShapeDtypeStruct((SLAB, LANES, columns), jnp.float32)
     vmem = pl.BlockSpec(memory_space=pltpu.VMEM)
     return pl.pallas_call(
         turn_kernel,
         out_shape=[out] * 2,
-        in_specs=[vmem],
+        in_specs=[vmem] * 2,
         out_specs=[vmem] * 2,
         compiler_params=pltpu.CompilerParams(vmem_limit_bytes=8 * 1024 * 1024),
         cost_estimate=pl.CostEstimate(flops=1000000, bytes_accessed=1000000, transcendentals=0),
         name="turn",
-    )(moments)
+    )(other, mine)
 
 
 def swap(block, bits):
@@ -402,49 +412,61 @@
     weight = jnp.sum(parts[:3].astype(jnp.float32), axis=0, keepdims=True)
 
     taps = len(TAPS)
-    material = pl.pallas_call(
+    material, pick = pl.pallas_call(
         material_kernel,
-        out_shape=jax.ShapeDtypeStruct((3 * taps, 8, LANES), jnp.float32),
+        out_shape=[
+            jax.ShapeDtypeStruct((3 * taps, 8, LANES), jnp.float32),
+            jax.ShapeDtypeStruct((256, WIDE), jnp.bfloat16),
+        ],
         in_specs=[smem, smem, hbm, hbm],
-        out_specs=vmem,
+        out_specs=[vmem] * 2,
         scratch_shapes=[
             pltpu.VMEM((2, planes) + region_label.shape[:0:-1], jnp.int32),
             pltpu.VMEM((len(OFFSETS), 16, LANES), jnp.float32),
             pltpu.SemaphoreType.DMA((2,)),
         ],
-        compiler_params=pltpu.CompilerParams(vmem_limit_bytes=8 * mib),
+        compiler_params=pltpu.CompilerParams(vmem_limit_bytes=52 * mib),
         cost_estimate=pl.CostEstimate(flops=40000000, bytes_accessed=1200000, transcendentals=0),
         name="material",
     )(region_eps, gain_rate, region_label.swapaxes(1, 2), gain_label.swapaxes(1, 2))
 
-    moments, cross = pl.pallas_call(
+    result = [
+        jax.ShapeDtypeStruct((SLAB, columns, LANES), jnp.float32),
+        jax.ShapeDtypeStruct((64, LANES), jnp.float32),
+    ]
+    kept = [
+        jax.ShapeDtypeStruct((planes, len(OFFSETS), columns, LANES), jnp.float32),
+        jax.ShapeDtypeStruct((6 * taps, 8, LANES), jnp.float32),
+    ]
+    moment_other, cross_other, shifted, folded = pl.pallas_call(
         moment_kernel,
-        out_shape=[
-            jax.ShapeDtypeStruct((2, SLAB, columns, LANES), jnp.float32),
-            jax.ShapeDtypeStruct((64, 256), jnp.float32),
-        ],
+        out_shape=result + kept,
         in_specs=[smem] + [vmem] * 7,
-        out_specs=[vmem] * 2,
-        scratch_shapes=[
-            pltpu.VMEM((planes, len(OFFSETS), columns, LANES), jnp.float32),
-            pltpu.VMEM((4 * taps, 8, LANES), jnp.float32),
-            pltpu.VMEM((6 * taps, 8, LANES), jnp.float32),
-        ],
-        compiler_params=pltpu.CompilerParams(vmem_limit_bytes=24 * mib),
+        out_specs=[vmem] * 4,
+        scratch_shapes=[pltpu.VMEM((4 * taps, 8, LANES), jnp.float32)],
+        compiler_params=pltpu.CompilerParams(vmem_limit_bytes=16 * mib),
         cost_estimate=pl.CostEstimate(flops=600000000, bytes_accessed=3000000, transcendentals=0),
         name="moments",
-    )(weight, material, own, ylo, yhi, xlo, xhi, jnp.asarray(selector()))
-
-    width = cross.shape[1] // 2
-    block = jnp.where(core == 0, cross[:, :width], cross[:, width:])
-    block = block + swap(jnp.where(core == 0, cross[:, width:], cross[:, :width]), dict(sx=1))
+    )(weight, material, own, ylo, yhi, xlo, xhi, pick)
+    received = swap(cross_other, dict(sx=1))
+    moment_mine, cross_mine = pl.pallas_call(
+        second_kernel,
+        out_shape=result,
+        in_specs=[vmem] * 2,
+        out_specs=[vmem] * 2,
+        compiler_params=pltpu.CompilerParams(vmem_limit_bytes=16 * mib),
+        cost_estimate=pl.CostEstimate(flops=100000000, bytes_accessed=1000000, transcendentals=0),
+        name="second",
+    )(shifted, folded)
+
+    block = cross_mine + received
     block = sum_of_four(block, dict(sy=1), dict(sy=3), dict(sy=2))
     block = sum_of_four(block, dict(quad=1), dict(quad=3), dict(quad=2))
     for step in (dict(quad=4), dict(quad=8)):
         block = block + swap(block, step)
-    block, moments = lax.optimization_barrier((block, moments))
+    block, moment_other = lax.optimization_barrier((block, moment_other))
     block = block + swap(block, dict(quad=8, sx=2))
-    first, second = turn(moments, columns)
+    first, second = turn(moment_other, moment_mine, columns)
     block, first, second = lax.optimization_barrier((block, first, second))
     other = swap(block, dict(sx=1))
     halves = (jnp.where(core == 0, block, other), jnp.where(core == 0, other, block))

time: 66.8 us -> 66.3 us (level)
  waiting for transfers between devices: 17.7 us -> 15.1 us
  Pallas kernels: 8.74 us -> 10.5 us
  local copies, waits for them, and re-layouts: 0.2 us -> 1.49 us
  starting transfers between devices: 37.6 us -> 36.7 us
    ppermute x17, waiting for transfers between devices: 17.7 us -> 15.1 us  [swap(): return lax.ppermute(block, axes, pairs)]
    pallas_call x3 -> x4, Pallas kernels: 7.21 us -> 9.06 us  [the longest x1 4.34 us: body(): pl.pallas_call(moment_kernel, out_shape=result + kept, in_specs=[smem] +...]
    unnamed x12 -> x6, local copies, waits for them, and re-layouts: 0.03 us -> 1.32 us
    ppermute x17, starting transfers between devices: 37.6 us -> 36.7 us  [swap(): return lax.ppermute(block, axes, pairs)]
  transfers between devices with their start and end apart: 17 -> 17, of which waited for: 14 -> 11; matrix products, arithmetic and copies ran while one was open for 0% -> 0% of each run, Pallas kernels for 4% -> 7%
where the time goes in v7:
time: 66.3 us; the launch traced here: 66.1 us
  starting transfers between devices  36.7 us (55%)
  waiting for transfers between devices  15.1 us (23%)
  Pallas kernels  10.5 us (16%)
  local copies, waits for them, and re-layouts  1.49 us (2%)
  between operations  1.47 us (2%)
  other arithmetic  0.82 us (1%)
    ppermute x17, starting transfers between devices, swap(): return lax.ppermute(block, axes, pairs)  36.7 us
    ppermute x17, waiting for transfers between devices, swap(): return lax.ppermute(block, axes, pairs)  15.1 us
    pallas_call x1, Pallas kernels, body(): pl.pallas_call(moment_kernel, out_shape=result + kept, in_specs=[smem] +...  4.34 us
    pallas_call x1, Pallas kernels, body(): pl.pallas_call(material_kernel, out_shape=[jax.ShapeDtypeStruct((3 * taps...  2.04 us
    pallas_call x1, Pallas kernels, body(): pl.pallas_call(second_kernel, out_shape=result, in_specs=[vmem] * 2, out_...  1.7 us
    pallas_call x1, Pallas kernels, body(): pl.pallas_call(slab_kernel, out_shape=[jax.ShapeDtypeStruct(shape, probes...  1.45 us
  transfers between devices with their start and end apart: 17, of which 11 were waited for; matrix products, arithmetic and copies ran while one was open for 0% of the time, Pallas kernels for 7%

profile of v7, /device:TPU:1, one launch (start us, length us, event | category | flops | bytes accessed | tf_op | source)
XLA Modules:
  0.0 66.1 jit_solution(16010569543135989864)
XLA Ops:
  1.3 1.5 %slab.1 = (bf16[8,128,128]{2,1,0:T(8,128)(2,1)S(1)}, bf16[192,128]{1,0:T(8,128)(2,1)S(1)}, bf16[192,128]{1,0:T(8,128)(2,1)S(1)}, bf16[96,128]{1,0:T(8,128)(2,1)S(1)}, bf16[96,128]{1,0:T(8,128)(2,1)S(1)}) custom-call(s32[1]{0:T(128)S(6)} %copy.13.quad_ref, bf16[64,128,128]{2,1,0:T(8,128)(2,1)} %bitcast.29), custom_call_target="tpu_custom_call" | custom-call | flops 10000000 | bytes 600000 | tf_op jit(solution)/shard_map/slab/pallas_call | solution.py:374
  2.7 5.8 %collective-permute-start.1 = (bf16[192,128]{1,0:T(8,128)(2,1)S(1)}, bf16[192,128]{1,0:T(8,128)(2,1)S(1)}, u32[]{:S(2)}, u32[]{:S(2)}) collective-permute-start(bf16[192,128]{1,0:T(8,128)(2,1)S(1)} %get-tuple-element.24), channel_id=1, source_target_pairs={{0,51},{1,50},{2,49},{3,48},{16,35},{17,34},{18,33},{19,32},{32,19... | collective-permute-start | bytes 147464 | tf_op jit(solution)/shard_map/ppermute | solution.py:349
  8.6 0.0 collective-permute-start
  8.6 1.0 %collective-permute-start.2 = (bf16[16,128]{1,0:T(8,128)(2,1)S(1)}, bf16[16,128]{1,0:T(8,128)(2,1)S(1)}, u32[]{:S(2)}, u32[]{:S(2)}) collective-permute-start(bf16[16,128]{1,0:T(8,128)(2,1)S(1)} %slice.54), channel_id=1, source_target_pairs={{0,32},{16,48},{32,0},{48,16},{64,96},{80,112},{96,64},{112,80},{1... | collective-permute-start | bytes 12296 | tf_op jit(solution)/shard_map/ppermute | solution.py:349
  9.5 0.0 copy-start
  9.5 0.7 copy-done
  10.2 0.0 copy-start.1
  10.2 0.7 copy-done.1
  10.9 2.0 %material.1 = (f32[75,8,128]{2,1,0:T(8,128)S(1)}, bf16[256,1664]{1,0:T(8,128)(2,1)S(1)}) custom-call(f32[8]{0:T(128)S(1)} %copy-done, f32[8]{0:T(128)S(1)} %copy-done.1, s32[64,32,64]{2,1,0:T(8,128)} %bitcast.30, s32[64,32,64]{2,1,0:T(8,128)} %bitcast.31), custom_call_target="tpu_custom_call" | custom-call | flops 40000000 | bytes 1200000 | tf_op jit(solution)/shard_map/material/pallas_call | solution.py:415
  12.9 0.0 collective-permute-done.1
  12.9 0.0 collective-permute-done
  13.0 0.0 collective-permute-done.2
  13.0 4.4 %collective-permute-start.5 = (bf16[16,128]{1,0:T(8,128)(2,1)S(1)}, bf16[16,128]{1,0:T(8,128)(2,1)S(1)}, u32[]{:S(2)}, u32[]{:S(2)}) collective-permute-start(bf16[16,128]{1,0:T(8,128)(2,1)S(1)} %fusion), channel_id=1, source_target_pairs={{0,192},{16,208},{32,224},{48,240},{64,128},{80,144},{96,160},{112... | collective-permute-start | bytes 12296 | tf_op jit(solution)/shard_map/ppermute | solution.py:349
  17.5 0.8 %collective-permute-start.3 = (bf16[176,128]{1,0:T(8,128)(2,1)S(1)}, bf16[176,128]{1,0:T(8,128)(2,1)S(1)}, u32[]{:S(2)}, u32[]{:S(2)}) collective-permute-start(bf16[176,128]{1,0:T(8,128)(2,1)S(1)} %get-tuple-element.57), channel_id=1, source_target_pairs={{0,68},{4,64},{8,76},{12,72},{16,84},{20,80},{24,92},{28,88},{32,1... | collective-permute-start | bytes 135176 | tf_op jit(solution)/shard_map/ppermute | solution.py:349
  18.2 3.6 %collective-permute-start.4 = (bf16[176,128]{1,0:T(8,128)(2,1)S(1)}, bf16[176,128]{1,0:T(8,128)(2,1)S(1)}, u32[]{:S(2)}, u32[]{:S(2)}) collective-permute-start(bf16[176,128]{1,0:T(8,128)(2,1)S(1)} %get-tuple-element.58), channel_id=1, source_target_pairs={{0,140},{4,136},{8,132},{12,128},{16,156},{20,152},{24,148},{28,14... | collective-permute-start | bytes 135176 | tf_op jit(solution)/shard_map/ppermute | solution.py:349
  21.9 0.0 collective-permute-done.3
  21.9 2.2 %collective-permute-done.4 = bf16[176,128]{1,0:T(8,128)(2,1)S(1)} collective-permute-done((bf16[176,128]{1,0:T(8,128)(2,1)S(1)}, bf16[176,128]{1,0:T(8,128)(2,1)S(1)}, u32[]{:S(2)}, u32[]{:S(2)}) %collective-permute-start.4) | collective-permute-done | bytes 45088 | tf_op jit(solution)/shard_map/ppermute | solution.py:349
  24.1 0.0 collective-permute-done.5
  24.1 4.3 %moments.1 = (f32[4,128,128]{2,1,0:T(8,128)S(1)}, f32[64,128]{1,0:T(8,128)S(1)}, f32[8,13,128,128]{3,2,1,0:T(8,128)S(1)}, f32[150,8,128]{2,1,0:T(8,128)S(1)}) custom-call(f32[1,128]{1,0:T(1,128)S(1)} %bitcast.28, f32[75,8,128]{2,1,0:T(8,128)S(1)} %get-tuple-element.27.material_ref, bf16[8,128,128]{2,1,0:T(8,128)(2,1)S(1)} %get-tuple-element.28.own_ref, ...), custom_call_target="tpu_custom_call" | custom-call | flops 600000000 | bytes 3000000 | tf_op jit(solution)/shard_map/moments/pallas_call | solution.py:441
  28.5 2.2 %collective-permute-start.6 = (f32[64,128]{1,0:T(8,128)S(1)}, f32[64,128]{1,0:T(8,128)S(1)}, u32[]{:S(2)}, u32[]{:S(2)}) collective-permute-start(f32[64,128]{1,0:T(8,128)S(1)} %get-tuple-element.33), channel_id=1, source_target_pairs={{0,4},{4,0},{8,12},{12,8},{1,5},{5,1},{9,13},{13,9},{2,6},{6,2},{1... | collective-permute-start | bytes 98312 | tf_op jit(solution)/shard_map/ppermute | solution.py:349
  30.7 1.7 %second.1 = (f32[4,128,128]{2,1,0:T(8,128)S(1)}, f32[64,128]{1,0:T(8,128)S(1)}) custom-call(f32[8,13,128,128]{3,2,1,0:T(8,128)S(1)} %get-tuple-element.30.shifted, f32[150,8,128]{2,1,0:T(8,128)S(1)} %get-tuple-element.31.folded), custom_call_target="tpu_custom_call" | custom-call | flops 100000000 | bytes 1000000 | tf_op jit(solution)/shard_map/second/pallas_call | solution.py:452
  32.4 0.0 collective-permute-done.6
  32.4 1.4 %collective-permute-start.9 = (f32[64,128]{1,0:T(8,128)S(1)}, f32[64,128]{1,0:T(8,128)S(1)}, u32[]{:S(2)}, u32[]{:S(2)}) collective-permute-start(f32[64,128]{1,0:T(8,128)S(1)} %add.58), channel_id=1, source_target_pairs={{0,2},{1,3},{2,0},{3,1},{4,6},{5,7},{6,4},{7,5},{8,10},{9,11},{10,... | collective-permute-start | bytes 98312 | tf_op jit(solution)/shard_map/ppermute | solution.py:349
  33.8 2.6 %collective-permute-start.8 = (f32[64,128]{1,0:T(8,128)S(1)}, f32[64,128]{1,0:T(8,128)S(1)}, u32[]{:S(2)}, u32[]{:S(2)}) collective-permute-start(f32[64,128]{1,0:T(8,128)S(1)} %add.58), channel_id=1, source_target_pairs={{0,3},{1,2},{2,1},{3,0},{4,7},{5,6},{6,5},{7,4},{8,11},{9,10},{10,... | collective-permute-start | bytes 98312 | tf_op jit(solution)/shard_map/ppermute | solution.py:349
  36.4 0.0 collective-permute-start.7
  36.4 0.3 collective-permute-done.9
  36.8 1.0 %collective-permute-done.8 = f32[64,128]{1,0:T(8,128)S(1)} collective-permute-done((f32[64,128]{1,0:T(8,128)S(1)}, f32[64,128]{1,0:T(8,128)S(1)}, u32[]{:S(2)}, u32[]{:S(2)}) %collective-permute-start.8) | collective-permute-done | bytes 32800 | tf_op jit(solution)/shard_map/ppermute | solution.py:349
  37.8 1.4 %collective-permute-done.7 = f32[64,128]{1,0:T(8,128)S(1)} collective-permute-done((f32[64,128]{1,0:T(8,128)S(1)}, f32[64,128]{1,0:T(8,128)S(1)}, u32[]{:S(2)}, u32[]{:S(2)}) %collective-permute-start.7) | collective-permute-done | bytes 32800 | tf_op jit(solution)/shard_map/ppermute | solution.py:349
  39.2 1.6 %collective-permute-start.12 = (f32[64,128]{1,0:T(8,128)S(1)}, f32[64,128]{1,0:T(8,128)S(1)}, u32[]{:S(2)}, u32[]{:S(2)}) collective-permute-start(f32[64,128]{1,0:T(8,128)S(1)} %add_add_fusion.1), channel_id=1, source_target_pairs={{0,32},{16,48},{32,0},{48,16},{64,96},{80,112},{96,64},{112,80},{1... | collective-permute-start | bytes 98312 | tf_op jit(solution)/shard_map/ppermute | solution.py:349
  40.8 2.2 %collective-permute-start.11 = (f32[64,128]{1,0:T(8,128)S(1)}, f32[64,128]{1,0:T(8,128)S(1)}, u32[]{:S(2)}, u32[]{:S(2)}) collective-permute-start(f32[64,128]{1,0:T(8,128)S(1)} %add_add_fusion.1), channel_id=1, source_target_pairs={{0,48},{16,32},{32,16},{48,0},{64,112},{80,96},{96,80},{112,64},{1... | collective-permute-start | bytes 98312 | tf_op jit(solution)/shard_map/ppermute | solution.py:349
  43.1 0.0 collective-permute-start.10
  43.1 0.5 collective-permute-done.12
  43.6 1.2 %collective-permute-done.11 = f32[64,128]{1,0:T(8,128)S(1)} collective-permute-done((f32[64,128]{1,0:T(8,128)S(1)}, f32[64,128]{1,0:T(8,128)S(1)}, u32[]{:S(2)}, u32[]{:S(2)}) %collective-permute-start.11) | collective-permute-done | bytes 32800 | tf_op jit(solution)/shard_map/ppermute | solution.py:349
  44.8 1.3 %collective-permute-done.10 = f32[64,128]{1,0:T(8,128)S(1)} collective-permute-done((f32[64,128]{1,0:T(8,128)S(1)}, f32[64,128]{1,0:T(8,128)S(1)}, u32[]{:S(2)}, u32[]{:S(2)}) %collective-permute-start.10) | collective-permute-done | bytes 32800 | tf_op jit(solution)/shard_map/ppermute | solution.py:349
  46.1 0.8 %collective-permute-start.13 = (f32[64,128]{1,0:T(8,128)S(1)}, f32[64,128]{1,0:T(8,128)S(1)}, u32[]{:S(2)}, u32[]{:S(2)}) collective-permute-start(f32[64,128]{1,0:T(8,128)S(1)} %add_add_fusion), channel_id=1, source_target_pairs={{0,64},{16,80},{32,96},{48,112},{64,0},{80,16},{96,32},{112,48},{1... | collective-permute-start | bytes 98312 | tf_op jit(solution)/shard_map/ppermute | solution.py:349
  46.9 2.1 %collective-permute-done.13 = f32[64,128]{1,0:T(8,128)S(1)} collective-permute-done((f32[64,128]{1,0:T(8,128)S(1)}, f32[64,128]{1,0:T(8,128)S(1)}, u32[]{:S(2)}, u32[]{:S(2)}) %collective-permute-start.13) | collective-permute-done | bytes 32800 | tf_op jit(solution)/shard_map/ppermute | solution.py:349
  49.0 0.4 collective-permute-start.14
  49.3 3.4 %collective-permute-done.14 = f32[64,128]{1,0:T(8,128)S(1)} collective-permute-done((f32[64,128]{1,0:T(8,128)S(1)}, f32[64,128]{1,0:T(8,128)S(1)}, u32[]{:S(2)}, u32[]{:S(2)}) %collective-permute-start.14) | collective-permute-done | bytes 32800 | tf_op jit(solution)/shard_map/ppermute | solution.py:349
  52.8 3.1 %collective-permute-start.15 = (f32[64,128]{1,0:T(8,128)S(1)}, f32[64,128]{1,0:T(8,128)S(1)}, u32[]{:S(2)}, u32[]{:S(2)}) collective-permute-start(f32[64,128]{1,0:T(8,128)S(1)} %add.66), channel_id=1, source_target_pairs={{0,136},{4,140},{8,128},{12,132},{16,152},{20,156},{24,144},{28,14... | collective-permute-start | bytes 98312 | tf_op jit(solution)/shard_map/ppermute | solution.py:349
  55.9 1.0 %turn.1 = (f32[4,128,128]{2,1,0:T(8,128)}, f32[4,128,128]{2,1,0:T(8,128)}) custom-call(f32[4,128,128]{2,1,0:T(8,128)S(1)} %get-tuple-element.36.other_ref, f32[4,128,128]{2,1,0:T(8,128)S(1)} %get-tuple-element.37.mine_ref), custom_call_target="tpu_custom_call" | custom-call | flops 1000000 | bytes 1000000 | tf_op jit(solution)/shard_map/turn/pallas_call | solution.py:331
  56.9 0.8 %collective-permute-done.15 = f32[64,128]{1,0:T(8,128)S(1)} collective-permute-done((f32[64,128]{1,0:T(8,128)S(1)}, f32[64,128]{1,0:T(8,128)S(1)}, u32[]{:S(2)}, u32[]{:S(2)}) %collective-permute-start.15) | collective-permute-done | bytes 32800 | tf_op jit(solution)/shard_map/ppermute | solution.py:349
  57.6 6.8 %collective-permute-start.16 = (f32[64,128]{1,0:T(8,128)S(1)}, f32[64,128]{1,0:T(8,128)S(1)}, u32[]{:S(2)}, u32[]{:S(2)}) collective-permute-start(f32[64,128]{1,0:T(8,128)S(1)} %add.67), channel_id=1, source_target_pairs={{0,4},{4,0},{8,12},{12,8},{1,5},{5,1},{9,13},{13,9},{2,6},{6,2},{1... | collective-permute-start | bytes 98312 | tf_op jit(solution)/shard_map/ppermute | solution.py:349
  64.4 0.9 %collective-permute-done.16 = f32[64,128]{1,0:T(8,128)S(1)} collective-permute-done((f32[64,128]{1,0:T(8,128)S(1)}, f32[64,128]{1,0:T(8,128)S(1)}, u32[]{:S(2)}, u32[]{:S(2)}) %collective-permute-start.16) | collective-permute-done | bytes 32800 | tf_op jit(solution)/shard_map/ppermute | solution.py:349
  65.3 0.1 slice_bitcast_fusion.3
  65.3 0.1 slice_bitcast_fusion.1
  65.5 0.7 %pad_maximum_fusion = f32[2,2,64,64]{3,2,1,0:T(8,128)} fusion(f32[1,2,64,64]{3,2,1,0:T(8,128)S(1)} %maximum_bitcast_fusion.1, f32[1,2,64,64]{3,2,1,0:T(8,128)S(1)} %maximum_bitcast_fusion), kind=kLoop, calls=%fused_computation | loop fusion | flops 16384 | bytes 131072 | tf_op jit(solution)/shard_map/stack | solution.py:473
  (23 shorter events, 0.2 us)
Async XLA Ops:
  2.7 10.2 %collective-permute-start.1 = (bf16[192,128]{1,0:T(8,128)(2,1)S(1)}, bf16[192,128]{1,0:T(8,128)(2,1)S(1)}, u32[]{:S(2)}, u32[]{:S(2)}) collective-permute-start(bf16[192,128]{1,0:T(8,128)(2,1)S(1)} %get-tuple-element.24), channel_id=1, source_target_pairs={{0,51},{1,50},{2,49},{3,48},{16,35},{17,34},{18,33},{19,32},{32,19... | collective-permute-start | bytes 147464 | tf_op jit(solution)/shard_map/ppermute | solution.py:349
  8.6 4.3 %collective-permute-start = (bf16[192,128]{1,0:T(8,128)(2,1)S(1)}, bf16[192,128]{1,0:T(8,128)(2,1)S(1)}, u32[]{:S(2)}, u32[]{:S(2)}) collective-permute-start(bf16[192,128]{1,0:T(8,128)(2,1)S(1)} %get-tuple-element.23), channel_id=1, source_target_pairs={{0,17},{1,16},{2,19},{3,18},{16,1},{17,0},{18,3},{19,2},{32,49},{3... | collective-permute-start | bytes 147464 | tf_op jit(solution)/shard_map/ppermute | solution.py:349
  8.6 4.4 %collective-permute-start.2 = (bf16[16,128]{1,0:T(8,128)(2,1)S(1)}, bf16[16,128]{1,0:T(8,128)(2,1)S(1)}, u32[]{:S(2)}, u32[]{:S(2)}) collective-permute-start(bf16[16,128]{1,0:T(8,128)(2,1)S(1)} %slice.54), channel_id=1, source_target_pairs={{0,32},{16,48},{32,0},{48,16},{64,96},{80,112},{96,64},{112,80},{1... | collective-permute-start | bytes 12296 | tf_op jit(solution)/shard_map/ppermute | solution.py:349
  9.5 0.7 copy-start
  10.2 0.7 copy-start.1
  13.0 11.1 %collective-permute-start.5 = (bf16[16,128]{1,0:T(8,128)(2,1)S(1)}, bf16[16,128]{1,0:T(8,128)(2,1)S(1)}, u32[]{:S(2)}, u32[]{:S(2)}) collective-permute-start(bf16[16,128]{1,0:T(8,128)(2,1)S(1)} %fusion), channel_id=1, source_target_pairs={{0,192},{16,208},{32,224},{48,240},{64,128},{80,144},{96,160},{112... | collective-permute-start | bytes 12296 | tf_op jit(solution)/shard_map/ppermute | solution.py:349
  17.5 4.4 %collective-permute-start.3 = (bf16[176,128]{1,0:T(8,128)(2,1)S(1)}, bf16[176,128]{1,0:T(8,128)(2,1)S(1)}, u32[]{:S(2)}, u32[]{:S(2)}) collective-permute-start(bf16[176,128]{1,0:T(8,128)(2,1)S(1)} %get-tuple-element.57), channel_id=1, source_target_pairs={{0,68},{4,64},{8,76},{12,72},{16,84},{20,80},{24,92},{28,88},{32,1... | collective-permute-start | bytes 135176 | tf_op jit(solution)/shard_map/ppermute | solution.py:349
  18.2 5.8 %collective-permute-start.4 = (bf16[176,128]{1,0:T(8,128)(2,1)S(1)}, bf16[176,128]{1,0:T(8,128)(2,1)S(1)}, u32[]{:S(2)}, u32[]{:S(2)}) collective-permute-start(bf16[176,128]{1,0:T(8,128)(2,1)S(1)} %get-tuple-element.58), channel_id=1, source_target_pairs={{0,140},{4,136},{8,132},{12,128},{16,156},{20,152},{24,148},{28,14... | collective-permute-start | bytes 135176 | tf_op jit(solution)/shard_map/ppermute | solution.py:349
  28.5 3.9 %collective-permute-start.6 = (f32[64,128]{1,0:T(8,128)S(1)}, f32[64,128]{1,0:T(8,128)S(1)}, u32[]{:S(2)}, u32[]{:S(2)}) collective-permute-start(f32[64,128]{1,0:T(8,128)S(1)} %get-tuple-element.33), channel_id=1, source_target_pairs={{0,4},{4,0},{8,12},{12,8},{1,5},{5,1},{9,13},{13,9},{2,6},{6,2},{1... | collective-permute-start | bytes 98312 | tf_op jit(solution)/shard_map/ppermute | solution.py:349
  32.4 4.4 %collective-permute-start.9 = (f32[64,128]{1,0:T(8,128)S(1)}, f32[64,128]{1,0:T(8,128)S(1)}, u32[]{:S(2)}, u32[]{:S(2)}) collective-permute-start(f32[64,128]{1,0:T(8,128)S(1)} %add.58), channel_id=1, source_target_pairs={{0,2},{1,3},{2,0},{3,1},{4,6},{5,7},{6,4},{7,5},{8,10},{9,11},{10,... | collective-permute-start | bytes 98312 | tf_op jit(solution)/shard_map/ppermute | solution.py:349
  33.8 4.0 %collective-permute-start.8 = (f32[64,128]{1,0:T(8,128)S(1)}, f32[64,128]{1,0:T(8,128)S(1)}, u32[]{:S(2)}, u32[]{:S(2)}) collective-permute-start(f32[64,128]{1,0:T(8,128)S(1)} %add.58), channel_id=1, source_target_pairs={{0,3},{1,2},{2,1},{3,0},{4,7},{5,6},{6,5},{7,4},{8,11},{9,10},{10,... | collective-permute-start | bytes 98312 | tf_op jit(solution)/shard_map/ppermute | solution.py:349
  36.4 2.8 %collective-permute-start.7 = (f32[64,128]{1,0:T(8,128)S(1)}, f32[64,128]{1,0:T(8,128)S(1)}, u32[]{:S(2)}, u32[]{:S(2)}) collective-permute-start(f32[64,128]{1,0:T(8,128)S(1)} %add.58), channel_id=1, source_target_pairs={{0,1},{1,0},{2,3},{3,2},{4,5},{5,4},{6,7},{7,6},{8,9},{9,8},{10,11... | collective-permute-start | bytes 98312 | tf_op jit(solution)/shard_map/ppermute | solution.py:349
  39.2 4.4 %collective-permute-start.12 = (f32[64,128]{1,0:T(8,128)S(1)}, f32[64,128]{1,0:T(8,128)S(1)}, u32[]{:S(2)}, u32[]{:S(2)}) collective-permute-start(f32[64,128]{1,0:T(8,128)S(1)} %add_add_fusion.1), channel_id=1, source_target_pairs={{0,32},{16,48},{32,0},{48,16},{64,96},{80,112},{96,64},{112,80},{1... | collective-permute-start | bytes 98312 | tf_op jit(solution)/shard_map/ppermute | solution.py:349
  40.8 4.0 %collective-permute-start.11 = (f32[64,128]{1,0:T(8,128)S(1)}, f32[64,128]{1,0:T(8,128)S(1)}, u32[]{:S(2)}, u32[]{:S(2)}) collective-permute-start(f32[64,128]{1,0:T(8,128)S(1)} %add_add_fusion.1), channel_id=1, source_target_pairs={{0,48},{16,32},{32,16},{48,0},{64,112},{80,96},{96,80},{112,64},{1... | collective-permute-start | bytes 98312 | tf_op jit(solution)/shard_map/ppermute | solution.py:349
  43.1 3.0 %collective-permute-start.10 = (f32[64,128]{1,0:T(8,128)S(1)}, f32[64,128]{1,0:T(8,128)S(1)}, u32[]{:S(2)}, u32[]{:S(2)}) collective-permute-start(f32[64,128]{1,0:T(8,128)S(1)} %add_add_fusion.1), channel_id=1, source_target_pairs={{0,16},{16,0},{32,48},{48,32},{64,80},{80,64},{96,112},{112,96},{1... | collective-permute-start | bytes 98312 | tf_op jit(solution)/shard_map/ppermute | solution.py:349
  46.1 2.9 %collective-permute-start.13 = (f32[64,128]{1,0:T(8,128)S(1)}, f32[64,128]{1,0:T(8,128)S(1)}, u32[]{:S(2)}, u32[]{:S(2)}) collective-permute-start(f32[64,128]{1,0:T(8,128)S(1)} %add_add_fusion), channel_id=1, source_target_pairs={{0,64},{16,80},{32,96},{48,112},{64,0},{80,16},{96,32},{112,48},{1... | collective-permute-start | bytes 98312 | tf_op jit(solution)/shard_map/ppermute | solution.py:349
  49.0 3.8 %collective-permute-start.14 = (f32[64,128]{1,0:T(8,128)S(1)}, f32[64,128]{1,0:T(8,128)S(1)}, u32[]{:S(2)}, u32[]{:S(2)}) collective-permute-start(f32[64,128]{1,0:T(8,128)S(1)} %add.65), channel_id=1, source_target_pairs={{0,128},{16,144},{32,160},{48,176},{64,192},{80,208},{96,224},{112... | collective-permute-start | bytes 98312 | tf_op jit(solution)/shard_map/ppermute | solution.py:349
  52.8 4.9 %collective-permute-start.15 = (f32[64,128]{1,0:T(8,128)S(1)}, f32[64,128]{1,0:T(8,128)S(1)}, u32[]{:S(2)}, u32[]{:S(2)}) collective-permute-start(f32[64,128]{1,0:T(8,128)S(1)} %add.66), channel_id=1, source_target_pairs={{0,136},{4,140},{8,128},{12,132},{16,152},{20,156},{24,144},{28,14... | collective-permute-start | bytes 98312 | tf_op jit(solution)/shard_map/ppermute | solution.py:349
  57.6 7.6 %collective-permute-start.16 = (f32[64,128]{1,0:T(8,128)S(1)}, f32[64,128]{1,0:T(8,128)S(1)}, u32[]{:S(2)}, u32[]{:S(2)}) collective-permute-start(f32[64,128]{1,0:T(8,128)S(1)} %add.67), channel_id=1, source_target_pairs={{0,4},{4,0},{8,12},{12,8},{1,5},{5,1},{9,13},{13,9},{2,6},{6,2},{1... | collective-permute-start | bytes 98312 | tf_op jit(solution)/shard_map/ppermute | solution.py:349

commit v8 on v6

--- a/solution.py
+++ b/solution.py
@@ -29,24 +29,27 @@
 PARTS = CORNERS + 16
 
 
-def source_cells():
-    cells = [(x, y) for x in range(CX) for y in range(CY)]
-    for y in (-1, -2, CY, CY + 1):
-        cells += [(x, y) for x in range(CX)]
-    for xs, near in (((-2, -1), -1), ((CX, CX + 1), CX)):
-        cells += [(x, y) for x in xs for y in range(CY)]
-        cells += [(near, -1), (near, CY)] + [None] * 14
-    return cells
-
-
-def selector():
-    row_of = {cell: row for row, cell in enumerate(source_cells()) if cell is not None}
-    pick = np.zeros((256, WIDE), np.float32)
-    for o, (dx, dy) in enumerate(OFFSETS):
-        for x in range(CX):
-            for y in range(CY):
-                pick[row_of[(x + dx, y + dy)], o * LANES + x * CY + y] = 1.0
-    return pick.astype(jnp.bfloat16)
+def cell_code(x, y):
+    return (x + 2) * 32 + y + 2
+
+
+def write_selector(pick_ref):
+    row = lax.broadcasted_iota(jnp.int32, (16, LANES), 0)
+    lane = lax.broadcasted_iota(jnp.int32, (16, LANES), 1)
+    own = cell_code(lax.shift_right_logical(lane, 3), lane & 7)
+
+    def pair_of_x(x):
+        return cell_code(x + lax.shift_right_logical(row, 3), row & 7)
+
+    tiles = [pair_of_x(2 * i) for i in range(CX // 2)]
+    tiles += [cell_code(row, y) for y in (-1, -2, CY, CY + 1)]
+    for first, near in ((-2, -1), (CX, CX)):
+        corners = jnp.where(row == 1, cell_code(near, CY), -1)
+        tiles += [pair_of_x(first), jnp.where(row == 0, cell_code(near, -1), corners)]
+    for i, tile in enumerate(tiles):
+        for off, (dx, dy) in enumerate(OFFSETS):
+            hit = jnp.where(tile == own + (dx * 32 + dy), 1.0, 0.0).astype(jnp.bfloat16)
+            pick_ref[i * 16 : i * 16 + 16, off * LANES : (off + 1) * LANES] = hit
 
 
 def slab_kernel(
@@ -125,7 +128,7 @@
         own_ref[p] = plane(me, p)
 
 
-def material_kernel(eps_ref, gain_ref, region_ref, level_ref, out_ref, labels, codes, sems):
+def material_kernel(eps_ref, gain_ref, region_ref, level_ref, out_ref, pick_ref, labels, codes, sems):
     planes = SLAB + 4
     start = lax.axis_index("quad") * SLAB
     first = jnp.clip(start - 2, 0, region_ref.shape[0] - planes)
@@ -136,6 +139,7 @@
     ]
     for copy in copies:
         copy.start()
+    write_selector(pick_ref)
     depth_y, depth_x = labels.shape[2:]
     lane = lax.broadcasted_iota(jnp.int32, (depth_x, LANES), 1)
     x_row = lax.broadcasted_iota(jnp.int32, (depth_x, LANES), 0) - lax.axis_index("sx") * CX
@@ -402,17 +406,20 @@
     weight = jnp.sum(parts[:3].astype(jnp.float32), axis=0, keepdims=True)
 
     taps = len(TAPS)
-    material = pl.pallas_call(
+    material, pick = pl.pallas_call(
         material_kernel,
-        out_shape=jax.ShapeDtypeStruct((3 * taps, 8, LANES), jnp.float32),
+        out_shape=[
+            jax.ShapeDtypeStruct((3 * taps, 8, LANES), jnp.float32),
+            jax.ShapeDtypeStruct((256, WIDE), jnp.bfloat16),
+        ],
         in_specs=[smem, smem, hbm, hbm],
-        out_specs=vmem,
+        out_specs=[vmem] * 2,
         scratch_shapes=[
             pltpu.VMEM((2, planes) + region_label.shape[:0:-1], jnp.int32),
             pltpu.VMEM((len(OFFSETS), 16, LANES), jnp.float32),
             pltpu.SemaphoreType.DMA((2,)),
         ],
-        compiler_params=pltpu.CompilerParams(vmem_limit_bytes=8 * mib),
+        compiler_params=pltpu.CompilerParams(vmem_limit_bytes=52 * mib),
         cost_estimate=pl.CostEstimate(flops=40000000, bytes_accessed=1200000, transcendentals=0),
         name="material",
     )(region_eps, gain_rate, region_label.swapaxes(1, 2), gain_label.swapaxes(1, 2))
@@ -433,17 +440,16 @@
         compiler_params=pltpu.CompilerParams(vmem_limit_bytes=24 * mib),
         cost_estimate=pl.CostEstimate(flops=600000000, bytes_accessed=3000000, transcendentals=0),
         name="moments",
-    )(weight, material, own, ylo, yhi, xlo, xhi, jnp.asarray(selector()))
+    )(weight, material, own, ylo, yhi, xlo, xhi, pick)
 
     width = cross.shape[1] // 2
     block = jnp.where(core == 0, cross[:, :width], cross[:, width:])
     block = block + swap(jnp.where(core == 0, cross[:, width:], cross[:, :width]), dict(sx=1))
     block = sum_of_four(block, dict(sy=1), dict(sy=3), dict(sy=2))
     block = sum_of_four(block, dict(quad=1), dict(quad=3), dict(quad=2))
-    for step in (dict(quad=4), dict(quad=8)):
-        block = block + swap(block, step)
+    block = sum_of_four(block, dict(quad=4), dict(quad=8, sx=2), dict(quad=12, sx=2))
     block, moments = lax.optimization_barrier((block, moments))
-    block = block + swap(block, dict(quad=8, sx=2))
+    block = block + swap(block, dict(quad=8))
     first, second = turn(moments, columns)
     block, first, second = lax.optimization_barrier((block, first, second))
     other = swap(block, dict(sx=1))

time: 66.8 us -> 65 us (0.973)
  waiting for transfers between devices: 17.7 us -> 13.9 us
  starting transfers between devices: 37.6 us -> 39.3 us
    ppermute x17 -> x18, waiting for transfers between devices: 17.7 us -> 13.9 us  [swap(): return lax.ppermute(block, axes, pairs)]
    ppermute x17 -> x18, starting transfers between devices: 37.6 us -> 39.3 us  [swap(): return lax.ppermute(block, axes, pairs)]
  transfers between devices with their start and end apart: 17 -> 18, of which waited for: 14 -> 14; matrix products, arithmetic and copies ran while one was open for 0% -> 0% of each run, Pallas kernels for 4% -> 5%
where the time goes in v8:
time: 65 us; the launch traced here: 64.9 us
  starting transfers between devices  39.3 us (60%)
  waiting for transfers between devices  13.9 us (21%)
  Pallas kernels  9.29 us (14%)
  between operations  1.45 us (2%)
  other arithmetic  0.82 us (1%)
    ppermute x18, starting transfers between devices, swap(): return lax.ppermute(block, axes, pairs)  39.3 us
    ppermute x18, waiting for transfers between devices, swap(): return lax.ppermute(block, axes, pairs)  13.9 us
    pallas_call x1, Pallas kernels, body(): pl.pallas_call(moment_kernel, out_shape=[jax.ShapeDtypeStruct((2, SLAB, c...  4.87 us
    pallas_call x1, Pallas kernels, body(): pl.pallas_call(material_kernel, out_shape=[jax.ShapeDtypeStruct((3 * taps...  2.04 us
    pallas_call x1, Pallas kernels, body(): pl.pallas_call(slab_kernel, out_shape=[jax.ShapeDtypeStruct(shape, probes...  1.45 us
  transfers between devices with their start and end apart: 18, of which 14 were waited for; matrix products, arithmetic and copies ran while one was open for 0% of the time, Pallas kernels for 5%

profile of v8, /device:TPU:1, one launch (start us, length us, event | category | flops | bytes accessed | tf_op | source)
XLA Modules:
  0.0 64.9 jit_solution(4690905130482312)
XLA Ops:
  0.6 0.0 copy-start.1
  0.6 0.0 copy-start
  1.3 1.5 %slab.1 = (bf16[8,128,128]{2,1,0:T(8,128)(2,1)S(1)}, bf16[192,128]{1,0:T(8,128)(2,1)S(1)}, bf16[192,128]{1,0:T(8,128)(2,1)S(1)}, bf16[96,128]{1,0:T(8,128)(2,1)S(1)}, bf16[96,128]{1,0:T(8,128)(2,1)S(1)}) custom-call(s32[1]{0:T(128)S(6)} %copy.13.quad_ref, bf16[64,128,128]{2,1,0:T(8,128)(2,1)} %bitcast.29), custom_call_target="tpu_custom_call" | custom-call | flops 10000000 | bytes 600000 | tf_op jit(solution)/shard_map/slab/pallas_call | solution.py:368
  2.8 5.8 %collective-permute-start.1 = (bf16[192,128]{1,0:T(8,128)(2,1)S(1)}, bf16[192,128]{1,0:T(8,128)(2,1)S(1)}, u32[]{:S(2)}, u32[]{:S(2)}) collective-permute-start(bf16[192,128]{1,0:T(8,128)(2,1)S(1)} %get-tuple-element.20), channel_id=1, source_target_pairs={{0,51},{1,50},{2,49},{3,48},{16,35},{17,34},{18,33},{19,32},{32,19... | collective-permute-start | bytes 147464 | tf_op jit(solution)/shard_map/ppermute | solution.py:343
  8.6 0.0 collective-permute-start
  8.6 1.0 %collective-permute-start.2 = (bf16[16,128]{1,0:T(8,128)(2,1)S(1)}, bf16[16,128]{1,0:T(8,128)(2,1)S(1)}, u32[]{:S(2)}, u32[]{:S(2)}) collective-permute-start(bf16[16,128]{1,0:T(8,128)(2,1)S(1)} %slice.62), channel_id=1, source_target_pairs={{0,32},{16,48},{32,0},{48,16},{64,96},{80,112},{96,64},{112,80},{1... | collective-permute-start | bytes 12296 | tf_op jit(solution)/shard_map/ppermute | solution.py:343
  9.6 0.0 copy-done.1
  9.6 0.0 copy-done
  9.6 2.0 %material.1 = (f32[75,8,128]{2,1,0:T(8,128)S(1)}, bf16[256,1664]{1,0:T(8,128)(2,1)S(1)}) custom-call(f32[8]{0:T(128)S(1)} %copy-done, f32[8]{0:T(128)S(1)} %copy-done.1, s32[64,32,64]{2,1,0:T(8,128)} %bitcast.30, s32[64,32,64]{2,1,0:T(8,128)} %bitcast.31), custom_call_target="tpu_custom_call" | custom-call | flops 40000000 | bytes 1200000 | tf_op jit(solution)/shard_map/material/pallas_call | solution.py:409
  11.6 0.0 collective-permute-done.1
  11.6 1.1 %collective-permute-done = bf16[192,128]{1,0:T(8,128)(2,1)S(1)} collective-permute-done((bf16[192,128]{1,0:T(8,128)(2,1)S(1)}, bf16[192,128]{1,0:T(8,128)(2,1)S(1)}, u32[]{:S(2)}, u32[]{:S(2)}) %collective-permute-start) | collective-permute-done | bytes 49184 | tf_op jit(solution)/shard_map/ppermute | solution.py:343
  12.8 0.1 collective-permute-done.2
  12.9 4.1 %collective-permute-start.5 = (bf16[16,128]{1,0:T(8,128)(2,1)S(1)}, bf16[16,128]{1,0:T(8,128)(2,1)S(1)}, u32[]{:S(2)}, u32[]{:S(2)}) collective-permute-start(bf16[16,128]{1,0:T(8,128)(2,1)S(1)} %fusion), channel_id=1, source_target_pairs={{0,192},{16,208},{32,224},{48,240},{64,128},{80,144},{96,160},{112... | collective-permute-start | bytes 12296 | tf_op jit(solution)/shard_map/ppermute | solution.py:343
  17.0 1.3 %collective-permute-start.3 = (bf16[176,128]{1,0:T(8,128)(2,1)S(1)}, bf16[176,128]{1,0:T(8,128)(2,1)S(1)}, u32[]{:S(2)}, u32[]{:S(2)}) collective-permute-start(bf16[176,128]{1,0:T(8,128)(2,1)S(1)} %get-tuple-element.49), channel_id=1, source_target_pairs={{0,68},{4,64},{8,76},{12,72},{16,84},{20,80},{24,92},{28,88},{32,1... | collective-permute-start | bytes 135176 | tf_op jit(solution)/shard_map/ppermute | solution.py:343
  18.3 3.6 %collective-permute-start.4 = (bf16[176,128]{1,0:T(8,128)(2,1)S(1)}, bf16[176,128]{1,0:T(8,128)(2,1)S(1)}, u32[]{:S(2)}, u32[]{:S(2)}) collective-permute-start(bf16[176,128]{1,0:T(8,128)(2,1)S(1)} %get-tuple-element.50), channel_id=1, source_target_pairs={{0,140},{4,136},{8,132},{12,128},{16,156},{20,152},{24,148},{28,14... | collective-permute-start | bytes 135176 | tf_op jit(solution)/shard_map/ppermute | solution.py:343
  21.9 0.0 collective-permute-done.3
  21.9 2.1 %collective-permute-done.4 = bf16[176,128]{1,0:T(8,128)(2,1)S(1)} collective-permute-done((bf16[176,128]{1,0:T(8,128)(2,1)S(1)}, bf16[176,128]{1,0:T(8,128)(2,1)S(1)}, u32[]{:S(2)}, u32[]{:S(2)}) %collective-permute-start.4) | collective-permute-done | bytes 45088 | tf_op jit(solution)/shard_map/ppermute | solution.py:343
  24.0 0.0 collective-permute-done.5
  24.0 4.9 %moments.1 = (f32[2,4,128,128]{3,2,1,0:T(8,128)S(1)}, f32[64,256]{1,0:T(8,128)S(1)}) custom-call(f32[1,128]{1,0:T(1,128)S(1)} %bitcast.28, f32[75,8,128]{2,1,0:T(8,128)S(1)} %get-tuple-element.23.material_ref, bf16[8,128,128]{2,1,0:T(8,128)(2,1)S(1)} %get-tuple-element.24.own_ref, bf16[160,128]{1,0:T(8,128)(2,1)S(1)} %get-tuple-element.36.ylo_ref, ...), custom_call_target="tpu_custom_call" | custom-call | flops 600000000 | bytes 3000000 | tf_op jit(solution)/shard_map/moments/pallas_call | solution.py:427
  28.9 2.2 %collective-permute-start.6 = (f32[64,128]{1,0:T(8,128)S(1)}, f32[64,128]{1,0:T(8,128)S(1)}, u32[]{:S(2)}, u32[]{:S(2)}) collective-permute-start(f32[64,128]{1,0:T(8,128)S(1)} %slice_select_fusion), channel_id=1, source_target_pairs={{0,4},{4,0},{8,12},{12,8},{1,5},{5,1},{9,13},{13,9},{2,6},{6,2},{1... | collective-permute-start | bytes 98312 | tf_op jit(solution)/shard_map/ppermute | solution.py:343
  31.2 0.9 %collective-permute-done.6 = f32[64,128]{1,0:T(8,128)S(1)} collective-permute-done((f32[64,128]{1,0:T(8,128)S(1)}, f32[64,128]{1,0:T(8,128)S(1)}, u32[]{:S(2)}, u32[]{:S(2)}) %collective-permute-start.6) | collective-permute-done | bytes 32800 | tf_op jit(solution)/shard_map/ppermute | solution.py:343
  32.0 1.0 %collective-permute-start.9 = (f32[64,128]{1,0:T(8,128)S(1)}, f32[64,128]{1,0:T(8,128)S(1)}, u32[]{:S(2)}, u32[]{:S(2)}) collective-permute-start(f32[64,128]{1,0:T(8,128)S(1)} %select_add_fusion), channel_id=1, source_target_pairs={{0,2},{1,3},{2,0},{3,1},{4,6},{5,7},{6,4},{7,5},{8,10},{9,11},{10,... | collective-permute-start | bytes 98312 | tf_op jit(solution)/shard_map/ppermute | solution.py:343
  33.1 2.7 %collective-permute-start.8 = (f32[64,128]{1,0:T(8,128)S(1)}, f32[64,128]{1,0:T(8,128)S(1)}, u32[]{:S(2)}, u32[]{:S(2)}) collective-permute-start(f32[64,128]{1,0:T(8,128)S(1)} %select_add_fusion), channel_id=1, source_target_pairs={{0,3},{1,2},{2,1},{3,0},{4,7},{5,6},{6,5},{7,4},{8,11},{9,10},{10,... | collective-permute-start | bytes 98312 | tf_op jit(solution)/shard_map/ppermute | solution.py:343
  35.8 0.0 collective-permute-start.7
  35.8 0.5 collective-permute-done.9
  36.3 1.2 %collective-permute-done.8 = f32[64,128]{1,0:T(8,128)S(1)} collective-permute-done((f32[64,128]{1,0:T(8,128)S(1)}, f32[64,128]{1,0:T(8,128)S(1)}, u32[]{:S(2)}, u32[]{:S(2)}) %collective-permute-start.8) | collective-permute-done | bytes 32800 | tf_op jit(solution)/shard_map/ppermute | solution.py:343
  37.5 1.1 %collective-permute-done.7 = f32[64,128]{1,0:T(8,128)S(1)} collective-permute-done((f32[64,128]{1,0:T(8,128)S(1)}, f32[64,128]{1,0:T(8,128)S(1)}, u32[]{:S(2)}, u32[]{:S(2)}) %collective-permute-start.7) | collective-permute-done | bytes 32800 | tf_op jit(solution)/shard_map/ppermute | solution.py:343
  38.6 1.5 %collective-permute-start.12 = (f32[64,128]{1,0:T(8,128)S(1)}, f32[64,128]{1,0:T(8,128)S(1)}, u32[]{:S(2)}, u32[]{:S(2)}) collective-permute-start(f32[64,128]{1,0:T(8,128)S(1)} %add_add_fusion.2), channel_id=1, source_target_pairs={{0,32},{16,48},{32,0},{48,16},{64,96},{80,112},{96,64},{112,80},{1... | collective-permute-start | bytes 98312 | tf_op jit(solution)/shard_map/ppermute | solution.py:343
  40.1 2.5 %collective-permute-start.11 = (f32[64,128]{1,0:T(8,128)S(1)}, f32[64,128]{1,0:T(8,128)S(1)}, u32[]{:S(2)}, u32[]{:S(2)}) collective-permute-start(f32[64,128]{1,0:T(8,128)S(1)} %add_add_fusion.2), channel_id=1, source_target_pairs={{0,48},{16,32},{32,16},{48,0},{64,112},{80,96},{96,80},{112,64},{1... | collective-permute-start | bytes 98312 | tf_op jit(solution)/shard_map/ppermute | solution.py:343
  42.6 0.0 collective-permute-start.10
  42.6 0.3 collective-permute-done.12
  43.0 1.1 %collective-permute-done.11 = f32[64,128]{1,0:T(8,128)S(1)} collective-permute-done((f32[64,128]{1,0:T(8,128)S(1)}, f32[64,128]{1,0:T(8,128)S(1)}, u32[]{:S(2)}, u32[]{:S(2)}) %collective-permute-start.11) | collective-permute-done | bytes 32800 | tf_op jit(solution)/shard_map/ppermute | solution.py:343
  44.1 1.6 %collective-permute-done.10 = f32[64,128]{1,0:T(8,128)S(1)} collective-permute-done((f32[64,128]{1,0:T(8,128)S(1)}, f32[64,128]{1,0:T(8,128)S(1)}, u32[]{:S(2)}, u32[]{:S(2)}) %collective-permute-start.10) | collective-permute-done | bytes 32800 | tf_op jit(solution)/shard_map/ppermute | solution.py:343
  45.7 2.2 %collective-permute-start.15 = (f32[64,128]{1,0:T(8,128)S(1)}, f32[64,128]{1,0:T(8,128)S(1)}, u32[]{:S(2)}, u32[]{:S(2)}) collective-permute-start(f32[64,128]{1,0:T(8,128)S(1)} %add_add_fusion.1), channel_id=1, source_target_pairs={{0,200},{4,204},{8,192},{12,196},{16,216},{20,220},{24,208},{28,21... | collective-permute-start | bytes 98312 | tf_op jit(solution)/shard_map/ppermute | solution.py:343
  47.9 2.4 %collective-permute-start.14 = (f32[64,128]{1,0:T(8,128)S(1)}, f32[64,128]{1,0:T(8,128)S(1)}, u32[]{:S(2)}, u32[]{:S(2)}) collective-permute-start(f32[64,128]{1,0:T(8,128)S(1)} %add_add_fusion.1), channel_id=1, source_target_pairs={{0,136},{4,140},{8,128},{12,132},{16,152},{20,156},{24,144},{28,14... | collective-permute-start | bytes 98312 | tf_op jit(solution)/shard_map/ppermute | solution.py:343
  50.2 0.2 collective-permute-start.13
  50.4 0.0 collective-permute-done.15
  50.4 2.3 %collective-permute-done.14 = f32[64,128]{1,0:T(8,128)S(1)} collective-permute-done((f32[64,128]{1,0:T(8,128)S(1)}, f32[64,128]{1,0:T(8,128)S(1)}, u32[]{:S(2)}, u32[]{:S(2)}) %collective-permute-start.14) | collective-permute-done | bytes 32800 | tf_op jit(solution)/shard_map/ppermute | solution.py:343
  52.7 0.3 collective-permute-done.13
  53.0 3.1 %collective-permute-start.16 = (f32[64,128]{1,0:T(8,128)S(1)}, f32[64,128]{1,0:T(8,128)S(1)}, u32[]{:S(2)}, u32[]{:S(2)}) collective-permute-start(f32[64,128]{1,0:T(8,128)S(1)} %add_add_fusion), channel_id=1, source_target_pairs={{0,128},{16,144},{32,160},{48,176},{64,192},{80,208},{96,224},{112... | collective-permute-start | bytes 98312 | tf_op jit(solution)/shard_map/ppermute | solution.py:343
  56.1 0.9 %turn.1 = (f32[4,128,128]{2,1,0:T(8,128)}, f32[4,128,128]{2,1,0:T(8,128)}) custom-call(f32[2,4,128,128]{3,2,1,0:T(8,128)S(1)} %get-tuple-element.29.moments_ref), custom_call_target="tpu_custom_call" | custom-call | flops 1000000 | bytes 1000000 | tf_op jit(solution)/shard_map/turn/pallas_call | solution.py:325
  57.0 0.5 collective-permute-done.16
  57.5 5.7 %collective-permute-start.17 = (f32[64,128]{1,0:T(8,128)S(1)}, f32[64,128]{1,0:T(8,128)S(1)}, u32[]{:S(2)}, u32[]{:S(2)}) collective-permute-start(f32[64,128]{1,0:T(8,128)S(1)} %add.71), channel_id=1, source_target_pairs={{0,4},{4,0},{8,12},{12,8},{1,5},{5,1},{9,13},{13,9},{2,6},{6,2},{1... | collective-permute-start | bytes 98312 | tf_op jit(solution)/shard_map/ppermute | solution.py:343
  63.2 0.9 %collective-permute-done.17 = f32[64,128]{1,0:T(8,128)S(1)} collective-permute-done((f32[64,128]{1,0:T(8,128)S(1)}, f32[64,128]{1,0:T(8,128)S(1)}, u32[]{:S(2)}, u32[]{:S(2)}) %collective-permute-start.17) | collective-permute-done | bytes 32800 | tf_op jit(solution)/shard_map/ppermute | solution.py:343
  64.0 0.1 slice_bitcast_fusion.3
  64.1 0.1 slice_bitcast_fusion.1
  64.2 0.7 %pad_maximum_fusion = f32[2,2,64,64]{3,2,1,0:T(8,128)} fusion(f32[1,2,64,64]{3,2,1,0:T(8,128)S(1)} %maximum_bitcast_fusion.1, f32[1,2,64,64]{3,2,1,0:T(8,128)S(1)} %maximum_bitcast_fusion), kind=kLoop, calls=%fused_computation | loop fusion | flops 16384 | bytes 131072 | tf_op jit(solution)/shard_map/stack | solution.py:457
  (23 shorter events, 0.2 us)
Async XLA Ops:
  0.6 9.0 %copy-start.1 = (f32[8]{0:T(128)S(1)}, f32[8]{0:T(128)}, u32[]{:S(2)}) copy-start(f32[8]{0:T(128)} %gain_ref.1) | copy-start | bytes 100
  0.6 8.9 %copy-start = (f32[8]{0:T(128)S(1)}, f32[8]{0:T(128)}, u32[]{:S(2)}) copy-start(f32[8]{0:T(128)} %eps_ref.1) | copy-start | bytes 100
  2.8 8.9 %collective-permute-start.1 = (bf16[192,128]{1,0:T(8,128)(2,1)S(1)}, bf16[192,128]{1,0:T(8,128)(2,1)S(1)}, u32[]{:S(2)}, u32[]{:S(2)}) collective-permute-start(bf16[192,128]{1,0:T(8,128)(2,1)S(1)} %get-tuple-element.20), channel_id=1, source_target_pairs={{0,51},{1,50},{2,49},{3,48},{16,35},{17,34},{18,33},{19,32},{32,19... | collective-permute-start | bytes 147464 | tf_op jit(solution)/shard_map/ppermute | solution.py:343
  8.6 4.1 %collective-permute-start = (bf16[192,128]{1,0:T(8,128)(2,1)S(1)}, bf16[192,128]{1,0:T(8,128)(2,1)S(1)}, u32[]{:S(2)}, u32[]{:S(2)}) collective-permute-start(bf16[192,128]{1,0:T(8,128)(2,1)S(1)} %get-tuple-element.19), channel_id=1, source_target_pairs={{0,17},{1,16},{2,19},{3,18},{16,1},{17,0},{18,3},{19,2},{32,49},{3... | collective-permute-start | bytes 147464 | tf_op jit(solution)/shard_map/ppermute | solution.py:343
  8.6 4.3 %collective-permute-start.2 = (bf16[16,128]{1,0:T(8,128)(2,1)S(1)}, bf16[16,128]{1,0:T(8,128)(2,1)S(1)}, u32[]{:S(2)}, u32[]{:S(2)}) collective-permute-start(bf16[16,128]{1,0:T(8,128)(2,1)S(1)} %slice.62), channel_id=1, source_target_pairs={{0,32},{16,48},{32,0},{48,16},{64,96},{80,112},{96,64},{112,80},{1... | collective-permute-start | bytes 12296 | tf_op jit(solution)/shard_map/ppermute | solution.py:343
  12.9 11.1 %collective-permute-start.5 = (bf16[16,128]{1,0:T(8,128)(2,1)S(1)}, bf16[16,128]{1,0:T(8,128)(2,1)S(1)}, u32[]{:S(2)}, u32[]{:S(2)}) collective-permute-start(bf16[16,128]{1,0:T(8,128)(2,1)S(1)} %fusion), channel_id=1, source_target_pairs={{0,192},{16,208},{32,224},{48,240},{64,128},{80,144},{96,160},{112... | collective-permute-start | bytes 12296 | tf_op jit(solution)/shard_map/ppermute | solution.py:343
  17.0 4.9 %collective-permute-start.3 = (bf16[176,128]{1,0:T(8,128)(2,1)S(1)}, bf16[176,128]{1,0:T(8,128)(2,1)S(1)}, u32[]{:S(2)}, u32[]{:S(2)}) collective-permute-start(bf16[176,128]{1,0:T(8,128)(2,1)S(1)} %get-tuple-element.49), channel_id=1, source_target_pairs={{0,68},{4,64},{8,76},{12,72},{16,84},{20,80},{24,92},{28,88},{32,1... | collective-permute-start | bytes 135176 | tf_op jit(solution)/shard_map/ppermute | solution.py:343
  18.3 5.7 %collective-permute-start.4 = (bf16[176,128]{1,0:T(8,128)(2,1)S(1)}, bf16[176,128]{1,0:T(8,128)(2,1)S(1)}, u32[]{:S(2)}, u32[]{:S(2)}) collective-permute-start(bf16[176,128]{1,0:T(8,128)(2,1)S(1)} %get-tuple-element.50), channel_id=1, source_target_pairs={{0,140},{4,136},{8,132},{12,128},{16,156},{20,152},{24,148},{28,14... | collective-permute-start | bytes 135176 | tf_op jit(solution)/shard_map/ppermute | solution.py:343
  28.9 3.1 %collective-permute-start.6 = (f32[64,128]{1,0:T(8,128)S(1)}, f32[64,128]{1,0:T(8,128)S(1)}, u32[]{:S(2)}, u32[]{:S(2)}) collective-permute-start(f32[64,128]{1,0:T(8,128)S(1)} %slice_select_fusion), channel_id=1, source_target_pairs={{0,4},{4,0},{8,12},{12,8},{1,5},{5,1},{9,13},{13,9},{2,6},{6,2},{1... | collective-permute-start | bytes 98312 | tf_op jit(solution)/shard_map/ppermute | solution.py:343
  32.0 4.3 %collective-permute-start.9 = (f32[64,128]{1,0:T(8,128)S(1)}, f32[64,128]{1,0:T(8,128)S(1)}, u32[]{:S(2)}, u32[]{:S(2)}) collective-permute-start(f32[64,128]{1,0:T(8,128)S(1)} %select_add_fusion), channel_id=1, source_target_pairs={{0,2},{1,3},{2,0},{3,1},{4,6},{5,7},{6,4},{7,5},{8,10},{9,11},{10,... | collective-permute-start | bytes 98312 | tf_op jit(solution)/shard_map/ppermute | solution.py:343
  33.1 4.4 %collective-permute-start.8 = (f32[64,128]{1,0:T(8,128)S(1)}, f32[64,128]{1,0:T(8,128)S(1)}, u32[]{:S(2)}, u32[]{:S(2)}) collective-permute-start(f32[64,128]{1,0:T(8,128)S(1)} %select_add_fusion), channel_id=1, source_target_pairs={{0,3},{1,2},{2,1},{3,0},{4,7},{5,6},{6,5},{7,4},{8,11},{9,10},{10,... | collective-permute-start | bytes 98312 | tf_op jit(solution)/shard_map/ppermute | solution.py:343
  35.8 2.8 %collective-permute-start.7 = (f32[64,128]{1,0:T(8,128)S(1)}, f32[64,128]{1,0:T(8,128)S(1)}, u32[]{:S(2)}, u32[]{:S(2)}) collective-permute-start(f32[64,128]{1,0:T(8,128)S(1)} %select_add_fusion), channel_id=1, source_target_pairs={{0,1},{1,0},{2,3},{3,2},{4,5},{5,4},{6,7},{7,6},{8,9},{9,8},{10,11... | collective-permute-start | bytes 98312 | tf_op jit(solution)/shard_map/ppermute | solution.py:343
  38.6 4.4 %collective-permute-start.12 = (f32[64,128]{1,0:T(8,128)S(1)}, f32[64,128]{1,0:T(8,128)S(1)}, u32[]{:S(2)}, u32[]{:S(2)}) collective-permute-start(f32[64,128]{1,0:T(8,128)S(1)} %add_add_fusion.2), channel_id=1, source_target_pairs={{0,32},{16,48},{32,0},{48,16},{64,96},{80,112},{96,64},{112,80},{1... | collective-permute-start | bytes 98312 | tf_op jit(solution)/shard_map/ppermute | solution.py:343
  40.1 4.0 %collective-permute-start.11 = (f32[64,128]{1,0:T(8,128)S(1)}, f32[64,128]{1,0:T(8,128)S(1)}, u32[]{:S(2)}, u32[]{:S(2)}) collective-permute-start(f32[64,128]{1,0:T(8,128)S(1)} %add_add_fusion.2), channel_id=1, source_target_pairs={{0,48},{16,32},{32,16},{48,0},{64,112},{80,96},{96,80},{112,64},{1... | collective-permute-start | bytes 98312 | tf_op jit(solution)/shard_map/ppermute | solution.py:343
  42.6 3.1 %collective-permute-start.10 = (f32[64,128]{1,0:T(8,128)S(1)}, f32[64,128]{1,0:T(8,128)S(1)}, u32[]{:S(2)}, u32[]{:S(2)}) collective-permute-start(f32[64,128]{1,0:T(8,128)S(1)} %add_add_fusion.2), channel_id=1, source_target_pairs={{0,16},{16,0},{32,48},{48,32},{64,80},{80,64},{96,112},{112,96},{1... | collective-permute-start | bytes 98312 | tf_op jit(solution)/shard_map/ppermute | solution.py:343
  45.7 4.8 %collective-permute-start.15 = (f32[64,128]{1,0:T(8,128)S(1)}, f32[64,128]{1,0:T(8,128)S(1)}, u32[]{:S(2)}, u32[]{:S(2)}) collective-permute-start(f32[64,128]{1,0:T(8,128)S(1)} %add_add_fusion.1), channel_id=1, source_target_pairs={{0,200},{4,204},{8,192},{12,196},{16,216},{20,220},{24,208},{28,21... | collective-permute-start | bytes 98312 | tf_op jit(solution)/shard_map/ppermute | solution.py:343
  47.9 4.9 %collective-permute-start.14 = (f32[64,128]{1,0:T(8,128)S(1)}, f32[64,128]{1,0:T(8,128)S(1)}, u32[]{:S(2)}, u32[]{:S(2)}) collective-permute-start(f32[64,128]{1,0:T(8,128)S(1)} %add_add_fusion.1), channel_id=1, source_target_pairs={{0,136},{4,140},{8,128},{12,132},{16,152},{20,156},{24,144},{28,14... | collective-permute-start | bytes 98312 | tf_op jit(solution)/shard_map/ppermute | solution.py:343
  50.2 2.8 %collective-permute-start.13 = (f32[64,128]{1,0:T(8,128)S(1)}, f32[64,128]{1,0:T(8,128)S(1)}, u32[]{:S(2)}, u32[]{:S(2)}) collective-permute-start(f32[64,128]{1,0:T(8,128)S(1)} %add_add_fusion.1), channel_id=1, source_target_pairs={{0,64},{16,80},{32,96},{48,112},{64,0},{80,16},{96,32},{112,48},{1... | collective-permute-start | bytes 98312 | tf_op jit(solution)/shard_map/ppermute | solution.py:343
  53.0 4.5 %collective-permute-start.16 = (f32[64,128]{1,0:T(8,128)S(1)}, f32[64,128]{1,0:T(8,128)S(1)}, u32[]{:S(2)}, u32[]{:S(2)}) collective-permute-start(f32[64,128]{1,0:T(8,128)S(1)} %add_add_fusion), channel_id=1, source_target_pairs={{0,128},{16,144},{32,160},{48,176},{64,192},{80,208},{96,224},{112... | collective-permute-start | bytes 98312 | tf_op jit(solution)/shard_map/ppermute | solution.py:343
  57.5 6.5 %collective-permute-start.17 = (f32[64,128]{1,0:T(8,128)S(1)}, f32[64,128]{1,0:T(8,128)S(1)}, u32[]{:S(2)}, u32[]{:S(2)}) collective-permute-start(f32[64,128]{1,0:T(8,128)S(1)} %add.71), channel_id=1, source_target_pairs={{0,4},{4,0},{8,12},{12,8},{1,5},{5,1},{9,13},{13,9},{2,6},{6,2},{1... | collective-permute-start | bytes 98312 | tf_op jit(solution)/shard_map/ppermute | solution.py:343

commit v9 on v8

--- a/solution.py
+++ b/solution.py
@@ -126,6 +126,25 @@
             out_ref[(p - 1) * 16 : p * 16] = x_edge(plane(me ^ bit, p, bit), high).astype(jnp.bfloat16)
     for p in range(SLAB + 4):
         own_ref[p] = plane(me, p)
+
+
+def pack_kernel(inner_ref, outer_ref, last_ref, first_ref, third_ref, fourth_ref, near_ref, beyond_ref):
+    even_y = (lax.axis_index("sy") & 1) == 0
+    inner = inner_ref[CORNERS:].astype(jnp.float32)
+    outer = outer_ref[CORNERS:].astype(jnp.float32)
+    low, high = jnp.where(even_y, outer, inner), jnp.where(even_y, inner, outer)
+    parts = (first_ref[PARTS:].astype(jnp.float32) + inner[16:]) + (
+        outer[16:] + last_ref[...].astype(jnp.float32)
+    )
+    row = lax.broadcasted_iota(jnp.int32, (16, LANES), 0)
+    for i, (layers_ref, out_ref) in enumerate(((third_ref, near_ref), (fourth_ref, beyond_ref))):
+        out_ref[:FAR] = layers_ref[...]
+        for p in range(SLAB):
+            at = i * SLAB + p
+            corner = jnp.where(row == 1, high[at : at + 1], 0.0)
+            corner = jnp.where(row == 0, low[at : at + 1], corner)
+            out_ref[FAR + p * 16 : FAR + (p + 1) * 16] = corner.astype(jnp.bfloat16)
+        out_ref[CORNERS:] = parts.astype(jnp.bfloat16)
 
 
 def material_kernel(eps_ref, gain_ref, region_ref, level_ref, out_ref, pick_ref, labels, codes, sems):
@@ -382,23 +401,23 @@
         name="slab",
     )(quad_index, probes.reshape(depth, cells_x * cells_y, columns))
 
-    def corner_rows(at):
-        cells = [inner[at : at + SLAB], outer[at : at + SLAB]]
-        low, high = jnp.where(even_y, cells[1], cells[0]), jnp.where(even_y, cells[0], cells[1])
-        rows = jnp.pad(jnp.stack([low, high], axis=1), ((0, 0), (0, 14), (0, 0)))
-        return rows.reshape(SLAB * 16, columns)
-
-    parts = first[PARTS:]
     inner = swap(first, dict(quad=1, sy=1))
     outer = swap(second, dict(quad=3, sy=3))
-    last = swap(parts, dict(quad=2))
-    parts = (parts + inner[PARTS:]) + (outer[PARTS:] + last)
+    last = swap(first[PARTS:], dict(quad=2))
     ylo = jnp.where(even_y, outer, inner)[:CORNERS]
     yhi = jnp.where(even_y, inner, outer)[:CORNERS]
-    third = jnp.concatenate([third, corner_rows(CORNERS), parts], axis=0)
-    fourth = jnp.concatenate([fourth, corner_rows(CORNERS + SLAB), parts], axis=0)
-    near = swap(third, dict(quad=4, sx=1))
-    beyond = swap(fourth, dict(quad=8, sx=3))
+    to_near, to_beyond = pl.pallas_call(
+        pack_kernel,
+        out_shape=[jax.ShapeDtypeStruct((CORNERS + 16, columns), probes.dtype)] * 2,
+        in_specs=[vmem] * 6,
+        out_specs=[vmem] * 2,
+        compiler_params=pltpu.CompilerParams(vmem_limit_bytes=4 * mib),
+        cost_estimate=pl.CostEstimate(flops=100000, bytes_accessed=200000, transcendentals=0),
+        name="pack",
+    )(inner, outer, last, first, third, fourth)
+    beyond = swap(to_beyond, dict(quad=8, sx=3))
+    near = swap(to_near, dict(quad=4, sx=1))
+    parts = to_near[CORNERS:]
     last = swap(parts, dict(quad=12))
     parts = (parts + near[CORNERS:]) + (beyond[CORNERS:] + last)
     xlo = jnp.where(even_x, beyond, near)[:CORNERS]

time: 65 us -> 65.4 us (level)
  waiting for transfers between devices: 13.9 us -> 17.1 us
  starting transfers between devices: 39.3 us -> 36.5 us
    ppermute x18, waiting for transfers between devices: 13.9 us -> 17.1 us  [swap(): return lax.ppermute(block, axes, pairs)]
    ppermute x18, starting transfers between devices: 39.3 us -> 36.5 us  [swap(): return lax.ppermute(block, axes, pairs)]
  transfers between devices with their start and end apart: 18 -> 18, of which waited for: 14 -> 13; matrix products, arithmetic and copies ran while one was open for 0% -> 0% of each run, Pallas kernels for 5% -> 5%
where the time goes in v9:
time: 65.4 us; the launch traced here: 65.2 us
  starting transfers between devices  36.5 us (56%)
  waiting for transfers between devices  17.1 us (26%)
  Pallas kernels  9.31 us (14%)
  between operations  1.43 us (2%)
  other arithmetic  0.79 us (1%)
    ppermute x18, starting transfers between devices, swap(): return lax.ppermute(block, axes, pairs)  36.5 us
    ppermute x18, waiting for transfers between devices, swap(): return lax.ppermute(block, axes, pairs)  17.1 us
    pallas_call x1, Pallas kernels, body(): pl.pallas_call(moment_kernel, out_shape=[jax.ShapeDtypeStruct((2, SLAB, c...  4.87 us
    pallas_call x1, Pallas kernels, body(): pl.pallas_call(material_kernel, out_shape=[jax.ShapeDtypeStruct((3 * taps...  2.04 us
    pallas_call x1, Pallas kernels, body(): pl.pallas_call(slab_kernel, out_shape=[jax.ShapeDtypeStruct(shape, probes...  1.45 us
  transfers between devices with their start and end apart: 18, of which 13 were waited for; matrix products, arithmetic and copies ran while one was open for 0% of the time, Pallas kernels for 5%

profile of v9, /device:TPU:1, one launch (start us, length us, event | category | flops | bytes accessed | tf_op | source)
XLA Modules:
  0.0 65.2 jit_solution(14764184435005153692)
XLA Ops:
  0.6 0.0 copy-start.1
  0.6 0.0 copy-start
  1.3 1.5 %slab.1 = (bf16[8,128,128]{2,1,0:T(8,128)(2,1)S(1)}, bf16[192,128]{1,0:T(8,128)(2,1)S(1)}, bf16[192,128]{1,0:T(8,128)(2,1)S(1)}, bf16[96,128]{1,0:T(8,128)(2,1)S(1)}, bf16[96,128]{1,0:T(8,128)(2,1)S(1)}) custom-call(s32[1]{0:T(128)S(6)} %copy.9.quad_ref, bf16[64,128,128]{2,1,0:T(8,128)(2,1)} %bitcast.19), custom_call_target="tpu_custom_call" | custom-call | flops 10000000 | bytes 600000 | tf_op jit(solution)/shard_map/slab/pallas_call | solution.py:387
  2.8 5.8 %collective-permute-start.1 = (bf16[192,128]{1,0:T(8,128)(2,1)S(1)}, bf16[192,128]{1,0:T(8,128)(2,1)S(1)}, u32[]{:S(2)}, u32[]{:S(2)}) collective-permute-start(bf16[192,128]{1,0:T(8,128)(2,1)S(1)} %get-tuple-element.22), channel_id=1, source_target_pairs={{0,51},{1,50},{2,49},{3,48},{16,35},{17,34},{18,33},{19,32},{32,19... | collective-permute-start | bytes 147464 | tf_op jit(solution)/shard_map/ppermute | solution.py:362
  8.6 0.0 collective-permute-start
  8.6 1.0 %collective-permute-start.2 = (bf16[16,128]{1,0:T(8,128)(2,1)S(1)}, bf16[16,128]{1,0:T(8,128)(2,1)S(1)}, u32[]{:S(2)}, u32[]{:S(2)}) collective-permute-start(bf16[16,128]{1,0:T(8,128)(2,1)S(1)} %slice.47), channel_id=1, source_target_pairs={{0,32},{16,48},{32,0},{48,16},{64,96},{80,112},{96,64},{112,80},{1... | collective-permute-start | bytes 12296 | tf_op jit(solution)/shard_map/ppermute | solution.py:362
  9.6 0.0 copy-done.1
  9.6 0.0 copy-done
  9.6 2.0 %material.1 = (f32[75,8,128]{2,1,0:T(8,128)S(1)}, bf16[256,1664]{1,0:T(8,128)(2,1)S(1)}) custom-call(f32[8]{0:T(128)S(1)} %copy-done, f32[8]{0:T(128)S(1)} %copy-done.1, s32[64,32,64]{2,1,0:T(8,128)} %bitcast.20, s32[64,32,64]{2,1,0:T(8,128)} %bitcast.21), custom_call_target="tpu_custom_call" | custom-call | flops 40000000 | bytes 1200000 | tf_op jit(solution)/shard_map/material/pallas_call | solution.py:428
  11.6 1.2 %collective-permute-done.2.last_ref = bf16[16,128]{1,0:T(8,128)(2,1)S(1)} collective-permute-done((bf16[16,128]{1,0:T(8,128)(2,1)S(1)}, bf16[16,128]{1,0:T(8,128)(2,1)S(1)}, u32[]{:S(2)}, u32[]{:S(2)}) %collective-permute-start.2) | collective-permute-done | bytes 4128 | tf_op jit(solution)/shard_map/ppermute | solution.py:362
  12.9 0.0 collective-permute-done.1.outer_ref
  12.9 0.0 collective-permute-done.inner_ref
  12.9 3.4 %collective-permute-start.3 = (bf16[176,128]{1,0:T(8,128)(2,1)S(1)}, bf16[176,128]{1,0:T(8,128)(2,1)S(1)}, u32[]{:S(2)}, u32[]{:S(2)}) collective-permute-start(bf16[176,128]{1,0:T(8,128)(2,1)S(1)} %get-tuple-element.25), channel_id=1, source_target_pairs={{0,68},{4,64},{8,76},{12,72},{16,84},{20,80},{24,92},{28,88},{32,1... | collective-permute-start | bytes 135176 | tf_op jit(solution)/shard_map/ppermute | solution.py:362
  16.3 2.5 %collective-permute-start.5 = (bf16[16,128]{1,0:T(8,128)(2,1)S(1)}, bf16[16,128]{1,0:T(8,128)(2,1)S(1)}, u32[]{:S(2)}, u32[]{:S(2)}) collective-permute-start(bf16[16,128]{1,0:T(8,128)(2,1)S(1)} %slice.48), channel_id=1, source_target_pairs={{0,192},{16,208},{32,224},{48,240},{64,128},{80,144},{96,160},{112... | collective-permute-start | bytes 12296 | tf_op jit(solution)/shard_map/ppermute | solution.py:362
  18.9 3.0 %collective-permute-start.4 = (bf16[176,128]{1,0:T(8,128)(2,1)S(1)}, bf16[176,128]{1,0:T(8,128)(2,1)S(1)}, u32[]{:S(2)}, u32[]{:S(2)}) collective-permute-start(bf16[176,128]{1,0:T(8,128)(2,1)S(1)} %get-tuple-element.26), channel_id=1, source_target_pairs={{0,140},{4,136},{8,132},{12,128},{16,156},{20,152},{24,148},{28,14... | collective-permute-start | bytes 135176 | tf_op jit(solution)/shard_map/ppermute | solution.py:362
  21.9 3.3 %collective-permute-done.4 = bf16[176,128]{1,0:T(8,128)(2,1)S(1)} collective-permute-done((bf16[176,128]{1,0:T(8,128)(2,1)S(1)}, bf16[176,128]{1,0:T(8,128)(2,1)S(1)}, u32[]{:S(2)}, u32[]{:S(2)}) %collective-permute-start.4) | collective-permute-done | bytes 45088 | tf_op jit(solution)/shard_map/ppermute | solution.py:362
  25.2 0.0 collective-permute-done.3
  25.2 0.0 collective-permute-done.5
  25.3 4.9 %moments.1 = (f32[2,4,128,128]{3,2,1,0:T(8,128)S(1)}, f32[64,256]{1,0:T(8,128)S(1)}) custom-call(f32[1,128]{1,0:T(1,128)S(1)} %bitcast.18, f32[75,8,128]{2,1,0:T(8,128)S(1)} %get-tuple-element.27.material_ref, bf16[8,128,128]{2,1,0:T(8,128)(2,1)S(1)} %get-tuple-element.28.own_ref, bf16[160,128]{1,0:T(8,128)(2,1)S(1)} %get-tuple-element.40.ylo_ref, ...), custom_call_target="tpu_custom_call" | custom-call | flops 600000000 | bytes 3000000 | tf_op jit(solution)/shard_map/moments/pallas_call | solution.py:446
  30.2 0.6 collective-permute-start.6
  30.7 0.9 %collective-permute-done.6 = f32[64,128]{1,0:T(8,128)S(1)} collective-permute-done((f32[64,128]{1,0:T(8,128)S(1)}, f32[64,128]{1,0:T(8,128)S(1)}, u32[]{:S(2)}, u32[]{:S(2)}) %collective-permute-start.6) | collective-permute-done | bytes 32800 | tf_op jit(solution)/shard_map/ppermute | solution.py:362
  31.6 1.1 %collective-permute-start.9 = (f32[64,128]{1,0:T(8,128)S(1)}, f32[64,128]{1,0:T(8,128)S(1)}, u32[]{:S(2)}, u32[]{:S(2)}) collective-permute-start(f32[64,128]{1,0:T(8,128)S(1)} %select_add_fusion), channel_id=1, source_target_pairs={{0,2},{1,3},{2,0},{3,1},{4,6},{5,7},{6,4},{7,5},{8,10},{9,11},{10,... | collective-permute-start | bytes 98312 | tf_op jit(solution)/shard_map/ppermute | solution.py:362
  32.7 2.7 %collective-permute-start.8 = (f32[64,128]{1,0:T(8,128)S(1)}, f32[64,128]{1,0:T(8,128)S(1)}, u32[]{:S(2)}, u32[]{:S(2)}) collective-permute-start(f32[64,128]{1,0:T(8,128)S(1)} %select_add_fusion), channel_id=1, source_target_pairs={{0,3},{1,2},{2,1},{3,0},{4,7},{5,6},{6,5},{7,4},{8,11},{9,10},{10,... | collective-permute-start | bytes 98312 | tf_op jit(solution)/shard_map/ppermute | solution.py:362
  35.4 0.0 collective-permute-start.7
  35.4 0.5 collective-permute-done.9
  35.9 1.2 %collective-permute-done.8 = f32[64,128]{1,0:T(8,128)S(1)} collective-permute-done((f32[64,128]{1,0:T(8,128)S(1)}, f32[64,128]{1,0:T(8,128)S(1)}, u32[]{:S(2)}, u32[]{:S(2)}) %collective-permute-start.8) | collective-permute-done | bytes 32800 | tf_op jit(solution)/shard_map/ppermute | solution.py:362
  37.1 1.1 %collective-permute-done.7 = f32[64,128]{1,0:T(8,128)S(1)} collective-permute-done((f32[64,128]{1,0:T(8,128)S(1)}, f32[64,128]{1,0:T(8,128)S(1)}, u32[]{:S(2)}, u32[]{:S(2)}) %collective-permute-start.7) | collective-permute-done | bytes 32800 | tf_op jit(solution)/shard_map/ppermute | solution.py:362
  38.2 1.5 %collective-permute-start.12 = (f32[64,128]{1,0:T(8,128)S(1)}, f32[64,128]{1,0:T(8,128)S(1)}, u32[]{:S(2)}, u32[]{:S(2)}) collective-permute-start(f32[64,128]{1,0:T(8,128)S(1)} %add_add_fusion.2), channel_id=1, source_target_pairs={{0,32},{16,48},{32,0},{48,16},{64,96},{80,112},{96,64},{112,80},{1... | collective-permute-start | bytes 98312 | tf_op jit(solution)/shard_map/ppermute | solution.py:362
  39.7 2.5 %collective-permute-start.11 = (f32[64,128]{1,0:T(8,128)S(1)}, f32[64,128]{1,0:T(8,128)S(1)}, u32[]{:S(2)}, u32[]{:S(2)}) collective-permute-start(f32[64,128]{1,0:T(8,128)S(1)} %add_add_fusion.2), channel_id=1, source_target_pairs={{0,48},{16,32},{32,16},{48,0},{64,112},{80,96},{96,80},{112,64},{1... | collective-permute-start | bytes 98312 | tf_op jit(solution)/shard_map/ppermute | solution.py:362
  42.2 0.0 collective-permute-start.10
  42.2 0.3 collective-permute-done.12
  42.5 1.1 %collective-permute-done.11 = f32[64,128]{1,0:T(8,128)S(1)} collective-permute-done((f32[64,128]{1,0:T(8,128)S(1)}, f32[64,128]{1,0:T(8,128)S(1)}, u32[]{:S(2)}, u32[]{:S(2)}) %collective-permute-start.11) | collective-permute-done | bytes 32800 | tf_op jit(solution)/shard_map/ppermute | solution.py:362
  43.7 1.6 %collective-permute-done.10 = f32[64,128]{1,0:T(8,128)S(1)} collective-permute-done((f32[64,128]{1,0:T(8,128)S(1)}, f32[64,128]{1,0:T(8,128)S(1)}, u32[]{:S(2)}, u32[]{:S(2)}) %collective-permute-start.10) | collective-permute-done | bytes 32800 | tf_op jit(solution)/shard_map/ppermute | solution.py:362
  45.3 3.1 %collective-permute-start.15 = (f32[64,128]{1,0:T(8,128)S(1)}, f32[64,128]{1,0:T(8,128)S(1)}, u32[]{:S(2)}, u32[]{:S(2)}) collective-permute-start(f32[64,128]{1,0:T(8,128)S(1)} %add_add_fusion.1), channel_id=1, source_target_pairs={{0,200},{4,204},{8,192},{12,196},{16,216},{20,220},{24,208},{28,21... | collective-permute-start | bytes 98312 | tf_op jit(solution)/shard_map/ppermute | solution.py:362
  48.3 2.0 %collective-permute-start.14 = (f32[64,128]{1,0:T(8,128)S(1)}, f32[64,128]{1,0:T(8,128)S(1)}, u32[]{:S(2)}, u32[]{:S(2)}) collective-permute-start(f32[64,128]{1,0:T(8,128)S(1)} %add_add_fusion.1), channel_id=1, source_target_pairs={{0,136},{4,140},{8,128},{12,132},{16,152},{20,156},{24,144},{28,14... | collective-permute-start | bytes 98312 | tf_op jit(solution)/shard_map/ppermute | solution.py:362
  50.3 0.0 collective-permute-start.13
  50.3 0.0 collective-permute-done.15
  50.3 2.9 %collective-permute-done.14 = f32[64,128]{1,0:T(8,128)S(1)} collective-permute-done((f32[64,128]{1,0:T(8,128)S(1)}, f32[64,128]{1,0:T(8,128)S(1)}, u32[]{:S(2)}, u32[]{:S(2)}) %collective-permute-start.14) | collective-permute-done | bytes 32800 | tf_op jit(solution)/shard_map/ppermute | solution.py:362
  53.2 0.2 collective-permute-done.13
  53.4 1.2 %collective-permute-start.16 = (f32[64,128]{1,0:T(8,128)S(1)}, f32[64,128]{1,0:T(8,128)S(1)}, u32[]{:S(2)}, u32[]{:S(2)}) collective-permute-start(f32[64,128]{1,0:T(8,128)S(1)} %add_add_fusion), channel_id=1, source_target_pairs={{0,128},{16,144},{32,160},{48,176},{64,192},{80,208},{96,224},{112... | collective-permute-start | bytes 98312 | tf_op jit(solution)/shard_map/ppermute | solution.py:362
  54.6 0.9 %turn.1 = (f32[4,128,128]{2,1,0:T(8,128)}, f32[4,128,128]{2,1,0:T(8,128)}) custom-call(f32[2,4,128,128]{3,2,1,0:T(8,128)S(1)} %get-tuple-element.33.moments_ref), custom_call_target="tpu_custom_call" | custom-call | flops 1000000 | bytes 1000000 | tf_op jit(solution)/shard_map/turn/pallas_call | solution.py:344
  55.5 1.9 %collective-permute-done.16 = f32[64,128]{1,0:T(8,128)S(1)} collective-permute-done((f32[64,128]{1,0:T(8,128)S(1)}, f32[64,128]{1,0:T(8,128)S(1)}, u32[]{:S(2)}, u32[]{:S(2)}) %collective-permute-start.16) | collective-permute-done | bytes 32800 | tf_op jit(solution)/shard_map/ppermute | solution.py:362
  57.4 6.2 %collective-permute-start.17 = (f32[64,128]{1,0:T(8,128)S(1)}, f32[64,128]{1,0:T(8,128)S(1)}, u32[]{:S(2)}, u32[]{:S(2)}) collective-permute-start(f32[64,128]{1,0:T(8,128)S(1)} %add.55), channel_id=1, source_target_pairs={{0,4},{4,0},{8,12},{12,8},{1,5},{5,1},{9,13},{13,9},{2,6},{6,2},{1... | collective-permute-start | bytes 98312 | tf_op jit(solution)/shard_map/ppermute | solution.py:362
  63.6 0.9 %collective-permute-done.17 = f32[64,128]{1,0:T(8,128)S(1)} collective-permute-done((f32[64,128]{1,0:T(8,128)S(1)}, f32[64,128]{1,0:T(8,128)S(1)}, u32[]{:S(2)}, u32[]{:S(2)}) %collective-permute-start.17) | collective-permute-done | bytes 32800 | tf_op jit(solution)/shard_map/ppermute | solution.py:362
  64.5 0.1 slice_bitcast_fusion.1
  64.6 0.7 %pad_maximum_fusion = f32[2,2,64,64]{3,2,1,0:T(8,128)} fusion(f32[1,2,64,64]{3,2,1,0:T(8,128)S(1)} %maximum_bitcast_fusion.1, f32[1,2,64,64]{3,2,1,0:T(8,128)S(1)} %maximum_bitcast_fusion), kind=kLoop, calls=%fused_computation | loop fusion | flops 16384 | bytes 131072 | tf_op jit(solution)/shard_map/stack | solution.py:476
  (17 shorter events, 0.1 us)
Async XLA Ops:
  0.6 9.0 %copy-start.1 = (f32[8]{0:T(128)S(1)}, f32[8]{0:T(128)}, u32[]{:S(2)}) copy-start(f32[8]{0:T(128)} %gain_ref.1) | copy-start | bytes 100
  0.6 8.9 %copy-start = (f32[8]{0:T(128)S(1)}, f32[8]{0:T(128)}, u32[]{:S(2)}) copy-start(f32[8]{0:T(128)} %eps_ref.1) | copy-start | bytes 100
  2.8 10.1 %collective-permute-start.1 = (bf16[192,128]{1,0:T(8,128)(2,1)S(1)}, bf16[192,128]{1,0:T(8,128)(2,1)S(1)}, u32[]{:S(2)}, u32[]{:S(2)}) collective-permute-start(bf16[192,128]{1,0:T(8,128)(2,1)S(1)} %get-tuple-element.22), channel_id=1, source_target_pairs={{0,51},{1,50},{2,49},{3,48},{16,35},{17,34},{18,33},{19,32},{32,19... | collective-permute-start | bytes 147464 | tf_op jit(solution)/shard_map/ppermute | solution.py:362
  8.6 4.3 %collective-permute-start = (bf16[192,128]{1,0:T(8,128)(2,1)S(1)}, bf16[192,128]{1,0:T(8,128)(2,1)S(1)}, u32[]{:S(2)}, u32[]{:S(2)}) collective-permute-start(bf16[192,128]{1,0:T(8,128)(2,1)S(1)} %get-tuple-element.21.first_ref), channel_id=1, source_target_pairs={{0,17},{1,16},{2,19},{3,18},{16,1},{17,0},{18,3},{19,2},{32,49},{3... | collective-permute-start | bytes 147464 | tf_op jit(solution)/shard_map/ppermute | solution.py:362
  8.6 4.3 %collective-permute-start.2 = (bf16[16,128]{1,0:T(8,128)(2,1)S(1)}, bf16[16,128]{1,0:T(8,128)(2,1)S(1)}, u32[]{:S(2)}, u32[]{:S(2)}) collective-permute-start(bf16[16,128]{1,0:T(8,128)(2,1)S(1)} %slice.47), channel_id=1, source_target_pairs={{0,32},{16,48},{32,0},{48,16},{64,96},{80,112},{96,64},{112,80},{1... | collective-permute-start | bytes 12296 | tf_op jit(solution)/shard_map/ppermute | solution.py:362
  12.9 12.3 %collective-permute-start.3 = (bf16[176,128]{1,0:T(8,128)(2,1)S(1)}, bf16[176,128]{1,0:T(8,128)(2,1)S(1)}, u32[]{:S(2)}, u32[]{:S(2)}) collective-permute-start(bf16[176,128]{1,0:T(8,128)(2,1)S(1)} %get-tuple-element.25), channel_id=1, source_target_pairs={{0,68},{4,64},{8,76},{12,72},{16,84},{20,80},{24,92},{28,88},{32,1... | collective-permute-start | bytes 135176 | tf_op jit(solution)/shard_map/ppermute | solution.py:362
  16.3 8.9 %collective-permute-start.5 = (bf16[16,128]{1,0:T(8,128)(2,1)S(1)}, bf16[16,128]{1,0:T(8,128)(2,1)S(1)}, u32[]{:S(2)}, u32[]{:S(2)}) collective-permute-start(bf16[16,128]{1,0:T(8,128)(2,1)S(1)} %slice.48), channel_id=1, source_target_pairs={{0,192},{16,208},{32,224},{48,240},{64,128},{80,144},{96,160},{112... | collective-permute-start | bytes 12296 | tf_op jit(solution)/shard_map/ppermute | solution.py:362
  18.9 6.3 %collective-permute-start.4 = (bf16[176,128]{1,0:T(8,128)(2,1)S(1)}, bf16[176,128]{1,0:T(8,128)(2,1)S(1)}, u32[]{:S(2)}, u32[]{:S(2)}) collective-permute-start(bf16[176,128]{1,0:T(8,128)(2,1)S(1)} %get-tuple-element.26), channel_id=1, source_target_pairs={{0,140},{4,136},{8,132},{12,128},{16,156},{20,152},{24,148},{28,14... | collective-permute-start | bytes 135176 | tf_op jit(solution)/shard_map/ppermute | solution.py:362
  30.2 1.4 %collective-permute-start.6 = (f32[64,128]{1,0:T(8,128)S(1)}, f32[64,128]{1,0:T(8,128)S(1)}, u32[]{:S(2)}, u32[]{:S(2)}) collective-permute-start(f32[64,128]{1,0:T(8,128)S(1)} %slice_select_fusion), channel_id=1, source_target_pairs={{0,4},{4,0},{8,12},{12,8},{1,5},{5,1},{9,13},{13,9},{2,6},{6,2},{1... | collective-permute-start | bytes 98312 | tf_op jit(solution)/shard_map/ppermute | solution.py:362
  31.6 4.3 %collective-permute-start.9 = (f32[64,128]{1,0:T(8,128)S(1)}, f32[64,128]{1,0:T(8,128)S(1)}, u32[]{:S(2)}, u32[]{:S(2)}) collective-permute-start(f32[64,128]{1,0:T(8,128)S(1)} %select_add_fusion), channel_id=1, source_target_pairs={{0,2},{1,3},{2,0},{3,1},{4,6},{5,7},{6,4},{7,5},{8,10},{9,11},{10,... | collective-permute-start | bytes 98312 | tf_op jit(solution)/shard_map/ppermute | solution.py:362
  32.7 4.4 %collective-permute-start.8 = (f32[64,128]{1,0:T(8,128)S(1)}, f32[64,128]{1,0:T(8,128)S(1)}, u32[]{:S(2)}, u32[]{:S(2)}) collective-permute-start(f32[64,128]{1,0:T(8,128)S(1)} %select_add_fusion), channel_id=1, source_target_pairs={{0,3},{1,2},{2,1},{3,0},{4,7},{5,6},{6,5},{7,4},{8,11},{9,10},{10,... | collective-permute-start | bytes 98312 | tf_op jit(solution)/shard_map/ppermute | solution.py:362
  35.4 2.8 %collective-permute-start.7 = (f32[64,128]{1,0:T(8,128)S(1)}, f32[64,128]{1,0:T(8,128)S(1)}, u32[]{:S(2)}, u32[]{:S(2)}) collective-permute-start(f32[64,128]{1,0:T(8,128)S(1)} %select_add_fusion), channel_id=1, source_target_pairs={{0,1},{1,0},{2,3},{3,2},{4,5},{5,4},{6,7},{7,6},{8,9},{9,8},{10,11... | collective-permute-start | bytes 98312 | tf_op jit(solution)/shard_map/ppermute | solution.py:362
  38.2 4.4 %collective-permute-start.12 = (f32[64,128]{1,0:T(8,128)S(1)}, f32[64,128]{1,0:T(8,128)S(1)}, u32[]{:S(2)}, u32[]{:S(2)}) collective-permute-start(f32[64,128]{1,0:T(8,128)S(1)} %add_add_fusion.2), channel_id=1, source_target_pairs={{0,32},{16,48},{32,0},{48,16},{64,96},{80,112},{96,64},{112,80},{1... | collective-permute-start | bytes 98312 | tf_op jit(solution)/shard_map/ppermute | solution.py:362
  39.7 4.0 %collective-permute-start.11 = (f32[64,128]{1,0:T(8,128)S(1)}, f32[64,128]{1,0:T(8,128)S(1)}, u32[]{:S(2)}, u32[]{:S(2)}) collective-permute-start(f32[64,128]{1,0:T(8,128)S(1)} %add_add_fusion.2), channel_id=1, source_target_pairs={{0,48},{16,32},{32,16},{48,0},{64,112},{80,96},{96,80},{112,64},{1... | collective-permute-start | bytes 98312 | tf_op jit(solution)/shard_map/ppermute | solution.py:362
  42.2 3.1 %collective-permute-start.10 = (f32[64,128]{1,0:T(8,128)S(1)}, f32[64,128]{1,0:T(8,128)S(1)}, u32[]{:S(2)}, u32[]{:S(2)}) collective-permute-start(f32[64,128]{1,0:T(8,128)S(1)} %add_add_fusion.2), channel_id=1, source_target_pairs={{0,16},{16,0},{32,48},{48,32},{64,80},{80,64},{96,112},{112,96},{1... | collective-permute-start | bytes 98312 | tf_op jit(solution)/shard_map/ppermute | solution.py:362
  45.3 5.1 %collective-permute-start.15 = (f32[64,128]{1,0:T(8,128)S(1)}, f32[64,128]{1,0:T(8,128)S(1)}, u32[]{:S(2)}, u32[]{:S(2)}) collective-permute-start(f32[64,128]{1,0:T(8,128)S(1)} %add_add_fusion.1), channel_id=1, source_target_pairs={{0,200},{4,204},{8,192},{12,196},{16,216},{20,220},{24,208},{28,21... | collective-permute-start | bytes 98312 | tf_op jit(solution)/shard_map/ppermute | solution.py:362
  48.3 4.9 %collective-permute-start.14 = (f32[64,128]{1,0:T(8,128)S(1)}, f32[64,128]{1,0:T(8,128)S(1)}, u32[]{:S(2)}, u32[]{:S(2)}) collective-permute-start(f32[64,128]{1,0:T(8,128)S(1)} %add_add_fusion.1), channel_id=1, source_target_pairs={{0,136},{4,140},{8,128},{12,132},{16,152},{20,156},{24,144},{28,14... | collective-permute-start | bytes 98312 | tf_op jit(solution)/shard_map/ppermute | solution.py:362
  50.3 3.1 %collective-permute-start.13 = (f32[64,128]{1,0:T(8,128)S(1)}, f32[64,128]{1,0:T(8,128)S(1)}, u32[]{:S(2)}, u32[]{:S(2)}) collective-permute-start(f32[64,128]{1,0:T(8,128)S(1)} %add_add_fusion.1), channel_id=1, source_target_pairs={{0,64},{16,80},{32,96},{48,112},{64,0},{80,16},{96,32},{112,48},{1... | collective-permute-start | bytes 98312 | tf_op jit(solution)/shard_map/ppermute | solution.py:362
  53.4 4.0 %collective-permute-start.16 = (f32[64,128]{1,0:T(8,128)S(1)}, f32[64,128]{1,0:T(8,128)S(1)}, u32[]{:S(2)}, u32[]{:S(2)}) collective-permute-start(f32[64,128]{1,0:T(8,128)S(1)} %add_add_fusion), channel_id=1, source_target_pairs={{0,128},{16,144},{32,160},{48,176},{64,192},{80,208},{96,224},{112... | collective-permute-start | bytes 98312 | tf_op jit(solution)/shard_map/ppermute | solution.py:362
  57.4 7.0 %collective-permute-start.17 = (f32[64,128]{1,0:T(8,128)S(1)}, f32[64,128]{1,0:T(8,128)S(1)}, u32[]{:S(2)}, u32[]{:S(2)}) collective-permute-start(f32[64,128]{1,0:T(8,128)S(1)} %add.55), channel_id=1, source_target_pairs={{0,4},{4,0},{8,12},{12,8},{1,5},{5,1},{9,13},{13,9},{2,6},{6,2},{1... | collective-permute-start | bytes 98312 | tf_op jit(solution)/shard_map/ppermute | solution.py:362

commit v10 on v9

--- a/solution.py
+++ b/solution.py
@@ -68,8 +68,8 @@
         pltpu.make_async_copy(probes_ref.at[pl.ds(base, to.shape[0])], to, sems.at[i])
         for i, (base, to) in enumerate(zip(bases, held))
     ]
-    edges = ((4, even_x), (8, jnp.logical_not(even_x)))
-    for i, step in enumerate((1, 3)):
+    edges = ((1, even_x), (8, jnp.logical_not(even_x)))
+    for i, step in enumerate((4, 3)):
         for j, (bit, high) in enumerate(edges):
             at = pl.multiple_of(jnp.where(high, LANES - 16, 0), 16)
             start = ((me ^ step) ^ bit) * SLAB
@@ -80,7 +80,7 @@
 
     def plane(slab, p, bit=0):
         z = jnp.clip(slab * SLAB + (p - 2), 0, depth - 1)
-        at = {0: 0, 4: 1, 8: 2}[bit]
+        at = {4: 1, 8: 2}.get(bit, 0)
         return held[at][z - bases[at]]
 
     def x_edge(values, high):
@@ -103,11 +103,11 @@
 
     for copy in copies:
         copy.wait()
-    sends = ((first_ref, whole[0], 1, even_y), (second_ref, whole[1], 3, jnp.logical_not(even_y)))
+    sends = ((first_ref, whole[0], 4, even_y), (second_ref, whole[1], 3, jnp.logical_not(even_y)))
     for send, (out_ref, scratch, step, high) in enumerate(sends):
         target = me ^ step
         for p in range(1, SLAB + 3):
-            scratch[(p - 1) * LANES : p * LANES] = plane(target, p).astype(jnp.float32)
+            scratch[(p - 1) * LANES : p * LANES] = plane(target, p, step).astype(jnp.float32)
         for at, start, count, deep in ((0, 0, SLAB + 2, 0), (FAR, LANES, SLAB, 1)):
             low = scratch[pl.ds(start + deep, count * CX, stride=CY), :]
             top = scratch[pl.ds(start + CY - 1 - deep, count * CX, stride=CY), :]
@@ -401,9 +401,9 @@
         name="slab",
     )(quad_index, probes.reshape(depth, cells_x * cells_y, columns))
 
-    inner = swap(first, dict(quad=1, sy=1))
+    inner = swap(first, dict(quad=4, sy=1))
     outer = swap(second, dict(quad=3, sy=3))
-    last = swap(first[PARTS:], dict(quad=2))
+    last = swap(first[PARTS:], dict(quad=7))
     ylo = jnp.where(even_y, outer, inner)[:CORNERS]
     yhi = jnp.where(even_y, inner, outer)[:CORNERS]
     to_near, to_beyond = pl.pallas_call(
@@ -416,9 +416,9 @@
         name="pack",
     )(inner, outer, last, first, third, fourth)
     beyond = swap(to_beyond, dict(quad=8, sx=3))
-    near = swap(to_near, dict(quad=4, sx=1))
+    near = swap(to_near, dict(quad=1, sx=1))
     parts = to_near[CORNERS:]
-    last = swap(parts, dict(quad=12))
+    last = swap(parts, dict(quad=9))
     parts = (parts + near[CORNERS:]) + (beyond[CORNERS:] + last)
     xlo = jnp.where(even_x, beyond, near)[:CORNERS]
     xhi = jnp.where(even_x, near, beyond)[:CORNERS]

time: 65.4 us -> 65 us (level)
  transfers between devices with their start and end apart: 18 -> 18, of which waited for: 13 -> 12; matrix products, arithmetic and copies ran while one was open for 0% -> 0% of each run, Pallas kernels for 5% -> 5%
where the time goes in v10:
time: 65 us; the launch traced here: 64.9 us
  starting transfers between devices  36.6 us (56%)
  waiting for transfers between devices  16.6 us (26%)
  Pallas kernels  9.31 us (14%)
  between operations  1.44 us (2%)
  other arithmetic  0.79 us (1%)
    ppermute x18, starting transfers between devices, swap(): return lax.ppermute(block, axes, pairs)  36.6 us
    ppermute x18, waiting for transfers between devices, swap(): return lax.ppermute(block, axes, pairs)  16.6 us
    pallas_call x1, Pallas kernels, body(): pl.pallas_call(moment_kernel, out_shape=[jax.ShapeDtypeStruct((2, SLAB, c...  4.87 us
    pallas_call x1, Pallas kernels, body(): pl.pallas_call(material_kernel, out_shape=[jax.ShapeDtypeStruct((3 * taps...  2.04 us
    pallas_call x1, Pallas kernels, body(): pl.pallas_call(slab_kernel, out_shape=[jax.ShapeDtypeStruct(shape, probes...  1.45 us
  transfers between devices with their start and end apart: 18, of which 12 were waited for; matrix products, arithmetic and copies ran while one was open for 0% of the time, Pallas kernels for 5%

profile of v10, /device:TPU:1, one launch (start us, length us, event | category | flops | bytes accessed | tf_op | source)
XLA Modules:
  0.0 64.9 jit_solution(5178010094000449784)
XLA Ops:
  0.6 0.0 copy-start.1
  0.6 0.0 copy-start
  1.3 1.5 %slab.1 = (bf16[8,128,128]{2,1,0:T(8,128)(2,1)S(1)}, bf16[192,128]{1,0:T(8,128)(2,1)S(1)}, bf16[192,128]{1,0:T(8,128)(2,1)S(1)}, bf16[96,128]{1,0:T(8,128)(2,1)S(1)}, bf16[96,128]{1,0:T(8,128)(2,1)S(1)}) custom-call(s32[1]{0:T(128)S(6)} %copy.9.quad_ref, bf16[64,128,128]{2,1,0:T(8,128)(2,1)} %bitcast.19), custom_call_target="tpu_custom_call" | custom-call | flops 10000000 | bytes 600000 | tf_op jit(solution)/shard_map/slab/pallas_call | solution.py:387
  2.8 5.8 %collective-permute-start.1 = (bf16[192,128]{1,0:T(8,128)(2,1)S(1)}, bf16[192,128]{1,0:T(8,128)(2,1)S(1)}, u32[]{:S(2)}, u32[]{:S(2)}) collective-permute-start(bf16[192,128]{1,0:T(8,128)(2,1)S(1)} %get-tuple-element.22), channel_id=1, source_target_pairs={{0,51},{1,50},{2,49},{3,48},{16,35},{17,34},{18,33},{19,32},{32,19... | collective-permute-start | bytes 147464 | tf_op jit(solution)/shard_map/ppermute | solution.py:362
  8.6 1.2 %collective-permute-start = (bf16[192,128]{1,0:T(8,128)(2,1)S(1)}, bf16[192,128]{1,0:T(8,128)(2,1)S(1)}, u32[]{:S(2)}, u32[]{:S(2)}) collective-permute-start(bf16[192,128]{1,0:T(8,128)(2,1)S(1)} %get-tuple-element.21.first_ref), channel_id=1, source_target_pairs={{0,65},{1,64},{2,67},{3,66},{16,81},{17,80},{18,83},{19,82},{32,97... | collective-permute-start | bytes 147464 | tf_op jit(solution)/shard_map/ppermute | solution.py:362
  9.8 0.3 collective-permute-start.2
  10.2 0.0 copy-done.1
  10.2 0.0 copy-done
  10.2 2.0 %material.1 = (f32[75,8,128]{2,1,0:T(8,128)S(1)}, bf16[256,1664]{1,0:T(8,128)(2,1)S(1)}) custom-call(f32[8]{0:T(128)S(1)} %copy-done, f32[8]{0:T(128)S(1)} %copy-done.1, s32[64,32,64]{2,1,0:T(8,128)} %bitcast.20, s32[64,32,64]{2,1,0:T(8,128)} %bitcast.21), custom_call_target="tpu_custom_call" | custom-call | flops 40000000 | bytes 1200000 | tf_op jit(solution)/shard_map/material/pallas_call | solution.py:428
  12.2 2.2 %collective-permute-done.2.last_ref = bf16[16,128]{1,0:T(8,128)(2,1)S(1)} collective-permute-done((bf16[16,128]{1,0:T(8,128)(2,1)S(1)}, bf16[16,128]{1,0:T(8,128)(2,1)S(1)}, u32[]{:S(2)}, u32[]{:S(2)}) %collective-permute-start.2) | collective-permute-done | bytes 4128 | tf_op jit(solution)/shard_map/ppermute | solution.py:362
  14.4 0.0 collective-permute-done.1.outer_ref
  14.4 0.0 collective-permute-done.inner_ref
  14.4 1.1 %collective-permute-start.3 = (bf16[176,128]{1,0:T(8,128)(2,1)S(1)}, bf16[176,128]{1,0:T(8,128)(2,1)S(1)}, u32[]{:S(2)}, u32[]{:S(2)}) collective-permute-start(bf16[176,128]{1,0:T(8,128)(2,1)S(1)} %get-tuple-element.25), channel_id=1, source_target_pairs={{0,20},{4,16},{8,28},{12,24},{16,4},{20,0},{24,12},{28,8},{32,52},... | collective-permute-start | bytes 135176 | tf_op jit(solution)/shard_map/ppermute | solution.py:362
  15.5 5.4 %collective-permute-start.5 = (bf16[16,128]{1,0:T(8,128)(2,1)S(1)}, bf16[16,128]{1,0:T(8,128)(2,1)S(1)}, u32[]{:S(2)}, u32[]{:S(2)}) collective-permute-start(bf16[16,128]{1,0:T(8,128)(2,1)S(1)} %slice.48), channel_id=1, source_target_pairs={{0,144},{16,128},{32,176},{48,160},{64,208},{80,192},{96,240},{112... | collective-permute-start | bytes 12296 | tf_op jit(solution)/shard_map/ppermute | solution.py:362
  21.0 1.6 %collective-permute-start.4 = (bf16[176,128]{1,0:T(8,128)(2,1)S(1)}, bf16[176,128]{1,0:T(8,128)(2,1)S(1)}, u32[]{:S(2)}, u32[]{:S(2)}) collective-permute-start(bf16[176,128]{1,0:T(8,128)(2,1)S(1)} %get-tuple-element.26), channel_id=1, source_target_pairs={{0,140},{4,136},{8,132},{12,128},{16,156},{20,152},{24,148},{28,14... | collective-permute-start | bytes 135176 | tf_op jit(solution)/shard_map/ppermute | solution.py:362
  22.6 4.0 %collective-permute-done.4 = bf16[176,128]{1,0:T(8,128)(2,1)S(1)} collective-permute-done((bf16[176,128]{1,0:T(8,128)(2,1)S(1)}, bf16[176,128]{1,0:T(8,128)(2,1)S(1)}, u32[]{:S(2)}, u32[]{:S(2)}) %collective-permute-start.4) | collective-permute-done | bytes 45088 | tf_op jit(solution)/shard_map/ppermute | solution.py:362
  26.6 0.0 collective-permute-done.3
  26.6 0.0 collective-permute-done.5
  26.6 4.9 %moments.1 = (f32[2,4,128,128]{3,2,1,0:T(8,128)S(1)}, f32[64,256]{1,0:T(8,128)S(1)}) custom-call(f32[1,128]{1,0:T(1,128)S(1)} %bitcast.18, f32[75,8,128]{2,1,0:T(8,128)S(1)} %get-tuple-element.27.material_ref, bf16[8,128,128]{2,1,0:T(8,128)(2,1)S(1)} %get-tuple-element.28.own_ref, bf16[160,128]{1,0:T(8,128)(2,1)S(1)} %get-tuple-element.40.ylo_ref, ...), custom_call_target="tpu_custom_call" | custom-call | flops 600000000 | bytes 3000000 | tf_op jit(solution)/shard_map/moments/pallas_call | solution.py:446
  31.5 0.1 collective-permute-start.6
  31.6 1.2 %collective-permute-done.6 = f32[64,128]{1,0:T(8,128)S(1)} collective-permute-done((f32[64,128]{1,0:T(8,128)S(1)}, f32[64,128]{1,0:T(8,128)S(1)}, u32[]{:S(2)}, u32[]{:S(2)}) %collective-permute-start.6) | collective-permute-done | bytes 32800 | tf_op jit(solution)/shard_map/ppermute | solution.py:362
  32.8 1.4 %collective-permute-start.9 = (f32[64,128]{1,0:T(8,128)S(1)}, f32[64,128]{1,0:T(8,128)S(1)}, u32[]{:S(2)}, u32[]{:S(2)}) collective-permute-start(f32[64,128]{1,0:T(8,128)S(1)} %select_add_fusion), channel_id=1, source_target_pairs={{0,2},{1,3},{2,0},{3,1},{4,6},{5,7},{6,4},{7,5},{8,10},{9,11},{10,... | collective-permute-start | bytes 98312 | tf_op jit(solution)/shard_map/ppermute | solution.py:362
  34.2 2.7 %collective-permute-start.8 = (f32[64,128]{1,0:T(8,128)S(1)}, f32[64,128]{1,0:T(8,128)S(1)}, u32[]{:S(2)}, u32[]{:S(2)}) collective-permute-start(f32[64,128]{1,0:T(8,128)S(1)} %select_add_fusion), channel_id=1, source_target_pairs={{0,3},{1,2},{2,1},{3,0},{4,7},{5,6},{6,5},{7,4},{8,11},{9,10},{10,... | collective-permute-start | bytes 98312 | tf_op jit(solution)/shard_map/ppermute | solution.py:362
  36.9 0.0 collective-permute-start.7
  36.9 0.3 collective-permute-done.9
  37.2 1.0 %collective-permute-done.8 = f32[64,128]{1,0:T(8,128)S(1)} collective-permute-done((f32[64,128]{1,0:T(8,128)S(1)}, f32[64,128]{1,0:T(8,128)S(1)}, u32[]{:S(2)}, u32[]{:S(2)}) %collective-permute-start.8) | collective-permute-done | bytes 32800 | tf_op jit(solution)/shard_map/ppermute | solution.py:362
  38.2 1.5 %collective-permute-done.7 = f32[64,128]{1,0:T(8,128)S(1)} collective-permute-done((f32[64,128]{1,0:T(8,128)S(1)}, f32[64,128]{1,0:T(8,128)S(1)}, u32[]{:S(2)}, u32[]{:S(2)}) %collective-permute-start.7) | collective-permute-done | bytes 32800 | tf_op jit(solution)/shard_map/ppermute | solution.py:362
  39.7 0.6 collective-permute-start.12
  40.3 2.5 %collective-permute-start.11 = (f32[64,128]{1,0:T(8,128)S(1)}, f32[64,128]{1,0:T(8,128)S(1)}, u32[]{:S(2)}, u32[]{:S(2)}) collective-permute-start(f32[64,128]{1,0:T(8,128)S(1)} %add_add_fusion.2), channel_id=1, source_target_pairs={{0,48},{16,32},{32,16},{48,0},{64,112},{80,96},{96,80},{112,64},{1... | collective-permute-start | bytes 98312 | tf_op jit(solution)/shard_map/ppermute | solution.py:362
  42.8 0.0 collective-permute-start.10
  42.8 1.3 %collective-permute-done.12 = f32[64,128]{1,0:T(8,128)S(1)} collective-permute-done((f32[64,128]{1,0:T(8,128)S(1)}, f32[64,128]{1,0:T(8,128)S(1)}, u32[]{:S(2)}, u32[]{:S(2)}) %collective-permute-start.12) | collective-permute-done | bytes 32800 | tf_op jit(solution)/shard_map/ppermute | solution.py:362
  44.1 0.3 collective-permute-done.11
  44.4 1.4 %collective-permute-done.10 = f32[64,128]{1,0:T(8,128)S(1)} collective-permute-done((f32[64,128]{1,0:T(8,128)S(1)}, f32[64,128]{1,0:T(8,128)S(1)}, u32[]{:S(2)}, u32[]{:S(2)}) %collective-permute-start.10) | collective-permute-done | bytes 32800 | tf_op jit(solution)/shard_map/ppermute | solution.py:362
  45.9 2.1 %collective-permute-start.15 = (f32[64,128]{1,0:T(8,128)S(1)}, f32[64,128]{1,0:T(8,128)S(1)}, u32[]{:S(2)}, u32[]{:S(2)}) collective-permute-start(f32[64,128]{1,0:T(8,128)S(1)} %add_add_fusion.1), channel_id=1, source_target_pairs={{0,200},{4,204},{8,192},{12,196},{16,216},{20,220},{24,208},{28,21... | collective-permute-start | bytes 98312 | tf_op jit(solution)/shard_map/ppermute | solution.py:362
  48.0 1.6 %collective-permute-start.14 = (f32[64,128]{1,0:T(8,128)S(1)}, f32[64,128]{1,0:T(8,128)S(1)}, u32[]{:S(2)}, u32[]{:S(2)}) collective-permute-start(f32[64,128]{1,0:T(8,128)S(1)} %add_add_fusion.1), channel_id=1, source_target_pairs={{0,136},{4,140},{8,128},{12,132},{16,152},{20,156},{24,144},{28,14... | collective-permute-start | bytes 98312 | tf_op jit(solution)/shard_map/ppermute | solution.py:362
  49.6 1.1 %collective-permute-start.13 = (f32[64,128]{1,0:T(8,128)S(1)}, f32[64,128]{1,0:T(8,128)S(1)}, u32[]{:S(2)}, u32[]{:S(2)}) collective-permute-start(f32[64,128]{1,0:T(8,128)S(1)} %add_add_fusion.1), channel_id=1, source_target_pairs={{0,64},{16,80},{32,96},{48,112},{64,0},{80,16},{96,32},{112,48},{1... | collective-permute-start | bytes 98312 | tf_op jit(solution)/shard_map/ppermute | solution.py:362
  50.6 0.0 collective-permute-done.15
  50.6 2.2 %collective-permute-done.14 = f32[64,128]{1,0:T(8,128)S(1)} collective-permute-done((f32[64,128]{1,0:T(8,128)S(1)}, f32[64,128]{1,0:T(8,128)S(1)}, u32[]{:S(2)}, u32[]{:S(2)}) %collective-permute-start.14) | collective-permute-done | bytes 32800 | tf_op jit(solution)/shard_map/ppermute | solution.py:362
  52.8 0.0 collective-permute-done.13
  52.8 3.7 %collective-permute-start.16 = (f32[64,128]{1,0:T(8,128)S(1)}, f32[64,128]{1,0:T(8,128)S(1)}, u32[]{:S(2)}, u32[]{:S(2)}) collective-permute-start(f32[64,128]{1,0:T(8,128)S(1)} %add_add_fusion), channel_id=1, source_target_pairs={{0,128},{16,144},{32,160},{48,176},{64,192},{80,208},{96,224},{112... | collective-permute-start | bytes 98312 | tf_op jit(solution)/shard_map/ppermute | solution.py:362
  56.5 0.9 %turn.1 = (f32[4,128,128]{2,1,0:T(8,128)}, f32[4,128,128]{2,1,0:T(8,128)}) custom-call(f32[2,4,128,128]{3,2,1,0:T(8,128)S(1)} %get-tuple-element.33.moments_ref), custom_call_target="tpu_custom_call" | custom-call | flops 1000000 | bytes 1000000 | tf_op jit(solution)/shard_map/turn/pallas_call | solution.py:344
  57.4 0.4 collective-permute-done.16
  57.8 5.4 %collective-permute-start.17 = (f32[64,128]{1,0:T(8,128)S(1)}, f32[64,128]{1,0:T(8,128)S(1)}, u32[]{:S(2)}, u32[]{:S(2)}) collective-permute-start(f32[64,128]{1,0:T(8,128)S(1)} %add.55), channel_id=1, source_target_pairs={{0,4},{4,0},{8,12},{12,8},{1,5},{5,1},{9,13},{13,9},{2,6},{6,2},{1... | collective-permute-start | bytes 98312 | tf_op jit(solution)/shard_map/ppermute | solution.py:362
  63.2 0.9 %collective-permute-done.17 = f32[64,128]{1,0:T(8,128)S(1)} collective-permute-done((f32[64,128]{1,0:T(8,128)S(1)}, f32[64,128]{1,0:T(8,128)S(1)}, u32[]{:S(2)}, u32[]{:S(2)}) %collective-permute-start.17) | collective-permute-done | bytes 32800 | tf_op jit(solution)/shard_map/ppermute | solution.py:362
  64.1 0.1 slice_bitcast_fusion.1
  64.2 0.7 %pad_maximum_fusion = f32[2,2,64,64]{3,2,1,0:T(8,128)} fusion(f32[1,2,64,64]{3,2,1,0:T(8,128)S(1)} %maximum_bitcast_fusion.1, f32[1,2,64,64]{3,2,1,0:T(8,128)S(1)} %maximum_bitcast_fusion), kind=kLoop, calls=%fused_computation | loop fusion | flops 16384 | bytes 131072 | tf_op jit(solution)/shard_map/stack | solution.py:476
  (17 shorter events, 0.1 us)
Async XLA Ops:
  0.6 9.6 %copy-start.1 = (f32[8]{0:T(128)S(1)}, f32[8]{0:T(128)}, u32[]{:S(2)}) copy-start(f32[8]{0:T(128)} %gain_ref.1) | copy-start | bytes 100
  0.6 9.5 %copy-start = (f32[8]{0:T(128)S(1)}, f32[8]{0:T(128)}, u32[]{:S(2)}) copy-start(f32[8]{0:T(128)} %eps_ref.1) | copy-start | bytes 100
  2.8 11.6 %collective-permute-start.1 = (bf16[192,128]{1,0:T(8,128)(2,1)S(1)}, bf16[192,128]{1,0:T(8,128)(2,1)S(1)}, u32[]{:S(2)}, u32[]{:S(2)}) collective-permute-start(bf16[192,128]{1,0:T(8,128)(2,1)S(1)} %get-tuple-element.22), channel_id=1, source_target_pairs={{0,51},{1,50},{2,49},{3,48},{16,35},{17,34},{18,33},{19,32},{32,19... | collective-permute-start | bytes 147464 | tf_op jit(solution)/shard_map/ppermute | solution.py:362
  8.6 5.8 %collective-permute-start = (bf16[192,128]{1,0:T(8,128)(2,1)S(1)}, bf16[192,128]{1,0:T(8,128)(2,1)S(1)}, u32[]{:S(2)}, u32[]{:S(2)}) collective-permute-start(bf16[192,128]{1,0:T(8,128)(2,1)S(1)} %get-tuple-element.21.first_ref), channel_id=1, source_target_pairs={{0,65},{1,64},{2,67},{3,66},{16,81},{17,80},{18,83},{19,82},{32,97... | collective-permute-start | bytes 147464 | tf_op jit(solution)/shard_map/ppermute | solution.py:362
  9.8 4.6 %collective-permute-start.2 = (bf16[16,128]{1,0:T(8,128)(2,1)S(1)}, bf16[16,128]{1,0:T(8,128)(2,1)S(1)}, u32[]{:S(2)}, u32[]{:S(2)}) collective-permute-start(bf16[16,128]{1,0:T(8,128)(2,1)S(1)} %slice.47), channel_id=1, source_target_pairs={{0,112},{16,96},{32,80},{48,64},{64,48},{80,32},{96,16},{112,0},{1... | collective-permute-start | bytes 12296 | tf_op jit(solution)/shard_map/ppermute | solution.py:362
  14.4 12.1 %collective-permute-start.3 = (bf16[176,128]{1,0:T(8,128)(2,1)S(1)}, bf16[176,128]{1,0:T(8,128)(2,1)S(1)}, u32[]{:S(2)}, u32[]{:S(2)}) collective-permute-start(bf16[176,128]{1,0:T(8,128)(2,1)S(1)} %get-tuple-element.25), channel_id=1, source_target_pairs={{0,20},{4,16},{8,28},{12,24},{16,4},{20,0},{24,12},{28,8},{32,52},... | collective-permute-start | bytes 135176 | tf_op jit(solution)/shard_map/ppermute | solution.py:362
  15.5 11.1 %collective-permute-start.5 = (bf16[16,128]{1,0:T(8,128)(2,1)S(1)}, bf16[16,128]{1,0:T(8,128)(2,1)S(1)}, u32[]{:S(2)}, u32[]{:S(2)}) collective-permute-start(bf16[16,128]{1,0:T(8,128)(2,1)S(1)} %slice.48), channel_id=1, source_target_pairs={{0,144},{16,128},{32,176},{48,160},{64,208},{80,192},{96,240},{112... | collective-permute-start | bytes 12296 | tf_op jit(solution)/shard_map/ppermute | solution.py:362
  21.0 5.6 %collective-permute-start.4 = (bf16[176,128]{1,0:T(8,128)(2,1)S(1)}, bf16[176,128]{1,0:T(8,128)(2,1)S(1)}, u32[]{:S(2)}, u32[]{:S(2)}) collective-permute-start(bf16[176,128]{1,0:T(8,128)(2,1)S(1)} %get-tuple-element.26), channel_id=1, source_target_pairs={{0,140},{4,136},{8,132},{12,128},{16,156},{20,152},{24,148},{28,14... | collective-permute-start | bytes 135176 | tf_op jit(solution)/shard_map/ppermute | solution.py:362
  31.5 1.3 %collective-permute-start.6 = (f32[64,128]{1,0:T(8,128)S(1)}, f32[64,128]{1,0:T(8,128)S(1)}, u32[]{:S(2)}, u32[]{:S(2)}) collective-permute-start(f32[64,128]{1,0:T(8,128)S(1)} %slice_select_fusion), channel_id=1, source_target_pairs={{0,4},{4,0},{8,12},{12,8},{1,5},{5,1},{9,13},{13,9},{2,6},{6,2},{1... | collective-permute-start | bytes 98312 | tf_op jit(solution)/shard_map/ppermute | solution.py:362
  32.8 4.4 %collective-permute-start.9 = (f32[64,128]{1,0:T(8,128)S(1)}, f32[64,128]{1,0:T(8,128)S(1)}, u32[]{:S(2)}, u32[]{:S(2)}) collective-permute-start(f32[64,128]{1,0:T(8,128)S(1)} %select_add_fusion), channel_id=1, source_target_pairs={{0,2},{1,3},{2,0},{3,1},{4,6},{5,7},{6,4},{7,5},{8,10},{9,11},{10,... | collective-permute-start | bytes 98312 | tf_op jit(solution)/shard_map/ppermute | solution.py:362
  34.2 4.0 %collective-permute-start.8 = (f32[64,128]{1,0:T(8,128)S(1)}, f32[64,128]{1,0:T(8,128)S(1)}, u32[]{:S(2)}, u32[]{:S(2)}) collective-permute-start(f32[64,128]{1,0:T(8,128)S(1)} %select_add_fusion), channel_id=1, source_target_pairs={{0,3},{1,2},{2,1},{3,0},{4,7},{5,6},{6,5},{7,4},{8,11},{9,10},{10,... | collective-permute-start | bytes 98312 | tf_op jit(solution)/shard_map/ppermute | solution.py:362
  36.9 2.8 %collective-permute-start.7 = (f32[64,128]{1,0:T(8,128)S(1)}, f32[64,128]{1,0:T(8,128)S(1)}, u32[]{:S(2)}, u32[]{:S(2)}) collective-permute-start(f32[64,128]{1,0:T(8,128)S(1)} %select_add_fusion), channel_id=1, source_target_pairs={{0,1},{1,0},{2,3},{3,2},{4,5},{5,4},{6,7},{7,6},{8,9},{9,8},{10,11... | collective-permute-start | bytes 98312 | tf_op jit(solution)/shard_map/ppermute | solution.py:362
  39.7 4.4 %collective-permute-start.12 = (f32[64,128]{1,0:T(8,128)S(1)}, f32[64,128]{1,0:T(8,128)S(1)}, u32[]{:S(2)}, u32[]{:S(2)}) collective-permute-start(f32[64,128]{1,0:T(8,128)S(1)} %add_add_fusion.2), channel_id=1, source_target_pairs={{0,32},{16,48},{32,0},{48,16},{64,96},{80,112},{96,64},{112,80},{1... | collective-permute-start | bytes 98312 | tf_op jit(solution)/shard_map/ppermute | solution.py:362
  40.3 4.1 %collective-permute-start.11 = (f32[64,128]{1,0:T(8,128)S(1)}, f32[64,128]{1,0:T(8,128)S(1)}, u32[]{:S(2)}, u32[]{:S(2)}) collective-permute-start(f32[64,128]{1,0:T(8,128)S(1)} %add_add_fusion.2), channel_id=1, source_target_pairs={{0,48},{16,32},{32,16},{48,0},{64,112},{80,96},{96,80},{112,64},{1... | collective-permute-start | bytes 98312 | tf_op jit(solution)/shard_map/ppermute | solution.py:362
  42.8 3.1 %collective-permute-start.10 = (f32[64,128]{1,0:T(8,128)S(1)}, f32[64,128]{1,0:T(8,128)S(1)}, u32[]{:S(2)}, u32[]{:S(2)}) collective-permute-start(f32[64,128]{1,0:T(8,128)S(1)} %add_add_fusion.2), channel_id=1, source_target_pairs={{0,16},{16,0},{32,48},{48,32},{64,80},{80,64},{96,112},{112,96},{1... | collective-permute-start | bytes 98312 | tf_op jit(solution)/shard_map/ppermute | solution.py:362
  45.9 4.8 %collective-permute-start.15 = (f32[64,128]{1,0:T(8,128)S(1)}, f32[64,128]{1,0:T(8,128)S(1)}, u32[]{:S(2)}, u32[]{:S(2)}) collective-permute-start(f32[64,128]{1,0:T(8,128)S(1)} %add_add_fusion.1), channel_id=1, source_target_pairs={{0,200},{4,204},{8,192},{12,196},{16,216},{20,220},{24,208},{28,21... | collective-permute-start | bytes 98312 | tf_op jit(solution)/shard_map/ppermute | solution.py:362
  48.0 4.9 %collective-permute-start.14 = (f32[64,128]{1,0:T(8,128)S(1)}, f32[64,128]{1,0:T(8,128)S(1)}, u32[]{:S(2)}, u32[]{:S(2)}) collective-permute-start(f32[64,128]{1,0:T(8,128)S(1)} %add_add_fusion.1), channel_id=1, source_target_pairs={{0,136},{4,140},{8,128},{12,132},{16,152},{20,156},{24,144},{28,14... | collective-permute-start | bytes 98312 | tf_op jit(solution)/shard_map/ppermute | solution.py:362
  49.6 3.3 %collective-permute-start.13 = (f32[64,128]{1,0:T(8,128)S(1)}, f32[64,128]{1,0:T(8,128)S(1)}, u32[]{:S(2)}, u32[]{:S(2)}) collective-permute-start(f32[64,128]{1,0:T(8,128)S(1)} %add_add_fusion.1), channel_id=1, source_target_pairs={{0,64},{16,80},{32,96},{48,112},{64,0},{80,16},{96,32},{112,48},{1... | collective-permute-start | bytes 98312 | tf_op jit(solution)/shard_map/ppermute | solution.py:362
  52.8 5.0 %collective-permute-start.16 = (f32[64,128]{1,0:T(8,128)S(1)}, f32[64,128]{1,0:T(8,128)S(1)}, u32[]{:S(2)}, u32[]{:S(2)}) collective-permute-start(f32[64,128]{1,0:T(8,128)S(1)} %add_add_fusion), channel_id=1, source_target_pairs={{0,128},{16,144},{32,160},{48,176},{64,192},{80,208},{96,224},{112... | collective-permute-start | bytes 98312 | tf_op jit(solution)/shard_map/ppermute | solution.py:362
  57.8 6.3 %collective-permute-start.17 = (f32[64,128]{1,0:T(8,128)S(1)}, f32[64,128]{1,0:T(8,128)S(1)}, u32[]{:S(2)}, u32[]{:S(2)}) collective-permute-start(f32[64,128]{1,0:T(8,128)S(1)} %add.55), channel_id=1, source_target_pairs={{0,4},{4,0},{8,12},{12,8},{1,5},{5,1},{9,13},{13,9},{2,6},{6,2},{1... | collective-permute-start | bytes 98312 | tf_op jit(solution)/shard_map/ppermute | solution.py:362

commit v11 on v8

--- a/solution.py
+++ b/solution.py
@@ -263,7 +263,7 @@
                 coef[4 * t + 2 * k + 1] += imag
         return carry
 
-    lax.fori_loop(0, QUAD // 2, one_pair, 0)
+    lax.fori_loop(0, QUAD // 2, one_pair, 0, unroll=2)
     for i in range(2 * len(TAPS)):
         real, imag = coef[2 * i], coef[2 * i + 1]
         real = real + pltpu.roll(real, SLAB, axis=0)

time: 65 us -> 65 us (level)
  no operation moved by 1% of the time
where the time goes in v11:
time: 65 us; the launch traced here: 64.9 us
  starting transfers between devices  39.3 us (60%)
  waiting for transfers between devices  13.9 us (21%)
  Pallas kernels  9.25 us (14%)
  between operations  1.45 us (2%)
  other arithmetic  0.82 us (1%)
    ppermute x18, starting transfers between devices, swap(): return lax.ppermute(block, axes, pairs)  39.3 us
    ppermute x18, waiting for transfers between devices, swap(): return lax.ppermute(block, axes, pairs)  13.9 us
    pallas_call x1, Pallas kernels, body(): pl.pallas_call(moment_kernel, out_shape=[jax.ShapeDtypeStruct((2, SLAB, c...  4.83 us
    pallas_call x1, Pallas kernels, body(): pl.pallas_call(material_kernel, out_shape=[jax.ShapeDtypeStruct((3 * taps...  2.04 us
    pallas_call x1, Pallas kernels, body(): pl.pallas_call(slab_kernel, out_shape=[jax.ShapeDtypeStruct(shape, probes...  1.45 us
  transfers between devices with their start and end apart: 18, of which 14 were waited for; matrix products, arithmetic and copies ran while one was open for 0% of the time, Pallas kernels for 5%

profile of v11, /device:TPU:1, one launch (start us, length us, event | category | flops | bytes accessed | tf_op | source)
XLA Modules:
  0.0 64.9 jit_solution(16538007619721339494)
XLA Ops:
  0.6 0.0 copy-start.1
  0.6 0.0 copy-start
  1.3 1.5 %slab.1 = (bf16[8,128,128]{2,1,0:T(8,128)(2,1)S(1)}, bf16[192,128]{1,0:T(8,128)(2,1)S(1)}, bf16[192,128]{1,0:T(8,128)(2,1)S(1)}, bf16[96,128]{1,0:T(8,128)(2,1)S(1)}, bf16[96,128]{1,0:T(8,128)(2,1)S(1)}) custom-call(s32[1]{0:T(128)S(6)} %copy.13.quad_ref, bf16[64,128,128]{2,1,0:T(8,128)(2,1)} %bitcast.29), custom_call_target="tpu_custom_call" | custom-call | flops 10000000 | bytes 600000 | tf_op jit(solution)/shard_map/slab/pallas_call | solution.py:368
  2.8 5.8 %collective-permute-start.1 = (bf16[192,128]{1,0:T(8,128)(2,1)S(1)}, bf16[192,128]{1,0:T(8,128)(2,1)S(1)}, u32[]{:S(2)}, u32[]{:S(2)}) collective-permute-start(bf16[192,128]{1,0:T(8,128)(2,1)S(1)} %get-tuple-element.20), channel_id=1, source_target_pairs={{0,51},{1,50},{2,49},{3,48},{16,35},{17,34},{18,33},{19,32},{32,19... | collective-permute-start | bytes 147464 | tf_op jit(solution)/shard_map/ppermute | solution.py:343
  8.6 0.0 collective-permute-start
  8.6 1.0 %collective-permute-start.2 = (bf16[16,128]{1,0:T(8,128)(2,1)S(1)}, bf16[16,128]{1,0:T(8,128)(2,1)S(1)}, u32[]{:S(2)}, u32[]{:S(2)}) collective-permute-start(bf16[16,128]{1,0:T(8,128)(2,1)S(1)} %slice.62), channel_id=1, source_target_pairs={{0,32},{16,48},{32,0},{48,16},{64,96},{80,112},{96,64},{112,80},{1... | collective-permute-start | bytes 12296 | tf_op jit(solution)/shard_map/ppermute | solution.py:343
  9.6 0.0 copy-done.1
  9.6 0.0 copy-done
  9.6 2.0 %material.1 = (f32[75,8,128]{2,1,0:T(8,128)S(1)}, bf16[256,1664]{1,0:T(8,128)(2,1)S(1)}) custom-call(f32[8]{0:T(128)S(1)} %copy-done, f32[8]{0:T(128)S(1)} %copy-done.1, s32[64,32,64]{2,1,0:T(8,128)} %bitcast.30, s32[64,32,64]{2,1,0:T(8,128)} %bitcast.31), custom_call_target="tpu_custom_call" | custom-call | flops 40000000 | bytes 1200000 | tf_op jit(solution)/shard_map/material/pallas_call | solution.py:409
  11.6 0.0 collective-permute-done.1
  11.6 1.1 %collective-permute-done = bf16[192,128]{1,0:T(8,128)(2,1)S(1)} collective-permute-done((bf16[192,128]{1,0:T(8,128)(2,1)S(1)}, bf16[192,128]{1,0:T(8,128)(2,1)S(1)}, u32[]{:S(2)}, u32[]{:S(2)}) %collective-permute-start) | collective-permute-done | bytes 49184 | tf_op jit(solution)/shard_map/ppermute | solution.py:343
  12.8 0.1 collective-permute-done.2
  12.9 4.1 %collective-permute-start.5 = (bf16[16,128]{1,0:T(8,128)(2,1)S(1)}, bf16[16,128]{1,0:T(8,128)(2,1)S(1)}, u32[]{:S(2)}, u32[]{:S(2)}) collective-permute-start(bf16[16,128]{1,0:T(8,128)(2,1)S(1)} %fusion), channel_id=1, source_target_pairs={{0,192},{16,208},{32,224},{48,240},{64,128},{80,144},{96,160},{112... | collective-permute-start | bytes 12296 | tf_op jit(solution)/shard_map/ppermute | solution.py:343
  17.0 1.3 %collective-permute-start.3 = (bf16[176,128]{1,0:T(8,128)(2,1)S(1)}, bf16[176,128]{1,0:T(8,128)(2,1)S(1)}, u32[]{:S(2)}, u32[]{:S(2)}) collective-permute-start(bf16[176,128]{1,0:T(8,128)(2,1)S(1)} %get-tuple-element.49), channel_id=1, source_target_pairs={{0,68},{4,64},{8,76},{12,72},{16,84},{20,80},{24,92},{28,88},{32,1... | collective-permute-start | bytes 135176 | tf_op jit(solution)/shard_map/ppermute | solution.py:343
  18.3 3.6 %collective-permute-start.4 = (bf16[176,128]{1,0:T(8,128)(2,1)S(1)}, bf16[176,128]{1,0:T(8,128)(2,1)S(1)}, u32[]{:S(2)}, u32[]{:S(2)}) collective-permute-start(bf16[176,128]{1,0:T(8,128)(2,1)S(1)} %get-tuple-element.50), channel_id=1, source_target_pairs={{0,140},{4,136},{8,132},{12,128},{16,156},{20,152},{24,148},{28,14... | collective-permute-start | bytes 135176 | tf_op jit(solution)/shard_map/ppermute | solution.py:343
  21.9 0.0 collective-permute-done.3
  21.9 2.1 %collective-permute-done.4 = bf16[176,128]{1,0:T(8,128)(2,1)S(1)} collective-permute-done((bf16[176,128]{1,0:T(8,128)(2,1)S(1)}, bf16[176,128]{1,0:T(8,128)(2,1)S(1)}, u32[]{:S(2)}, u32[]{:S(2)}) %collective-permute-start.4) | collective-permute-done | bytes 45088 | tf_op jit(solution)/shard_map/ppermute | solution.py:343
  24.0 0.0 collective-permute-done.5
  24.0 4.8 %moments.1 = (f32[2,4,128,128]{3,2,1,0:T(8,128)S(1)}, f32[64,256]{1,0:T(8,128)S(1)}) custom-call(f32[1,128]{1,0:T(1,128)S(1)} %bitcast.28, f32[75,8,128]{2,1,0:T(8,128)S(1)} %get-tuple-element.23.material_ref, bf16[8,128,128]{2,1,0:T(8,128)(2,1)S(1)} %get-tuple-element.24.own_ref, bf16[160,128]{1,0:T(8,128)(2,1)S(1)} %get-tuple-element.36.ylo_ref, ...), custom_call_target="tpu_custom_call" | custom-call | flops 600000000 | bytes 3000000 | tf_op jit(solution)/shard_map/moments/pallas_call | solution.py:427
  28.9 2.2 %collective-permute-start.6 = (f32[64,128]{1,0:T(8,128)S(1)}, f32[64,128]{1,0:T(8,128)S(1)}, u32[]{:S(2)}, u32[]{:S(2)}) collective-permute-start(f32[64,128]{1,0:T(8,128)S(1)} %slice_select_fusion), channel_id=1, source_target_pairs={{0,4},{4,0},{8,12},{12,8},{1,5},{5,1},{9,13},{13,9},{2,6},{6,2},{1... | collective-permute-start | bytes 98312 | tf_op jit(solution)/shard_map/ppermute | solution.py:343
  31.1 0.9 %collective-permute-done.6 = f32[64,128]{1,0:T(8,128)S(1)} collective-permute-done((f32[64,128]{1,0:T(8,128)S(1)}, f32[64,128]{1,0:T(8,128)S(1)}, u32[]{:S(2)}, u32[]{:S(2)}) %collective-permute-start.6) | collective-permute-done | bytes 32800 | tf_op jit(solution)/shard_map/ppermute | solution.py:343
  32.0 1.0 %collective-permute-start.9 = (f32[64,128]{1,0:T(8,128)S(1)}, f32[64,128]{1,0:T(8,128)S(1)}, u32[]{:S(2)}, u32[]{:S(2)}) collective-permute-start(f32[64,128]{1,0:T(8,128)S(1)} %select_add_fusion), channel_id=1, source_target_pairs={{0,2},{1,3},{2,0},{3,1},{4,6},{5,7},{6,4},{7,5},{8,10},{9,11},{10,... | collective-permute-start | bytes 98312 | tf_op jit(solution)/shard_map/ppermute | solution.py:343
  33.0 2.7 %collective-permute-start.8 = (f32[64,128]{1,0:T(8,128)S(1)}, f32[64,128]{1,0:T(8,128)S(1)}, u32[]{:S(2)}, u32[]{:S(2)}) collective-permute-start(f32[64,128]{1,0:T(8,128)S(1)} %select_add_fusion), channel_id=1, source_target_pairs={{0,3},{1,2},{2,1},{3,0},{4,7},{5,6},{6,5},{7,4},{8,11},{9,10},{10,... | collective-permute-start | bytes 98312 | tf_op jit(solution)/shard_map/ppermute | solution.py:343
  35.8 0.0 collective-permute-start.7
  35.8 0.5 collective-permute-done.9
  36.3 1.2 %collective-permute-done.8 = f32[64,128]{1,0:T(8,128)S(1)} collective-permute-done((f32[64,128]{1,0:T(8,128)S(1)}, f32[64,128]{1,0:T(8,128)S(1)}, u32[]{:S(2)}, u32[]{:S(2)}) %collective-permute-start.8) | collective-permute-done | bytes 32800 | tf_op jit(solution)/shard_map/ppermute | solution.py:343
  37.5 1.1 %collective-permute-done.7 = f32[64,128]{1,0:T(8,128)S(1)} collective-permute-done((f32[64,128]{1,0:T(8,128)S(1)}, f32[64,128]{1,0:T(8,128)S(1)}, u32[]{:S(2)}, u32[]{:S(2)}) %collective-permute-start.7) | collective-permute-done | bytes 32800 | tf_op jit(solution)/shard_map/ppermute | solution.py:343
  38.6 1.5 %collective-permute-start.12 = (f32[64,128]{1,0:T(8,128)S(1)}, f32[64,128]{1,0:T(8,128)S(1)}, u32[]{:S(2)}, u32[]{:S(2)}) collective-permute-start(f32[64,128]{1,0:T(8,128)S(1)} %add_add_fusion.2), channel_id=1, source_target_pairs={{0,32},{16,48},{32,0},{48,16},{64,96},{80,112},{96,64},{112,80},{1... | collective-permute-start | bytes 98312 | tf_op jit(solution)/shard_map/ppermute | solution.py:343
  40.1 2.5 %collective-permute-start.11 = (f32[64,128]{1,0:T(8,128)S(1)}, f32[64,128]{1,0:T(8,128)S(1)}, u32[]{:S(2)}, u32[]{:S(2)}) collective-permute-start(f32[64,128]{1,0:T(8,128)S(1)} %add_add_fusion.2), channel_id=1, source_target_pairs={{0,48},{16,32},{32,16},{48,0},{64,112},{80,96},{96,80},{112,64},{1... | collective-permute-start | bytes 98312 | tf_op jit(solution)/shard_map/ppermute | solution.py:343
  42.6 0.0 collective-permute-start.10
  42.6 0.3 collective-permute-done.12
  42.9 1.1 %collective-permute-done.11 = f32[64,128]{1,0:T(8,128)S(1)} collective-permute-done((f32[64,128]{1,0:T(8,128)S(1)}, f32[64,128]{1,0:T(8,128)S(1)}, u32[]{:S(2)}, u32[]{:S(2)}) %collective-permute-start.11) | collective-permute-done | bytes 32800 | tf_op jit(solution)/shard_map/ppermute | solution.py:343
  44.1 1.6 %collective-permute-done.10 = f32[64,128]{1,0:T(8,128)S(1)} collective-permute-done((f32[64,128]{1,0:T(8,128)S(1)}, f32[64,128]{1,0:T(8,128)S(1)}, u32[]{:S(2)}, u32[]{:S(2)}) %collective-permute-start.10) | collective-permute-done | bytes 32800 | tf_op jit(solution)/shard_map/ppermute | solution.py:343
  45.6 2.2 %collective-permute-start.15 = (f32[64,128]{1,0:T(8,128)S(1)}, f32[64,128]{1,0:T(8,128)S(1)}, u32[]{:S(2)}, u32[]{:S(2)}) collective-permute-start(f32[64,128]{1,0:T(8,128)S(1)} %add_add_fusion.1), channel_id=1, source_target_pairs={{0,200},{4,204},{8,192},{12,196},{16,216},{20,220},{24,208},{28,21... | collective-permute-start | bytes 98312 | tf_op jit(solution)/shard_map/ppermute | solution.py:343
  47.8 2.4 %collective-permute-start.14 = (f32[64,128]{1,0:T(8,128)S(1)}, f32[64,128]{1,0:T(8,128)S(1)}, u32[]{:S(2)}, u32[]{:S(2)}) collective-permute-start(f32[64,128]{1,0:T(8,128)S(1)} %add_add_fusion.1), channel_id=1, source_target_pairs={{0,136},{4,140},{8,128},{12,132},{16,152},{20,156},{24,144},{28,14... | collective-permute-start | bytes 98312 | tf_op jit(solution)/shard_map/ppermute | solution.py:343
  50.2 0.2 collective-permute-start.13
  50.4 0.0 collective-permute-done.15
  50.4 2.3 %collective-permute-done.14 = f32[64,128]{1,0:T(8,128)S(1)} collective-permute-done((f32[64,128]{1,0:T(8,128)S(1)}, f32[64,128]{1,0:T(8,128)S(1)}, u32[]{:S(2)}, u32[]{:S(2)}) %collective-permute-start.14) | collective-permute-done | bytes 32800 | tf_op jit(solution)/shard_map/ppermute | solution.py:343
  52.7 0.3 collective-permute-done.13
  53.0 3.1 %collective-permute-start.16 = (f32[64,128]{1,0:T(8,128)S(1)}, f32[64,128]{1,0:T(8,128)S(1)}, u32[]{:S(2)}, u32[]{:S(2)}) collective-permute-start(f32[64,128]{1,0:T(8,128)S(1)} %add_add_fusion), channel_id=1, source_target_pairs={{0,128},{16,144},{32,160},{48,176},{64,192},{80,208},{96,224},{112... | collective-permute-start | bytes 98312 | tf_op jit(solution)/shard_map/ppermute | solution.py:343
  56.1 0.9 %turn.1 = (f32[4,128,128]{2,1,0:T(8,128)}, f32[4,128,128]{2,1,0:T(8,128)}) custom-call(f32[2,4,128,128]{3,2,1,0:T(8,128)S(1)} %get-tuple-element.29.moments_ref), custom_call_target="tpu_custom_call" | custom-call | flops 1000000 | bytes 1000000 | tf_op jit(solution)/shard_map/turn/pallas_call | solution.py:325
  57.0 0.5 collective-permute-done.16
  57.5 5.7 %collective-permute-start.17 = (f32[64,128]{1,0:T(8,128)S(1)}, f32[64,128]{1,0:T(8,128)S(1)}, u32[]{:S(2)}, u32[]{:S(2)}) collective-permute-start(f32[64,128]{1,0:T(8,128)S(1)} %add.71), channel_id=1, source_target_pairs={{0,4},{4,0},{8,12},{12,8},{1,5},{5,1},{9,13},{13,9},{2,6},{6,2},{1... | collective-permute-start | bytes 98312 | tf_op jit(solution)/shard_map/ppermute | solution.py:343
  63.1 0.9 %collective-permute-done.17 = f32[64,128]{1,0:T(8,128)S(1)} collective-permute-done((f32[64,128]{1,0:T(8,128)S(1)}, f32[64,128]{1,0:T(8,128)S(1)}, u32[]{:S(2)}, u32[]{:S(2)}) %collective-permute-start.17) | collective-permute-done | bytes 32800 | tf_op jit(solution)/shard_map/ppermute | solution.py:343
  64.0 0.1 slice_bitcast_fusion.3
  64.1 0.1 slice_bitcast_fusion.1
  64.2 0.7 %pad_maximum_fusion = f32[2,2,64,64]{3,2,1,0:T(8,128)} fusion(f32[1,2,64,64]{3,2,1,0:T(8,128)S(1)} %maximum_bitcast_fusion.1, f32[1,2,64,64]{3,2,1,0:T(8,128)S(1)} %maximum_bitcast_fusion), kind=kLoop, calls=%fused_computation | loop fusion | flops 16384 | bytes 131072 | tf_op jit(solution)/shard_map/stack | solution.py:457
  (23 shorter events, 0.2 us)
Async XLA Ops:
  0.6 9.0 %copy-start.1 = (f32[8]{0:T(128)S(1)}, f32[8]{0:T(128)}, u32[]{:S(2)}) copy-start(f32[8]{0:T(128)} %gain_ref.1) | copy-start | bytes 100
  0.6 8.9 %copy-start = (f32[8]{0:T(128)S(1)}, f32[8]{0:T(128)}, u32[]{:S(2)}) copy-start(f32[8]{0:T(128)} %eps_ref.1) | copy-start | bytes 100
  2.8 8.9 %collective-permute-start.1 = (bf16[192,128]{1,0:T(8,128)(2,1)S(1)}, bf16[192,128]{1,0:T(8,128)(2,1)S(1)}, u32[]{:S(2)}, u32[]{:S(2)}) collective-permute-start(bf16[192,128]{1,0:T(8,128)(2,1)S(1)} %get-tuple-element.20), channel_id=1, source_target_pairs={{0,51},{1,50},{2,49},{3,48},{16,35},{17,34},{18,33},{19,32},{32,19... | collective-permute-start | bytes 147464 | tf_op jit(solution)/shard_map/ppermute | solution.py:343
  8.6 4.1 %collective-permute-start = (bf16[192,128]{1,0:T(8,128)(2,1)S(1)}, bf16[192,128]{1,0:T(8,128)(2,1)S(1)}, u32[]{:S(2)}, u32[]{:S(2)}) collective-permute-start(bf16[192,128]{1,0:T(8,128)(2,1)S(1)} %get-tuple-element.19), channel_id=1, source_target_pairs={{0,17},{1,16},{2,19},{3,18},{16,1},{17,0},{18,3},{19,2},{32,49},{3... | collective-permute-start | bytes 147464 | tf_op jit(solution)/shard_map/ppermute | solution.py:343
  8.6 4.3 %collective-permute-start.2 = (bf16[16,128]{1,0:T(8,128)(2,1)S(1)}, bf16[16,128]{1,0:T(8,128)(2,1)S(1)}, u32[]{:S(2)}, u32[]{:S(2)}) collective-permute-start(bf16[16,128]{1,0:T(8,128)(2,1)S(1)} %slice.62), channel_id=1, source_target_pairs={{0,32},{16,48},{32,0},{48,16},{64,96},{80,112},{96,64},{112,80},{1... | collective-permute-start | bytes 12296 | tf_op jit(solution)/shard_map/ppermute | solution.py:343
  12.9 11.1 %collective-permute-start.5 = (bf16[16,128]{1,0:T(8,128)(2,1)S(1)}, bf16[16,128]{1,0:T(8,128)(2,1)S(1)}, u32[]{:S(2)}, u32[]{:S(2)}) collective-permute-start(bf16[16,128]{1,0:T(8,128)(2,1)S(1)} %fusion), channel_id=1, source_target_pairs={{0,192},{16,208},{32,224},{48,240},{64,128},{80,144},{96,160},{112... | collective-permute-start | bytes 12296 | tf_op jit(solution)/shard_map/ppermute | solution.py:343
  17.0 4.9 %collective-permute-start.3 = (bf16[176,128]{1,0:T(8,128)(2,1)S(1)}, bf16[176,128]{1,0:T(8,128)(2,1)S(1)}, u32[]{:S(2)}, u32[]{:S(2)}) collective-permute-start(bf16[176,128]{1,0:T(8,128)(2,1)S(1)} %get-tuple-element.49), channel_id=1, source_target_pairs={{0,68},{4,64},{8,76},{12,72},{16,84},{20,80},{24,92},{28,88},{32,1... | collective-permute-start | bytes 135176 | tf_op jit(solution)/shard_map/ppermute | solution.py:343
  18.3 5.7 %collective-permute-start.4 = (bf16[176,128]{1,0:T(8,128)(2,1)S(1)}, bf16[176,128]{1,0:T(8,128)(2,1)S(1)}, u32[]{:S(2)}, u32[]{:S(2)}) collective-permute-start(bf16[176,128]{1,0:T(8,128)(2,1)S(1)} %get-tuple-element.50), channel_id=1, source_target_pairs={{0,140},{4,136},{8,132},{12,128},{16,156},{20,152},{24,148},{28,14... | collective-permute-start | bytes 135176 | tf_op jit(solution)/shard_map/ppermute | solution.py:343
  28.9 3.1 %collective-permute-start.6 = (f32[64,128]{1,0:T(8,128)S(1)}, f32[64,128]{1,0:T(8,128)S(1)}, u32[]{:S(2)}, u32[]{:S(2)}) collective-permute-start(f32[64,128]{1,0:T(8,128)S(1)} %slice_select_fusion), channel_id=1, source_target_pairs={{0,4},{4,0},{8,12},{12,8},{1,5},{5,1},{9,13},{13,9},{2,6},{6,2},{1... | collective-permute-start | bytes 98312 | tf_op jit(solution)/shard_map/ppermute | solution.py:343
  32.0 4.3 %collective-permute-start.9 = (f32[64,128]{1,0:T(8,128)S(1)}, f32[64,128]{1,0:T(8,128)S(1)}, u32[]{:S(2)}, u32[]{:S(2)}) collective-permute-start(f32[64,128]{1,0:T(8,128)S(1)} %select_add_fusion), channel_id=1, source_target_pairs={{0,2},{1,3},{2,0},{3,1},{4,6},{5,7},{6,4},{7,5},{8,10},{9,11},{10,... | collective-permute-start | bytes 98312 | tf_op jit(solution)/shard_map/ppermute | solution.py:343
  33.0 4.4 %collective-permute-start.8 = (f32[64,128]{1,0:T(8,128)S(1)}, f32[64,128]{1,0:T(8,128)S(1)}, u32[]{:S(2)}, u32[]{:S(2)}) collective-permute-start(f32[64,128]{1,0:T(8,128)S(1)} %select_add_fusion), channel_id=1, source_target_pairs={{0,3},{1,2},{2,1},{3,0},{4,7},{5,6},{6,5},{7,4},{8,11},{9,10},{10,... | collective-permute-start | bytes 98312 | tf_op jit(solution)/shard_map/ppermute | solution.py:343
  35.8 2.8 %collective-permute-start.7 = (f32[64,128]{1,0:T(8,128)S(1)}, f32[64,128]{1,0:T(8,128)S(1)}, u32[]{:S(2)}, u32[]{:S(2)}) collective-permute-start(f32[64,128]{1,0:T(8,128)S(1)} %select_add_fusion), channel_id=1, source_target_pairs={{0,1},{1,0},{2,3},{3,2},{4,5},{5,4},{6,7},{7,6},{8,9},{9,8},{10,11... | collective-permute-start | bytes 98312 | tf_op jit(solution)/shard_map/ppermute | solution.py:343
  38.6 4.4 %collective-permute-start.12 = (f32[64,128]{1,0:T(8,128)S(1)}, f32[64,128]{1,0:T(8,128)S(1)}, u32[]{:S(2)}, u32[]{:S(2)}) collective-permute-start(f32[64,128]{1,0:T(8,128)S(1)} %add_add_fusion.2), channel_id=1, source_target_pairs={{0,32},{16,48},{32,0},{48,16},{64,96},{80,112},{96,64},{112,80},{1... | collective-permute-start | bytes 98312 | tf_op jit(solution)/shard_map/ppermute | solution.py:343
  40.1 4.0 %collective-permute-start.11 = (f32[64,128]{1,0:T(8,128)S(1)}, f32[64,128]{1,0:T(8,128)S(1)}, u32[]{:S(2)}, u32[]{:S(2)}) collective-permute-start(f32[64,128]{1,0:T(8,128)S(1)} %add_add_fusion.2), channel_id=1, source_target_pairs={{0,48},{16,32},{32,16},{48,0},{64,112},{80,96},{96,80},{112,64},{1... | collective-permute-start | bytes 98312 | tf_op jit(solution)/shard_map/ppermute | solution.py:343
  42.6 3.1 %collective-permute-start.10 = (f32[64,128]{1,0:T(8,128)S(1)}, f32[64,128]{1,0:T(8,128)S(1)}, u32[]{:S(2)}, u32[]{:S(2)}) collective-permute-start(f32[64,128]{1,0:T(8,128)S(1)} %add_add_fusion.2), channel_id=1, source_target_pairs={{0,16},{16,0},{32,48},{48,32},{64,80},{80,64},{96,112},{112,96},{1... | collective-permute-start | bytes 98312 | tf_op jit(solution)/shard_map/ppermute | solution.py:343
  45.6 4.8 %collective-permute-start.15 = (f32[64,128]{1,0:T(8,128)S(1)}, f32[64,128]{1,0:T(8,128)S(1)}, u32[]{:S(2)}, u32[]{:S(2)}) collective-permute-start(f32[64,128]{1,0:T(8,128)S(1)} %add_add_fusion.1), channel_id=1, source_target_pairs={{0,200},{4,204},{8,192},{12,196},{16,216},{20,220},{24,208},{28,21... | collective-permute-start | bytes 98312 | tf_op jit(solution)/shard_map/ppermute | solution.py:343
  47.8 4.9 %collective-permute-start.14 = (f32[64,128]{1,0:T(8,128)S(1)}, f32[64,128]{1,0:T(8,128)S(1)}, u32[]{:S(2)}, u32[]{:S(2)}) collective-permute-start(f32[64,128]{1,0:T(8,128)S(1)} %add_add_fusion.1), channel_id=1, source_target_pairs={{0,136},{4,140},{8,128},{12,132},{16,152},{20,156},{24,144},{28,14... | collective-permute-start | bytes 98312 | tf_op jit(solution)/shard_map/ppermute | solution.py:343
  50.2 2.8 %collective-permute-start.13 = (f32[64,128]{1,0:T(8,128)S(1)}, f32[64,128]{1,0:T(8,128)S(1)}, u32[]{:S(2)}, u32[]{:S(2)}) collective-permute-start(f32[64,128]{1,0:T(8,128)S(1)} %add_add_fusion.1), channel_id=1, source_target_pairs={{0,64},{16,80},{32,96},{48,112},{64,0},{80,16},{96,32},{112,48},{1... | collective-permute-start | bytes 98312 | tf_op jit(solution)/shard_map/ppermute | solution.py:343
  53.0 4.5 %collective-permute-start.16 = (f32[64,128]{1,0:T(8,128)S(1)}, f32[64,128]{1,0:T(8,128)S(1)}, u32[]{:S(2)}, u32[]{:S(2)}) collective-permute-start(f32[64,128]{1,0:T(8,128)S(1)} %add_add_fusion), channel_id=1, source_target_pairs={{0,128},{16,144},{32,160},{48,176},{64,192},{80,208},{96,224},{112... | collective-permute-start | bytes 98312 | tf_op jit(solution)/shard_map/ppermute | solution.py:343
  57.5 6.5 %collective-permute-start.17 = (f32[64,128]{1,0:T(8,128)S(1)}, f32[64,128]{1,0:T(8,128)S(1)}, u32[]{:S(2)}, u32[]{:S(2)}) collective-permute-start(f32[64,128]{1,0:T(8,128)S(1)} %add.71), channel_id=1, source_target_pairs={{0,4},{4,0},{8,12},{12,8},{1,5},{5,1},{9,13},{13,9},{2,6},{6,2},{1... | collective-permute-start | bytes 98312 | tf_op jit(solution)/shard_map/ppermute | solution.py:343
